TPU v7x, 32 devices: a whole 2x2x4 slice. The times are simulated.
32 devices in a mesh: dp: 4 (over z), seq: 8 (over y, x, core).
Axes of the slice: x: 2, y: 2, z: 4, core: 2. Of those that a mesh axis runs over, the one named last changes fastest.
Arguments:
- inputs: bfloat16 [4, 4096, 1536], P('dp', 'seq'), may hold values from -6 to 6
- segments: int32 [4, 4096], P('dp'), may hold values from 0 to 3, as said below
- attn_gain: bfloat16 [1536], P(('dp', 'seq')), may hold values from 0.5 to 1.5
- query_weight: bfloat16 [1536, 1536], P(('dp', 'seq')), may hold values from -0.15625 to 0.15625
- key_weight: bfloat16 [1536, 1536], P(('dp', 'seq')), may hold values from -0.15625 to 0.15625
- value_weight: bfloat16 [1536, 1536], P(('dp', 'seq')), may hold values from -0.15625 to 0.15625
- output_weight: bfloat16 [1536, 1536], P(('dp', 'seq')), may hold values from -2.5 to 2.5
- persistent: bfloat16 [1536, 64], P(('dp', 'seq')), may hold values from -6 to 6
- memory_first: bfloat16 [1536, 384], P(('dp', 'seq')), may hold values from -0.625 to 0.625
- memory_second: bfloat16 [1536, 384], P(('dp', 'seq')), may hold values from -0.3125 to 0.3125
- rate_weight: bfloat16 [1536, 16], P(('dp', 'seq')), may hold values from -0.15625 to 0.15625
- decay_logit: float32 [16], replicated, may hold values from -4 to -1.4
- momentum_logit: float32 [16], replicated, may hold values from 0 to 2.2
- ffn_gain: bfloat16 [1536], P(('dp', 'seq')), may hold values from 0.5 to 1.5
- gate_weight: bfloat16 [1536, 4096], P(('dp', 'seq')), may hold values from -0.15625 to 0.15625
- up_weight: bfloat16 [1536, 4096], P(('dp', 'seq')), may hold values from -0.15625 to 0.15625
- down_weight: bfloat16 [4096, 1536], P(('dp', 'seq')), may hold values from -0.09375 to 0.09375
- cotangent: bfloat16 [4, 4096, 1536], P('dp', 'seq'), may hold values from -6 to 6
Outputs:
- result: bfloat16 [4, 4096, 1536], P('dp', 'seq')
- grad_inputs: bfloat16 [4, 4096, 1536], P('dp', 'seq')
- grad_attn_gain: float32 [1536], P(('dp', 'seq'))
- grad_query_weight: float32 [1536, 1536], P(('dp', 'seq'))
- grad_key_weight: float32 [1536, 1536], P(('dp', 'seq'))
- grad_value_weight: float32 [1536, 1536], P(('dp', 'seq'))
- grad_output_weight: float32 [1536, 1536], P(('dp', 'seq'))
- grad_persistent: float32 [1536, 64], P(('dp', 'seq'))
- grad_memory_first: float32 [1536, 384], P(('dp', 'seq'))
- grad_memory_second: float32 [1536, 384], P(('dp', 'seq'))
- grad_rate_weight: float32 [1536, 16], P(('dp', 'seq'))
- grad_decay_logit: float32 [16], replicated
- grad_momentum_logit: float32 [16], replicated
- grad_ffn_gain: float32 [1536], P(('dp', 'seq'))
- grad_gate_weight: float32 [1536, 4096], P(('dp', 'seq'))
- grad_up_weight: float32 [1536, 4096], P(('dp', 'seq'))
- grad_down_weight: float32 [4096, 1536], P(('dp', 'seq'))
Inputs may be any that keep to these rules, and one draw needn't show every extreme that they name: `segments`: ids never fall along a row and the first token of a row has id 0. In every row one document covers all tokens but some of the first 512 and some of the last 512; all other document boundaries lie inside those two blocks.
All inputs are finite; a program needn't handle non-finite values.
Results may differ from a plain program's by a relative error of at most 0.022.
Values may be sent and summed in bfloat16 or wider, within the bound.
No kernel may reach another device: no remote copies, remote signals or barrier semaphores. Data moves between devices by JAX's collectives and lax.ppermute only.
A program may use at most 576 MiB of HBM per device.

v0:
```python
import jax
import jax.numpy as jnp
from jax import lax
from jax.sharding import PartitionSpec as P

D = 1536
H = 16
HD = 96
MH = 384
NP = 64
GROUP = 512


HIGH = lax.Precision.HIGHEST
norm_epsilon = 1e-06
rate_numerator = 2.0
masked_score = -1e30


def from_behind(value, axis, steps):
    count = lax.axis_size(axis)
    leading, last = (max(0, -steps), min(count, count - steps))
    return lax.ppermute(value, axis, [(source, source + steps) for source in range(leading, last)])


def head_normed(values):
    return values * lax.rsqrt(jnp.mean(values * values, axis=-1, keepdims=True) + norm_epsilon)


def recall(first, second, probes):
    inner = jnp.einsum("chd,hdm->chm", probes, first, precision=HIGH)
    return jnp.einsum("chm,hdm->chd", jax.nn.silu(inner), second, precision=HIGH)


def mix_block(state_first, state_second, init_first, init_second, probe_values, retain_values):
    kept = retain_values[:, None, None]
    return kept * recall(state_first, state_second, probe_values) + (1.0 - kept) * recall(
        init_first, init_second, probe_values
    )


def memory_step(
    state, first_init, second_init, keys, values, rates, update_mask, carry_flag, decay, momentum
):
    base_first = carry_flag * state[0] + (1.0 - carry_flag) * first_init
    base_second = carry_flag * state[1] + (1.0 - carry_flag) * second_init
    weights = rates * update_mask[:, None]

    def inner_loss(first, second):
        error = recall(first, second, keys) - values
        return 0.5 * jnp.sum(weights[:, :, None] * error * error) / keys.shape[0]

    grad_first, grad_second = jax.grad(inner_loss, argnums=(0, 1))(base_first, base_second)
    speed_first = momentum[:, None, None] * carry_flag * state[2] - grad_first
    speed_second = momentum[:, None, None] * carry_flag * state[3] - grad_second
    keep = (1.0 - decay)[:, None, None]
    return jnp.stack(
        [
            keep * base_first + speed_first,
            keep * base_second + speed_second,
            speed_first,
            speed_second,
        ]
    )


def visible(ids):
    order = jnp.arange(GROUP)
    local = jnp.logical_and(order[None, :] <= order[:, None], ids[None, :] == ids[:, None])
    return jnp.concatenate([jnp.ones((GROUP, NP), bool), local, local], axis=1)


def norm_back(grad_normed, values, inverse, gain):
    normal = values * inverse
    scaled = grad_normed * gain
    grad_gain = jnp.sum(grad_normed * normal, axis=0)
    grad_values = inverse * (scaled - normal * jnp.mean(scaled * normal, axis=-1, keepdims=True))
    return (grad_values, grad_gain)


def matmul_rows(left, right):
    return jnp.einsum("cd,ce->de", left, right, preferred_element_type=jnp.float32)


def matmul_back(left, right):
    return jnp.einsum("ce,de->cd", left, right, preferred_element_type=jnp.float32)


def on_device(
    inputs,
    segments,
    attn_gain,
    query_weight,
    key_weight,
    value_weight,
    output_weight,
    persistent,
    memory_first,
    memory_second,
    rate_weight,
    decay_logit,
    momentum_logit,
    ffn_gain,
    gate_weight,
    up_weight,
    down_weight,
    cotangent,
):
    position = lax.axis_index("seq")
    chain = lax.axis_size("seq")
    scale = HD ** (-0.5)
    rate_scale = rate_numerator / MH
    width_all = NP + 2 * GROUP
    front = NP + GROUP

    def fetch_attention():
        fetched = (
            lax.all_gather(attn_gain, ("dp", "seq"), axis=0, tiled=True),
            lax.all_gather(query_weight, ("dp", "seq"), axis=0, tiled=True),
            lax.all_gather(key_weight, ("dp", "seq"), axis=0, tiled=True),
            lax.all_gather(value_weight, ("dp", "seq"), axis=0, tiled=True),
            lax.all_gather(output_weight, ("dp", "seq"), axis=0, tiled=True),
            lax.all_gather(persistent, ("dp", "seq"), axis=0, tiled=True),
            lax.all_gather(memory_first, ("dp", "seq"), axis=0, tiled=True),
            lax.all_gather(memory_second, ("dp", "seq"), axis=0, tiled=True),
            lax.all_gather(rate_weight, ("dp", "seq"), axis=0, tiled=True),
        )
        (
            gain_raw,
            w_query,
            w_key,
            w_value,
            w_output,
            persist_cols,
            first_flat,
            second_flat,
            w_rate,
        ) = fetched
        return (
            gain_raw.astype(jnp.float32),
            w_query,
            w_key,
            w_value,
            w_output,
            persist_cols,
            first_flat.astype(jnp.float32).reshape(H, HD, MH),
            second_flat.astype(jnp.float32).reshape(H, HD, MH),
            w_rate,
        )

    tokens = inputs[0].astype(jnp.float32)
    row_ids = segments[0]
    group_ids = lax.dynamic_slice_in_dim(row_ids, position * GROUP, GROUP)
    before = lax.dynamic_index_in_dim(row_ids, jnp.maximum(position * GROUP - 1, 0), keepdims=False)
    first_id = group_ids[0]
    last_id = group_ids[GROUP - 1]
    joined = jnp.logical_and(position > 0, first_id == before)
    carry_flag = jnp.logical_and(joined, first_id == last_id).astype(jnp.float32)
    retain = jnp.logical_and(joined, group_ids == first_id).astype(jnp.float32)
    update_mask = (group_ids == last_id).astype(jnp.float32)
    allowed = visible(group_ids)
    gain_one, w_query, w_key, w_value, w_output, persist_cols, first_init, second_init, w_rate = (
        fetch_attention()
    )
    inverse_one = lax.rsqrt(jnp.mean(tokens * tokens, axis=-1, keepdims=True) + norm_epsilon)
    normed = (tokens * inverse_one * gain_one).astype(jnp.bfloat16)
    query = jnp.dot(normed, w_query, preferred_element_type=jnp.float32)
    local_keys = jnp.dot(normed, w_key, preferred_element_type=jnp.float32)
    local_values = jnp.dot(normed, w_value, preferred_element_type=jnp.float32)
    rate_sigmoid = jax.nn.sigmoid(jnp.dot(normed, w_rate, preferred_element_type=jnp.float32))
    rates = rate_scale * rate_sigmoid
    probes, probe_pull = jax.vjp(head_normed, query.reshape(GROUP, H, HD))
    mem_keys, key_pull = jax.vjp(head_normed, local_keys.reshape(GROUP, H, HD))
    mem_values = local_values.reshape(GROUP, H, HD)
    decay = jax.nn.sigmoid(decay_logit)
    momentum = jax.nn.sigmoid(momentum_logit)

    def advance(
        state, init_first, init_second, keys, values, rate_values, decay_values, momentum_values
    ):
        return memory_step(
            state,
            init_first,
            init_second,
            keys,
            values,
            rate_values,
            update_mask,
            carry_flag,
            decay_values,
            momentum_values,
        )

    blank = jnp.zeros((4, H, HD, MH), jnp.float32)

    def forward_turn(turn, carry):
        message, saved = carry
        mine = position == turn
        saved = jnp.where(mine, message, saved)
        sent = lax.cond(
            mine,
            lambda: advance(
                message, first_init, second_init, mem_keys, mem_values, rates, decay, momentum
            ),
            lambda: message,
        )
        return (from_behind(sent.astype(jnp.bfloat16), "seq", 1).astype(sent.dtype), saved)

    unused, saved = lax.fori_loop(0, chain, forward_turn, (blank, blank))

    def recall_local(state_first, state_second, init_first, init_second, probe_values):
        return mix_block(state_first, state_second, init_first, init_second, probe_values, retain)

    recalled, recall_pull = jax.vjp(
        recall_local, saved[0], saved[1], first_init, second_init, probes
    )
    recalled = recalled.reshape(GROUP, D).astype(jnp.bfloat16)
    context = jnp.concatenate([persist_cols.T, recalled], axis=0)
    keys_all = jnp.concatenate(
        [jnp.dot(context, w_key, preferred_element_type=jnp.float32), local_keys], axis=0
    ).astype(jnp.bfloat16)
    values_all = jnp.concatenate(
        [jnp.dot(context, w_value, preferred_element_type=jnp.float32), local_values], axis=0
    ).astype(jnp.bfloat16)
    query_low = query.astype(jnp.bfloat16)

    def attention_scores():
        raw = (
            jnp.einsum(
                "qhd,khd->hqk",
                query_low.reshape(GROUP, H, HD),
                keys_all.reshape(width_all, H, HD),
                preferred_element_type=jnp.float32,
            )
            * scale
        )
        return jnp.where(allowed[None], raw, masked_score)

    scores = attention_scores()
    top = jnp.max(scores, axis=-1, keepdims=True)
    log_total = top + jnp.log(jnp.sum(jnp.exp(scores - top), axis=-1, keepdims=True))
    chances = jnp.exp(scores - log_total)
    mixed = jnp.einsum(
        "hqk,khd->qhd",
        chances.astype(jnp.bfloat16),
        values_all.reshape(width_all, H, HD),
        preferred_element_type=jnp.float32,
    ).reshape(GROUP, D)
    mixed_low = mixed.astype(jnp.bfloat16)
    middle = tokens + jnp.dot(mixed_low, w_output, preferred_element_type=jnp.float32)
    gain_raw, w_gate, w_up, w_down = (
        lax.all_gather(ffn_gain, ("dp", "seq"), axis=0, tiled=True),
        lax.all_gather(gate_weight, ("dp", "seq"), axis=0, tiled=True),
        lax.all_gather(up_weight, ("dp", "seq"), axis=0, tiled=True),
        lax.all_gather(down_weight, ("dp", "seq"), axis=0, tiled=True),
    )
    gain_two = gain_raw.astype(jnp.float32)
    inverse_two = lax.rsqrt(jnp.mean(middle * middle, axis=-1, keepdims=True) + norm_epsilon)
    normed_two = (middle * inverse_two * gain_two).astype(jnp.bfloat16)
    gate = jnp.dot(normed_two, w_gate, preferred_element_type=jnp.float32)
    up = jnp.dot(normed_two, w_up, preferred_element_type=jnp.float32)
    gate_sigmoid = jax.nn.sigmoid(gate)
    gate_silu = gate * gate_sigmoid
    hidden = (gate_silu * up).astype(jnp.bfloat16)
    result = (middle + jnp.dot(hidden, w_down, preferred_element_type=jnp.float32)).astype(
        jnp.bfloat16
    )
    grad_out = cotangent[0]
    grad_down_w = matmul_rows(hidden, grad_out)
    grad_hidden = matmul_back(grad_out, w_down)
    grad_gate = (grad_hidden * up * gate_sigmoid * (1.0 + gate * (1.0 - gate_sigmoid))).astype(
        jnp.bfloat16
    )
    grad_up = (grad_hidden * gate_silu).astype(jnp.bfloat16)
    grad_gate_w = matmul_rows(normed_two, grad_gate)
    grad_up_w = matmul_rows(normed_two, grad_up)
    grad_normed_two = matmul_back(grad_gate, w_gate) + matmul_back(grad_up, w_up)
    grad_middle_norm, grad_gain_two = norm_back(grad_normed_two, middle, inverse_two, gain_two)
    grad_middle = grad_out.astype(jnp.float32) + grad_middle_norm
    ffn_parts = (
        lax.psum_scatter(grad_gain_two, ("dp", "seq"), scatter_dimension=0, tiled=True),
        lax.psum_scatter(grad_gate_w, ("dp", "seq"), scatter_dimension=0, tiled=True),
        lax.psum_scatter(grad_up_w, ("dp", "seq"), scatter_dimension=0, tiled=True),
        lax.psum_scatter(grad_down_w, ("dp", "seq"), scatter_dimension=0, tiled=True),
    )
    gain_one, w_query, w_key, w_value, w_output, persist_cols, first_init, second_init, w_rate = (
        fetch_attention()
    )
    grad_attended = grad_middle.astype(jnp.bfloat16)
    grad_output_w = matmul_rows(mixed_low, grad_attended)
    grad_mixed = matmul_back(grad_attended, w_output).astype(jnp.bfloat16).reshape(GROUP, H, HD)
    chances = jnp.exp(attention_scores() - log_total)
    grad_values_all = jnp.einsum(
        "hqk,qhd->khd", chances.astype(jnp.bfloat16), grad_mixed, preferred_element_type=jnp.float32
    ).reshape(width_all, D)
    grad_chances = jnp.einsum(
        "qhd,khd->hqk",
        grad_mixed,
        values_all.reshape(width_all, H, HD),
        preferred_element_type=jnp.float32,
    )
    grad_scores = chances * (grad_chances - jnp.sum(chances * grad_chances, axis=-1, keepdims=True))
    grad_scores_low = grad_scores.astype(jnp.bfloat16)
    grad_query_att = (
        jnp.einsum(
            "hqk,khd->qhd",
            grad_scores_low,
            keys_all.reshape(width_all, H, HD),
            preferred_element_type=jnp.float32,
        ).reshape(GROUP, D)
        * scale
    )
    grad_keys_all = (
        jnp.einsum(
            "hqk,qhd->khd",
            grad_scores_low,
            query_low.reshape(GROUP, H, HD),
            preferred_element_type=jnp.float32,
        ).reshape(width_all, D)
        * scale
    )
    grad_context_keys = grad_keys_all[:front].astype(jnp.bfloat16)
    grad_context_values = grad_values_all[:front].astype(jnp.bfloat16)
    grad_context = matmul_back(grad_context_keys, w_key) + matmul_back(grad_context_values, w_value)
    grad_persist = grad_context[:NP].T
    grad_recalled = grad_context[NP:].reshape(GROUP, H, HD)
    grad_saved_first, grad_saved_second, grad_first_recall, grad_second_recall, grad_probes = (
        recall_pull(grad_recalled)
    )
    recall_state = jnp.stack(
        [
            grad_saved_first,
            grad_saved_second,
            jnp.zeros_like(grad_saved_first),
            jnp.zeros_like(grad_saved_second),
        ]
    )
    zero_kept = (
        jnp.zeros((H, HD, MH), jnp.float32),
        jnp.zeros((H, HD, MH), jnp.float32),
        jnp.zeros((GROUP, H, HD), jnp.float32),
        jnp.zeros((GROUP, H, HD), jnp.float32),
        jnp.zeros((GROUP, H), jnp.float32),
        jnp.zeros((H,), jnp.float32),
        jnp.zeros((H,), jnp.float32),
    )

    def backward_turn(count, carry):
        message, kept = carry
        mine = position == chain - 1 - count

        def pull():
            unused_state, pullback = jax.vjp(
                advance,
                saved,
                first_init,
                second_init,
                mem_keys,
                mem_values,
                rates,
                decay,
                momentum,
            )
            gradients = pullback(message)
            return (gradients[0] + recall_state, tuple(gradients[1:]))

        sent, kept = lax.cond(mine, pull, lambda: (message, kept))
        return (from_behind(sent.astype(jnp.bfloat16), "seq", -1).astype(sent.dtype), kept)

    unused, kept = lax.fori_loop(0, chain, backward_turn, (blank, zero_kept))
    (
        grad_first_init,
        grad_second_init,
        grad_mem_keys,
        grad_mem_values,
        grad_rates,
        grad_decay,
        grad_momentum,
    ) = kept
    grad_first_init = grad_first_init + grad_first_recall
    grad_second_init = grad_second_init + grad_second_recall
    grad_query = (grad_query_att + probe_pull(grad_probes)[0].reshape(GROUP, D)).astype(
        jnp.bfloat16
    )
    grad_local_keys = (grad_keys_all[front:] + key_pull(grad_mem_keys)[0].reshape(GROUP, D)).astype(
        jnp.bfloat16
    )
    grad_local_values = (grad_values_all[front:] + grad_mem_values.reshape(GROUP, D)).astype(
        jnp.bfloat16
    )
    grad_rate_logits = (grad_rates * rate_scale * rate_sigmoid * (1.0 - rate_sigmoid)).astype(
        jnp.bfloat16
    )
    grad_query_w = matmul_rows(normed, grad_query)
    grad_key_w = matmul_rows(context, grad_context_keys) + matmul_rows(normed, grad_local_keys)
    grad_value_w = matmul_rows(context, grad_context_values) + matmul_rows(
        normed, grad_local_values
    )
    grad_rate_w = matmul_rows(normed, grad_rate_logits)
    grad_normed = (
        matmul_back(grad_query, w_query)
        + matmul_back(grad_local_keys, w_key)
        + matmul_back(grad_local_values, w_value)
        + matmul_back(grad_rate_logits, w_rate)
    )
    grad_tokens_one, grad_gain_one = norm_back(grad_normed, tokens, inverse_one, gain_one)
    grad_inputs = (grad_middle + grad_tokens_one).astype(jnp.bfloat16)
    attention_parts = (
        lax.psum_scatter(grad_gain_one, ("dp", "seq"), scatter_dimension=0, tiled=True),
        lax.psum_scatter(grad_query_w, ("dp", "seq"), scatter_dimension=0, tiled=True),
        lax.psum_scatter(grad_key_w, ("dp", "seq"), scatter_dimension=0, tiled=True),
        lax.psum_scatter(grad_value_w, ("dp", "seq"), scatter_dimension=0, tiled=True),
        lax.psum_scatter(grad_output_w, ("dp", "seq"), scatter_dimension=0, tiled=True),
        lax.psum_scatter(grad_persist, ("dp", "seq"), scatter_dimension=0, tiled=True),
        lax.psum_scatter(
            grad_first_init.reshape(D, MH), ("dp", "seq"), scatter_dimension=0, tiled=True
        ),
        lax.psum_scatter(
            grad_second_init.reshape(D, MH), ("dp", "seq"), scatter_dimension=0, tiled=True
        ),
        lax.psum_scatter(grad_rate_w, ("dp", "seq"), scatter_dimension=0, tiled=True),
    )
    decay_parts = lax.psum(
        (grad_decay * decay * (1.0 - decay), grad_momentum * momentum * (1.0 - momentum)),
        ("dp", "seq"),
    )
    return (
        result[None],
        grad_inputs[None],
        attention_parts[0],
        attention_parts[1],
        attention_parts[2],
        attention_parts[3],
        attention_parts[4],
        attention_parts[5],
        attention_parts[6],
        attention_parts[7],
        attention_parts[8],
        decay_parts[0],
        decay_parts[1],
        ffn_parts[0],
        ffn_parts[1],
        ffn_parts[2],
        ffn_parts[3],
    )


def solution(mesh):
    in_specs = (
        P("dp", "seq", None),
        P("dp", None),
        P(("dp", "seq")),
        P(("dp", "seq"), None),
        P(("dp", "seq"), None),
        P(("dp", "seq"), None),
        P(("dp", "seq"), None),
        P(("dp", "seq"), None),
        P(("dp", "seq"), None),
        P(("dp", "seq"), None),
        P(("dp", "seq"), None),
        P(),
        P(),
        P(("dp", "seq")),
        P(("dp", "seq"), None),
        P(("dp", "seq"), None),
        P(("dp", "seq"), None),
        P("dp", "seq", None),
    )
    out_specs = (
        P("dp", "seq", None),
        P("dp", "seq", None),
        P(("dp", "seq")),
        P(("dp", "seq"), None),
        P(("dp", "seq"), None),
        P(("dp", "seq"), None),
        P(("dp", "seq"), None),
        P(("dp", "seq"), None),
        P(("dp", "seq"), None),
        P(("dp", "seq"), None),
        P(("dp", "seq"), None),
        P(),
        P(),
        P(("dp", "seq")),
        P(("dp", "seq"), None),
        P(("dp", "seq"), None),
        P(("dp", "seq"), None),
    )
    return jax.shard_map(
        on_device, mesh=mesh, in_specs=in_specs, out_specs=out_specs, check_vma=False
    )
```

profile of v0, /device:TPU:2, one launch (start us, length us, event | category | flops | bytes accessed | tf_op | source)
XLA Modules:
  0.0 6129.4 jit_solution(6896908999973261454)
XLA Ops:
  15.2 41.4 all-reduce.9
  65.2 36.4 all-gather
  101.8 44.6 all_gather.47
  156.0 32.2 all-gather.19.cloned.1.call-done
  196.4 57.1 all-gather.15.cloned.1.call-done
  267.0 51.7 all-gather.17.cloned.1.call-done
  346.7 1053.2 %while.47 = (s32[]{:T(128)}, f32[4,16,96,384]{3,2,1,0:T(8,128)}, f32[4,16,96,384]{3,2,1,0:T(8,128)}, s32[]{:T(128)}, f32[16]{0:T(128)S(1)}, /*index=5*/f32[]{:T(...) while((s32[]{:T(128)}, f32[4,16,96,384]{3,2,1,0:T(8,128)}, ...), condition=%wide.region_5.6_spmd.clone, body=%wide.region_2.5_spmd.clone.sunk | while | flops 18205720576 | bytes 338333120 | solution.py:209
  384.0 75.4 %collective-permute-done = bf16[4,16,96,384]{3,2,1,0:T(8,128)(2,1)} collective-permute-done((bf16[4,16,96,384]{3,2,1,0:T(8,128)(2,1)}, bf16[4,16,96,384]{3,2,1,0:T(8,128)(2,1)}, u32[]{:S(2)}, u32[]{:S(2)}) %collective-permute-start) | collective-permute-done | bytes 4718624 | tf_op jit(solution)/shard_map/while/body/eval_jaxpr/ppermute | solution.py:23
  488.1 210.6 %collective-permute-done = bf16[4,16,96,384]{3,2,1,0:T(8,128)(2,1)} collective-permute-done((bf16[4,16,96,384]{3,2,1,0:T(8,128)(2,1)}, bf16[4,16,96,384]{3,2,1,0:T(8,128)(2,1)}, u32[]{:S(2)}, u32[]{:S(2)}) %collective-permute-start) | collective-permute-done | bytes 4718624 | tf_op jit(solution)/shard_map/while/body/eval_jaxpr/ppermute | solution.py:23
  719.7 95.1 %conditional.6 = (f32[4,16,96,384]{3,2,1,0:T(8,128)}) conditional(s32[]{:T(128)} %convert_element_type.349, f32[4,16,96,384]{3,2,1,0:T(8,128)} %get-tuple-element.1193, (f32[16]{0:T(128)S(1)}, f32[]{:T(128)}, f32[4,16,96,384]{3,2,1,0:T(8,128)}, f32[16,96,384]{2,1,0:T(8,128)}, f32[16]{0:T(128)S(1)}, /*index=5*/f32[16,96,384]{2,1,0:T(8,128)}, ...), branch_computations={%region_3.3_spmd, %region_4.4_spmd} | conditional | flops 18193924096 | bytes 253398176 | solution.py:200
  719.7 14.8 fusion.24
  750.5 17.4 fusion.18
  767.9 14.2 fusion.16
  782.1 22.0 bitcast_subtract_fusion.1
  823.1 53.8 collective-permute-done
  903.4 51.4 collective-permute-start
  989.1 45.4 collective-permute-start
  1071.3 141.4 %collective-permute-start = (bf16[4,16,96,384]{3,2,1,0:T(8,128)(2,1)}, bf16[4,16,96,384]{3,2,1,0:T(8,128)(2,1)}, u32[]{:S(2)}, u32[]{:S(2)}) collective-permute-start(bf16[4,16,96,384]{3,2,1,0:T(8,128)(2,1)} %convert_element_type.350), channel_id=1, source_target_pairs={{0,1},{1,2},{2,3},{3,4},{4,5},{5,6},{6,7},{8,9},{9,10},{10,11},{11... | collective-permute-start | bytes 14155784 | tf_op jit(solution)/shard_map/while/body/eval_jaxpr/ppermute | solution.py:23
  1247.0 48.8 collective-permute-start
  1330.1 50.5 collective-permute-start
  1454.8 19.2 fusion.242
  1474.0 14.4 exponential_reduce_fusion
  1489.1 16.3 fusion.186
  1536.5 19.0 multiply_convert_fusion.1
  1588.9 28.9 multiply_reduce_fusion
  1617.7 18.2 convolution_bitcast_fusion
  1635.9 29.9 multiply_convert_fusion
  1695.3 15.8 fusion.101
  1711.1 18.0 fusion.103
  1729.1 21.8 fusion.183
  1776.6 2451.9 %while.48 = (s32[]{:T(128)}, f32[4,16,96,384]{3,2,1,0:T(8,128)}, f32[16,96,384]{2,1,0:T(8,128)}, f32[16,96,384]{2,1,0:T(8,128)}, f32[512,16,96]{0,2,1:T(8,128)},...) while((s32[]{:T(128)}, f32[4,16,96,384]{3,2,1,0:T(8,128)}, ...), condition=%wide.region_22.23_spmd.clone, body=%wide.region_13.22_spmd.clone.sunk | while | flops 47340675072 | bytes 735255744 | solution.py:370
  1795.8 54.6 collective-permute-done.1
  1873.8 146.3 %collective-permute-done.1 = bf16[4,16,96,384]{3,2,1,0:T(8,128)(2,1)} collective-permute-done((bf16[4,16,96,384]{3,2,1,0:T(8,128)(2,1)}, bf16[4,16,96,384]{3,2,1,0:T(8,128)(2,1)}, u32[]{:S(2)}, u32[]{:S(2)}) %collective-permute-start.1) | collective-permute-done | bytes 4718624 | tf_op jit(solution)/shard_map/while/body/eval_jaxpr/ppermute | solution.py:23
  2043.5 54.7 collective-permute-done.1
  2121.6 57.0 collective-permute-done.1
  2202.1 1272.5 %collective-permute-done.1 = bf16[4,16,96,384]{3,2,1,0:T(8,128)(2,1)} collective-permute-done((bf16[4,16,96,384]{3,2,1,0:T(8,128)(2,1)}, bf16[4,16,96,384]{3,2,1,0:T(8,128)(2,1)}, u32[]{:S(2)}, u32[]{:S(2)}) %collective-permute-start.1) | collective-permute-done | bytes 4718624 | tf_op jit(solution)/shard_map/while/body/eval_jaxpr/ppermute | solution.py:23
  3489.7 254.3 %conditional.7 = ((f32[4,16,96,384]{3,2,1,0:T(8,128)}, f32[16,96,384]{2,1,0:T(8,128)}, f32[16,96,384]{2,1,0:T(8,128)}, f32[512,16,96]{0,2,1:T(8,128)}, f32[512,1...) conditional(s32[]{:T(128)} %convert_element_type.352, (f32[4,16,96,384]{3,2,1,0:T(8,128)}, ...), branch_computations={%region_14.14_spmd, %region_15.0_spmd} | conditional | flops 47333597184 | bytes 656612160 | solution.py:367
  3501.4 15.4 fusion.73
  3516.8 21.3 fusion.35
  3538.1 16.4 fusion.70
  3564.1 17.8 fusion.53
  3583.5 14.6 fusion.56
  3598.1 18.7 fusion.42
  3616.8 18.9 fusion.60
  3635.7 15.8 fusion.67
  3651.5 14.1 fusion.54
  3665.6 31.4 fusion.32
  3697.0 17.9 broadcast_multiply_fusion.3
  3752.3 51.9 collective-permute-done.1
  3826.1 257.8 %collective-permute-start.1 = (bf16[4,16,96,384]{3,2,1,0:T(8,128)(2,1)}, bf16[4,16,96,384]{3,2,1,0:T(8,128)(2,1)}, u32[]{:S(2)}, u32[]{:S(2)}) collective-permute-start(bf16[4,16,96,384]{3,2,1,0:T(8,128)(2,1)} %convert_element_type.353), channel_id=1, source_target_pairs={{1,0},{2,1},{3,2},{4,3},{5,4},{6,5},{7,6},{9,8},{10,9},{11,10},{12... | collective-permute-start | bytes 14155784 | tf_op jit(solution)/shard_map/while/body/eval_jaxpr/ppermute | solution.py:23
  4083.9 51.9 collective-permute-done.1
  4161.4 51.9 collective-permute-done.1
  4236.9 15.5 fusion.180
  4264.0 17.7 fusion.189
  4416.6 205.8 %all-reduce.8 = (f32[1536]{0:T(1024)S(1)}, f32[16]{0:T(128)}, f32[16]{0:T(128)}, f32[1536]{0:T(1024)S(1)}) all-reduce(f32[1536]{0:T(1024)S(1)} %get-tuple-element.866, f32[16]{0:T(128)S(1)} %subtract_multiply_fusion.8, f32[16]{0:T(128)S(1)} %subtract_multiply_fusion.7, ...), channel_id=2, replica_groups=mesh['dp'=4,'seq'=8] {'dp','seq'}, use_global_device_ids=true, to_apply=%region_26.27.clone | all-reduce | flops 3104 | bytes 24832
  4641.3 54.0 reduce-scatter.24.cloned.1.call-done
  4695.3 104.7 %reduce-scatter.26.cloned.1.call-done = f32[48,384]{1,0:T(8,128)} async-done(((f32[1536,384]{1,0:T(8,128)}), f32[48,384]{1,0:T(8,128)}) %reduce-scatter.26.cloned.1.call-update) | async-done | bytes 73744 | tf_op jit(solution)/shard_map/reduce_scatter | solution.py:418
  4800.0 141.1 %reduce-scatter.16.cloned.1.call-done = f32[48,1536]{1,0:T(8,128)} async-done(((f32[1536,1536]{1,0:T(8,128)}), f32[48,1536]{1,0:T(8,128)}) %reduce-scatter.16.cloned.1.call-update) | async-done | bytes 294928 | tf_op jit(solution)/shard_map/reduce_scatter | solution.py:410
  4941.1 141.7 %reduce-scatter.18.cloned.1.call-done = f32[48,1536]{1,0:T(8,128)} async-done(((f32[1536,1536]{1,0:T(8,128)}), f32[48,1536]{1,0:T(8,128)}) %reduce-scatter.18.cloned.1.call-update) | async-done | bytes 294928 | tf_op jit(solution)/shard_map/reduce_scatter | solution.py:411
  5082.8 141.2 %reduce-scatter.20.cloned.1.call-done = f32[48,1536]{1,0:T(8,128)} async-done(((f32[1536,1536]{1,0:T(8,128)}), f32[48,1536]{1,0:T(8,128)}) %reduce-scatter.20.cloned.1.call-update) | async-done | bytes 294928 | tf_op jit(solution)/shard_map/reduce_scatter | solution.py:412
  5224.0 141.9 %reduce-scatter.22.cloned.1.call-done = f32[48,1536]{1,0:T(8,128)} async-done(((f32[1536,1536]{1,0:T(8,128)}), f32[48,1536]{1,0:T(8,128)}) %reduce-scatter.22.cloned.1.call-update) | async-done | bytes 294928 | tf_op jit(solution)/shard_map/reduce_scatter | solution.py:413
  5365.9 251.3 %reduce-scatter.28.cloned.1.call-done = f32[48,4096]{1,0:T(8,128)} async-done(((f32[1536,4096]{1,0:T(8,128)}), f32[48,4096]{1,0:T(8,128)}) %reduce-scatter.28.cloned.1.call-update) | async-done | bytes 786448 | tf_op jit(solution)/shard_map/reduce_scatter | solution.py:282
  5617.2 253.2 %reduce-scatter.30.cloned.1.call-done = f32[48,4096]{1,0:T(8,128)} async-done(((f32[1536,4096]{1,0:T(8,128)}), f32[48,4096]{1,0:T(8,128)}) %reduce-scatter.30.cloned.1.call-update) | async-done | bytes 786448 | tf_op jit(solution)/shard_map/reduce_scatter | solution.py:283
  5870.4 251.9 %reduce-scatter.32.cloned.1.call-done = f32[128,1536]{1,0:T(8,128)} async-done(((f32[4096,1536]{1,0:T(8,128)}), f32[128,1536]{1,0:T(8,128)}) %reduce-scatter.32.cloned.1.call-update) | async-done | bytes 786448 | tf_op jit(solution)/shard_map/reduce_scatter | solution.py:284
  (529 shorter events, 945.4 us)
Async XLA Ops:
  7.2 141.6 %copy-start.22 = (bf16[1,512,1536]{2,1,0:T(8,128)(2,1)S(1)}, bf16[1,512,1536]{2,1,0:T(8,128)(2,1)}, u32[]{:S(2)}) copy-start(bf16[1,512,1536]{2,1,0:T(8,128)(2,1)} %param.26) | copy-start | bytes 4718596
  7.2 58.0 copy-start.100
  7.2 94.6 %copy-start.98 = (bf16[48,64]{1,0:T(8,128)(2,1)S(1)}, bf16[48,64]{1,0:T(8,128)(2,1)}, u32[]{:S(2)}) copy-start(bf16[48,64]{1,0:T(8,128)(2,1)} %param.33) | copy-start | bytes 18436
  7.2 139.8 %copy-start.107 = (f32[16]{0:T(128)S(1)}, f32[16]{0:T(128)}, u32[]{:S(2)}) copy-start(f32[16]{0:T(128)} %param.38) | copy-start | bytes 196
  7.2 139.8 %copy-start.108 = (f32[16]{0:T(128)S(1)}, f32[16]{0:T(128)}, u32[]{:S(2)}) copy-start(f32[16]{0:T(128)} %param.37) | copy-start | bytes 196
  7.2 142.8 %all-gather.11.cloned.1.call-start = ((), (), s32[]{:S(2)}) async-start(), calls=%async_computation.11 | async-start | bytes 1216512 | tf_op jit(solution)/shard_map/all_gather | solution.py:124
  8.0 145.0 %all-gather.13.cloned.1.call-start = ((), (), s32[]{:S(2)}) async-start(), calls=%async_computation.12 | async-start | bytes 1216512 | tf_op jit(solution)/shard_map/all_gather | solution.py:125
  8.7 179.5 %all-gather.19.cloned.1.call-start = ((), (), s32[]{:S(2)}) async-start(), calls=%async_computation.15 | async-start | bytes 4866048 | tf_op jit(solution)/shard_map/all_gather | solution.py:119
  9.5 244.0 %all-gather.15.cloned.1.call-start = ((), (), s32[]{:S(2)}) async-start(), calls=%async_computation.13 | async-start | bytes 4866048 | tf_op jit(solution)/shard_map/all_gather | solution.py:120
  10.0 308.7 %all-gather.17.cloned.1.call-start = ((), (), s32[]{:S(2)}) async-start(), calls=%async_computation.14 | async-start | bytes 4866048 | tf_op jit(solution)/shard_map/all_gather | solution.py:121
  10.6 1494.7 %all-gather.21.cloned.1.call-start = ((), (), s32[]{:S(2)}) async-start(), calls=%async_computation.16 | async-start | bytes 4866048 | tf_op jit(solution)/shard_map/all_gather | solution.py:122
  11.2 1501.5 %all-gather.23.cloned.1.call-start = ((), (), s32[]{:S(2)}) async-start(), calls=%async_computation.17 | async-start | bytes 12976128 | tf_op jit(solution)/shard_map/all_gather | solution.py:253
  11.9 1512.9 %all-gather.25.cloned.1.call-start = ((), (), s32[]{:S(2)}) async-start(), calls=%async_computation.18 | async-start | bytes 12976128 | tf_op jit(solution)/shard_map/all_gather | solution.py:254
  12.7 1523.8 %all-gather.27.cloned.1.call-start = ((), (), s32[]{:S(2)}) async-start(), calls=%async_computation.19 | async-start | bytes 12976128 | tf_op jit(solution)/shard_map/all_gather | solution.py:255
  13.4 4626.5 %reduce-scatter.36.cloned.1.call-start = ((), (), s32[]{:S(2)}) async-start(), calls=%async_computation.30 | async-start | bytes 811008
  56.6 268.8 %copy-start.65 = (f32[1536]{0:T(1024)}, f32[1536]{0:T(1024)S(1)}, u32[]{:S(2)}) copy-start(f32[1536]{0:T(1024)S(1)} %convert_element_type.184) | copy-start | bytes 18436
  58.4 266.9 %copy-start.82 = (f32[512]{0:T(512)}, f32[512]{0:T(512)S(1)}, u32[]{:S(2)}) copy-start(f32[512]{0:T(512)S(1)} %add_rsqrt_fusion.1) | copy-start | bytes 6148
  101.8 51.2 copy-start.76
  266.9 58.4 copy-start.79
  266.9 78.0 %copy-start.72 = (f32[512,16]{0,1:T(8,128)}, f32[512,16]{0,1:T(8,128)S(1)}, u32[]{:S(2)}) copy-start(f32[512,16]{0,1:T(8,128)S(1)} %fusion.219) | copy-start | bytes 98308
  346.7 1053.3 %copy-start.53 = (f32[512,16]{0,1:T(8,128)S(1)}, f32[512,16]{0,1:T(8,128)}, u32[]{:S(2)}) copy-start(f32[512,16]{0,1:T(8,128)} %copy-done.52) | copy-start | bytes 98308
  381.9 77.5 %collective-permute-start = (bf16[4,16,96,384]{3,2,1,0:T(8,128)(2,1)}, bf16[4,16,96,384]{3,2,1,0:T(8,128)(2,1)}, u32[]{:S(2)}, u32[]{:S(2)}) collective-permute-start(bf16[4,16,96,384]{3,2,1,0:T(8,128)(2,1)} %convert_element_type.350), channel_id=1, source_target_pairs={{0,1},{1,2},{2,3},{3,4},{4,5},{5,6},{6,7},{8,9},{9,10},{10,11},{11... | collective-permute-start | bytes 14155784 | tf_op jit(solution)/shard_map/while/body/eval_jaxpr/ppermute | solution.py:23
  486.2 212.5 %collective-permute-start = (bf16[4,16,96,384]{3,2,1,0:T(8,128)(2,1)}, bf16[4,16,96,384]{3,2,1,0:T(8,128)(2,1)}, u32[]{:S(2)}, u32[]{:S(2)}) collective-permute-start(bf16[4,16,96,384]{3,2,1,0:T(8,128)(2,1)} %convert_element_type.350), channel_id=1, source_target_pairs={{0,1},{1,2},{2,3},{3,4},{4,5},{5,6},{6,7},{8,9},{9,10},{10,11},{11... | collective-permute-start | bytes 14155784 | tf_op jit(solution)/shard_map/while/body/eval_jaxpr/ppermute | solution.py:23
  736.5 31.4 copy-start.11
  821.2 55.7 collective-permute-start
  903.4 59.2 collective-permute-start
  989.1 55.7 collective-permute-start
  1071.3 149.2 %collective-permute-start = (bf16[4,16,96,384]{3,2,1,0:T(8,128)(2,1)}, bf16[4,16,96,384]{3,2,1,0:T(8,128)(2,1)}, u32[]{:S(2)}, u32[]{:S(2)}) collective-permute-start(bf16[4,16,96,384]{3,2,1,0:T(8,128)(2,1)} %convert_element_type.350), channel_id=1, source_target_pairs={{0,1},{1,2},{2,3},{3,4},{4,5},{5,6},{6,7},{8,9},{9,10},{10,11},{11... | collective-permute-start | bytes 14155784 | tf_op jit(solution)/shard_map/while/body/eval_jaxpr/ppermute | solution.py:23
  1247.0 56.6 collective-permute-start
  1330.1 58.3 collective-permute-start
  1635.9 29.9 copy-start.38
  1776.6 2452.0 %copy-start.92 = (f32[512,16]{0,1:T(8,128)S(1)}, f32[512,16]{0,1:T(8,128)}, u32[]{:S(2)}) copy-start(f32[512,16]{0,1:T(8,128)} %get-tuple-element.983) | copy-start | bytes 98308
  1776.6 2452.7 %copy-start.66 = (f32[1536]{0:T(1024)S(1)}, f32[1536]{0:T(1024)}, u32[]{:S(2)}) copy-start(f32[1536]{0:T(1024)} %copy-done.65) | copy-start | bytes 18436
  1776.6 2452.7 %copy-start.83 = (f32[512]{0:T(512)S(1)}, f32[512]{0:T(512)}, u32[]{:S(2)}) copy-start(f32[512]{0:T(512)} %copy-done.82) | copy-start | bytes 6148
  1793.9 56.5 collective-permute-start.1
  1795.8 61.7 %copy-start.4 = (f32[512,16,96]{0,2,1:T(8,128)S(1)}, f32[512,16,96]{0,2,1:T(8,128)}, u32[]{:S(2)}) copy-start(f32[512,16,96]{0,2,1:T(8,128)} %get-tuple-element.1406) | copy-start | bytes 9437188 | tf_op jit(solution)/shard_map/while
  1871.9 148.2 %collective-permute-start.1 = (bf16[4,16,96,384]{3,2,1,0:T(8,128)(2,1)}, bf16[4,16,96,384]{3,2,1,0:T(8,128)(2,1)}, u32[]{:S(2)}, u32[]{:S(2)}) collective-permute-start(bf16[4,16,96,384]{3,2,1,0:T(8,128)(2,1)} %convert_element_type.353), channel_id=1, source_target_pairs={{1,0},{2,1},{3,2},{4,3},{5,4},{6,5},{7,6},{9,8},{10,9},{11,10},{12... | collective-permute-start | bytes 14155784 | tf_op jit(solution)/shard_map/while/body/eval_jaxpr/ppermute | solution.py:23
  1873.8 153.4 %copy-start.4 = (f32[512,16,96]{0,2,1:T(8,128)S(1)}, f32[512,16,96]{0,2,1:T(8,128)}, u32[]{:S(2)}) copy-start(f32[512,16,96]{0,2,1:T(8,128)} %get-tuple-element.1406) | copy-start | bytes 9437188 | tf_op jit(solution)/shard_map/while
  2041.6 56.6 collective-permute-start.1
  2043.5 61.9 %copy-start.4 = (f32[512,16,96]{0,2,1:T(8,128)S(1)}, f32[512,16,96]{0,2,1:T(8,128)}, u32[]{:S(2)}) copy-start(f32[512,16,96]{0,2,1:T(8,128)} %get-tuple-element.1406) | copy-start | bytes 9437188 | tf_op jit(solution)/shard_map/while
  2119.7 58.9 collective-permute-start.1
  2121.6 64.1 %copy-start.4 = (f32[512,16,96]{0,2,1:T(8,128)S(1)}, f32[512,16,96]{0,2,1:T(8,128)}, u32[]{:S(2)}) copy-start(f32[512,16,96]{0,2,1:T(8,128)} %get-tuple-element.1406) | copy-start | bytes 9437188 | tf_op jit(solution)/shard_map/while
  2200.1 1274.5 %collective-permute-start.1 = (bf16[4,16,96,384]{3,2,1,0:T(8,128)(2,1)}, bf16[4,16,96,384]{3,2,1,0:T(8,128)(2,1)}, u32[]{:S(2)}, u32[]{:S(2)}) collective-permute-start(bf16[4,16,96,384]{3,2,1,0:T(8,128)(2,1)} %convert_element_type.353), channel_id=1, source_target_pairs={{1,0},{2,1},{3,2},{4,3},{5,4},{6,5},{7,6},{9,8},{10,9},{11,10},{12... | collective-permute-start | bytes 14155784 | tf_op jit(solution)/shard_map/while/body/eval_jaxpr/ppermute | solution.py:23
  2202.1 1279.7 %copy-start.4 = (f32[512,16,96]{0,2,1:T(8,128)S(1)}, f32[512,16,96]{0,2,1:T(8,128)}, u32[]{:S(2)}) copy-start(f32[512,16,96]{0,2,1:T(8,128)} %get-tuple-element.1406) | copy-start | bytes 9437188 | tf_op jit(solution)/shard_map/while
  3554.5 43.6 slice-start
  3564.1 34.0 slice-start.1
  3564.1 34.0 slice-start.2
  3665.6 31.4 copy-start.6
  3750.4 53.9 collective-permute-start.1
  3752.3 59.1 copy-start.4
  3826.1 309.7 %collective-permute-start.1 = (bf16[4,16,96,384]{3,2,1,0:T(8,128)(2,1)}, bf16[4,16,96,384]{3,2,1,0:T(8,128)(2,1)}, u32[]{:S(2)}, u32[]{:S(2)}) collective-permute-start(bf16[4,16,96,384]{3,2,1,0:T(8,128)(2,1)} %convert_element_type.353), channel_id=1, source_target_pairs={{1,0},{2,1},{3,2},{4,3},{5,4},{6,5},{7,6},{9,8},{10,9},{11,10},{12... | collective-permute-start | bytes 14155784 | tf_op jit(solution)/shard_map/while/body/eval_jaxpr/ppermute | solution.py:23
  4083.9 59.1 copy-start.4
  4157.3 56.1 collective-permute-start.1
  4161.4 59.1 copy-start.4
  4232.8 408.5 %reduce-scatter.34.cloned.1.call-start = ((), (), s32[]{:S(2)}) async-start(), calls=%async_computation.29 | async-start | bytes 811008
  4236.8 458.5 %reduce-scatter.24.cloned.1.call-start = ((), (), s32[]{:S(2)}) async-start(), calls=%async_computation.24 | async-start | bytes 2433024 | tf_op jit(solution)/shard_map/reduce_scatter | solution.py:415
  4252.4 547.6 %reduce-scatter.26.cloned.1.call-start = ((), (), s32[]{:S(2)}) async-start(), calls=%async_computation.25 | async-start | bytes 2433024 | tf_op jit(solution)/shard_map/reduce_scatter | solution.py:418
  4281.7 659.4 %reduce-scatter.16.cloned.1.call-start = ((), (), s32[]{:S(2)}) async-start(), calls=%async_computation.20 | async-start | bytes 9732096 | tf_op jit(solution)/shard_map/reduce_scatter | solution.py:410
  4314.2 768.6 %reduce-scatter.18.cloned.1.call-start = ((), (), s32[]{:S(2)}) async-start(), calls=%async_computation.21 | async-start | bytes 9732096 | tf_op jit(solution)/shard_map/reduce_scatter | solution.py:411
  4332.4 891.7 %reduce-scatter.20.cloned.1.call-start = ((), (), s32[]{:S(2)}) async-start(), calls=%async_computation.22 | async-start | bytes 9732096 | tf_op jit(solution)/shard_map/reduce_scatter | solution.py:412
  4346.7 1019.3 %reduce-scatter.22.cloned.1.call-start = ((), (), s32[]{:S(2)}) async-start(), calls=%async_computation.23 | async-start | bytes 9732096 | tf_op jit(solution)/shard_map/reduce_scatter | solution.py:413
  4355.0 1262.2 %reduce-scatter.28.cloned.1.call-start = ((), (), s32[]{:S(2)}) async-start(), calls=%async_computation.26 | async-start | bytes 25952256 | tf_op jit(solution)/shard_map/reduce_scatter | solution.py:282
  4370.4 1500.0 %reduce-scatter.30.cloned.1.call-start = ((), (), s32[]{:S(2)}) async-start(), calls=%async_computation.27 | async-start | bytes 25952256 | tf_op jit(solution)/shard_map/reduce_scatter | solution.py:283
  4384.5 1737.8 %reduce-scatter.32.cloned.1.call-start = ((), (), s32[]{:S(2)}) async-start(), calls=%async_computation.28 | async-start | bytes 25952256 | tf_op jit(solution)/shard_map/reduce_scatter | solution.py:284
  (109 other events, 1021.7 us)
Sparse Core Ops, SparseCore 0:
  11.0 55.2 all-gather.10
  69.2 53.1 all-gather.12
  125.3 62.8 all-gather.18
  191.0 62.4 all-gather.14
  256.2 62.4 all-gather.16
  321.5 62.4 all-gather.20
  386.8 109.9 all-gather.22
  499.6 100.5 all-gather.24
  603.1 111.7 all-gather.26
  4232.9 258.3 reduce-scatter.35
  4497.0 94.5 reduce-scatter.33
  4597.2 98.0 reduce-scatter.23
  4702.0 97.9 reduce-scatter.25
  4806.4 134.7 reduce-scatter.15
  4948.5 134.3 reduce-scatter.17
  5089.1 134.8 reduce-scatter.19
  5231.4 134.5 reduce-scatter.21
  5372.8 244.3 reduce-scatter.27
  5625.3 245.0 reduce-scatter.29
  5877.2 245.0 reduce-scatter.31
where the time goes:
time: 6140 us; the launch traced here: 6130 us
  waiting for transfers between devices  3750 us (61%)
  matrix products  803 us (13%)
  starting transfers between devices  618 us (10%)
  other arithmetic  497 us (8%)
  blocking collectives  328 us (5%)
  local copies, waits for them, and re-layouts  73.2 us (1%)
    ppermute x16, waiting for transfers between devices, from_behind(): lax.ppermute(value, axis, [(source, source + steps) for source in range(l...  2120 us
    ppermute x16, starting transfers between devices, from_behind(): lax.ppermute(value, axis, [(source, source + steps) for source in range(l...  617 us
    dot_general x17, matrix products, recall(): jnp.einsum('chm,hdm->chd', jax.nn.silu(inner), second, precision=HIGH)  282 us
    reduce_scatter x1, waiting for transfers between devices, on_device(): lax.psum_scatter(grad_up_w, ('dp', 'seq'), scatter_dimension=0, tiled=True)  253 us
    reduce_scatter x1, waiting for transfers between devices, on_device(): lax.psum_scatter(grad_down_w, ('dp', 'seq'), scatter_dimension=0, tiled=T...  252 us
    reduce_scatter x1, waiting for transfers between devices, on_device(): lax.psum_scatter(grad_gate_w, ('dp', 'seq'), scatter_dimension=0, tiled=T...  251 us
    unnamed x2, blocking collectives  247 us
    dot_general x13, matrix products, recall(): inner = jnp.einsum('chd,hdm->chm', probes, first, precision=HIGH)  195 us
  transfers between devices with their start and end apart: 36, of which 28 were waited for; matrix products, arithmetic and copies ran while one was open for 11% of the time, Pallas kernels for 0%

commit v1 on v0

v1 whole, which is shorter than its diff:
```python
import jax
import jax.numpy as jnp
from jax import lax
from jax.experimental import pallas as pl
from jax.experimental.pallas import tpu as pltpu
from jax.sharding import PartitionSpec as P

D = 1536
H = 16
HD = 96
MH = 384
NP = 64
GROUP = 512
RATE_ROWS = 16
norm_epsilon = 1e-06
f32 = jnp.float32
bf16 = jnp.bfloat16


def dot_nn(left, right):
    return lax.dot_general(left, right, (((1,), (0,)), ((), ())), preferred_element_type=f32)


def dot_tn(left, right):
    return lax.dot_general(left, right, (((0,), (0,)), ((), ())), preferred_element_type=f32)


def dot_nt(left, right):
    return lax.dot_general(left, right, (((1,), (1,)), ((), ())), preferred_element_type=f32)


def inverse_root(values):
    return lax.rsqrt(jnp.mean(values * values, axis=0, keepdims=True) + norm_epsilon)


def memory_forward_kernel(
    heads,
    blocks,
    flags,
    keys_ref,
    values_ref,
    probes_ref,
    rates_ref,
    retain_ref,
    update_ref,
    first_ref,
    second_ref,
    scalars_ref,
    recalled_ref,
    saved_ref,
    state,
):
    turn = pl.program_id(0)

    @pl.when(turn == 0)
    def blank():
        state[...] = jnp.zeros_like(state)

    saved_ref[0] = state[...]
    retain = retain_ref[0]

    def recall_with(first, second, head):
        rows = slice(head * HD, (head + 1) * HD)
        raw = probes_ref[0, rows, :].astype(f32)
        probes = (raw * inverse_root(raw)).astype(bf16)
        inner = dot_tn(first[rows, :].astype(bf16), probes)
        return dot_nn(second[rows, :].astype(bf16), jax.nn.silu(inner).astype(bf16))

    only_state = flags[1, turn] * (1 - flags[2, turn])
    only_init = flags[2, turn] * (1 - flags[1, turn])

    @pl.when(only_state == 1)
    def from_state():
        for head in range(heads):
            recalled_ref[0, head * HD : (head + 1) * HD, :] = recall_with(
                state[0], state[1], head
            ).astype(bf16)

    @pl.when(only_init == 1)
    def from_init():
        for head in range(heads):
            recalled_ref[0, head * HD : (head + 1) * HD, :] = recall_with(
                first_ref[...], second_ref[...], head
            ).astype(bf16)

    @pl.when(only_state + only_init == 0)
    def from_both():
        for head in range(heads):
            recalled_ref[0, head * HD : (head + 1) * HD, :] = (
                retain * recall_with(state[0], state[1], head)
                + (1.0 - retain) * recall_with(first_ref[...], second_ref[...], head)
            ).astype(bf16)

    @pl.when(turn < blocks - 1)
    def step():
        carry = flags[0, turn].astype(f32)
        for head in range(heads):
            rows = slice(head * HD, (head + 1) * HD)
            keep = scalars_ref[0, head]
            push = scalars_ref[1, head] * carry
            base_first = jnp.where(carry > 0.5, state[0, rows, :], first_ref[rows, :])
            base_second = jnp.where(carry > 0.5, state[1, rows, :], second_ref[rows, :])
            raw = keys_ref[0, rows, :].astype(f32)
            keys = (raw * inverse_root(raw)).astype(bf16)
            second_low = base_second.astype(bf16)
            inner = dot_tn(base_first.astype(bf16), keys)
            gate = jax.nn.sigmoid(inner)
            active = inner * gate
            slope = gate + active * (1.0 - gate)
            active_low = active.astype(bf16)
            weight = rates_ref[0, head : head + 1, :].astype(f32) * update_ref[0] * (1.0 / GROUP)
            error = dot_nn(second_low, active_low) - values_ref[0, rows, :].astype(f32)
            pull = (error * weight).astype(bf16)
            inner_pull = (dot_tn(second_low, pull) * slope).astype(bf16)
            speed_first = push * state[2, rows, :] - dot_nt(keys, inner_pull)
            speed_second = push * state[3, rows, :] - dot_nt(pull, active_low)
            state[0, rows, :] = keep * base_first + speed_first
            state[1, rows, :] = keep * base_second + speed_second
            state[2, rows, :] = speed_first
            state[3, rows, :] = speed_second


def memory_forward(flags, packed, probes, retain, update, first, second, scalars):
    chips, rows, width = probes.shape
    heads = rows // HD
    blocks = chips * width // GROUP
    per = width // GROUP

    def block(turn, flags):
        return (turn // per, 0, (turn % per) ^ flags[3, 0])

    def by_turn(turn, flags):
        return (turn, 0, 0)

    def whole(turn, flags):
        return (0, 0)

    def value_block(turn, flags):
        return (turn // per, 1, (turn % per) ^ flags[3, 0])

    def rate_block(turn, flags):
        return (turn // per, 2 * rows // RATE_ROWS, (turn % per) ^ flags[3, 0])

    part = pl.BlockSpec((1, rows, GROUP), block)
    line = pl.BlockSpec((1, 1, GROUP), by_turn)
    return pl.pallas_call(
        lambda *refs: memory_forward_kernel(heads, blocks, *refs),
        grid_spec=pltpu.PrefetchScalarGridSpec(
            num_scalar_prefetch=1,
            grid=(blocks,),
            in_specs=[
                part,
                pl.BlockSpec((1, rows, GROUP), value_block),
                part,
                pl.BlockSpec((1, RATE_ROWS, GROUP), rate_block),
                line,
                line,
                pl.BlockSpec((rows, MH), whole),
                pl.BlockSpec((rows, MH), whole),
                pl.BlockSpec(memory_space=pltpu.SMEM),
            ],
            out_specs=[
                part,
                pl.BlockSpec((1, 4, rows, MH), lambda turn, flags: (turn, 0, 0, 0)),
            ],
            scratch_shapes=[pltpu.VMEM((4, rows, MH), f32)],
        ),
        out_shape=[
            jax.ShapeDtypeStruct(probes.shape, bf16),
            jax.ShapeDtypeStruct((blocks, 4, rows, MH), f32),
        ],
        compiler_params=pltpu.CompilerParams(vmem_limit_bytes=50 * 2**20),
        cost_estimate=pl.CostEstimate(
            flops=blocks * heads * 7 * 2 * GROUP * HD * MH * 4,
            bytes_accessed=blocks * 6 * rows * MH * 4,
            transcendentals=blocks * heads * 2 * MH * GROUP,
        ),
    )(flags, packed, packed, probes, packed, retain, update, first, second, scalars)


def memory_backward_kernel(
    heads,
    blocks,
    flags,
    keys_ref,
    values_ref,
    probes_ref,
    rates_ref,
    retain_ref,
    update_ref,
    first_ref,
    second_ref,
    scalars_ref,
    saved_ref,
    pull_ref,
    grads_ref,
    grad_first_ref,
    grad_second_ref,
    grad_scalars_ref,
    message,
):
    count = pl.program_id(0)
    turn = blocks - 1 - count

    @pl.when(count == 0)
    def blank():
        message[...] = jnp.zeros_like(message)
        grad_first_ref[...] = jnp.zeros_like(grad_first_ref)
        grad_second_ref[...] = jnp.zeros_like(grad_second_ref)
        grad_scalars_ref[...] = jnp.zeros_like(grad_scalars_ref)

    grads_ref[...] = jnp.zeros_like(grads_ref)
    size = heads * HD
    rate_row = 2 * size
    probe_row = 2 * size + RATE_ROWS

    @pl.when(count > 0)
    def step():
        carry = flags[0, turn].astype(f32)
        grad_rates = []
        for head in range(heads):
            rows = slice(head * HD, (head + 1) * HD)
            keep = scalars_ref[0, head]
            push = scalars_ref[1, head] * carry
            base_first = jnp.where(carry > 0.5, saved_ref[0, 0, rows, :], first_ref[rows, :])
            base_second = jnp.where(carry > 0.5, saved_ref[0, 1, rows, :], second_ref[rows, :])
            grad_a = message[0, rows, :]
            grad_b = message[1, rows, :]
            grad_sa = message[2, rows, :] + grad_a
            grad_sb = message[3, rows, :] + grad_b
            momentum_part = carry * (
                jnp.sum(saved_ref[0, 2, rows, :] * grad_sa, axis=0, keepdims=True)
                + jnp.sum(saved_ref[0, 3, rows, :] * grad_sb, axis=0, keepdims=True)
            )
            decay_part = -(
                jnp.sum(base_first * grad_a, axis=0, keepdims=True)
                + jnp.sum(base_second * grad_b, axis=0, keepdims=True)
            )
            grad_scalars_ref[2 * head : 2 * head + 1, :] += decay_part
            grad_scalars_ref[2 * head + 1 : 2 * head + 2, :] += momentum_part
            back_a = (-grad_sa).astype(bf16)
            back_b = (-grad_sb).astype(bf16)
            raw = keys_ref[0, rows, :].astype(f32)
            inverse = inverse_root(raw)
            normal = raw * inverse
            keys = normal.astype(bf16)
            first_low = base_first.astype(bf16)
            second_low = base_second.astype(bf16)
            inner = dot_tn(first_low, keys)
            gate = jax.nn.sigmoid(inner)
            active = inner * gate
            slope = gate + active * (1.0 - gate)
            bend = gate * (1.0 - gate) * (2.0 + inner - 2.0 * active)
            active_low = active.astype(bf16)
            weight = update_ref[0] * (1.0 / GROUP)
            rate = rates_ref[0, head : head + 1, :].astype(f32)
            error = dot_nn(second_low, active_low) - values_ref[0, rows, :].astype(f32)
            pull = (error * (rate * weight)).astype(bf16)
            spread = dot_tn(second_low, pull)
            inner_pull = (spread * slope).astype(bf16)
            back_inner = dot_tn(back_a, keys)
            back_spread = (back_inner * slope).astype(bf16)
            grad_pull = dot_nn(back_b, active_low) + dot_nn(second_low, back_spread)
            grad_rates.append(jnp.sum(grad_pull * error, axis=0, keepdims=True) * weight)
            grad_error = grad_pull * (rate * weight)
            grad_error_low = grad_error.astype(bf16)
            grads_ref[0, size + head * HD : size + (head + 1) * HD, :] = (-grad_error).astype(bf16)
            grad_active = dot_tn(back_b, pull) + dot_tn(second_low, grad_error_low)
            grad_inner = (back_inner * spread * bend + grad_active * slope).astype(bf16)
            grad_normal = dot_nn(back_a, inner_pull) + dot_nn(first_low, grad_inner)
            grads_ref[0, rows, :] = (
                inverse
                * (grad_normal - normal * jnp.mean(grad_normal * normal, axis=0, keepdims=True))
            ).astype(bf16)
            base_grad_a = keep * grad_a + dot_nt(keys, grad_inner)
            base_grad_b = (
                keep * grad_b + dot_nt(pull, back_spread) + dot_nt(grad_error_low, active_low)
            )
            message[0, rows, :] = carry * base_grad_a
            message[1, rows, :] = carry * base_grad_b
            message[2, rows, :] = push * grad_sa
            message[3, rows, :] = push * grad_sb
            grad_first_ref[rows, :] += (1.0 - carry) * base_grad_a
            grad_second_ref[rows, :] += (1.0 - carry) * base_grad_b
        grad_rates.append(jnp.zeros((RATE_ROWS - heads, GROUP), f32))
        grads_ref[0, rate_row : rate_row + RATE_ROWS, :] = jnp.concatenate(
            grad_rates, axis=0
        ).astype(bf16)

    retain = retain_ref[0]

    def recall_back(first, second, grad_recalled, head):
        rows = slice(head * HD, (head + 1) * HD)
        raw = probes_ref[0, rows, :].astype(f32)
        inverse = inverse_root(raw)
        normal = raw * inverse
        probes = normal.astype(bf16)
        first_low = first[rows, :].astype(bf16)
        inner = dot_tn(first_low, probes)
        gate = jax.nn.sigmoid(inner)
        active = inner * gate
        slope = gate + active * (1.0 - gate)
        grad_inner = (dot_tn(second[rows, :].astype(bf16), grad_recalled) * slope).astype(bf16)
        grad_second = dot_nt(grad_recalled, active.astype(bf16))
        grad_first = dot_nt(probes, grad_inner)
        grad_normal = dot_nn(first_low, grad_inner)
        grad_probes = inverse * (
            grad_normal - normal * jnp.mean(grad_normal * normal, axis=0, keepdims=True)
        )
        return grad_first, grad_second, grad_probes

    only_state = flags[1, turn] * (1 - flags[2, turn])
    only_init = flags[2, turn] * (1 - flags[1, turn])

    def from_state(whole, add):
        for head in range(heads):
            rows = slice(head * HD, (head + 1) * HD)
            grad_recalled = pull_ref[0, rows, :]
            if not whole:
                grad_recalled = (grad_recalled.astype(f32) * retain).astype(bf16)
            grad_first, grad_second, grad_probes = recall_back(
                saved_ref[0, 0], saved_ref[0, 1], grad_recalled, head
            )
            message[0, rows, :] += grad_first
            message[1, rows, :] += grad_second
            spot = slice(probe_row + head * HD, probe_row + (head + 1) * HD)
            grads_ref[0, spot, :] = grad_probes.astype(bf16)

    def from_init(whole, add):
        for head in range(heads):
            rows = slice(head * HD, (head + 1) * HD)
            grad_recalled = pull_ref[0, rows, :]
            if not whole:
                grad_recalled = (grad_recalled.astype(f32) * (1.0 - retain)).astype(bf16)
            grad_first, grad_second, grad_probes = recall_back(
                first_ref[...], second_ref[...], grad_recalled, head
            )
            grad_first_ref[rows, :] += grad_first
            grad_second_ref[rows, :] += grad_second
            spot = slice(probe_row + head * HD, probe_row + (head + 1) * HD)
            if add:
                grad_probes = grad_probes + grads_ref[0, spot, :].astype(f32)
            grads_ref[0, spot, :] = grad_probes.astype(bf16)

    @pl.when(only_state == 1)
    def state_alone():
        from_state(True, False)

    @pl.when(only_init == 1)
    def init_alone():
        from_init(True, False)

    @pl.when(only_state + only_init == 0)
    def both():
        from_state(False, False)
        from_init(False, True)


def memory_backward(
    flags, packed, probes, retain, update, first, second, scalars, saved, pull
):
    chips, rows, width = probes.shape
    heads = rows // HD
    blocks = chips * width // GROUP
    per = width // GROUP
    all_rows = 3 * rows + RATE_ROWS

    def block(count, flags):
        turn = blocks - 1 - count
        return (turn // per, 0, (turn % per) ^ flags[3, 0])

    def by_turn(count, flags):
        return (blocks - 1 - count, 0, 0)

    def whole(count, flags):
        return (0, 0)

    def value_block(count, flags):
        turn = blocks - 1 - count
        return (turn // per, 1, (turn % per) ^ flags[3, 0])

    def rate_block(count, flags):
        turn = blocks - 1 - count
        return (turn // per, 2 * rows // RATE_ROWS, (turn % per) ^ flags[3, 0])

    part = pl.BlockSpec((1, rows, GROUP), block)
    line = pl.BlockSpec((1, 1, GROUP), by_turn)
    matrix = pl.BlockSpec((rows, MH), whole)
    return pl.pallas_call(
        lambda *refs: memory_backward_kernel(heads, blocks, *refs),
        grid_spec=pltpu.PrefetchScalarGridSpec(
            num_scalar_prefetch=1,
            grid=(blocks,),
            in_specs=[
                part,
                pl.BlockSpec((1, rows, GROUP), value_block),
                part,
                pl.BlockSpec((1, RATE_ROWS, GROUP), rate_block),
                line,
                line,
                matrix,
                matrix,
                pl.BlockSpec(memory_space=pltpu.SMEM),
                pl.BlockSpec(
                    (1, 4, rows, MH), lambda count, flags: (blocks - 1 - count, 0, 0, 0)
                ),
                part,
            ],
            out_specs=[
                pl.BlockSpec((1, all_rows, GROUP), block),
                matrix,
                matrix,
                pl.BlockSpec((8, MH), whole),
            ],
            scratch_shapes=[pltpu.VMEM((4, rows, MH), f32)],
        ),
        out_shape=[
            jax.ShapeDtypeStruct((chips, all_rows, width), bf16),
            jax.ShapeDtypeStruct((rows, MH), f32),
            jax.ShapeDtypeStruct((rows, MH), f32),
            jax.ShapeDtypeStruct((8, MH), f32),
        ],
        compiler_params=pltpu.CompilerParams(vmem_limit_bytes=56 * 2**20),
        cost_estimate=pl.CostEstimate(
            flops=blocks * heads * 19 * 2 * GROUP * HD * MH * 4,
            bytes_accessed=blocks * 8 * rows * MH * 4,
            transcendentals=blocks * heads * 2 * MH * GROUP,
        ),
    )(flags, packed, packed, probes, packed, retain, update, first, second, scalars, saved, pull)


QUERIES = 256


def visible_bias(bias_ref, row_ref, col_ref):
    shape = bias_ref.shape[1:]
    key = lax.broadcasted_iota(jnp.int32, shape, 0)
    query = lax.broadcasted_iota(jnp.int32, shape, 1)
    for block in range(bias_ref.shape[0]):
        seen = jnp.logical_and(key <= query, col_ref[block] == row_ref[block])
        bias_ref[block] = jnp.where(seen, 0.0, -1e30)


def attention_forward_kernel(
    scale,
    q_ref,
    k_ref,
    v_ref,
    kr_ref,
    vr_ref,
    kp_ref,
    vp_ref,
    row_ref,
    col_ref,
    mixed_ref,
    total_ref,
    bias_ref,
):
    @pl.when(jnp.logical_and(pl.program_id(0) == 0, pl.program_id(1) == 0))
    def fill():
        visible_bias(bias_ref, row_ref, col_ref)

    block = pl.program_id(1)
    for part in range(GROUP // QUERIES):
        lanes = slice(part * QUERIES, (part + 1) * QUERIES)
        upto = (part + 1) * QUERIES
        query = q_ref[:, lanes]
        bias = bias_ref[block, :upto, lanes]
        s_p = dot_tn(kp_ref[...], query) * scale
        s_r = dot_tn(kr_ref[:, :upto], query) * scale + bias
        s_l = dot_tn(k_ref[:, :upto], query) * scale + bias
        top = jnp.maximum(
            jnp.max(s_p, axis=0, keepdims=True),
            jnp.maximum(
                jnp.max(s_r, axis=0, keepdims=True), jnp.max(s_l, axis=0, keepdims=True)
            ),
        )
        e_p = jnp.exp(s_p - top)
        e_r = jnp.exp(s_r - top)
        e_l = jnp.exp(s_l - top)
        total = (
            jnp.sum(e_p, axis=0, keepdims=True)
            + jnp.sum(e_r, axis=0, keepdims=True)
            + jnp.sum(e_l, axis=0, keepdims=True)
        )
        mixed = (
            dot_nn(vp_ref[...], e_p.astype(bf16))
            + dot_nn(vr_ref[:, :upto], e_r.astype(bf16))
            + dot_nn(v_ref[:, :upto], e_l.astype(bf16))
        )
        mixed_ref[:, lanes] = (mixed / total).astype(bf16)
        total_ref[0, :, lanes] = top + jnp.log(total)


def attention_specs(width):
    main = pl.BlockSpec((HD, GROUP), lambda head, block: (head, block))
    side = pl.BlockSpec((HD, NP), lambda head, block: (head, 0))
    count = width // GROUP
    row = pl.BlockSpec((count, 1, GROUP), lambda head, block: (0, 0, 0))
    col = pl.BlockSpec((count, GROUP, 1), lambda head, block: (0, 0, 0))
    line = pl.BlockSpec((1, 1, GROUP), lambda head, block: (head, 0, block))
    return main, side, row, col, line


def attention_forward(scale, q, k, v, kr, vr, kp, vp, row, col):
    rows, width = q.shape
    main, side, row_spec, col_spec, line = attention_specs(width)
    heads, count = rows // HD, width // GROUP
    return pl.pallas_call(
        lambda *refs: attention_forward_kernel(scale, *refs),
        grid=(heads, count),
        in_specs=[main, main, main, main, main, side, side, row_spec, col_spec],
        out_specs=[main, line],
        out_shape=[
            jax.ShapeDtypeStruct((rows, width), bf16),
            jax.ShapeDtypeStruct((heads, 1, width), f32),
        ],
        scratch_shapes=[pltpu.VMEM((count, GROUP, GROUP), f32)],
        compiler_params=pltpu.CompilerParams(vmem_limit_bytes=50 * 2**20),
        cost_estimate=pl.CostEstimate(
            flops=heads * count * 4 * GROUP * 1088 * HD * 4,
            bytes_accessed=6 * rows * width * 2,
            transcendentals=heads * count * GROUP * 1088,
        ),
    )(q, k, v, kr, vr, kp, vp, row, col)


def attention_backward_kernel(
    scale,
    q_ref,
    k_ref,
    v_ref,
    kr_ref,
    vr_ref,
    kp_ref,
    vp_ref,
    row_ref,
    col_ref,
    mixed_ref,
    total_ref,
    grad_ref,
    gq_ref,
    gk_ref,
    gv_ref,
    gkr_ref,
    gvr_ref,
    gkp_ref,
    gvp_ref,
    bias_ref,
):
    @pl.when(jnp.logical_and(pl.program_id(0) == 0, pl.program_id(1) == 0))
    def fill():
        visible_bias(bias_ref, row_ref, col_ref)

    block = pl.program_id(1)

    @pl.when(block == 0)
    def blank():
        gkp_ref[...] = jnp.zeros_like(gkp_ref)
        gvp_ref[...] = jnp.zeros_like(gvp_ref)

    parts = GROUP // QUERIES
    sums = {}
    for part in reversed(range(parts)):
        lanes = slice(part * QUERIES, (part + 1) * QUERIES)
        upto = (part + 1) * QUERIES
        query = q_ref[:, lanes]
        grad = grad_ref[:, lanes]
        bias = bias_ref[block, :upto, lanes] - total_ref[0, :, lanes]
        mean = jnp.sum(
            grad.astype(f32) * mixed_ref[:, lanes].astype(f32), axis=0, keepdims=True
        )
        grad_query = jnp.zeros((HD, QUERIES), f32)
        for name, keys, values, extra in (
            ("p", kp_ref[...], vp_ref[...], -total_ref[0, :, lanes]),
            ("r", kr_ref[:, :upto], vr_ref[:, :upto], bias),
            ("l", k_ref[:, :upto], v_ref[:, :upto], bias),
        ):
            chances = jnp.exp(dot_tn(keys, query) * scale + extra)
            slope = (chances * (dot_tn(values, grad) - mean)).astype(bf16)
            grad_query += dot_nn(keys, slope)
            grad_keys = dot_nt(query, slope)
            grad_values = dot_nt(grad, chances.astype(bf16))
            if name in sums:
                old_keys, old_values = sums[name]
                if name == "p":
                    sums[name] = (old_keys + grad_keys, old_values + grad_values)
                else:
                    sums[name] = (
                        jnp.concatenate([old_keys[:, :upto] + grad_keys, old_keys[:, upto:]], axis=1),
                        jnp.concatenate(
                            [old_values[:, :upto] + grad_values, old_values[:, upto:]], axis=1
                        ),
                    )
            else:
                sums[name] = (grad_keys, grad_values)
        gq_ref[:, lanes] = grad_query * scale
    gkp_ref[...] += sums["p"][0] * scale
    gvp_ref[...] += sums["p"][1]
    gkr_ref[...] = (sums["r"][0] * scale).astype(bf16)
    gvr_ref[...] = sums["r"][1].astype(bf16)
    gk_ref[...] = sums["l"][0] * scale
    gv_ref[...] = sums["l"][1]


def attention_backward(scale, q, k, v, kr, vr, kp, vp, row, col, mixed, total, grad):
    rows, width = q.shape
    main, side, row_spec, col_spec, line = attention_specs(width)
    heads, count = rows // HD, width // GROUP
    wide = jax.ShapeDtypeStruct((rows, width), f32)
    low = jax.ShapeDtypeStruct((rows, width), bf16)
    return pl.pallas_call(
        lambda *refs: attention_backward_kernel(scale, *refs),
        grid=(heads, count),
        in_specs=[main, main, main, main, main, side, side, row_spec, col_spec, main, line, main],
        out_specs=[main, main, main, main, main, side, side],
        out_shape=[
            wide,
            wide,
            wide,
            low,
            low,
            jax.ShapeDtypeStruct((rows, NP), f32),
            jax.ShapeDtypeStruct((rows, NP), f32),
        ],
        scratch_shapes=[pltpu.VMEM((count, GROUP, GROUP), f32)],
        compiler_params=pltpu.CompilerParams(vmem_limit_bytes=50 * 2**20),
        cost_estimate=pl.CostEstimate(
            flops=heads * count * 10 * GROUP * 1088 * HD * 4,
            bytes_accessed=14 * rows * width * 2,
            transcendentals=heads * count * GROUP * 1088,
        ),
    )(q, k, v, kr, vr, kp, vp, row, col, mixed, total, grad)


rate_numerator = 2.0


def matmul(left, right, left_dim, right_dim, out=f32):
    return lax.dot_general(
        left, right, (((left_dim,), (right_dim,)), ((), ())), preferred_element_type=f32
    ).astype(out)


def core_swap(value):
    return lax.ppermute(value, "core", [(0, 1), (1, 0)])


def gather_chips(value):
    return lax.all_gather(value, ("dp", "chip"), axis=0, tiled=True)


def scatter_chips(value):
    return lax.psum_scatter(value, ("dp", "chip"), scatter_dimension=0, tiled=True)


def by_core(core, mine, other, axis=0):
    return jnp.where(
        core == 0,
        jnp.concatenate([mine, other], axis=axis),
        jnp.concatenate([other, mine], axis=axis),
    )


def inverse_rms(values):
    return lax.rsqrt(jnp.mean(values * values, axis=-1, keepdims=True) + norm_epsilon)


def norm_back(grad_normed, values, inverse, gain):
    normal = values * inverse
    scaled = grad_normed * gain
    grad_gain = jnp.sum(grad_normed * normal, axis=0)
    grad_values = inverse * (scaled - normal * jnp.mean(scaled * normal, axis=-1, keepdims=True))
    return (grad_values, grad_gain)


def on_device(
    inputs,
    segments,
    attn_gain,
    query_weight,
    key_weight,
    value_weight,
    output_weight,
    persistent,
    memory_first,
    memory_second,
    rate_weight,
    decay_logit,
    momentum_logit,
    ffn_gain,
    gate_weight,
    up_weight,
    down_weight,
    cotangent,
):
    groups, chips, core_count = (lax.axis_size("dp"), lax.axis_size("chip"), 2)
    core = lax.axis_index("core")
    chip = lax.axis_index("chip")
    position = chip * core_count + core
    chain = chips * core_count
    devices = groups * chain
    scale = HD ** (-0.5)
    rate_scale = rate_numerator / MH
    half = D // 2
    core_heads = H // core_count
    heads = core_heads // chips
    rows = heads * HD
    width = 2 * GROUP
    shard = query_weight.shape[0]
    ff_shard = down_weight.shape[0]
    ff_half = gate_weight.shape[1] // 2

    def columns_of(which):
        def cut(weight):
            return lax.dynamic_slice_in_dim(weight, which * (weight.shape[1] // 2), weight.shape[1] // 2, 1)

        rate = cut(rate_weight)
        tail = jnp.concatenate([rate, persistent, attn_gain[:, None]], axis=1)
        tail = jnp.pad(tail, ((0, 0), (0, 128 - tail.shape[1])))
        return jnp.concatenate([cut(key_weight), cut(value_weight), cut(query_weight), tail], axis=1)

    w_one = gather_chips(by_core(core, columns_of(core), core_swap(columns_of(1 - core))))

    tokens = inputs[0]
    tokens_other = core_swap(tokens)
    grad_out = cotangent[0]
    grad_out_pair = jnp.concatenate([grad_out, core_swap(grad_out)], axis=0)

    mem_all = lax.all_gather(
        jnp.concatenate([memory_first, memory_second], axis=1),
        ("dp", "chip", "core"),
        axis=0,
        tiled=True,
    )
    mem_mine = lax.dynamic_slice_in_dim(mem_all, core * half + chip * rows, rows, 0).astype(f32)
    first_init, second_init = mem_mine[:, :MH], mem_mine[:, MH:]

    out_order = [(s, 2 * (s % (devices // 2)) + s // (devices // 2)) for s in range(devices)]
    w_output = gather_chips(lax.ppermute(output_weight, ("dp", "chip", "core"), out_order))

    def ff_columns(which):
        def cut(weight):
            parts = weight.reshape(shard, devices // 2, 2, ff_shard)
            return lax.dynamic_index_in_dim(parts, which, 2, keepdims=False).reshape(shard, ff_half)

        return jnp.concatenate([cut(gate_weight), cut(up_weight)], axis=1)

    w_gate_up = gather_chips(by_core(core, ff_columns(core), core_swap(ff_columns(1 - core))))
    w_down = gather_chips(down_weight)
    gain_two = lax.all_gather(ffn_gain, ("dp", "chip", "core"), axis=0, tiled=True).astype(f32)

    ids = segments[0].reshape(chain, GROUP)
    first_id, last_id = ids[:, 0], ids[:, GROUP - 1]
    before = jnp.concatenate([first_id[:1], ids[:-1, GROUP - 1]])
    joined = jnp.logical_and(jnp.arange(chain) > 0, first_id == before)
    carry = jnp.logical_and(joined, first_id == last_id)
    kept = jnp.logical_and(joined[:, None], ids == first_id[:, None])
    retain = kept.astype(f32)[:, None, :]
    update = (ids == last_id[:, None]).astype(f32)[:, None, :]
    flags = jnp.stack(
        [
            carry.astype(jnp.int32),
            jnp.any(kept, axis=1).astype(jnp.int32),
            jnp.logical_not(jnp.all(kept, axis=1)).astype(jnp.int32),
            jnp.full((chain,), core, jnp.int32),
        ]
    )
    pair_ids = jnp.stack(
        [
            lax.dynamic_index_in_dim(ids, position, keepdims=False),
            lax.dynamic_index_in_dim(ids, chip * core_count + 1 - core, keepdims=False),
        ]
    )
    id_row, id_col = pair_ids[:, None, :], pair_ids[:, :, None]
    decay = jax.nn.sigmoid(decay_logit)
    momentum = jax.nn.sigmoid(momentum_logit)
    head_at = core * core_heads + chip * heads
    scalars = jnp.stack(
        [
            lax.dynamic_slice_in_dim(1.0 - decay, head_at, heads),
            lax.dynamic_slice_in_dim(momentum, head_at, heads),
        ]
    )

    gain_at = 3 * half + core_heads + NP
    gain_one = w_one[:, gain_at].astype(f32)
    tokens_pair = jnp.concatenate([tokens, tokens_other], axis=0).astype(f32)
    inverse_one = inverse_rms(tokens_pair)
    normed = (tokens_pair * inverse_one * gain_one).astype(bf16)
    low = matmul(w_one[:, : 3 * half], normed, 0, 1, bf16)
    keys, values, query = low[:half], low[half : 2 * half], low[2 * half :]
    rate_sigmoid = jax.nn.sigmoid(matmul(w_one[:, 3 * half :], normed, 0, 1)[:core_heads])
    rates = (rate_scale * rate_sigmoid).astype(bf16).reshape(chips, heads, width)
    packed = jnp.concatenate(
        [
            keys.reshape(chips, rows, width),
            values.reshape(chips, rows, width),
            jnp.pad(rates, ((0, 0), (0, RATE_ROWS - heads), (0, 0))),
        ],
        axis=1,
    )
    packed = lax.all_to_all(packed, "chip", 0, 0, tiled=True)
    probes = lax.all_to_all(query.reshape(chips, rows, width), "chip", 0, 0, tiled=True)
    recalled, saved = memory_forward(
        flags, packed, probes, retain, update, first_init, second_init, scalars
    )
    recalled = lax.all_to_all(recalled, "chip", 0, 0, tiled=True).reshape(half, width)

    def flip(value):
        return jnp.concatenate([value[:, GROUP:], value[:, :GROUP]], axis=1)

    recalled_other = core_swap(flip(recalled))
    persist = w_one[:, gain_at - NP : gain_at]
    context = jnp.concatenate([by_core(core, recalled, recalled_other), persist], axis=1)
    low_context = matmul(w_one[:, : 2 * half], context, 0, 0, bf16)
    keys_r, values_r = low_context[:half, :width], low_context[half:, :width]
    keys_p, values_p = low_context[:half, width:], low_context[half:, width:]
    mixed, total = attention_forward(
        scale, query, keys, values, keys_r, values_r, keys_p, values_p, id_row, id_col
    )

    def pair_sum(partial):
        return partial[:GROUP] + core_swap(partial[GROUP:].astype(bf16)).astype(f32)

    def pair_rows(own):
        return jnp.concatenate([own, core_swap(own)], axis=0)

    middle = tokens.astype(f32) + pair_sum(matmul(mixed, w_output, 0, 0))
    inverse_two = inverse_rms(middle)
    normed_two = pair_rows((middle * inverse_two * gain_two).astype(bf16))
    gate = matmul(normed_two, w_gate_up[:, :ff_half], 1, 0)
    up = matmul(normed_two, w_gate_up[:, ff_half:], 1, 0)
    gate_sigmoid = jax.nn.sigmoid(gate)
    gate_silu = gate * gate_sigmoid
    hidden = (gate_silu * up).astype(bf16)
    result = (middle + pair_sum(matmul(hidden, w_down, 1, 0))).astype(bf16)

    grad_down_w = matmul(hidden, grad_out_pair, 0, 0, bf16)
    grad_hidden = matmul(grad_out_pair, w_down, 1, 1)
    grad_gate = (grad_hidden * up * gate_sigmoid * (1.0 + gate * (1.0 - gate_sigmoid))).astype(bf16)
    grad_up = (grad_hidden * gate_silu).astype(bf16)
    grad_gate_up = jnp.concatenate([grad_gate, grad_up], axis=1)
    grad_gate_up_w = matmul(normed_two, grad_gate_up, 0, 0, bf16)
    grad_normed_two = pair_sum(matmul(grad_gate_up, w_gate_up, 1, 1))
    grad_middle_norm, grad_gain_two = norm_back(grad_normed_two, middle, inverse_two, gain_two)
    grad_middle = grad_out.astype(f32) + grad_middle_norm
    down_part = scatter_chips(grad_down_w).astype(f32)
    gate_up_part = scatter_chips(grad_gate_up_w)

    grad_attended = pair_rows(grad_middle.astype(bf16))
    grad_output_w = matmul(mixed, grad_attended, 1, 0, bf16)
    output_part = scatter_chips(grad_output_w)
    grad_mixed = matmul(w_output, grad_attended, 1, 1, bf16)
    (
        grad_query_att,
        grad_keys_att,
        grad_values_att,
        grad_keys_r,
        grad_values_r,
        grad_keys_p,
        grad_values_p,
    ) = attention_backward(
        scale,
        query,
        keys,
        values,
        keys_r,
        values_r,
        keys_p,
        values_p,
        id_row,
        id_col,
        mixed,
        total,
        grad_mixed,
    )
    grad_low_context = jnp.concatenate(
        [
            jnp.concatenate([grad_keys_r, grad_keys_p.astype(bf16)], axis=1),
            jnp.concatenate([grad_values_r, grad_values_p.astype(bf16)], axis=1),
        ],
        axis=0,
    )
    grad_context = matmul(w_one[:, : 2 * half], grad_low_context, 1, 0)
    grad_persist = grad_context[:, width:]
    pull = (
        lax.dynamic_slice_in_dim(grad_context, core * half, half, 0)[:, :width]
        + core_swap(
            flip(
                lax.dynamic_slice_in_dim(grad_context, (1 - core) * half, half, 0)[:, :width]
            ).astype(bf16)
        ).astype(f32)
    ).astype(bf16)
    pull = lax.all_to_all(pull.reshape(chips, rows, width), "chip", 0, 0, tiled=True)
    grad_context_w = matmul(context, grad_low_context, 1, 1)
    grads, grad_first, grad_second, grad_scalars = memory_backward(
        flags, packed, probes, retain, update, first_init, second_init, scalars, saved, pull
    )
    grads = lax.all_to_all(grads, "chip", 0, 0, tiled=True)
    cuts = (rows, 2 * rows, 2 * rows + RATE_ROWS)
    grad_keys = grad_keys_att + grads[:, : cuts[0]].reshape(half, width).astype(f32)
    grad_values = grad_values_att + grads[:, cuts[0] : cuts[1]].reshape(half, width).astype(f32)
    grad_query = grad_query_att + grads[:, cuts[2] :].reshape(half, width).astype(f32)
    grad_rates = grads[:, cuts[1] : cuts[1] + heads].reshape(core_heads, width).astype(f32)
    grad_rate_logits = grad_rates * rate_scale * rate_sigmoid * (1.0 - rate_sigmoid)
    grad_low = jnp.concatenate(
        [
            grad_keys.astype(bf16),
            grad_values.astype(bf16),
            grad_query.astype(bf16),
            jnp.pad(grad_rate_logits.astype(bf16), ((0, 128 - core_heads), (0, 0))),
        ],
        axis=0,
    )
    grad_one_w = matmul(normed, grad_low, 0, 1)
    grad_normed = matmul(grad_low, w_one, 0, 1)
    grad_normed_own = pair_sum(grad_normed)
    grad_tokens_one, grad_gain_one = norm_back(
        grad_normed_own, tokens.astype(f32), inverse_one[:GROUP], gain_one
    )
    grad_inputs = (grad_middle + grad_tokens_one).astype(bf16)
    one_part = scatter_chips(
        jnp.concatenate(
            [
                grad_one_w[:, : 2 * half] + grad_context_w,
                grad_one_w[:, 2 * half : 3 * half],
                grad_one_w[:, 3 * half : 3 * half + core_heads],
                grad_persist,
                jnp.zeros((D, 128 - core_heads - NP), f32),
            ],
            axis=1,
        ).astype(bf16)
    )
    zeros = jnp.zeros((D, 2 * MH), bf16)
    mem_part = lax.psum_scatter(
        lax.dynamic_update_slice_in_dim(
            zeros,
            jnp.concatenate([grad_first, grad_second], axis=1).astype(bf16),
            core * half + chip * rows,
            0,
        ),
        ("dp", "chip", "core"),
        scatter_dimension=0,
        tiled=True,
    ).astype(f32)
    scalar_sums = jnp.sum(grad_scalars, axis=1)[: 2 * heads].reshape(heads, 2)
    spots = jnp.zeros((2, H), f32)
    spots = lax.dynamic_update_slice(spots, scalar_sums.T, (0, head_at))
    sums = lax.psum(
        jnp.concatenate([grad_gain_one, grad_gain_two, spots.reshape(-1)]), ("dp", "chip", "core")
    )
    index = (lax.axis_index("dp") * chips + chip) * core_count + core
    gain_one_part = lax.dynamic_slice_in_dim(sums, index * shard, shard)
    gain_two_part = lax.dynamic_slice_in_dim(sums, D + index * shard, shard)
    grad_decay = sums[2 * D : 2 * D + H] * decay * (1.0 - decay)
    grad_momentum = sums[2 * D + H :] * momentum * (1.0 - momentum)

    def own_rows(part):
        mine = lax.dynamic_slice_in_dim(part, core * shard, shard, 0)
        other = core_swap(lax.dynamic_slice_in_dim(part, (1 - core) * shard, shard, 0))
        return mine, other

    mine, other = own_rows(one_part)
    mine, other = mine.astype(f32), other.astype(f32)

    def whole_columns(start, size):
        return by_core(core, mine[:, start : start + size], other[:, start : start + size], 1)

    rate_at = 3 * half
    persist_part = (mine + other)[:, rate_at + core_heads : rate_at + core_heads + NP]

    def ff_rows(mine, other):
        pair = jnp.stack([mine, other]).reshape(2, shard, devices // 2, ff_shard).astype(f32)
        pair = jnp.where(core == 0, pair, pair[::-1])
        return pair.transpose(1, 2, 0, 3).reshape(shard, 2 * ff_half)

    mine_ff, other_ff = own_rows(gate_up_part)
    gate_part = ff_rows(mine_ff[:, :ff_half], other_ff[:, :ff_half])
    up_part = ff_rows(mine_ff[:, ff_half:], other_ff[:, ff_half:])
    output_own = lax.ppermute(
        output_part, ("dp", "chip", "core"), [(d, s) for s, d in out_order]
    ).astype(f32)
    return (
        result[None],
        grad_inputs[None],
        gain_one_part,
        whole_columns(2 * half, half),
        whole_columns(0, half),
        whole_columns(half, half),
        output_own,
        persist_part,
        mem_part[:, :MH],
        mem_part[:, MH:],
        whole_columns(rate_at, core_heads),
        grad_decay,
        grad_momentum,
        gain_two_part,
        gate_part,
        up_part,
        down_part,
    )


def solution(mesh):
    split = jax.sharding.Mesh(
        mesh.devices.reshape(mesh.shape["dp"], mesh.shape["seq"] // 2, 2), ("dp", "chip", "core")
    )
    row = P("dp", ("chip", "core"), None)
    vector = P(("dp", "chip", "core"))
    matrix = P(("dp", "chip", "core"), None)
    in_specs = (
        row,
        P("dp", None),
        vector,
        matrix,
        matrix,
        matrix,
        matrix,
        matrix,
        matrix,
        matrix,
        matrix,
        P(),
        P(),
        vector,
        matrix,
        matrix,
        matrix,
        row,
    )
    out_specs = (
        row,
        row,
        vector,
        matrix,
        matrix,
        matrix,
        matrix,
        matrix,
        matrix,
        matrix,
        matrix,
        P(),
        P(),
        vector,
        matrix,
        matrix,
        matrix,
    )
    return jax.shard_map(
        on_device, mesh=split, in_specs=in_specs, out_specs=out_specs, check_vma=False
    )
```

time: 6140 us -> 1460 us (0.24)
  waiting for transfers between devices: 3750 us -> 861 us
  matrix products: 803 us -> 184 us
  starting transfers between devices: 618 us -> 34.6 us
  other arithmetic: 497 us -> 51.8 us
  blocking collectives: 328 us -> 110 us
  Pallas kernels: 0 us -> 124 us
    ppermute x16, waiting for transfers between devices: 2120 us -> 23.6 us  [the longest x14 15.8 us: core_swap(): return lax.ppermute(value, 'core', [(0, 1), (1, 0)])]
    reduce_scatter x9 -> x5, waiting for transfers between devices: 1480 us -> 485 us  [the longest x4 458 us: scatter_chips(): lax.psum_scatter(value, ('dp', 'chip'), scatter_dimension=0, tiled=True)]
    dot_general x65 -> x17, matrix products: 800 us -> 184 us  [matmul(): lax.dot_general(left, right, (((left_dim,), (right_dim,)), ((), ())), pre...]
    ppermute x16, starting transfers between devices: 617 us -> 13.6 us  [the longest x14 5.25 us: core_swap(): return lax.ppermute(value, 'core', [(0, 1), (1, 0)])]
    convert_element_type x40 -> x21, other arithmetic: 257 us -> 16.3 us  [the longest x1 5 us: on_device(): grad_attended = pair_rows(grad_middle.astype(bf16))]
    unnamed x2 -> x1, blocking collectives: 247 us -> 42.6 us
    pallas_call x0 -> x4, Pallas kernels: none -> 124 us  [the longest x1 45.3 us: memory_backward(): pl.pallas_call(lambda *refs: memory_backward_kernel(heads, blocks, *refs)...]
    all_gather x9 -> x5, waiting for transfers between devices: 141 us -> 252 us  [the longest x4 235 us: gather_chips(): return lax.all_gather(value, ('dp', 'chip'), axis=0, tiled=True)]
  transfers between devices with their start and end apart: 36 -> 30, of which waited for: 28 -> 22; matrix products, arithmetic and copies ran while one was open for 11% -> 14% of each run, Pallas kernels for 0% -> 6%
where the time goes in v1:
time: 1460 us; the launch traced here: 1450 us
  waiting for transfers between devices  861 us (59%)
  matrix products  184 us (13%)
  Pallas kernels  124 us (8%)
  blocking collectives  110 us (8%)
  local copies, waits for them, and re-layouts  70.4 us (5%)
  other arithmetic  51.8 us (4%)
  starting transfers between devices  34.6 us (2%)
  between operations  15.6 us (1%)
    reduce_scatter x4, waiting for transfers between devices, scatter_chips(): lax.psum_scatter(value, ('dp', 'chip'), scatter_dimension=0, tiled=True)  458 us
    all_gather x4, waiting for transfers between devices, gather_chips(): return lax.all_gather(value, ('dp', 'chip'), axis=0, tiled=True)  235 us
    dot_general x17, matrix products, matmul(): lax.dot_general(left, right, (((left_dim,), (right_dim,)), ((), ())), pre...  184 us
    all_to_all x1, waiting for transfers between devices, on_device(): grads = lax.all_to_all(grads, 'chip', 0, 0, tiled=True)  54.5 us
    pallas_call x1, Pallas kernels, memory_backward(): pl.pallas_call(lambda *refs: memory_backward_kernel(heads, blocks, *refs)...  45.3 us
    unnamed x1, blocking collectives  42.6 us
    psum x1, blocking collectives, on_device(): lax.psum(jnp.concatenate([grad_gain_one, grad_gain_two, spots.reshape(-1)...  41.4 us
    pallas_call x1, Pallas kernels, attention_backward(): pl.pallas_call(lambda *refs: attention_backward_kernel(scale, *refs), gri...  33.3 us
  transfers between devices with their start and end apart: 30, of which 22 were waited for; matrix products, arithmetic and copies ran while one was open for 14% of the time, Pallas kernels for 6%

profile of v1, /device:TPU:2, one launch (start us, length us, event | category | flops | bytes accessed | tf_op | source)
XLA Modules:
  0.0 1451.0 jit_solution(760829556036332903)
XLA Ops:
  15.8 3.4 collective-permute-start.3
  19.2 3.1 collective-permute-done.3
  24.2 4.6 dynamic-slice_reduce_fusion.2
  28.9 2.6 collective-permute-start.6
  34.4 3.0 collective-permute-done.1
  38.1 82.1 %all-gather.6.cloned.1.call-done = bf16[1536,2432]{1,0:T(8,128)(2,1)} async-done(((bf16[96,2432]{1,0:T(8,128)(2,1)}), bf16[1536,2432]{1,0:T(8,128)(2,1)}) %all-gather.6.cloned.1.call-update) | async-done | bytes 7471120 | tf_op jit(solution)/shard_map/all_gather | solution.py:650
  121.5 10.1 fusion.13
  131.7 2.3 fusion.79
  134.0 4.4 all-to-all-start.1
  140.2 3.2 multiply_convert_fusion.5
  143.5 3.2 fusion.24
  146.7 11.7 all-to-all-done.1.refs_3_
  158.5 5.2 all-to-all-start
  166.7 16.6 %all-gather.8.cloned.1.call-done = bf16[1536,768]{1,0:T(8,128)(2,1)} async-done(((bf16[48,768]{1,0:T(8,128)(2,1)}), bf16[1536,768]{1,0:T(8,128)(2,1)}) %all-gather.8.cloned.1.call-update) | async-done | bytes 2359312 | tf_op jit(solution)/shard_map/all_gather | solution.py:730
  184.3 19.2 %all-to-all-done.refs_1_.refs_2_.refs_4_ = bf16[4,400,1024]{2,1,0:T(8,128)(2,1)} async-done(((bf16[4,400,1024]{2,1,0:T(8,128)(2,1)}), bf16[4,400,1024]{2,1,0:T(8,128)(2,1)}, u32[]{:S(2)}, u32[]{:S(2)}) %all-to-all-start) | async-done | bytes 3276832 | tf_op jit(solution)/shard_map/all_to_all | solution.py:803
  203.5 23.5 %shard_map.305 = (bf16[4,192,1024]{2,1,0:T(8,128)(2,1)S(1)}, f32[8,4,192,384]{3,2,1,0:T(8,128)}) custom-call(s32[4,8]{1,0:T(4,128)S(1)} %add_add_fusion.refs_0_, bf16[4,400,1024]{2,1,0:T(8,128)(2,1)} %all-to-all-done.refs_1_.refs_2_.refs_4_, bf16[4,400,1024]{2,1,0:T(8,128)(2,1)} %all-to-all-done.refs_1_.refs_2_.refs_4_, ...), custom_call_target="tpu_custom_call" | custom-call | flops 16911433728 | bytes 14155776 | tf_op jit(solution)/shard_map/pallas_call | solution.py:146
  227.0 25.8 %all_to_all.25 = bf16[4,192,1024]{2,1,0:T(8,128)(2,1)S(1)} all-to-all(bf16[4,192,1024]{2,1,0:T(8,128)(2,1)S(1)} %get-tuple-element.32), channel_id=1, replica_groups=mesh['dp'=4,'chip'=4,'core'=2] {'chip'}, dimensions={0} | all-to-all | bytes 3145728 | tf_op jit(solution)/shard_map/all_to_all | solution.py:808
  255.8 2.3 collective-permute-done.2
  258.1 2.9 maximum_select_fusion
  261.1 9.5 convolution_convert_fusion.2
  270.6 2.1 fusion.81
  272.8 21.5 %shard_map.306 = (bf16[768,1024]{1,0:T(8,128)(2,1)S(1)}, f32[8,1,1024]{2,1,0:T(1,128)S(1)}) custom-call(bf16[768,1024]{1,0:T(8,128)(2,1)} %get-tuple-element.107.refs_0_, bf16[768,1024]{1,0:T(8,128)(2,1)} %get-tuple-element.106.refs_1_, bf16[768,1024]{1,0:T(8,128)(2,1)} %get-tuple-element.105.refs_2_, bf16[768,1024]{1,0:T(8,128)(2,1)} %get-tuple-element.111.refs_3_, ...), custom_call_target="tpu_custom_call" | custom-call | flops 13690208256 | bytes 9437184 | tf_op jit(solution)/shard_map/pallas_call | solution.py:509
  294.3 5.0 fusion.89
  303.2 42.6 %all-reduce.4 = bf16[1536]{0:T(1024)(128)(2,1)S(1)} all-reduce(bf16[1536]{0:T(1024)(128)(2,1)S(1)} %dynamic-update-slice), channel_id=1, replica_groups=mesh['dp'=4,'chip'=4,'core'=2] {'dp','chip','core'}, use_global_device_ids=true, to_apply=%add.4 | all-reduce | flops 1536 | bytes 6144
  345.7 3.0 multiply_reduce_fusion.2
  350.9 11.4 all-gather.14.cloned.1.call-done
  362.3 11.8 fusion.38
  374.1 141.7 %all-gather.12.cloned.1.call-done = bf16[1536,4096]{1,0:T(8,128)(2,1)} async-done(((bf16[96,4096]{1,0:T(8,128)(2,1)}), bf16[1536,4096]{1,0:T(8,128)(2,1)}) %all-gather.12.cloned.1.call-update) | async-done | bytes 12582928 | tf_op jit(solution)/shard_map/all_gather | solution.py:650
  515.8 11.4 fusion.9
  527.3 17.7 %multiply_convert_fusion.1 = (bf16[1024,2048]{1,0:T(8,128)(2,1)}, bf16[1024,2048]{1,0:T(8,128)(2,1)}, bf16[1024,2048]{1,0:T(8,128)(2,1)}) fusion(f32[1024,2048]{1,0:T(8,128)} %fusion.38, f32[1024,2048]{1,0:T(8,128)} %fusion.9, bf16[1536,4096]{1,0:T(8,128)(2,1)} %all-gather.12.cloned.1.call-done, bf16[512,1536]{1,0:T(8,128)(2,1)} %collective-permute-done.5, ...), kind=kOutput, calls=%fused_computation.7 | convolution fusion | flops 6480199680 | bytes 38797312 | tf_op jit(solution)/shard_map/dot_general | solution.py:640
  544.9 18.9 %fusion.16 = f32[1024,1536]{1,0:T(8,128)S(1)} fusion(bf16[1536,4096]{1,0:T(8,128)(2,1)} %all-gather.12.cloned.1.call-done, bf16[1024,2048]{1,0:T(8,128)(2,1)} %get-tuple-element.100, bf16[1024,2048]{1,0:T(8,128)(2,1)} %get-tuple-element.99), kind=kOutput, calls=%fused_computation.28 | convolution fusion | flops 12901679104 | bytes 27262976 | tf_op jit(solution)/shard_map/dot_general | solution.py:640
  564.1 8.7 fusion.90
  576.6 5.0 fusion.77
  582.0 3.0 collective-permute-done.10
  585.1 4.8 fusion.42.refs_11_
  589.9 33.3 %shard_map.307 = (f32[768,1024]{1,0:T(8,128)}, f32[768,1024]{1,0:T(8,128)}, f32[768,1024]{1,0:T(8,128)}, bf16[768,1024]{1,0:T(8,128)(2,1)S(1)}, bf16[768,1024]{1...) custom-call(bf16[768,1024]{1,0:T(8,128)(2,1)} %get-tuple-element.107.refs_0_, ...), custom_call_target="tpu_custom_call" | custom-call | flops 34225520640 | bytes 22020096 | tf_op jit(solution)/shard_map/pallas_call | solution.py:612
  623.3 7.3 fusion.18
  631.5 3.0 collective-permute-done.11
  636.2 2.7 copy.114
  638.9 4.9 all-to-all-start.3
  643.8 5.7 convolution_convert_fusion.3
  649.6 14.9 %all-to-all-done.3.refs_11_ = bf16[4,192,1024]{2,1,0:T(8,128)(2,1)} async-done(((bf16[4,192,1024]{2,1,0:T(8,128)(2,1)}), bf16[4,192,1024]{2,1,0:T(8,128)(2,1)}, u32[]{:S(2)}, u32[]{:S(2)}) %all-to-all-start.3) | async-done | bytes 1572896 | tf_op jit(solution)/shard_map/all_to_all | solution.py:895
  664.5 45.3 %shard_map.308 = (bf16[4,592,1024]{2,1,0:T(8,128)(2,1)}, f32[192,384]{1,0:T(8,128)}, f32[192,384]{1,0:T(8,128)}, f32[8,384]{1,0:T(8,128)}) custom-call(s32[4,8]{1,0:T(4,128)} %copy-done.5, bf16[4,400,1024]{2,1,0:T(8,128)(2,1)} %all-to-all-done.refs_1_.refs_2_.refs_4_, bf16[4,400,1024]{2,1,0:T(8,128)(2,1)} %all-to-all-done.refs_1_.refs_2_.refs_4_, ...), custom_call_target="tpu_custom_call" | custom-call | flops 45902462976 | bytes 18874368 | tf_op jit(solution)/shard_map/pallas_call | solution.py:389
  714.2 11.6 convolution_convert_fusion.1
  725.8 5.7 all-to-all-start.4
  733.2 54.5 %all-to-all-done.4 = bf16[4,592,1024]{2,1,0:T(8,128)(2,1)} async-done(((bf16[4,592,1024]{2,1,0:T(8,128)(2,1)}), bf16[4,592,1024]{2,1,0:T(8,128)(2,1)}, u32[]{:S(2)}, u32[]{:S(2)}) %all-to-all-start.4) | async-done | bytes 4849696 | tf_op jit(solution)/shard_map/all_to_all | solution.py:900
  788.6 3.1 fusion.78
  799.1 14.2 fusion.69
  813.3 4.7 slice.388
  818.0 11.7 fusion.1
  829.7 11.9 concatenate.162
  843.0 20.1 %convolution_convert_fusion = bf16[1536,4096]{1,0:T(8,128)(2,1)} fusion(bf16[1024,2048]{1,0:T(8,128)(2,1)} %get-tuple-element.100, bf16[1024,2048]{1,0:T(8,128)(2,1)} %get-tuple-element.99, bf16[512,1536]{1,0:T(8,128)(2,1)} %collective-permute-done.5, bf16[512,1536]{1,0:T(8,128)(2,1)S(1)} %copy-done.24), kind=kOutput, calls=%fused_computation | convolution fusion | flops 12914262016 | bytes 24117248 | tf_op jit(solution)/shard_map/dot_general | solution.py:640
  864.6 12.3 fusion.71
  876.8 2.6 copy-done.13
  880.8 4.9 collective-permute-start.14
  886.3 4.8 collective-permute-done.14
  891.8 27.2 %reduce-scatter.10.cloned.1.call-done = bf16[48,768]{1,0:T(8,128)(2,1)} async-done(((bf16[1536,768]{1,0:T(8,128)(2,1)}), bf16[48,768]{1,0:T(8,128)(2,1)}) %reduce-scatter.10.cloned.1.call-update) | async-done | bytes 73744 | tf_op jit(solution)/shard_map/reduce_scatter | solution.py:936
  920.5 3.0 fusion.30
  923.5 41.4 %psum.7 = f32[3104]{0:T(1024)S(1)} all-reduce(f32[3104]{0:T(1024)S(1)} %pad_maximum_fusion.25), channel_id=1, replica_groups=mesh['dp'=4,'chip'=4,'core'=2] {'dp','chip','core'}, use_global_device_ids=true, to_apply=%region_9.10 | all-reduce | flops 3104 | bytes 24832 | tf_op jit(solution)/shard_map/psum | solution.py:950
  966.1 5.1 fusion.41
  971.2 98.4 %reduce-scatter.14.cloned.1.call-done = bf16[128,1536]{1,0:T(8,128)(2,1)} async-done(((bf16[2048,1536]{1,0:T(8,128)(2,1)}), bf16[128,1536]{1,0:T(8,128)(2,1)}) %reduce-scatter.14.cloned.1.call-update) | async-done | bytes 393232 | tf_op jit(solution)/shard_map/reduce_scatter | solution.py:654
  1069.5 2.0 convert_element_type.277
  1071.5 156.0 %reduce-scatter.6.cloned.1.call-done = bf16[96,2432]{1,0:T(8,128)(2,1)} async-done(((bf16[1536,2432]{1,0:T(8,128)(2,1)}), bf16[96,2432]{1,0:T(8,128)(2,1)}) %reduce-scatter.6.cloned.1.call-update) | async-done | bytes 466960 | tf_op jit(solution)/shard_map/reduce_scatter | solution.py:654
  1232.5 203.3 %reduce-scatter.12.cloned.1.call-done = bf16[96,4096]{1,0:T(8,128)(2,1)} async-done(((bf16[1536,4096]{1,0:T(8,128)(2,1)}), bf16[96,4096]{1,0:T(8,128)(2,1)}) %reduce-scatter.12.cloned.1.call-update) | async-done | bytes 786448 | tf_op jit(solution)/shard_map/reduce_scatter | solution.py:654
  (288 shorter events, 72.5 us)
Async XLA Ops:
  7.2 8.6 copy-start.54
  7.2 16.4 %copy-start.30 = (bf16[48,4096]{1,0:T(8,128)(2,1)S(1)}, bf16[48,4096]{1,0:T(8,128)(2,1)}, u32[]{:S(2)}) copy-start(bf16[48,4096]{1,0:T(8,128)(2,1)} %param.32) | copy-start | bytes 1179652
  7.2 16.7 %copy-start.31 = (bf16[48,4096]{1,0:T(8,128)(2,1)S(1)}, bf16[48,4096]{1,0:T(8,128)(2,1)}, u32[]{:S(2)}) copy-start(bf16[48,4096]{1,0:T(8,128)(2,1)} %param.33) | copy-start | bytes 1179652
  7.2 113.0 %all-gather.6.cloned.1.call-start = ((), (), s32[]{:S(2)}) async-start(), calls=%async_computation.10 | async-start | bytes 7938048 | tf_op jit(solution)/shard_map/all_gather | solution.py:650
  11.8 1.6 collective-permute-start
  14.2 169.0 %all-gather.8.cloned.1.call-start = ((), (), s32[]{:S(2)}) async-start(), calls=%async_computation.11 | async-start | bytes 2433024 | tf_op jit(solution)/shard_map/all_gather | solution.py:730
  15.7 278.6 %all-gather.10.cloned.1.call-start = ((), (), s32[]{:S(2)}) async-start(), calls=%async_computation.12 | async-start | bytes 2506752 | tf_op jit(solution)/shard_map/all_gather | solution.py:650
  15.8 6.5 collective-permute-start.3
  23.0 339.4 %all-gather.14.cloned.1.call-start = ((), (), s32[]{:S(2)}) async-start(), calls=%async_computation.14 | async-start | bytes 6684672 | tf_op jit(solution)/shard_map/all_gather | solution.py:650
  23.5 492.3 %all-gather.12.cloned.1.call-start = ((), (), s32[]{:S(2)}) async-start(), calls=%async_computation.13 | async-start | bytes 13369344 | tf_op jit(solution)/shard_map/all_gather | solution.py:650
  24.1 9.8 copy-start.11
  28.9 3.9 collective-permute-start.6
  33.9 3.5 collective-permute-start.1
  37.4 94.3 %copy-start.21 = (bf16[512,1536]{1,0:T(8,128)(2,1)}, bf16[512,1536]{1,0:T(8,128)(2,1)S(1)}, u32[]{:S(2)}) copy-start(bf16[512,1536]{1,0:T(8,128)(2,1)S(1)} %collective-permute-done.1) | copy-start | bytes 4718596
  38.1 102.1 %copy-start.47 = (f32[1024]{0:T(1024)}, f32[1024]{0:T(1024)S(1)}, u32[]{:S(2)}) copy-start(f32[1024]{0:T(1024)S(1)} %add_rsqrt_fusion) | copy-start | bytes 12292
  121.5 18.7 %copy-start.39 = (f32[1536]{0:T(1024)}, f32[1536]{0:T(1024)S(1)}, u32[]{:S(2)}) copy-start(f32[1536]{0:T(1024)S(1)} %convert_reduce_fusion) | copy-start | bytes 18436
  134.0 4.9 copy-start.41
  134.0 24.5 %all-to-all-start.1 = ((bf16[4,192,1024]{2,1,0:T(8,128)(2,1)}), bf16[4,192,1024]{2,1,0:T(8,128)(2,1)S(1)}, u32[]{:S(2)}, u32[]{:S(2)}) async-start(bf16[4,192,1024]{2,1,0:T(8,128)(2,1)} %bitcast.6), calls=%async_computation.1 | async-start | bytes 3145728 | tf_op jit(solution)/shard_map/all_to_all | solution.py:804
  146.7 17.0 %copy-start.49 = (f32[16]{0:T(128)S(1)}, f32[16]{0:T(128)}, u32[]{:S(2)}) copy-start(f32[16]{0:T(128)} %param.30) | copy-start | bytes 196
  146.7 17.0 %copy-start.55 = (f32[16]{0:T(128)S(1)}, f32[16]{0:T(128)}, u32[]{:S(2)}) copy-start(f32[16]{0:T(128)} %param.29) | copy-start | bytes 196
  158.5 45.0 %copy-start = (bf16[4,192,1024]{2,1,0:T(8,128)(2,1)}, bf16[4,192,1024]{2,1,0:T(8,128)(2,1)S(1)}, u32[]{:S(2)}) copy-start(bf16[4,192,1024]{2,1,0:T(8,128)(2,1)S(1)} %all-to-all-done.1.refs_3_) | copy-start | bytes 4718596
  158.5 45.0 %all-to-all-start = ((bf16[4,400,1024]{2,1,0:T(8,128)(2,1)}), bf16[4,400,1024]{2,1,0:T(8,128)(2,1)}, u32[]{:S(2)}, u32[]{:S(2)}) async-start(bf16[4,400,1024]{2,1,0:T(8,128)(2,1)} %fusion.24), calls=%async_computation | async-start | bytes 6553600 | tf_op jit(solution)/shard_map/all_to_all | solution.py:803
  164.4 62.6 %copy-start.6 = (f32[2,2]{1,0:T(2,128)}, f32[2,2]{1,0:T(2,128)S(1)}, u32[]{:S(2)}) copy-start(f32[2,2]{1,0:T(2,128)S(1)} %pad_maximum_fusion.26.refs_9_) | copy-start | bytes 52
  166.6 60.4 %copy-start.5 = (s32[4,8]{1,0:T(4,128)}, s32[4,8]{1,0:T(4,128)S(1)}, u32[]{:S(2)}) copy-start(s32[4,8]{1,0:T(4,128)S(1)} %add_add_fusion.refs_0_) | copy-start | bytes 388
  166.7 60.3 %copy-start.3 = (f32[8,1,512]{2,1,0:T(1,128)}, f32[8,1,512]{2,1,0:T(1,128)S(1)}, u32[]{:S(2)}) copy-start(f32[8,1,512]{2,1,0:T(1,128)S(1)} %get-tuple-element.147.refs_6_) | copy-start | bytes 49156
  166.7 60.3 %copy-start.4 = (f32[8,1,512]{2,1,0:T(1,128)}, f32[8,1,512]{2,1,0:T(1,128)S(1)}, u32[]{:S(2)}) copy-start(f32[8,1,512]{2,1,0:T(1,128)S(1)} %get-tuple-element.148.refs_5_) | copy-start | bytes 49156
  184.3 42.7 %copy-start.1 = (f32[192,384]{1,0:T(8,128)}, f32[192,384]{1,0:T(8,128)S(1)}, u32[]{:S(2)}) copy-start(f32[192,384]{1,0:T(8,128)S(1)} %get-tuple-element.119.refs_8_) | copy-start | bytes 884740
  184.3 42.7 %copy-start.2 = (f32[192,384]{1,0:T(8,128)}, f32[192,384]{1,0:T(8,128)S(1)}, u32[]{:S(2)}) copy-start(f32[192,384]{1,0:T(8,128)S(1)} %get-tuple-element.120.refs_7_) | copy-start | bytes 884740
  254.4 3.8 collective-permute-start.2
  255.8 5.2 copy-start.32
  261.1 9.5 copy-start.16
  294.3 5.0 copy-start.7
  302.5 43.3 %collective-permute-start.4 = (bf16[512,1536]{1,0:T(8,128)(2,1)}, bf16[512,1536]{1,0:T(8,128)(2,1)S(1)}, u32[]{:S(2)}, u32[]{:S(2)}) collective-permute-start(bf16[512,1536]{1,0:T(8,128)(2,1)} %slice.392), channel_id=1, source_target_pairs={{0,1},{1,0},{2,3},{3,2},{4,5},{5,4},{6,7},{7,6},{8,9},{9,8},{10,11... | collective-permute-start | bytes 4718600 | tf_op jit(solution)/shard_map/ppermute | solution.py:646
  302.6 48.3 %collective-permute-start.8 = (bf16[512,1536]{1,0:T(8,128)(2,1)}, bf16[512,1536]{1,0:T(8,128)(2,1)}, u32[]{:S(2)}, u32[]{:S(2)}) collective-permute-start(bf16[512,1536]{1,0:T(8,128)(2,1)} %bitcast.14), channel_id=1, source_target_pairs={{0,1},{1,0},{2,3},{3,2},{4,5},{5,4},{6,7},{7,6},{8,9},{9,8},{10,11... | collective-permute-start | bytes 4718600 | tf_op jit(solution)/shard_map/ppermute | solution.py:646
  350.8 176.5 %copy-start.23 = (bf16[512,1536]{1,0:T(8,128)(2,1)}, bf16[512,1536]{1,0:T(8,128)(2,1)S(1)}, u32[]{:S(2)}) copy-start(bf16[512,1536]{1,0:T(8,128)(2,1)S(1)} %multiply_convert_fusion.3) | copy-start | bytes 4718596
  350.8 23.3 %collective-permute-start.5 = (bf16[512,1536]{1,0:T(8,128)(2,1)S(1)}, bf16[512,1536]{1,0:T(8,128)(2,1)}, u32[]{:S(2)}, u32[]{:S(2)}) collective-permute-start(bf16[512,1536]{1,0:T(8,128)(2,1)S(1)} %multiply_convert_fusion.3), channel_id=1, source_target_pairs={{0,1},{1,0},{2,3},{3,2},{4,5},{5,4},{6,7},{7,6},{8,9},{9,8},{10,11... | collective-permute-start | bytes 4718600 | tf_op jit(solution)/shard_map/ppermute | solution.py:646
  544.9 19.2 %copy-start.57 = (bf16[1024,2048]{1,0:T(8,128)(2,1)S(1)}, bf16[1024,2048]{1,0:T(8,128)(2,1)}, u32[]{:S(2)}) copy-start(bf16[1024,2048]{1,0:T(8,128)(2,1)} %get-tuple-element.101) | copy-start | bytes 12582916
  564.0 9.6 collective-permute-start.9
  573.1 3.6 collective-permute-start.7
  576.4 8.7 copy-start.52
  581.6 8.2 copy-start.29
  581.6 3.4 collective-permute-start.10
  585.1 38.2 %slice-start = ((s8[7471104]{0:T(1024)(128)(4,1)}), s8[4194304]{0:T(1024)(128)(4,1)S(1)}, s32[]{:S(2)}) async-start(s8[7471104]{0:T(1024)(128)(4,1)} %bitcast.115), calls=%async_computation.20 | async-start | bytes 8388608
  589.9 33.4 %slice-start.1 = ((s8[7471104]{0:T(1024)(128)(4,1)}), s8[3276800]{0:T(1024)(128)(4,1)S(1)}, s32[]{:S(2)}) async-start(s8[7471104]{0:T(1024)(128)(4,1)} %bitcast.115), calls=%async_computation.21 | async-start | bytes 6553600
  623.2 7.4 copy-start.34
  623.3 7.3 copy-start.36
  631.1 3.5 collective-permute-start.11
  636.2 7.6 copy-start.8
  638.9 25.6 %all-to-all-start.3 = ((bf16[4,192,1024]{2,1,0:T(8,128)(2,1)}), bf16[4,192,1024]{2,1,0:T(8,128)(2,1)}, u32[]{:S(2)}, u32[]{:S(2)}) async-start(bf16[4,192,1024]{2,1,0:T(8,128)(2,1)} %bitcast.104), calls=%async_computation.3 | async-start | bytes 3145728 | tf_op jit(solution)/shard_map/all_to_all | solution.py:895
  643.8 236.9 %reduce-scatter.8.cloned.1.call-start = ((), (), s32[]{:S(2)}) async-start(), calls=%async_computation.16 | async-start | bytes 2506752 | tf_op jit(solution)/shard_map/reduce_scatter | solution.py:654
  649.6 269.5 %reduce-scatter.10.cloned.1.call-start = ((), (), s32[]{:S(2)}) async-start(), calls=%async_computation.17 | async-start | bytes 2433024 | tf_op jit(solution)/shard_map/reduce_scatter | solution.py:936
  714.1 355.4 %reduce-scatter.14.cloned.1.call-start = ((), (), s32[]{:S(2)}) async-start(), calls=%async_computation.19 | async-start | bytes 6684672 | tf_op jit(solution)/shard_map/reduce_scatter | solution.py:654
  725.8 62.8 %copy-start.43 = (f32[8,1024]{1,0:T(8,128)S(1)}, f32[8,1024]{1,0:T(8,128)}, u32[]{:S(2)}) copy-start(f32[8,1024]{1,0:T(8,128)} %get-tuple-element.156) | copy-start | bytes 98308
  725.8 61.9 %all-to-all-start.4 = ((bf16[4,592,1024]{2,1,0:T(8,128)(2,1)}), bf16[4,592,1024]{2,1,0:T(8,128)(2,1)}, u32[]{:S(2)}, u32[]{:S(2)}) async-start(bf16[4,592,1024]{2,1,0:T(8,128)(2,1)} %get-tuple-element.41), calls=%async_computation.4 | async-start | bytes 9699328 | tf_op jit(solution)/shard_map/all_to_all | solution.py:900
  731.4 496.1 %reduce-scatter.6.cloned.1.call-start = ((), (), s32[]{:S(2)}) async-start(), calls=%async_computation.15 | async-start | bytes 7938048 | tf_op jit(solution)/shard_map/reduce_scatter | solution.py:654
  788.6 9.0 copy-start.44
  841.6 594.2 %reduce-scatter.12.cloned.1.call-start = ((), (), s32[]{:S(2)}) async-start(), calls=%async_computation.18 | async-start | bytes 13369344 | tf_op jit(solution)/shard_map/reduce_scatter | solution.py:654
  879.4 6.3 copy-start.46
  880.8 39.8 %collective-permute-start.12 = (bf16[512,1536]{1,0:T(8,128)(2,1)}, bf16[512,1536]{1,0:T(8,128)(2,1)S(1)}, u32[]{:S(2)}, u32[]{:S(2)}) collective-permute-start(bf16[512,1536]{1,0:T(8,128)(2,1)} %slice.389), channel_id=1, source_target_pairs={{0,1},{1,0},{2,3},{3,2},{4,5},{5,4},{6,7},{7,6},{8,9},{9,8},{10,11... | collective-permute-start | bytes 4718600 | tf_op jit(solution)/shard_map/ppermute | solution.py:646
  880.8 10.3 collective-permute-start.14
  920.5 45.0 %copy-start.50 = (f32[16]{0:T(128)S(1)}, f32[16]{0:T(128)}, u32[]{:S(2)}) copy-start(f32[16]{0:T(128)} %param.30) | copy-start | bytes 196
  920.5 45.0 %copy-start.51 = (f32[16]{0:T(128)S(1)}, f32[16]{0:T(128)}, u32[]{:S(2)}) copy-start(f32[16]{0:T(128)} %get-tuple-element.98) | copy-start | bytes 196
  1228.6 1.6 collective-permute-start.13
  1436.8 2.5 collective-permute-start.15
  (27 other events, 78.5 us)
Sparse Core Ops, SparseCore 0:
  14.4 105.8 all-gather.5
  123.7 59.5 all-gather.7
  186.6 78.0 all-gather.9
  267.3 94.9 all-gather.13
  365.5 150.2 all-gather.11
  649.7 165.0 reduce-scatter.7
  821.0 98.0 reduce-scatter.9
  924.3 145.1 reduce-scatter.13
  1074.9 152.5 reduce-scatter.5
  1233.0 202.7 reduce-scatter.11

commit v2 on v1

v2 whole, which is shorter than its diff:
```python
import jax
import jax.numpy as jnp
from jax import lax
from jax.experimental import pallas as pl
from jax.experimental.pallas import tpu as pltpu
from jax.sharding import PartitionSpec as P

D = 1536
H = 16
HD = 96
MH = 384
NP = 64
GROUP = 512
RATE_ROWS = 16
RATE_SCALE = 2.0 / 384
norm_epsilon = 1e-06
f32 = jnp.float32
bf16 = jnp.bfloat16


def dot_nn(left, right):
    return lax.dot_general(left, right, (((1,), (0,)), ((), ())), preferred_element_type=f32)


def dot_tn(left, right):
    return lax.dot_general(left, right, (((0,), (0,)), ((), ())), preferred_element_type=f32)


def dot_nt(left, right):
    return lax.dot_general(left, right, (((1,), (1,)), ((), ())), preferred_element_type=f32)


def inverse_root(values):
    return lax.rsqrt(jnp.mean(values * values, axis=0, keepdims=True) + norm_epsilon)


def spot(heads, head, which):
    at = 2 * head + which if which < 2 else 2 * heads + head
    return slice(at * HD, (at + 1) * HD)


def memory_forward_kernel(
    heads,
    blocks,
    flags,
    main_ref,
    retain_ref,
    update_ref,
    first_ref,
    second_ref,
    scalars_ref,
    recalled_ref,
    saved_ref,
    state,
):
    turn = pl.program_id(0)

    @pl.when(turn == 0)
    def blank():
        state[...] = jnp.zeros_like(state)

    saved_ref[0] = state[...]
    retain = retain_ref[0]

    def recall_with(first, second, head):
        rows = slice(head * HD, (head + 1) * HD)
        raw = main_ref[spot(heads, head, 2), :].astype(f32)
        probes = (raw * inverse_root(raw)).astype(bf16)
        inner = dot_tn(first[rows, :].astype(bf16), probes)
        return dot_nn(second[rows, :].astype(bf16), jax.nn.silu(inner).astype(bf16))

    only_state = flags[1, turn] * (1 - flags[2, turn])
    only_init = flags[2, turn] * (1 - flags[1, turn])

    @pl.when(only_state == 1)
    def from_state():
        for head in range(heads):
            recalled_ref[0, head * HD : (head + 1) * HD, :] = recall_with(
                state[0], state[1], head
            ).astype(bf16)

    @pl.when(only_init == 1)
    def from_init():
        for head in range(heads):
            recalled_ref[0, head * HD : (head + 1) * HD, :] = recall_with(
                first_ref[...], second_ref[...], head
            ).astype(bf16)

    @pl.when(only_state + only_init == 0)
    def from_both():
        for head in range(heads):
            recalled_ref[0, head * HD : (head + 1) * HD, :] = (
                retain * recall_with(state[0], state[1], head)
                + (1.0 - retain) * recall_with(first_ref[...], second_ref[...], head)
            ).astype(bf16)

    @pl.when(turn < blocks - 1)
    def step():
        carry = flags[0, turn].astype(f32)
        for head in range(heads):
            rows = slice(head * HD, (head + 1) * HD)
            keep = scalars_ref[0, head]
            push = scalars_ref[1, head] * carry
            base_first = jnp.where(carry > 0.5, state[0, rows, :], first_ref[rows, :])
            base_second = jnp.where(carry > 0.5, state[1, rows, :], second_ref[rows, :])
            raw = main_ref[spot(heads, head, 0), :].astype(f32)
            keys = (raw * inverse_root(raw)).astype(bf16)
            second_low = base_second.astype(bf16)
            inner = dot_tn(base_first.astype(bf16), keys)
            gate = jax.nn.sigmoid(inner)
            active = inner * gate
            slope = gate + active * (1.0 - gate)
            active_low = active.astype(bf16)
            at = 3 * heads * HD + head
            rate = RATE_SCALE * jax.nn.sigmoid(main_ref[at : at + 1, :].astype(f32))
            weight = rate * update_ref[0] * (1.0 / GROUP)
            error = dot_nn(second_low, active_low) - main_ref[spot(heads, head, 1), :].astype(f32)
            pull = (error * weight).astype(bf16)
            inner_pull = (dot_tn(second_low, pull) * slope).astype(bf16)
            speed_first = push * state[2, rows, :] - dot_nt(keys, inner_pull)
            speed_second = push * state[3, rows, :] - dot_nt(pull, active_low)
            state[0, rows, :] = keep * base_first + speed_first
            state[1, rows, :] = keep * base_second + speed_second
            state[2, rows, :] = speed_first
            state[3, rows, :] = speed_second


def memory_forward(flags, main, retain, update, first, second, scalars, chips):
    rows = (main.shape[0] - RATE_ROWS) // 3
    heads = rows // HD
    width = main.shape[1] // chips
    blocks = main.shape[1] // GROUP
    per = width // GROUP

    def block(turn, flags):
        return (0, ((turn // per) ^ flags[4, 0]) * per + ((turn % per) ^ flags[3, 0]))

    def by_chip(turn, flags):
        return (turn // per, 0, turn % per)

    def by_turn(turn, flags):
        return (turn, 0, 0)

    def whole(turn, flags):
        return (0, 0)

    line = pl.BlockSpec((1, 1, GROUP), by_turn)
    return pl.pallas_call(
        lambda *refs: memory_forward_kernel(heads, blocks, *refs),
        grid_spec=pltpu.PrefetchScalarGridSpec(
            num_scalar_prefetch=1,
            grid=(blocks,),
            in_specs=[
                pl.BlockSpec((3 * rows + RATE_ROWS, GROUP), block),
                line,
                line,
                pl.BlockSpec((rows, MH), whole),
                pl.BlockSpec((rows, MH), whole),
                pl.BlockSpec(memory_space=pltpu.SMEM),
            ],
            out_specs=[
                pl.BlockSpec((1, rows, GROUP), by_chip),
                pl.BlockSpec((1, 4, rows, MH), lambda turn, flags: (turn, 0, 0, 0)),
            ],
            scratch_shapes=[pltpu.VMEM((4, rows, MH), f32)],
        ),
        out_shape=[
            jax.ShapeDtypeStruct((chips, rows, width), bf16),
            jax.ShapeDtypeStruct((blocks, 4, rows, MH), f32),
        ],
        compiler_params=pltpu.CompilerParams(vmem_limit_bytes=50 * 2**20),
        cost_estimate=pl.CostEstimate(
            flops=blocks * heads * 7 * 2 * GROUP * HD * MH * 4,
            bytes_accessed=blocks * 6 * rows * MH * 4,
            transcendentals=blocks * heads * 2 * MH * GROUP,
        ),
    )(flags, main, retain, update, first, second, scalars)


def memory_backward_kernel(
    heads,
    blocks,
    flags,
    main_ref,
    retain_ref,
    update_ref,
    first_ref,
    second_ref,
    scalars_ref,
    saved_ref,
    pull_ref,
    grads_ref,
    grad_first_ref,
    grad_second_ref,
    grad_scalars_ref,
    message,
):
    count = pl.program_id(0)
    turn = blocks - 1 - count

    @pl.when(count == 0)
    def blank():
        message[...] = jnp.zeros_like(message)
        grad_first_ref[...] = jnp.zeros_like(grad_first_ref)
        grad_second_ref[...] = jnp.zeros_like(grad_second_ref)
        grad_scalars_ref[...] = jnp.zeros_like(grad_scalars_ref)

    rate_row = 3 * heads * HD

    @pl.when(count == 0)
    def last():
        for head in range(heads):
            grads_ref[spot(heads, head, 0), :] = jnp.zeros((HD, GROUP), bf16)
            grads_ref[spot(heads, head, 1), :] = jnp.zeros((HD, GROUP), bf16)
        grads_ref[rate_row:, :] = jnp.zeros((RATE_ROWS, GROUP), bf16)

    @pl.when(count > 0)
    def step():
        carry = flags[0, turn].astype(f32)
        grad_rates = []
        for head in range(heads):
            rows = slice(head * HD, (head + 1) * HD)
            keep = scalars_ref[0, head]
            push = scalars_ref[1, head] * carry
            base_first = jnp.where(carry > 0.5, saved_ref[0, 0, rows, :], first_ref[rows, :])
            base_second = jnp.where(carry > 0.5, saved_ref[0, 1, rows, :], second_ref[rows, :])
            grad_a = message[0, rows, :]
            grad_b = message[1, rows, :]
            grad_sa = message[2, rows, :] + grad_a
            grad_sb = message[3, rows, :] + grad_b
            momentum_part = carry * (
                jnp.sum(saved_ref[0, 2, rows, :] * grad_sa, axis=0, keepdims=True)
                + jnp.sum(saved_ref[0, 3, rows, :] * grad_sb, axis=0, keepdims=True)
            )
            decay_part = -(
                jnp.sum(base_first * grad_a, axis=0, keepdims=True)
                + jnp.sum(base_second * grad_b, axis=0, keepdims=True)
            )
            grad_scalars_ref[2 * head : 2 * head + 1, :] += decay_part
            grad_scalars_ref[2 * head + 1 : 2 * head + 2, :] += momentum_part
            back_a = (-grad_sa).astype(bf16)
            back_b = (-grad_sb).astype(bf16)
            raw = main_ref[spot(heads, head, 0), :].astype(f32)
            inverse = inverse_root(raw)
            normal = raw * inverse
            keys = normal.astype(bf16)
            first_low = base_first.astype(bf16)
            second_low = base_second.astype(bf16)
            inner = dot_tn(first_low, keys)
            gate = jax.nn.sigmoid(inner)
            active = inner * gate
            slope = gate + active * (1.0 - gate)
            bend = gate * (1.0 - gate) * (2.0 + inner - 2.0 * active)
            active_low = active.astype(bf16)
            weight = update_ref[0] * (1.0 / GROUP)
            at = rate_row + head
            rate_sigmoid = jax.nn.sigmoid(main_ref[at : at + 1, :].astype(f32))
            rate = RATE_SCALE * rate_sigmoid
            error = dot_nn(second_low, active_low) - main_ref[spot(heads, head, 1), :].astype(f32)
            pull = (error * (rate * weight)).astype(bf16)
            spread = dot_tn(second_low, pull)
            inner_pull = (spread * slope).astype(bf16)
            back_inner = dot_tn(back_a, keys)
            back_spread = (back_inner * slope).astype(bf16)
            grad_pull = dot_nn(back_b, active_low) + dot_nn(second_low, back_spread)
            grad_rates.append(
                jnp.sum(grad_pull * error, axis=0, keepdims=True)
                * weight
                * rate
                * (1.0 - rate_sigmoid)
            )
            grad_error = grad_pull * (rate * weight)
            grad_error_low = grad_error.astype(bf16)
            grads_ref[spot(heads, head, 1), :] = (-grad_error).astype(bf16)
            grad_active = dot_tn(back_b, pull) + dot_tn(second_low, grad_error_low)
            grad_inner = (back_inner * spread * bend + grad_active * slope).astype(bf16)
            grad_normal = dot_nn(back_a, inner_pull) + dot_nn(first_low, grad_inner)
            grads_ref[spot(heads, head, 0), :] = (
                inverse
                * (grad_normal - normal * jnp.mean(grad_normal * normal, axis=0, keepdims=True))
            ).astype(bf16)
            base_grad_a = keep * grad_a + dot_nt(keys, grad_inner)
            base_grad_b = (
                keep * grad_b + dot_nt(pull, back_spread) + dot_nt(grad_error_low, active_low)
            )
            message[0, rows, :] = carry * base_grad_a
            message[1, rows, :] = carry * base_grad_b
            message[2, rows, :] = push * grad_sa
            message[3, rows, :] = push * grad_sb
            grad_first_ref[rows, :] += (1.0 - carry) * base_grad_a
            grad_second_ref[rows, :] += (1.0 - carry) * base_grad_b
        grad_rates.append(jnp.zeros((RATE_ROWS - heads, GROUP), f32))
        grads_ref[rate_row:, :] = jnp.concatenate(
            grad_rates, axis=0
        ).astype(bf16)

    retain = retain_ref[0]

    def recall_back(first, second, grad_recalled, head):
        rows = slice(head * HD, (head + 1) * HD)
        raw = main_ref[spot(heads, head, 2), :].astype(f32)
        inverse = inverse_root(raw)
        normal = raw * inverse
        probes = normal.astype(bf16)
        first_low = first[rows, :].astype(bf16)
        inner = dot_tn(first_low, probes)
        gate = jax.nn.sigmoid(inner)
        active = inner * gate
        slope = gate + active * (1.0 - gate)
        grad_inner = (dot_tn(second[rows, :].astype(bf16), grad_recalled) * slope).astype(bf16)
        grad_second = dot_nt(grad_recalled, active.astype(bf16))
        grad_first = dot_nt(probes, grad_inner)
        grad_normal = dot_nn(first_low, grad_inner)
        grad_probes = inverse * (
            grad_normal - normal * jnp.mean(grad_normal * normal, axis=0, keepdims=True)
        )
        return grad_first, grad_second, grad_probes

    only_state = flags[1, turn] * (1 - flags[2, turn])
    only_init = flags[2, turn] * (1 - flags[1, turn])

    def from_state(whole):
        for head in range(heads):
            rows = slice(head * HD, (head + 1) * HD)
            grad_recalled = pull_ref[0, rows, :]
            if not whole:
                grad_recalled = (grad_recalled.astype(f32) * retain).astype(bf16)
            grad_first, grad_second, grad_probes = recall_back(
                saved_ref[0, 0], saved_ref[0, 1], grad_recalled, head
            )
            message[0, rows, :] += grad_first
            message[1, rows, :] += grad_second
            grads_ref[spot(heads, head, 2), :] = grad_probes.astype(bf16)

    def from_init(whole):
        for head in range(heads):
            rows = slice(head * HD, (head + 1) * HD)
            grad_recalled = pull_ref[0, rows, :]
            if not whole:
                grad_recalled = (grad_recalled.astype(f32) * (1.0 - retain)).astype(bf16)
            grad_first, grad_second, grad_probes = recall_back(
                first_ref[...], second_ref[...], grad_recalled, head
            )
            grad_first_ref[rows, :] += grad_first
            grad_second_ref[rows, :] += grad_second
            if not whole:
                grad_probes = grad_probes + grads_ref[spot(heads, head, 2), :].astype(f32)
            grads_ref[spot(heads, head, 2), :] = grad_probes.astype(bf16)

    @pl.when(only_state == 1)
    def state_alone():
        from_state(True)

    @pl.when(only_init == 1)
    def init_alone():
        from_init(True)

    @pl.when(only_state + only_init == 0)
    def both():
        from_state(False)
        from_init(False)


def memory_backward(
    flags, main, retain, update, first, second, scalars, saved, pull
):
    chips, rows, width = pull.shape
    heads = rows // HD
    blocks = chips * width // GROUP
    per = width // GROUP
    all_rows = 3 * rows + RATE_ROWS

    def block(count, flags):
        turn = blocks - 1 - count
        return (0, ((turn // per) ^ flags[4, 0]) * per + ((turn % per) ^ flags[3, 0]))

    def by_chip(count, flags):
        turn = blocks - 1 - count
        return (turn // per, 0, turn % per)

    def by_turn(count, flags):
        return (blocks - 1 - count, 0, 0)

    def whole(count, flags):
        return (0, 0)

    line = pl.BlockSpec((1, 1, GROUP), by_turn)
    matrix = pl.BlockSpec((rows, MH), whole)
    return pl.pallas_call(
        lambda *refs: memory_backward_kernel(heads, blocks, *refs),
        grid_spec=pltpu.PrefetchScalarGridSpec(
            num_scalar_prefetch=1,
            grid=(blocks,),
            in_specs=[
                pl.BlockSpec((3 * rows + RATE_ROWS, GROUP), block),
                line,
                line,
                matrix,
                matrix,
                pl.BlockSpec(memory_space=pltpu.SMEM),
                pl.BlockSpec(
                    (1, 4, rows, MH), lambda count, flags: (blocks - 1 - count, 0, 0, 0)
                ),
                pl.BlockSpec((1, rows, GROUP), by_chip),
            ],
            out_specs=[
                pl.BlockSpec((all_rows, GROUP), block),
                matrix,
                matrix,
                pl.BlockSpec((8, MH), whole),
            ],
            scratch_shapes=[pltpu.VMEM((4, rows, MH), f32)],
        ),
        out_shape=[
            jax.ShapeDtypeStruct((all_rows, chips * width), bf16),
            jax.ShapeDtypeStruct((rows, MH), f32),
            jax.ShapeDtypeStruct((rows, MH), f32),
            jax.ShapeDtypeStruct((8, MH), f32),
        ],
        compiler_params=pltpu.CompilerParams(vmem_limit_bytes=56 * 2**20),
        cost_estimate=pl.CostEstimate(
            flops=blocks * heads * 19 * 2 * GROUP * HD * MH * 4,
            bytes_accessed=blocks * 8 * rows * MH * 4,
            transcendentals=blocks * heads * 2 * MH * GROUP,
        ),
    )(flags, main, retain, update, first, second, scalars, saved, pull)


QUERIES = 256


def visible_bias(bias_ref, row_ref, col_ref):
    shape = bias_ref.shape[1:]
    key = lax.broadcasted_iota(jnp.int32, shape, 0)
    query = lax.broadcasted_iota(jnp.int32, shape, 1)
    for block in range(bias_ref.shape[0]):
        seen = jnp.logical_and(key <= query, col_ref[block] == row_ref[block])
        bias_ref[block] = jnp.where(seen, 0.0, -1e30)


def attention_forward_kernel(
    scale, core, low_ref, query_ref, far_ref, side_ref, row_ref, col_ref, mixed_ref, total_ref, bias_ref
):
    @pl.when(jnp.logical_and(pl.program_id(0) == 0, pl.program_id(1) == 0))
    def fill():
        visible_bias(bias_ref, row_ref, col_ref)

    block = pl.program_id(1)
    for part in range(GROUP // QUERIES):
        lanes = slice(part * QUERIES, (part + 1) * QUERIES)
        upto = (part + 1) * QUERIES
        query = query_ref[:, lanes]
        bias = bias_ref[block, :upto, lanes]
        s_p = dot_tn(side_ref[:HD], query) * scale
        s_r = dot_tn(far_ref[:HD, :upto], query) * scale + bias
        s_l = dot_tn(low_ref[:HD, :upto], query) * scale + bias
        top = jnp.maximum(
            jnp.max(s_p, axis=0, keepdims=True),
            jnp.maximum(
                jnp.max(s_r, axis=0, keepdims=True), jnp.max(s_l, axis=0, keepdims=True)
            ),
        )
        e_p = jnp.exp(s_p - top)
        e_r = jnp.exp(s_r - top)
        e_l = jnp.exp(s_l - top)
        total = (
            jnp.sum(e_p, axis=0, keepdims=True)
            + jnp.sum(e_r, axis=0, keepdims=True)
            + jnp.sum(e_l, axis=0, keepdims=True)
        )
        mixed = (
            dot_nn(side_ref[HD:], e_p.astype(bf16))
            + dot_nn(far_ref[HD:, :upto], e_r.astype(bf16))
            + dot_nn(low_ref[HD:, :upto], e_l.astype(bf16))
        )
        mixed_ref[:, lanes] = (mixed / total).astype(bf16)
        total_ref[0, :, lanes] = top + jnp.log(total)


def attention_specs(rows, width):
    count = width // GROUP
    heads = rows // HD
    low = pl.BlockSpec((2 * HD, GROUP), lambda head, block, core: (head, block))
    query = pl.BlockSpec((HD, GROUP), lambda head, block, core: (2 * heads + head, block))
    far = pl.BlockSpec((2 * HD, GROUP), lambda head, block, core: (head, block ^ core[0]))
    side = pl.BlockSpec((2 * HD, NP), lambda head, block, core: (head, 0))
    row = pl.BlockSpec((count, 1, GROUP), lambda head, block, core: (0, 0, 0))
    col = pl.BlockSpec((count, GROUP, 1), lambda head, block, core: (0, 0, 0))
    main = pl.BlockSpec((HD, GROUP), lambda head, block, core: (head, block))
    line = pl.BlockSpec((1, 1, GROUP), lambda head, block, core: (head, 0, block))
    return low, query, far, side, row, col, main, line


def attention_forward(scale, core, low, far, side, row, col):
    rows, width = low.shape[0] // 3, low.shape[1]
    low_spec, query_spec, far_spec, side_spec, row_spec, col_spec, main, line = attention_specs(
        rows, width
    )
    heads, count = rows // HD, width // GROUP
    return pl.pallas_call(
        lambda *refs: attention_forward_kernel(scale, *refs),
        grid_spec=pltpu.PrefetchScalarGridSpec(
            num_scalar_prefetch=1,
            grid=(heads, count),
            in_specs=[low_spec, query_spec, far_spec, side_spec, row_spec, col_spec],
            out_specs=[main, line],
            scratch_shapes=[pltpu.VMEM((count, GROUP, GROUP), f32)],
        ),
        out_shape=[
            jax.ShapeDtypeStruct((rows, width), bf16),
            jax.ShapeDtypeStruct((heads, 1, width), f32),
        ],
        compiler_params=pltpu.CompilerParams(vmem_limit_bytes=50 * 2**20),
        cost_estimate=pl.CostEstimate(
            flops=heads * count * 4 * GROUP * 1088 * HD * 4,
            bytes_accessed=6 * rows * width * 2,
            transcendentals=heads * count * GROUP * 1088,
        ),
    )(core, low, low, far, side, row, col)


def attention_backward_kernel(
    scale,
    core,
    low_ref,
    query_ref,
    far_ref,
    side_ref,
    row_ref,
    col_ref,
    mixed_ref,
    total_ref,
    grad_ref,
    grads_ref,
    grad_far_ref,
    grad_side_ref,
    bias_ref,
):
    @pl.when(jnp.logical_and(pl.program_id(0) == 0, pl.program_id(1) == 0))
    def fill():
        visible_bias(bias_ref, row_ref, col_ref)

    block = pl.program_id(1)

    @pl.when(block == 0)
    def blank():
        grad_side_ref[...] = jnp.zeros_like(grad_side_ref)

    parts = GROUP // QUERIES
    sums = {}
    for part in reversed(range(parts)):
        lanes = slice(part * QUERIES, (part + 1) * QUERIES)
        upto = (part + 1) * QUERIES
        query = query_ref[:, lanes]
        grad = grad_ref[:, lanes]
        bias = bias_ref[block, :upto, lanes] - total_ref[0, :, lanes]
        mean = jnp.sum(
            grad.astype(f32) * mixed_ref[:, lanes].astype(f32), axis=0, keepdims=True
        )
        grad_query = jnp.zeros((HD, QUERIES), f32)
        for name, keys, values, extra in (
            ("p", side_ref[:HD], side_ref[HD:], -total_ref[0, :, lanes]),
            ("r", far_ref[:HD, :upto], far_ref[HD:, :upto], bias),
            ("l", low_ref[:HD, :upto], low_ref[HD:, :upto], bias),
        ):
            chances = jnp.exp(dot_tn(keys, query) * scale + extra)
            slope = (chances * (dot_tn(values, grad) - mean)).astype(bf16)
            grad_query += dot_nn(keys, slope)
            grad_keys = dot_nt(query, slope)
            grad_values = dot_nt(grad, chances.astype(bf16))
            if name in sums:
                old_keys, old_values = sums[name]
                if name == "p":
                    sums[name] = (old_keys + grad_keys, old_values + grad_values)
                else:
                    sums[name] = (
                        jnp.concatenate([old_keys[:, :upto] + grad_keys, old_keys[:, upto:]], axis=1),
                        jnp.concatenate(
                            [old_values[:, :upto] + grad_values, old_values[:, upto:]], axis=1
                        ),
                    )
            else:
                sums[name] = (grad_keys, grad_values)
        grads_ref[2 * HD :, lanes] = (grad_query * scale).astype(bf16)
    grad_side_ref[:HD] += sums["p"][0] * scale
    grad_side_ref[HD:] += sums["p"][1]
    grad_far_ref[:HD] = (sums["r"][0] * scale).astype(bf16)
    grad_far_ref[HD:] = sums["r"][1].astype(bf16)
    grads_ref[:HD] = (sums["l"][0] * scale).astype(bf16)
    grads_ref[HD : 2 * HD] = sums["l"][1].astype(bf16)


def attention_backward(scale, core, low, far, side, row, col, mixed, total, grad):
    rows, width = low.shape[0] // 3, low.shape[1]
    low_spec, query_spec, far_spec, side_spec, row_spec, col_spec, main, line = attention_specs(
        rows, width
    )
    heads, count = rows // HD, width // GROUP
    return pl.pallas_call(
        lambda *refs: attention_backward_kernel(scale, *refs),
        grid_spec=pltpu.PrefetchScalarGridSpec(
            num_scalar_prefetch=1,
            grid=(heads, count),
            in_specs=[
                low_spec,
                query_spec,
                far_spec,
                side_spec,
                row_spec,
                col_spec,
                main,
                line,
                main,
            ],
            out_specs=[
                pl.BlockSpec((3 * HD, GROUP), lambda head, block, core: (head, block)),
                far_spec,
                side_spec,
            ],
            scratch_shapes=[pltpu.VMEM((count, GROUP, GROUP), f32)],
        ),
        out_shape=[
            jax.ShapeDtypeStruct((3 * rows, width), bf16),
            jax.ShapeDtypeStruct((2 * rows, width), bf16),
            jax.ShapeDtypeStruct((2 * rows, NP), f32),
        ],
        compiler_params=pltpu.CompilerParams(vmem_limit_bytes=50 * 2**20),
        cost_estimate=pl.CostEstimate(
            flops=heads * count * 10 * GROUP * 1088 * HD * 4,
            bytes_accessed=14 * rows * width * 2,
            transcendentals=heads * count * GROUP * 1088,
        ),
    )(core, low, low, far, side, row, col, mixed, total, grad)


def head_of(core, chip, turn, chips, heads):
    return core * chips * heads + turn * chips + chip


def pack_weights(chips, heads, key, value, query, rate, gains, side):
    shard = key.shape[0]

    def kernel(key_ref, value_ref, query_ref, rate_ref, gains_ref, side_ref, out_ref):
        for core in range(2):
            order = [
                head_of(core, chip, turn, chips, heads)
                for chip in range(chips)
                for turn in range(heads)
            ]
            end = 3 * D // 2
            out_ref[core, :, end:] = jnp.zeros((shard, 128), bf16)
            out_ref[core, :, end : end + NP] = side_ref[...]
            out_ref[core, :, end + NP : end + NP + 2] = gains_ref[...]
            for at, head in enumerate(order):
                columns = slice(head * HD, (head + 1) * HD)
                low = 2 * at * HD
                out_ref[core, :, low : low + HD] = key_ref[:, columns]
                out_ref[core, :, low + HD : low + 2 * HD] = value_ref[:, columns]
                low = D + at * HD
                out_ref[core, :, low : low + HD] = query_ref[:, columns]
                low = end + NP + 2 + at
                out_ref[core, :, low : low + 1] = rate_ref[:, head : head + 1]

    return pl.pallas_call(
        kernel, out_shape=jax.ShapeDtypeStruct((2, shard, 3 * D // 2 + 128), bf16)
    )(key, value, query, rate, gains, side)


def pack_columns(chain, gate, up):
    shard, whole = gate.shape
    own = whole // chain

    def kernel(gate_ref, up_ref, out_ref):
        groups = out_ref.shape[2] // (2 * size)
        for place in range(chain):
            for which, ref in enumerate((gate_ref, up_ref)):
                for group in range(groups):
                    at = which * own + group * size
                    start = (group * chain + place) * size
                    out_ref[place, :, at : at + size] = ref[:, start : start + size]

    size = whole // (D // shard)
    return pl.pallas_call(
        kernel, out_shape=jax.ShapeDtypeStruct((chain, shard, 2 * own), bf16)
    )(gate, up)


def unpack_columns(parts, gate, up, gain):
    chain, shard, both = parts.shape
    own = both // 2
    whole = gate.shape[1]
    size = whole // (D // shard)

    def kernel(parts_ref, gate_ref, up_ref, gain_ref, gate_out, up_out, gain_out):
        total = jnp.zeros((shard, 1), f32)
        for which, (ref, out) in enumerate(((gate_ref, gate_out), (up_ref, up_out))):
            for place in range(chain):
                for group in range(own // size):
                    at = which * own + group * size
                    start = (group * chain + place) * size
                    out[:, start : start + size] = parts_ref[place, :, at : at + size].astype(f32)
            total += jnp.sum(out[...] * ref[...].astype(f32), axis=1, keepdims=True)
        gain_out[...] = total / gain_ref[...].astype(f32)

    return pl.pallas_call(
        kernel,
        out_shape=[
            jax.ShapeDtypeStruct((shard, whole), f32),
            jax.ShapeDtypeStruct((shard, whole), f32),
            jax.ShapeDtypeStruct((shard, 1), f32),
        ],
    )(parts, gate, up, gain)


def unpack_weights(chips, heads, parts, context, key, value, query, rate, gain):
    shard = key.shape[0]

    def kernel(parts_ref, context_ref, key_ref, value_ref, query_ref, rate_ref, gain_ref, *outs):
        key_out, value_out, query_out, rate_out, gain_out = outs
        total = jnp.zeros((shard, 1), f32)
        for core in range(2):
            for chip in range(chips):
                place = chip * 2 + core
                for turn in range(heads):
                    head = head_of(core, chip, turn, chips, heads)
                    rate_out[:, head : head + 1] = parts_ref[
                        place, :, 3 * heads * HD + turn : 3 * heads * HD + turn + 1
                    ].astype(f32)
                    columns = slice(head * HD, (head + 1) * HD)
                    for which, (weight, out) in enumerate(
                        ((key_ref, key_out), (value_ref, value_out), (query_ref, query_out))
                    ):
                        grad = parts_ref[place, :, spot(heads, turn, which)].astype(f32)
                        total += jnp.sum(
                            grad * weight[:, columns].astype(f32), axis=1, keepdims=True
                        )
                        if which < 2:
                            near = (2 * (chip * heads + turn) + which) * HD
                            grad += context_ref[core, :, near : near + HD].astype(f32)
                        out[:, columns] = grad
        total += jnp.sum(rate_out[...] * rate_ref[...].astype(f32), axis=1, keepdims=True)
        gain_out[...] = total / gain_ref[...].astype(f32)

    wide = jax.ShapeDtypeStruct((shard, D), f32)
    return pl.pallas_call(
        kernel,
        out_shape=[
            wide,
            wide,
            wide,
            jax.ShapeDtypeStruct((shard, H), f32),
            jax.ShapeDtypeStruct((shard, 1), f32),
        ],
    )(parts, context, key, value, query, rate, gain)


def project_blocks(first, blocks, tokens, gain, weight, old=()):
    columns = weight.shape[0]
    count = len(tokens)

    def kernel(*refs):
        gain_ref, weight_ref = refs[count : count + 2]
        normed_ref, main_ref = refs[-2:]
        for at in range(count):

            @pl.when(pl.program_id(0) == at)
            def one(tokens_ref=refs[at]):
                wide = tokens_ref[...].astype(f32)
                scale = lax.rsqrt(jnp.mean(wide * wide, axis=1, keepdims=True) + norm_epsilon)
                low = (wide * scale * gain_ref[...]).astype(bf16)
                normed_ref[...] = low
                main_ref[...] = dot_nt(weight_ref[...], low).astype(bf16)

    return pl.pallas_call(
        kernel,
        grid=(count,),
        in_specs=[pl.BlockSpec((GROUP, D), lambda i: (0, 0))] * count
        + [
            pl.BlockSpec((1, D), lambda i: (0, 0)),
            pl.BlockSpec((columns, D), lambda i: (0, 0)),
        ]
        + [pl.BlockSpec(memory_space=pl.ANY)] * len(old),
        out_specs=[
            pl.BlockSpec((GROUP, D), lambda i: (first + i, 0)),
            pl.BlockSpec((columns, GROUP), lambda i: (0, first + i)),
        ],
        out_shape=[
            jax.ShapeDtypeStruct((blocks * GROUP, D), bf16),
            jax.ShapeDtypeStruct((columns, blocks * GROUP), bf16),
        ],
        input_output_aliases={count + 2: 0, count + 3: 1} if old else {},
        compiler_params=pltpu.CompilerParams(vmem_limit_bytes=52 * 2**20),
        cost_estimate=pl.CostEstimate(
            flops=count * 2 * GROUP * D * columns * 2,
            bytes_accessed=count * (GROUP * D * 4 + columns * GROUP * 2) + columns * D * 2,
            transcendentals=0,
        ),
    )(*tokens, gain, weight, *old)


def merge_blocks(chip, groups, grads, grad_part, normed, weight):
    columns, tokens = grads.shape
    chips, part_rows, width = grad_part.shape
    heads = part_rows // (3 * HD)
    blocks = tokens // GROUP
    per = width // GROUP
    cut = D // groups

    def kernel(
        chip_ref, grads_ref, part_ref, normed_ref, weight_ref, out_ref, weight_out, total, held
    ):
        at = pl.program_id(0)
        for head in range(heads):
            for which in range(3):
                low = (3 * head + which) * HD
                there = spot(heads, head, which)
                held[there, :] = (
                    grads_ref[there, :].astype(f32) + part_ref[0, low : low + HD, :].astype(f32)
                ).astype(bf16)
        held[part_rows:, :] = grads_ref[part_rows:, :]
        merged = held[...]
        out_ref[...] = dot_tn(merged, weight_ref[...]).astype(bf16)
        part = dot_nn(merged, normed_ref[...])

        @pl.when(at == 0)
        def first():
            total[...] = part

        @pl.when(at > 0)
        def more():
            total[...] += part

        @pl.when(at == blocks - 1)
        def last():
            for group in range(groups):
                weight_out[group] = total[:, group * cut : (group + 1) * cut].astype(bf16)

    def spread(at, chip_ref):
        return ((at // per) ^ chip_ref[0], 0, at % per)

    return pl.pallas_call(
        kernel,
        grid_spec=pltpu.PrefetchScalarGridSpec(
            num_scalar_prefetch=1,
            grid=(blocks,),
            in_specs=[
                pl.BlockSpec((columns, GROUP), lambda at, chip_ref: (0, at)),
                pl.BlockSpec((1, part_rows, GROUP), spread),
                pl.BlockSpec((GROUP, D), lambda at, chip_ref: (at, 0)),
                pl.BlockSpec((columns, D), lambda at, chip_ref: (0, 0)),
            ],
            out_specs=[
                pl.BlockSpec((GROUP, D), lambda at, chip_ref: (at, 0)),
                pl.BlockSpec((groups, columns, cut), lambda at, chip_ref: (0, 0, 0)),
            ],
            scratch_shapes=[pltpu.VMEM((columns, D), f32), pltpu.VMEM((columns, GROUP), bf16)],
        ),
        out_shape=[
            jax.ShapeDtypeStruct((tokens, D), bf16),
            jax.ShapeDtypeStruct((groups, columns, cut), bf16),
        ],
        compiler_params=pltpu.CompilerParams(vmem_limit_bytes=50 * 2**20),
        cost_estimate=pl.CostEstimate(
            flops=blocks * 4 * GROUP * D * columns * 2,
            bytes_accessed=blocks * GROUP * (D * 4 + columns * 4),
            transcendentals=0,
        ),
    )(chip, grads, grad_part, normed, weight)


def ffn_chunk(place, chunks, normed, grad, w_gate_up, w_down, old=()):
    own = w_down.shape[0]

    def kernel(*refs):
        w_gate_up_ref, w_down_ref = refs[4:6]
        all_normed, all_grad, all_hidden, all_grads, out_ref, back_ref = refs[-6:]
        for at in range(2):

            @pl.when(pl.program_id(0) == at)
            def one(normed_ref=refs[at], grad_ref=refs[2 + at]):
                low = normed_ref[...]
                grad_low = grad_ref[...]
                all_normed[...] = low
                all_grad[...] = grad_low
                gate = dot_nn(low, w_gate_up_ref[:, :own])
                up = dot_nn(low, w_gate_up_ref[:, own:])
                gate_sigmoid = jax.nn.sigmoid(gate)
                gate_silu = gate * gate_sigmoid
                hidden = (gate_silu * up).astype(bf16)
                all_hidden[...] = hidden
                out_ref[0] = dot_nn(hidden, w_down_ref[...]).astype(bf16)
                grad_hidden = dot_nt(grad_low, w_down_ref[...])
                slope = gate_sigmoid * (1.0 + gate * (1.0 - gate_sigmoid))
                all_grads[:, :own] = (grad_hidden * up * slope).astype(bf16)
                all_grads[:, own:] = (grad_hidden * gate_silu).astype(bf16)
                back_ref[0] = dot_nt(all_grads[...], w_gate_up_ref[...]).astype(bf16)

    tokens = chunks * 2 * GROUP
    whole = pl.BlockSpec((GROUP, D), lambda i: (0, 0))
    return pl.pallas_call(
        kernel,
        grid=(2,),
        in_specs=[whole] * 4
        + [
            pl.BlockSpec((D, 2 * own), lambda i: (0, 0)),
            pl.BlockSpec((own, D), lambda i: (0, 0)),
        ]
        + [pl.BlockSpec(memory_space=pl.ANY)] * len(old),
        out_specs=[
            pl.BlockSpec((GROUP, D), lambda i: (2 * place + i, 0)),
            pl.BlockSpec((GROUP, D), lambda i: (2 * place + i, 0)),
            pl.BlockSpec((GROUP, own), lambda i: (2 * place + i, 0)),
            pl.BlockSpec((GROUP, 2 * own), lambda i: (2 * place + i, 0)),
            pl.BlockSpec((1, GROUP, D), lambda i: (i, 0, 0)),
            pl.BlockSpec((1, GROUP, D), lambda i: (i, 0, 0)),
        ],
        out_shape=[
            jax.ShapeDtypeStruct((tokens, D), bf16),
            jax.ShapeDtypeStruct((tokens, D), bf16),
            jax.ShapeDtypeStruct((tokens, own), bf16),
            jax.ShapeDtypeStruct((tokens, 2 * own), bf16),
            jax.ShapeDtypeStruct((2, GROUP, D), bf16),
            jax.ShapeDtypeStruct((2, GROUP, D), bf16),
        ],
        input_output_aliases={6 + at: at for at in range(len(old))},
        compiler_params=pltpu.CompilerParams(vmem_limit_bytes=56 * 2**20),
        cost_estimate=pl.CostEstimate(
            flops=2 * GROUP * D * own * 12, bytes_accessed=20 * GROUP * D, transcendentals=2 * GROUP * own
        ),
    )(*normed, *grad, w_gate_up, w_down, *old)


def tokens_product(left, right):
    tokens, rows = left.shape
    columns = right.shape[1]
    steps = tokens // GROUP

    def kernel(left_ref, right_ref, out_ref, total):
        at = pl.program_id(0)
        part = dot_tn(left_ref[...], right_ref[...])

        @pl.when(at == 0)
        def first():
            total[...] = part

        @pl.when(at > 0)
        def more():
            total[...] += part

        @pl.when(at == steps - 1)
        def last():
            out_ref[...] = total[...].astype(bf16)

    return pl.pallas_call(
        kernel,
        grid=(steps,),
        in_specs=[
            pl.BlockSpec((GROUP, rows), lambda at: (at, 0)),
            pl.BlockSpec((GROUP, columns), lambda at: (at, 0)),
        ],
        out_specs=pl.BlockSpec((rows, columns), lambda at: (0, 0)),
        out_shape=jax.ShapeDtypeStruct((rows, columns), bf16),
        scratch_shapes=[pltpu.VMEM((rows, columns), f32)],
        compiler_params=pltpu.CompilerParams(vmem_limit_bytes=50 * 2**20),
        cost_estimate=pl.CostEstimate(
            flops=2 * tokens * rows * columns,
            bytes_accessed=2 * tokens * (rows + columns),
            transcendentals=0,
        ),
    )(left, right)


def matmul(left, right, left_dim, right_dim, out=f32):
    return lax.dot_general(
        left, right, (((left_dim,), (right_dim,)), ((), ())), preferred_element_type=f32
    ).astype(out)


def core_swap(value):
    return lax.ppermute(value, "core", [(0, 1), (1, 0)])


def gather_chips(value):
    return lax.all_gather(value, ("dp", "chip"), axis=0, tiled=True)


def scatter_chips(value):
    return lax.psum_scatter(value, ("dp", "chip"), scatter_dimension=0, tiled=True)


def after(value, *events):
    return lax.optimization_barrier((value, *events))[0]


def chip_swap(value, step):
    count = lax.axis_size("chip")
    return lax.ppermute(value, "chip", [(index, index ^ step) for index in range(count)])


def chip_parts(value):
    count = lax.axis_size("chip")
    if count != 4:
        return [value] + [chip_swap(value, step) for step in range(1, count)]
    middle = value.shape[0] // 2
    along = chip_swap(value, 1)
    across = chip_swap(value, 2)
    corner = jnp.concatenate([chip_swap(along[:middle], 2), chip_swap(across[middle:], 1)], axis=0)
    return [value, along, across, corner]


def corner_sums(corner, parts, *events):
    middle = corner.shape[0] // 2
    from_along = chip_swap(corner[:middle], 1)
    from_across = chip_swap(corner[middle:], 2)
    if events:
        from_along, from_across = after(from_along, *events), after(from_across, *events)
    from_along, from_across = from_along.astype(f32), from_across.astype(f32)
    first = jnp.concatenate(
        [parts[1][:middle].astype(f32), parts[1][middle:].astype(f32) + from_across], axis=0
    )
    second = jnp.concatenate(
        [parts[2][:middle].astype(f32) + from_along, parts[2][middle:].astype(f32)], axis=0
    )
    return first.astype(bf16), second.astype(bf16)


def side_sums(own, first, second, *events):
    first, second = chip_swap(first, 1), chip_swap(second, 2)
    if events:
        first, second = after(first, *events), after(second, *events)
    return own.astype(f32) + first.astype(f32) + second.astype(f32)


def chip_sums(parts):
    count = lax.axis_size("chip")
    if count != 4:
        total = parts[0].astype(f32)
        for step in range(1, count):
            total = total + chip_swap(parts[step].astype(bf16), step).astype(f32)
        return total
    return side_sums(parts[0], *corner_sums(parts[3].astype(bf16), parts))


def line_gather(value):
    count = lax.axis_size("dp")
    index = lax.axis_index("dp")
    up = down = value
    found = [value] * count
    for step in range(1, count):
        up = lax.ppermute(up, "dp", [(at, at + 1) for at in range(count - 1)])
        down = lax.ppermute(down, "dp", [(at + 1, at) for at in range(count - 1)])
        for at in range(count):
            found[at] = jnp.where(
                index - at == step, up, jnp.where(at - index == step, down, found[at])
            )
    return jnp.stack(found)


def sum_everywhere(value, marks):
    steps = [("core", 1)]
    for axis in ("chip", "dp"):
        step = 1
        while step < lax.axis_size(axis):
            steps.append((axis, step))
            step *= 2
    for at, (axis, step) in enumerate(steps):
        pairs = [(index, index ^ step) for index in range(lax.axis_size(axis))]
        other = lax.ppermute(value, axis, pairs)
        value = value + (after(other, marks[at]) if at < len(marks) else other)
    return value


def by_core(core, mine, other, axis=0):
    return jnp.where(
        core == 0,
        jnp.concatenate([mine, other], axis=axis),
        jnp.concatenate([other, mine], axis=axis),
    )


def inverse_rms(values):
    return lax.rsqrt(jnp.mean(values * values, axis=-1, keepdims=True) + norm_epsilon)


def norm_back(grad_normed, values, inverse, gain):
    normal = values * inverse
    scaled = grad_normed * gain
    return inverse * (scaled - normal * jnp.mean(scaled * normal, axis=-1, keepdims=True))


def on_device(
    inputs,
    segments,
    attn_gain,
    query_weight,
    key_weight,
    value_weight,
    output_weight,
    persistent,
    memory_first,
    memory_second,
    rate_weight,
    decay_logit,
    momentum_logit,
    ffn_gain,
    gate_weight,
    up_weight,
    down_weight,
    cotangent,
):
    groups, chips, core_count = (lax.axis_size("dp"), lax.axis_size("chip"), 2)
    core = lax.axis_index("core")
    chip = lax.axis_index("chip")
    position = chip * core_count + core
    chain = chips * core_count
    devices = groups * chain
    scale = HD ** (-0.5)
    half = D // 2
    core_heads = H // core_count
    heads = core_heads // chips
    rows = heads * HD
    width = 2 * GROUP
    all_rows = 3 * rows + RATE_ROWS
    shard = query_weight.shape[0]
    ff_own = gate_weight.shape[1] // chain
    pieces = devices // 2
    per_head = max(HD // shard, 1)
    near = 2 * shard == HD and core_heads == heads * chips

    tokens = inputs[0]
    grad_out = cotangent[0]

    if chips == 4:
        along, across = chip_swap(tokens, 1), chip_swap(tokens, 2)
    w_sides = pack_weights(
        chips,
        heads,
        key_weight,
        value_weight,
        query_weight,
        rate_weight,
        jnp.stack([attn_gain, ffn_gain], axis=1),
        persistent,
    )
    w_side = lax.dynamic_index_in_dim(w_sides, core, 0, keepdims=False)
    w_side_other = core_swap(lax.dynamic_index_in_dim(w_sides, 1 - core, 0, keepdims=False))
    w_pair = gather_chips(by_core(core, w_side, w_side_other))
    w_context = w_pair[:, : 2 * half]
    w_tail = w_pair[:, 3 * half :]
    persist = w_tail[:, :NP]
    mem_shard = jnp.concatenate([memory_first, memory_second], axis=1)
    if near:
        mem_pair = by_core(core, mem_shard, core_swap(mem_shard))
        mem_line = line_gather(mem_pair).reshape(groups * 2 * shard, 2 * MH)
        mem_mine = lax.dynamic_slice_in_dim(mem_line, core * rows, rows, 0)
    else:
        mem_all = lax.all_gather(mem_shard, ("dp", "chip", "core"), axis=0, tiled=True)
        mem_all = lax.dynamic_slice_in_dim(mem_all, core * half, half, 0)
        mem_all = mem_all.reshape(heads, chips, HD, 2 * MH)
        mem_mine = lax.dynamic_index_in_dim(mem_all, chip, 1, keepdims=False).reshape(rows, 2 * MH)
    mem_mine = mem_mine.astype(f32)
    first_init, second_init = mem_mine[:, :MH], mem_mine[:, MH:]
    if chips == 4:
        cut = GROUP // 2
        corner = jnp.concatenate(
            [chip_swap(along[:cut], 2), chip_swap(across[cut:], 1)], axis=0
        )
        token_halves = [tokens, along, across, corner]
    else:
        token_halves = chip_parts(tokens)
    w_gate_up = lax.all_to_all(
        pack_columns(chain, gate_weight, up_weight), ("chip", "core"), 0, 0, tiled=True
    ).reshape(chain * shard, 2 * ff_own)
    w_main = jnp.concatenate(
        [
            lax.dynamic_slice_in_dim(w_pair, chip * 2 * rows, 2 * rows, 1),
            lax.dynamic_slice_in_dim(w_pair, 2 * half + chip * rows, rows, 1),
            lax.dynamic_slice_in_dim(w_tail, NP + 2 + chip * heads, heads, 1),
            jnp.zeros((D, RATE_ROWS - heads), bf16),
        ],
        axis=1,
    )
    w_flat = after(w_main, w_gate_up).T
    gains = w_tail[:, NP : NP + 2].astype(f32).T
    gain_one, gain_two = gains[:1], gains[1:]

    ids = segments[0].reshape(chain, GROUP)
    first_id, last_id = ids[:, 0], ids[:, GROUP - 1]
    before = jnp.concatenate([first_id[:1], ids[:-1, GROUP - 1]])
    joined = jnp.logical_and(jnp.arange(chain) > 0, first_id == before)
    carry = jnp.logical_and(joined, first_id == last_id)
    kept = jnp.logical_and(joined[:, None], ids == first_id[:, None])
    retain = kept.astype(f32)[:, None, :]
    update = (ids == last_id[:, None]).astype(f32)[:, None, :]
    flags = jnp.stack(
        [
            carry.astype(jnp.int32),
            jnp.any(kept, axis=1).astype(jnp.int32),
            jnp.logical_not(jnp.all(kept, axis=1)).astype(jnp.int32),
            jnp.full((chain,), core, jnp.int32),
            jnp.full((chain,), chip, jnp.int32),
        ]
    )
    pair_ids = jnp.stack(
        [
            lax.dynamic_index_in_dim(ids, position, keepdims=False),
            lax.dynamic_index_in_dim(ids, chip * core_count + 1 - core, keepdims=False),
        ]
    )
    id_row, id_col = pair_ids[:, None, :], pair_ids[:, :, None]
    core_index = core.astype(jnp.int32)[None]
    decay = jax.nn.sigmoid(decay_logit)
    momentum = jax.nn.sigmoid(momentum_logit)

    def own_heads(value):
        return lax.dynamic_index_in_dim(
            value.reshape(core_count, heads, chips)[core], chip, 1, keepdims=False
        )

    scalars = jnp.stack([own_heads(1.0 - decay), own_heads(momentum)])

    token_blocks = []
    for part in token_halves:
        token_blocks += [part, core_swap(part)]
    placed = ()
    for start in range(0, chain, 8):
        placed = project_blocks(
            start, chain, token_blocks[start : start + 8], gain_one, w_flat, placed
        )
    normed_all, main = placed

    out_order = []
    for side in range(2):
        for piece in range(pieces):
            spot_, part = divmod(piece, per_head)
            at_chip, turn = divmod(spot_, heads)
            source = side * pieces + (turn * chips + at_chip) * per_head + part
            out_order.append((source, 2 * piece + side))
    out_moved = lax.ppermute(output_weight, ("dp", "chip", "core"), out_order)
    w_output = gather_chips(after(out_moved, token_halves[3]))

    w_gate_up = lax.all_gather(w_gate_up, "dp", axis=0, tiled=True)
    w_down = lax.all_gather(down_weight, "dp", axis=0, tiled=True)

    def pair_rows(own):
        return jnp.concatenate([own, core_swap(own)], axis=0)

    if chips == 4:
        grad_along, grad_across = [chip_swap(after(grad_out, main), step) for step in (1, 2)]
    recalled, saved = memory_forward(
        flags, main, retain, update, first_init, second_init, scalars, chips
    )
    normed = normed_all[:width]
    low = matmul(w_pair[:, : 3 * half], normed, 0, 1, bf16)
    side = matmul(w_context, persist, 0, 0, bf16)
    recalled = after(lax.all_to_all(recalled, "chip", 0, 0, tiled=True), low, side)
    recalled = recalled.reshape(chips, heads, HD, width).swapaxes(0, 1).reshape(half, width)
    context = by_core(core, recalled, core_swap(recalled))
    if chips == 4:
        grad_along, grad_across = after(grad_along, context), after(grad_across, context)
        grad_corner = (chip_swap(grad_along[:cut], 2), chip_swap(grad_across[cut:], 1))
        grad_halves = [grad_out, grad_along, grad_across, grad_corner]
    else:
        grad_halves = chip_parts(after(grad_out, context))

    far = matmul(w_context, context, 0, 0, bf16)
    mixed, total = attention_forward(scale, core_index, low, far, side, id_row, id_col)

    def pair_sum(left, right, left_dim, right_dim):
        def block(which):
            return lax.slice_in_dim(
                left, which * GROUP, (which + 1) * GROUP, axis=1 - left_dim
            )

        other = core_swap(matmul(block(1), right, left_dim, right_dim, bf16))
        return matmul(block(0), right, left_dim, right_dim) + other.astype(f32)

    middle = tokens.astype(f32) + pair_sum(mixed, w_output, 0, 0)
    inverse_two = inverse_rms(middle)
    normed_own = (middle * inverse_two * gain_two).astype(bf16)
    if chips == 4:
        normed_halves = [normed_own, chip_swap(normed_own, 1), chip_swap(normed_own, 2), None]
    else:
        normed_halves = chip_parts(normed_own)

    outs, grad_normeds, arrays = [], [], ()
    for step in range(chips):
        normed_half, grad_half = normed_halves[step], grad_halves[step]
        if chips == 4 and 0 < step < 3:
            normed_half = after(normed_half, outs[0])
            normed_halves[step] = normed_half
        elif chips == 4 and step == 3:
            normed_half = jnp.concatenate([after(part, outs[2]) for part in normed_corner], axis=0)
            grad_half = jnp.concatenate([after(part, outs[2]) for part in grad_half], axis=0)
        if chips == 4 and step == 2:
            normed_corner = (
                chip_swap(normed_halves[1][:cut], 2),
                chip_swap(normed_halves[2][cut:], 1),
            )
        *arrays, out, grad_normed = ffn_chunk(
            step,
            chips,
            (normed_half, core_swap(normed_half)),
            (grad_half, core_swap(grad_half)),
            w_gate_up,
            w_down,
            arrays,
        )
        outs.append(out)
        grad_normeds.append(grad_normed)
    all_normed, all_grad, all_hidden, all_grad_gate_up = arrays

    def pair_sums(parts, *events):
        return [
            part[0].astype(f32) + core_swap(after(part, *events)[1]).astype(f32) for part in parts
        ]

    grad_normeds = pair_sums(grad_normeds)
    if chips == 4:
        corner_low = grad_normeds[3].astype(bf16)
        grad_down_w = tokens_product(after(all_hidden, corner_low), all_grad)
        first_sum, second_sum = corner_sums(corner_low, grad_normeds, grad_down_w)
        grad_gate_up_w = tokens_product(
            after(all_normed, first_sum, second_sum), all_grad_gate_up
        )
        grad_normed_two = side_sums(grad_normeds[0], first_sum, second_sum, grad_gate_up_w)
        outs = pair_sums(outs, grad_gate_up_w)
    else:
        grad_normed_two = chip_sums(grad_normeds)
        grad_down_w = tokens_product(all_hidden, all_grad)
        grad_gate_up_w = tokens_product(all_normed, all_grad_gate_up)
        outs = pair_sums(outs)
    grad_middle = grad_out.astype(f32) + norm_back(grad_normed_two, middle, inverse_two, gain_two)
    down_part = lax.psum_scatter(grad_down_w, "dp", scatter_dimension=0, tiled=True).astype(f32)
    gate_up_scattered = lax.psum_scatter(grad_gate_up_w, "dp", scatter_dimension=0, tiled=True)

    grad_attended = pair_rows(grad_middle.astype(bf16))
    grad_output_w = matmul(mixed, grad_attended, 1, 0, bf16)
    grad_mixed = matmul(w_output, grad_attended, 1, 1, bf16)
    if chips == 4:
        out_corner = after(outs[3].astype(bf16), grad_normed_two)
        out_first, out_second = corner_sums(out_corner, outs, grad_mixed, grad_output_w)
        events = (out_first, out_second)
    else:
        events = ()
    grad_part, grad_far, grad_side = attention_backward(
        scale,
        core_index,
        low,
        far,
        side,
        id_row,
        id_col,
        mixed,
        total,
        after(grad_mixed, grad_output_w, *events),
    )
    grad_side = grad_side.astype(bf16)
    if chips == 4:
        out_sum = side_sums(outs[0], out_first, out_second, grad_far)
    else:
        out_sum = chip_sums(outs)
    result = (middle + out_sum).astype(bf16)

    def half_rows(which):
        return lax.dynamic_slice_in_dim(w_context, which * half, half, 0)

    pull_other = core_swap(matmul(half_rows(1 - core), grad_far, 1, 0, bf16))
    pull = (matmul(half_rows(core), grad_far, 1, 0) + pull_other.astype(f32)).astype(bf16)
    pull = pull.reshape(heads, chips, HD, width).swapaxes(0, 1).reshape(chips, rows, width)
    pull = lax.all_to_all(after(pull, out_sum), "chip", 0, 0, tiled=True)
    grad_part = lax.all_to_all(
        after(grad_part.reshape(chips, 3 * rows, width), pull), "chip", 0, 0, tiled=True
    )
    grad_context_w = jnp.concatenate(
        [
            (matmul(context, grad_far, 1, 1) + matmul(persist, grad_side, 1, 1)).astype(bf16),
            matmul(w_context, grad_side, 1, 0, bf16),
            jnp.zeros((D, 128 - NP), bf16),
        ],
        axis=1,
    )
    context_part = lax.psum_scatter(grad_context_w, "dp", scatter_dimension=0, tiled=True)
    context_part = context_part.reshape(chips, 2 * shard, 2 * half + 128)
    grads, grad_first, grad_second, grad_scalars = memory_backward(
        flags,
        main,
        retain,
        update,
        first_init,
        second_init,
        scalars,
        saved,
        after(pull, down_part, grad_context_w),
    )
    grad_tokens, grad_heads_w = merge_blocks(
        chip.astype(jnp.int32)[None],
        groups,
        grads,
        after(grad_part, grads),
        normed_all,
        w_flat,
    )
    grad_blocks = grad_tokens.reshape(chips, 2, GROUP, D)
    grad_normeds = [
        grad_blocks[step, 0].astype(f32) + core_swap(grad_blocks[step, 1]).astype(f32)
        for step in range(chips)
    ]
    grad_mem = jnp.concatenate([grad_first, grad_second], axis=1).astype(bf16)
    if near and MH == D // groups:
        spread = jnp.zeros((groups, 4 * shard, MH), bf16)
        spread = lax.dynamic_update_slice_in_dim(
            spread,
            jnp.concatenate(
                [grad_first.reshape(heads, HD, MH), grad_second.reshape(heads, HD, MH)], axis=1
            ).astype(bf16),
            core * heads,
            0,
        )
        grad_heads_w = jnp.concatenate([grad_heads_w, spread], axis=1)
    heads_part = lax.all_to_all(grad_heads_w, "dp", 0, 0, tiled=True)
    tokens_wide = tokens.astype(f32)
    if chips == 4:
        first_sum, second_sum = corner_sums(grad_normeds[3].astype(bf16), grad_normeds)
        marks = (grad_tokens, first_sum)
        heads_part = after(heads_part, first_sum, second_sum)
    else:
        marks = (grad_tokens, grad_tokens)
    heads_sum = jnp.sum(heads_part.astype(f32), axis=0).astype(bf16)
    heads_part = lax.all_to_all(
        jnp.concatenate(
            [
                heads_sum[:all_rows].T.reshape(chain, shard, all_rows),
                gate_up_scattered.reshape(chain, shard, 2 * ff_own),
            ],
            axis=2,
        ),
        ("chip", "core"),
        0,
        0,
        tiled=True,
    )
    gate_up_part = heads_part[:, :, all_rows:]
    heads_part = heads_part[:, :, :all_rows]
    context_part = after(context_part, *marks)
    context_part = chip_sums(
        [
            lax.dynamic_index_in_dim(context_part, chip ^ step, 0, keepdims=False)
            for step in range(chips)
        ]
    ).astype(bf16)
    if chips == 4:
        grad_normed = side_sums(grad_normeds[0], first_sum, second_sum, heads_sum)
    else:
        grad_normed = chip_sums(grad_normeds)
    grad_tokens_one = norm_back(grad_normed, tokens_wide, inverse_rms(tokens_wide), gain_one)
    grad_inputs = (grad_middle + grad_tokens_one).astype(bf16)
    marks = (*marks, heads_sum, grad_normed, heads_part)

    def own_rows(part):
        mine = lax.dynamic_slice_in_dim(part, core * shard, shard, 0)
        other = core_swap(lax.dynamic_slice_in_dim(part, (1 - core) * shard, shard, 0))
        return mine, other

    mine, other = own_rows(context_part)
    persist_part = (mine.astype(f32) + other.astype(f32))[:, 2 * half : 2 * half + NP]
    by_side = by_core(core, mine[None], other[None])
    grad_keys_own, grad_values_own, grad_queries_own, grad_rates_own, gain_one_part = (
        unpack_weights(
            chips,
            heads,
            heads_part,
            by_side,
            key_weight,
            value_weight,
            query_weight,
            rate_weight,
            attn_gain[:, None],
        )
    )
    gate_part, up_part, gain_two_part = unpack_columns(
        gate_up_part, gate_weight, up_weight, ffn_gain[:, None]
    )
    parts = grad_output_w.reshape(groups, chips, shard, D)
    output_part = chip_sums(
        [
            lax.dynamic_index_in_dim(parts, chip ^ step, 1, keepdims=False)
            for step in range(chips)
        ]
    ).astype(bf16)
    output_part = lax.psum_scatter(
        output_part.reshape(groups * shard, D), "dp", scatter_dimension=0, tiled=True
    )
    if near and MH == D // groups:
        mem_sum = heads_sum[all_rows:]
        mem_sum = jnp.concatenate([mem_sum[: 2 * shard], mem_sum[2 * shard :]], axis=1)
        mine, other = own_rows(mem_sum)
        mem_part = mine.astype(f32) + other.astype(f32)
    elif near:
        spread = jnp.zeros((groups, 2 * shard, 2 * MH), bf16)
        spread = lax.dynamic_update_slice_in_dim(
            spread, grad_mem.reshape(heads, 2 * shard, 2 * MH), core * heads, 0
        )
        mem_line = lax.all_to_all(spread, "dp", 0, 0, tiled=True)
        mine, other = own_rows(jnp.sum(mem_line.astype(f32), axis=0).astype(bf16))
        mem_part = mine.astype(f32) + other.astype(f32)
    else:
        spread = jnp.zeros((heads, chips, HD, 2 * MH), bf16)
        spread = lax.dynamic_update_slice_in_dim(
            spread, grad_mem.reshape(heads, 1, HD, 2 * MH), chip, 1
        ).reshape(half, 2 * MH)
        spread = lax.dynamic_update_slice_in_dim(
            jnp.zeros((D, 2 * MH), bf16), spread, core * half, 0
        )
        mem_part = lax.psum_scatter(
            spread, ("dp", "chip", "core"), scatter_dimension=0, tiled=True
        ).astype(f32)
    scalar_sums = jnp.sum(grad_scalars, axis=1)[: 2 * heads].reshape(1, heads, 1, 2)
    spots = lax.dynamic_update_slice(
        jnp.zeros((core_count, heads, chips, 2), f32), scalar_sums, (core, 0, chip, 0)
    )
    sums = sum_everywhere(spots.reshape(H, 2), marks)
    grad_decay = sums[:, 0] * decay * (1.0 - decay)
    grad_momentum = sums[:, 1] * momentum * (1.0 - momentum)
    output_own = lax.ppermute(
        output_part, ("dp", "chip", "core"), [(d, s) for s, d in out_order]
    ).astype(f32)
    return (
        result[None],
        grad_inputs[None],
        gain_one_part[:, 0],
        grad_queries_own,
        grad_keys_own,
        grad_values_own,
        output_own,
        persist_part,
        mem_part[:, :MH],
        mem_part[:, MH:],
        grad_rates_own,
        grad_decay,
        grad_momentum,
        gain_two_part[:, 0],
        gate_part,
        up_part,
        down_part,
    )


def solution(mesh):
    split = jax.sharding.Mesh(
        mesh.devices.reshape(mesh.shape["dp"], mesh.shape["seq"] // 2, 2), ("dp", "chip", "core")
    )
    row = P("dp", ("chip", "core"), None)
    vector = P(("dp", "chip", "core"))
    matrix = P(("dp", "chip", "core"), None)
    in_specs = (
        row,
        P("dp", None),
        vector,
        matrix,
        matrix,
        matrix,
        matrix,
        matrix,
        matrix,
        matrix,
        matrix,
        P(),
        P(),
        vector,
        matrix,
        matrix,
        matrix,
        row,
    )
    out_specs = (
        row,
        row,
        vector,
        matrix,
        matrix,
        matrix,
        matrix,
        matrix,
        matrix,
        matrix,
        matrix,
        P(),
        P(),
        vector,
        matrix,
        matrix,
        matrix,
    )
    return jax.shard_map(
        on_device, mesh=split, in_specs=in_specs, out_specs=out_specs, check_vma=False
    )
```

time: 1460 us -> 928 us (0.64)
  waiting for transfers between devices: 861 us -> 254 us
  Pallas kernels: 124 us -> 294 us
  matrix products: 184 us -> 67.5 us
  blocking collectives: 110 us -> 0 us
  starting transfers between devices: 34.6 us -> 99.3 us
  other arithmetic: 51.8 us -> 96 us
  local copies, waits for them, and re-layouts: 70.4 us -> 90 us
    reduce_scatter x5 -> x4, waiting for transfers between devices: 485 us -> 0.06 us  [the longest x1 0.02 us: on_device(): lax.psum_scatter(grad_context_w, 'dp', scatter_dimension=0, tiled=True)]
    all_gather x4 -> x2, waiting for transfers between devices: 235 us -> 4.86 us  [gather_chips(): return lax.all_gather(value, ('dp', 'chip'), axis=0, tiled=True)]
    ppermute x1 -> x44, waiting for transfers between devices: 3.07 us -> 221 us  [the longest x32 172 us: chip_swap(): lax.ppermute(value, 'chip', [(index, index ^ step) for index in range(cou...]
    pallas_call x0 -> x12, Pallas kernels: none -> 170 us  [the longest x4 73.7 us: ffn_chunk(): pl.pallas_call(kernel, grid=(2,), in_specs=[whole] * 4 + [pl.BlockSpec((D...]
    dot_general x17 -> x12, matrix products: 184 us -> 67.5 us  [matmul(): lax.dot_general(left, right, (((left_dim,), (right_dim,)), ((), ())), pre...]
    all_to_all x4 -> x6, waiting for transfers between devices: 100 us -> 11.1 us  [the longest x1 7.76 us: on_device(): lax.all_to_all(after(grad_part.reshape(chips, 3 * rows, width), pull), 'c...]
    ppermute x1 -> x44, starting transfers between devices: 3.4 us -> 62.7 us  [the longest x32 31.2 us: chip_swap(): lax.ppermute(value, 'chip', [(index, index ^ step) for index in range(cou...]
    unnamed x1 -> x0, blocking collectives: 42.6 us -> none
  transfers between devices with their start and end apart: 30 -> 91, of which waited for: 22 -> 36; matrix products, arithmetic and copies ran while one was open for 14% -> 24% of each run, Pallas kernels for 6% -> 31%
where the time goes in v2:
time: 928 us; the launch traced here: 917 us
  Pallas kernels  294 us (32%)
  waiting for transfers between devices  254 us (27%)
  starting transfers between devices  99.3 us (11%)
  other arithmetic  96 us (10%)
  local copies, waits for them, and re-layouts  90 us (10%)
  matrix products  67.5 us (7%)
  between operations  16 us (2%)
    ppermute x32, waiting for transfers between devices, chip_swap(): lax.ppermute(value, 'chip', [(index, index ^ step) for index in range(cou...  172 us
    pallas_call x4, Pallas kernels, ffn_chunk(): pl.pallas_call(kernel, grid=(2,), in_specs=[whole] * 4 + [pl.BlockSpec((D...  73.7 us
    dot_general x12, matrix products, matmul(): lax.dot_general(left, right, (((left_dim,), (right_dim,)), ((), ())), pre...  67.5 us
    pallas_call x1, Pallas kernels, memory_backward(): pl.pallas_call(lambda *refs: memory_backward_kernel(heads, blocks, *refs)...  44.9 us
    pallas_call x2, Pallas kernels, tokens_product(): pl.pallas_call(kernel, grid=(steps,), in_specs=[pl.BlockSpec((GROUP, rows...  37.5 us
    pallas_call x1, Pallas kernels, attention_backward(): pl.pallas_call(lambda *refs: attention_backward_kernel(scale, *refs), gri...  33.8 us
    unnamed x168, local copies, waits for them, and re-layouts  32.4 us
    ppermute x32, starting transfers between devices, chip_swap(): lax.ppermute(value, 'chip', [(index, index ^ step) for index in range(cou...  31.2 us
  transfers between devices with their start and end apart: 91, of which 36 were waited for; matrix products, arithmetic and copies ran while one was open for 24% of the time, Pallas kernels for 31%

profile of v2, /device:TPU:2, one launch (start us, length us, event | category | flops | bytes accessed | tf_op | source)
XLA Modules:
  0.0 916.6 jit_solution(17627629305645590396)
XLA Ops:
  18.1 44.8 %collective-permute-done.2.refs_2_ = bf16[512,1536]{1,0:T(8,128)(2,1)} collective-permute-done((bf16[512,1536]{1,0:T(8,128)(2,1)S(1)}, bf16[512,1536]{1,0:T(8,128)(2,1)}, u32[]{:S(2)}, u32[]{:S(2)}) %collective-permute-start.2) | collective-permute-done | bytes 1572896 | tf_op jit(solution)/shard_map/ppermute | solution.py:997
  66.8 5.0 collective-permute-start.17
  71.8 10.9 %collective-permute-done.6 = bf16[256,1536]{1,0:T(8,128)(2,1)S(1)} collective-permute-done((bf16[256,1536]{1,0:T(8,128)(2,1)S(1)}, bf16[256,1536]{1,0:T(8,128)(2,1)S(1)}, u32[]{:S(2)}, u32[]{:S(2)}) %collective-permute-start.6) | collective-permute-done | bytes 786464 | tf_op jit(solution)/shard_map/ppermute | solution.py:997
  83.6 8.3 collective-permute-done.7
  96.0 4.2 all-to-all-start
  108.8 5.0 collective-permute-done.10
  113.8 6.5 collective-permute-start.11
  124.5 4.4 collective-permute-start.12
  133.1 12.4 %collective-permute-done.15 = bf16[96,768]{1,0:T(8,128)(2,1)S(1)} collective-permute-done((bf16[96,768]{1,0:T(8,128)(2,1)S(1)}, bf16[96,768]{1,0:T(8,128)(2,1)S(1)}, u32[]{:S(2)}, u32[]{:S(2)}) %collective-permute-start.15) | collective-permute-done | bytes 147488 | tf_op jit(solution)/shard_map/ppermute | solution.py:1051
  146.5 4.9 all-gather.5.cloned.1.call-done
  165.2 19.1 %shard_map.307 = (bf16[4096,1536]{1,0:T(8,128)(2,1)}, bf16[592,4096]{1,0:T(8,128)(2,1)}) custom-call(bf16[512,1536]{1,0:T(8,128)(2,1)S(1)} %bitcast.224, bf16[512,1536]{1,0:T(8,128)(2,1)} %collective-permute-done.1.refs_1_, bf16[512,1536]{1,0:T(8,128)(2,1)} %collective-permute-done.2.refs_2_, bf16[512,1536]{1,0:T(8,128)(2,1)} %collective-permute-done.3.refs_3_, ...), custom_call_target="tpu_custom_call" | custom-call | flops 14898167808 | bytes 31834112 | tf_op jit(solution)/shard_map/pallas_call | solution.py:774
  184.3 23.3 %shard_map.308 = (bf16[4,192,1024]{2,1,0:T(8,128)(2,1)}, f32[8,4,192,384]{3,2,1,0:T(8,128)}) custom-call(s32[5,8]{1,0:T(8,128)S(1)} %stack.47.refs_0_, bf16[592,4096]{1,0:T(8,128)(2,1)} %get-tuple-element.107.refs_1_, f32[8,1,512]{2,1,0:T(1,128)S(1)} %get-tuple-element.315.refs_2_, f32[8,1,512]{2,1,0:T(1,128)S(1)} %get-tuple-element.314.refs_3_, ...), custom_call_target="tpu_custom_call" | custom-call | flops 16911433728 | bytes 14155776 | tf_op jit(solution)/shard_map/pallas_call | solution.py:148
  207.7 3.6 all-to-all-start.1
  211.3 12.9 %fusion.2.refs_1_.refs_2_ = bf16[2304,1024]{1,0:T(8,128)(2,1)} fusion(bf16[1536,2432]{1,0:T(8,128)(2,1)} %all-gather.5.cloned.1.call-done, bf16[4096,1536]{1,0:T(8,128)(2,1)} %get-tuple-element.106.normed_ref), kind=kOutput, calls=%fused_computation.3 | convolution fusion | flops 7250116608 | bytes 14942208 | tf_op jit(solution)/shard_map/dot_general | solution.py:974
  224.1 3.9 convolution_convert_fusion.3.refs_4_
  235.2 3.8 maximum_select_fusion
  239.0 10.1 %convolution_convert_fusion.refs_3_ = bf16[1536,1024]{1,0:T(8,128)(2,1)} fusion(bf16[1536,1024]{1,0:T(8,128)(2,1)S(1)} %maximum_select_fusion, bf16[1536,2432]{1,0:T(8,128)(2,1)} %all-gather.5.cloned.1.call-done), kind=kOutput, calls=%fused_computation.8 | convolution fusion | flops 4833411072 | bytes 11010048 | tf_op jit(solution)/shard_map/dot_general | solution.py:974
  249.1 21.7 %shard_map.309 = (bf16[768,1024]{1,0:T(8,128)(2,1)S(1)}, f32[8,1,1024]{2,1,0:T(1,128)S(1)}) custom-call(s32[1]{0:T(128)} %bitcast.1.refs_0_, bf16[2304,1024]{1,0:T(8,128)(2,1)} %fusion.2.refs_1_.refs_2_, bf16[2304,1024]{1,0:T(8,128)(2,1)} %fusion.2.refs_1_.refs_2_, bf16[1536,1024]{1,0:T(8,128)(2,1)} %convolution_convert_fusion.refs_3_, ...), custom_call_target="tpu_custom_call" | custom-call | flops 13690208256 | bytes 9437184 | tf_op jit(solution)/shard_map/pallas_call | solution.py:500
  271.9 3.5 convolution_convert_fusion.2
  276.6 3.6 collective-permute-done.18
  287.6 25.9 %collective-permute-done.28.refs_2_ = bf16[512,1536]{1,0:T(8,128)(2,1)} collective-permute-done((bf16[512,1536]{1,0:T(8,128)(2,1)}, bf16[512,1536]{1,0:T(8,128)(2,1)}, u32[]{:S(2)}, u32[]{:S(2)}) %collective-permute-start.28) | collective-permute-done | bytes 1572896 | tf_op jit(solution)/shard_map/ppermute | solution.py:997
  316.9 18.6 %shard_map.310 = (bf16[4096,1536]{1,0:T(8,128)(2,1)}, bf16[4096,1536]{1,0:T(8,128)(2,1)}, bf16[4096,512]{1,0:T(8,128)(2,1)}, bf16[4096,1024]{1,0:T(8,128)(2,1)},...) custom-call(bf16[512,1536]{1,0:T(8,128)(2,1)} %multiply_convert_fusion.refs_0_, ...), custom_call_target="tpu_custom_call" | custom-call | flops 9663676416 | bytes 15728640 | tf_op jit(solution)/shard_map/pallas_call | solution.py:900
  335.5 10.9 %collective-permute-done.21.refs_0_ = bf16[512,1536]{1,0:T(8,128)(2,1)} collective-permute-done((bf16[512,1536]{1,0:T(8,128)(2,1)}, bf16[512,1536]{1,0:T(8,128)(2,1)}, u32[]{:S(2)}, u32[]{:S(2)}) %collective-permute-start.21) | collective-permute-done | bytes 1572896 | tf_op jit(solution)/shard_map/ppermute | solution.py:997
  346.9 9.7 %collective-permute-done.23.refs_0_ = bf16[512,1536]{1,0:T(8,128)(2,1)} collective-permute-done((bf16[512,1536]{1,0:T(8,128)(2,1)}, bf16[512,1536]{1,0:T(8,128)(2,1)}, u32[]{:S(2)}, u32[]{:S(2)}) %collective-permute-start.23) | collective-permute-done | bytes 1572896 | tf_op jit(solution)/shard_map/ppermute | solution.py:997
  366.4 18.3 %shard_map.311 = (bf16[4096,1536]{1,0:T(8,128)(2,1)}, bf16[4096,1536]{1,0:T(8,128)(2,1)}, bf16[4096,512]{1,0:T(8,128)(2,1)}, bf16[4096,1024]{1,0:T(8,128)(2,1)},...) custom-call(bf16[512,1536]{1,0:T(8,128)(2,1)} %collective-permute-do, ...), custom_call_target="tpu_custom_call", output_to_operand_aliasing={{0}: (6, {}), {1}: (7, {}), {2}: (8, {}), {3}: (9, {})} | custom-call | flops 9663676416 | bytes 15728640 | tf_op jit(solution)/shard_map/pallas_call | solution.py:900
  387.0 18.3 %shard_map.312 = (bf16[4096,1536]{1,0:T(8,128)(2,1)}, bf16[4096,1536]{1,0:T(8,128)(2,1)}, bf16[4096,512]{1,0:T(8,128)(2,1)}, bf16[4096,1024]{1,0:T(8,128)(2,1)},...) custom-call(bf16[512,1536]{1,0:T(8,128)(2,1)} %collective-permute-do, ...), custom_call_target="tpu_custom_call", output_to_operand_aliasing={{0}: (6, {}), {1}: (7, {}), {2}: (8, {}), {3}: (9, {})} | custom-call | flops 9663676416 | bytes 15728640 | tf_op jit(solution)/shard_map/pallas_call | solution.py:900
  415.5 18.5 %shard_map.313 = (bf16[4096,1536]{1,0:T(8,128)(2,1)}, bf16[4096,1536]{1,0:T(8,128)(2,1)}, bf16[4096,512]{1,0:T(8,128)(2,1)}, bf16[4096,1024]{1,0:T(8,128)(2,1)},...) custom-call(bf16[512,1536]{1,0:T(8,128)(2,1)} %copy-done.32, ...), custom_call_target="tpu_custom_call", output_to_operand_aliasing={{0}: (6, {}), {1}: (7, {}), {2}: (8, {}), {3}: (9, {})} | custom-call | flops 9663676416 | bytes 15728640 | tf_op jit(solution)/shard_map/pallas_call | solution.py:900
  444.9 14.2 %shard_map.314 = bf16[512,1536]{1,0:T(8,128)(2,1)} custom-call(bf16[4096,512]{1,0:T(8,128)(2,1)} %get-tuple-element.139.left_ref, bf16[4096,1536]{1,0:T(8,128)(2,1)} %get-tuple-element.140.right_ref), custom_call_target="tpu_custom_call" | custom-call | flops 6442450944 | bytes 16777216 | tf_op jit(solution)/shard_map/pallas_call | solution.py:954
  470.7 23.3 %shard_map.315 = bf16[1536,1024]{1,0:T(8,128)(2,1)} custom-call(bf16[4096,1536]{1,0:T(8,128)(2,1)} %get-tuple-element.144.left_ref, bf16[4096,1024]{1,0:T(8,128)(2,1)} %get-tuple-element.145.right_ref), custom_call_target="tpu_custom_call" | custom-call | flops 12884901888 | bytes 20971520 | tf_op jit(solution)/shard_map/pallas_call | solution.py:954
  494.0 8.1 collective-permute-done.44
  504.1 4.5 multiply_reduce_fusion
  508.6 4.7 fusion.75
  513.4 3.7 collective-permute-done.47
  517.1 4.9 convolution_convert_fusion.1
  524.3 7.0 collective-permute-done.66
  535.3 5.1 slice.402
  540.5 6.5 collective-permute-done.67
  570.1 6.5 fusion.31.refs_9_
  576.7 3.8 collective-permute-done.46
  588.3 33.8 %shard_map.316 = (bf16[2304,1024]{1,0:T(8,128)(2,1)}, bf16[1536,1024]{1,0:T(8,128)(2,1)}, f32[1536,64]{1,0:T(8,128)S(1)}) custom-call(s32[1]{0:T(128)} %bitcast.1.refs_0_, bf16[2304,1024]{1,0:T(8,128)(2,1)} %fusion.2.refs_1_.refs_2_, bf16[2304,1024]{1,0:T(8,128)(2,1)} %fusion.2.refs_1_.refs_2_, bf16[1536,1024]{1,0:T(8,128)(2,1)} %convolution_convert_fusion.refs_3_, ...), custom_call_target="tpu_custom_call" | custom-call | flops 34225520640 | bytes 22020096 | tf_op jit(solution)/shard_map/pallas_call | solution.py:599
  622.1 6.4 fusion.28
  630.5 9.4 %add_convert_fusion = bf16[1536,1536]{0,1:T(8,128)(2,1)} fusion(f32[1536,1536]{0,1:T(8,128)S(1)} %fusion.50, bf16[1536,1024]{1,0:T(8,128)(2,1)S(1)} %copy-done.35, bf16[1536,1024]{1,0:T(8,128)(2,1)} %get-tuple-element.160), kind=kOutput, calls=%fused_computation | convolution fusion | flops 4836556800 | bytes 20447232 | tf_op jit(solution)/shard_map/dot_general | solution.py:974
  645.0 4.7 fusion.32
  649.7 4.3 all-to-all-start.2
  654.0 3.9 convolution_convert_fusion.4
  657.9 6.6 maximum_maximum_fusion
  664.5 7.8 copy.144
  674.7 6.0 all-to-all-start.3
  680.7 44.9 %shard_map.317 = (bf16[592,4096]{1,0:T(8,128)(2,1)}, f32[192,384]{1,0:T(8,128)}, f32[192,384]{1,0:T(8,128)}, f32[8,384]{1,0:T(8,128)}) custom-call(s32[5,8]{1,0:T(8,128)} %copy-done.13, bf16[592,4096]{1,0:T(8,128)(2,1)} %get-tuple-element.107.refs_1_, f32[8,1,512]{2,1,0:T(1,128)} %copy-done.12, f32[8,1,512]{2,1,0:T(1,128)} %copy-done.11, ...), custom_call_target="tpu_custom_call" | custom-call | flops 45902462976 | bytes 18874368 | tf_op jit(solution)/shard_map/pallas_call | solution.py:389
  725.6 7.8 all-to-all-done.3.part_ref
  733.4 25.1 %shard_map.318 = (bf16[4096,1536]{1,0:T(8,128)(2,1)}, bf16[4,592,384]{2,1,0:T(8,128)(2,1)S(1)}) custom-call(s32[1]{0:T(128)} %bitcast.41.chip_ref, bf16[592,4096]{1,0:T(8,128)(2,1)} %get-tuple-element.167.grads_ref, bf16[4,576,1024]{2,1,0:T(8,128)(2,1)} %all-to-all-done.3.part_ref, bf16[4096,1536]{1,0:T(8,128)(2,1)} %get-tuple-element.106.normed_ref, ...), custom_call_target="tpu_custom_call" | custom-call | flops 29796335616 | bytes 34865152 | tf_op jit(solution)/shard_map/pallas_call | solution.py:841
  758.5 6.3 slice_bitcast_fusion.6
  769.3 4.8 all-to-all-start.4
  774.1 7.3 convert_add_fusion.3
  789.1 12.5 %collective-permute-done.56 = bf16[256,1536]{1,0:T(8,128)(2,1)} collective-permute-done((bf16[256,1536]{1,0:T(8,128)(2,1)S(1)}, bf16[256,1536]{1,0:T(8,128)(2,1)}, u32[]{:S(2)}, u32[]{:S(2)}) %collective-permute-start.56) | collective-permute-done | bytes 786464 | tf_op jit(solution)/shard_map/ppermute | solution.py:997
  804.8 3.5 collective-permute-done.59
  816.6 27.1 %collective-permute-done.73 = f32[16,2]{0,1:T(2,128)S(1)} collective-permute-done((f32[16,2]{0,1:T(2,128)S(1)}, f32[16,2]{0,1:T(2,128)S(1)}, u32[]{:S(2)}, u32[]{:S(2)}) %collective-permute-start.73) | collective-permute-done | bytes 160 | tf_op jit(solution)/shard_map/ppermute | solution.py:1068
  850.5 4.6 all-to-all-start.5
  859.1 3.5 collective-permute-start.75
  862.7 12.2 %collective-permute-done.61 = bf16[48,1664]{1,0:T(8,128)(2,1)S(1)} collective-permute-done((bf16[48,1664]{1,0:T(8,128)(2,1)S(1)}, bf16[48,1664]{1,0:T(8,128)(2,1)S(1)}, u32[]{:S(2)}, u32[]{:S(2)}) %collective-permute-start.61) | collective-permute-done | bytes 159776 | tf_op jit(solution)/shard_map/ppermute | solution.py:997
  878.3 4.3 fusion.7
  882.7 3.0 collective-permute-start.76
  887.0 4.1 fusion.33
  893.3 7.8 shard_map.319
  (480 shorter events, 214.8 us)
Async XLA Ops:
  7.2 144.2 %all-gather.5.cloned.1.call-start = ((), (), s32[]{:S(2)}) async-start(), calls=%async_computation.10 | async-start | bytes 7938048 | tf_op jit(solution)/shard_map/all_gather | solution.py:984
  15.9 256.0 %all-gather.7.cloned.1.call-start = ((), (), s32[]{:S(2)}) async-start(), calls=%async_computation.11 | async-start | bytes 2506752 | tf_op jit(solution)/shard_map/all_gather | solution.py:984
  16.0 46.9 %collective-permute-start.2 = (bf16[512,1536]{1,0:T(8,128)(2,1)S(1)}, bf16[512,1536]{1,0:T(8,128)(2,1)}, u32[]{:S(2)}, u32[]{:S(2)}) collective-permute-start(bf16[512,1536]{1,0:T(8,128)(2,1)S(1)} %bitcast.221), channel_id=1, source_target_pairs={{0,2},{2,0},{4,6},{6,4},{1,3},{3,1},{5,7},{7,5},{8,10},{10,8},{12,... | collective-permute-start | bytes 4718600 | tf_op jit(solution)/shard_map/ppermute | solution.py:997
  16.1 49.4 %collective-permute-start.4 = (bf16[512,1536]{1,0:T(8,128)(2,1)S(1)}, bf16[512,1536]{1,0:T(8,128)(2,1)}, u32[]{:S(2)}, u32[]{:S(2)}) collective-permute-start(bf16[512,1536]{1,0:T(8,128)(2,1)S(1)} %bitcast.222), channel_id=1, source_target_pairs={{0,4},{2,6},{4,0},{6,2},{1,5},{3,7},{5,1},{7,3},{8,12},{10,14},{12... | collective-permute-start | bytes 4718600 | tf_op jit(solution)/shard_map/ppermute | solution.py:997
  64.1 18.6 %collective-permute-start.6 = (bf16[256,1536]{1,0:T(8,128)(2,1)S(1)}, bf16[256,1536]{1,0:T(8,128)(2,1)S(1)}, u32[]{:S(2)}, u32[]{:S(2)}) collective-permute-start(bf16[256,1536]{1,0:T(8,128)(2,1)S(1)} %slice.397), channel_id=1, source_target_pairs={{0,4},{2,6},{4,0},{6,2},{1,5},{3,7},{5,1},{7,3},{8,12},{10,14},{12... | collective-permute-start | bytes 2359304 | tf_op jit(solution)/shard_map/ppermute | solution.py:997
  66.7 25.2 %collective-permute-start.7 = (bf16[256,1536]{1,0:T(8,128)(2,1)S(1)}, bf16[256,1536]{1,0:T(8,128)(2,1)S(1)}, u32[]{:S(2)}, u32[]{:S(2)}) collective-permute-start(bf16[256,1536]{1,0:T(8,128)(2,1)S(1)} %slice.398), channel_id=1, source_target_pairs={{0,2},{2,0},{4,6},{6,4},{1,3},{3,1},{5,7},{7,5},{8,10},{10,8},{12,... | collective-permute-start | bytes 2359304 | tf_op jit(solution)/shard_map/ppermute | solution.py:997
  66.8 26.1 %collective-permute-start.17 = (bf16[48,1536]{1,0:T(8,128)(2,1)S(1)}, bf16[48,1536]{1,0:T(8,128)(2,1)S(1)}, u32[]{:S(2)}, u32[]{:S(2)}) collective-permute-start(bf16[48,1536]{1,0:T(8,128)(2,1)S(1)} %copy-done.71), channel_id=1, source_target_pairs={{0,0},{1,2},{8,4},{9,6},{2,8},{3,10},{10,12},{11,14},{4,16},{5,18}... | collective-permute-start | bytes 442376 | tf_op jit(solution)/shard_map/ppermute | solution.py:1239
  93.6 71.6 %collective-permute-start.1 = (bf16[512,1536]{1,0:T(8,128)(2,1)S(1)}, bf16[512,1536]{1,0:T(8,128)(2,1)}, u32[]{:S(2)}, u32[]{:S(2)}) collective-permute-start(bf16[512,1536]{1,0:T(8,128)(2,1)S(1)} %bitcast.223), channel_id=1, source_target_pairs={{0,1},{1,0},{2,3},{3,2},{4,5},{5,4},{6,7},{7,6},{8,9},{9,8},{10,11... | collective-permute-start | bytes 4718600 | tf_op jit(solution)/shard_map/ppermute | solution.py:980
  96.0 67.1 %all-to-all-start = ((bf16[8,48,1024]{2,1,0:T(8,128)(2,1)}), bf16[8,48,1024]{2,1,0:T(8,128)(2,1)}, u32[]{:S(2)}, u32[]{:S(2)}) async-start(bf16[8,48,1024]{2,1,0:T(8,128)(2,1)} %shard_map.306), calls=%async_computation | async-start | bytes 1572864 | tf_op jit(solution)/shard_map/all_to_all | solution.py:1171
  100.2 213.9 %all-gather.11.cloned.1.call-start = ((), (), s32[]{:S(2)}) async-start(), calls=%async_computation.13 | async-start | bytes 1966080 | tf_op jit(solution)/shard_map/all_gather | solution.py:1243
  106.7 13.5 %collective-permute-start.13 = (bf16[96,768]{1,0:T(8,128)(2,1)S(1)}, bf16[96,768]{1,0:T(8,128)(2,1)S(1)}, u32[]{:S(2)}, u32[]{:S(2)}) collective-permute-start(bf16[96,768]{1,0:T(8,128)(2,1)S(1)} %maximum_select_fusion.3), channel_id=1, source_target_pairs={{8,0},{16,8},{24,16},{9,1},{17,9},{25,17},{10,2},{18,10},{26,18},{... | collective-permute-start | bytes 442376 | tf_op jit(solution)/shard_map/ppermute | solution.py:1051
  131.1 14.3 %collective-permute-start.15 = (bf16[96,768]{1,0:T(8,128)(2,1)S(1)}, bf16[96,768]{1,0:T(8,128)(2,1)S(1)}, u32[]{:S(2)}, u32[]{:S(2)}) collective-permute-start(bf16[96,768]{1,0:T(8,128)(2,1)S(1)} %collective-permute-done.14), channel_id=1, source_target_pairs={{8,0},{16,8},{24,16},{9,1},{17,9},{25,17},{10,2},{18,10},{26,18},{... | collective-permute-start | bytes 442376 | tf_op jit(solution)/shard_map/ppermute | solution.py:1051
  145.8 19.4 %collective-permute-start.3 = (bf16[512,1536]{1,0:T(8,128)(2,1)}, bf16[512,1536]{1,0:T(8,128)(2,1)}, u32[]{:S(2)}, u32[]{:S(2)}) collective-permute-start(bf16[512,1536]{1,0:T(8,128)(2,1)} %collective-permute-done.2.refs_2_), channel_id=1, source_target_pairs={{0,1},{1,0},{2,3},{3,2},{4,5},{5,4},{6,7},{7,6},{8,9},{9,8},{10,11... | collective-permute-start | bytes 4718600 | tf_op jit(solution)/shard_map/ppermute | solution.py:980
  145.9 19.3 %collective-permute-start.5 = (bf16[512,1536]{1,0:T(8,128)(2,1)}, bf16[512,1536]{1,0:T(8,128)(2,1)}, u32[]{:S(2)}, u32[]{:S(2)}) collective-permute-start(bf16[512,1536]{1,0:T(8,128)(2,1)} %collective-permute-done.4.refs_4_), channel_id=1, source_target_pairs={{0,1},{1,0},{2,3},{3,2},{4,5},{5,4},{6,7},{7,6},{8,9},{9,8},{10,11... | collective-permute-start | bytes 4718600 | tf_op jit(solution)/shard_map/ppermute | solution.py:980
  146.4 18.8 %collective-permute-start.8 = (bf16[512,1536]{1,0:T(8,128)(2,1)}, bf16[512,1536]{1,0:T(8,128)(2,1)}, u32[]{:S(2)}, u32[]{:S(2)}) collective-permute-start(bf16[512,1536]{1,0:T(8,128)(2,1)} %constant_dynamic-update-slice_fusion.refs_6_), channel_id=1, source_target_pairs={{0,1},{1,0},{2,3},{3,2},{4,5},{5,4},{6,7},{7,6},{8,9},{9,8},{10,11... | collective-permute-start | bytes 4718600 | tf_op jit(solution)/shard_map/ppermute | solution.py:980
  207.7 22.5 %all-to-all-start.1 = ((bf16[4,192,1024]{2,1,0:T(8,128)(2,1)}), bf16[4,192,1024]{2,1,0:T(8,128)(2,1)S(1)}, u32[]{:S(2)}, u32[]{:S(2)}) async-start(bf16[4,192,1024]{2,1,0:T(8,128)(2,1)} %get-tuple-element.108), calls=%async_computation.1 | async-start | bytes 3145728 | tf_op jit(solution)/shard_map/all_to_all | solution.py:1256
  211.2 105.6 %all-gather.9.cloned.1.call-start = ((), (), s32[]{:S(2)}) async-start(), calls=%async_computation.12 | async-start | bytes 3932160 | tf_op jit(solution)/shard_map/all_gather | solution.py:1242
  232.6 335.6 %reduce-scatter.7.cloned.1.call-start = ((), (), s32[]{:S(2)}) async-start(), calls=%async_computation.14 | async-start | bytes 1966080 | tf_op jit(solution)/shard_map/reduce_scatter | solution.py:1334
  275.6 38.0 %collective-permute-start.20 = (bf16[512,1536]{1,0:T(8,128)(2,1)}, bf16[512,1536]{1,0:T(8,128)(2,1)}, u32[]{:S(2)}, u32[]{:S(2)}) collective-permute-start(bf16[512,1536]{1,0:T(8,128)(2,1)} %bitcast.23.refs_2_), channel_id=1, source_target_pairs={{0,1},{1,0},{2,3},{3,2},{4,5},{5,4},{6,7},{7,6},{8,9},{9,8},{10,11... | collective-permute-start | bytes 4718600 | tf_op jit(solution)/shard_map/ppermute | solution.py:980
  276.0 37.6 %collective-permute-start.28 = (bf16[512,1536]{1,0:T(8,128)(2,1)}, bf16[512,1536]{1,0:T(8,128)(2,1)}, u32[]{:S(2)}, u32[]{:S(2)}) collective-permute-start(bf16[512,1536]{1,0:T(8,128)(2,1)} %bitcast.23.refs_2_), channel_id=1, source_target_pairs={{0,2},{2,0},{4,6},{6,4},{1,3},{3,1},{5,7},{7,5},{8,10},{10,8},{12,... | collective-permute-start | bytes 4718600 | tf_op jit(solution)/shard_map/ppermute | solution.py:997
  285.4 31.4 %collective-permute-start.19 = (bf16[512,1536]{1,0:T(8,128)(2,1)}, bf16[512,1536]{1,0:T(8,128)(2,1)}, u32[]{:S(2)}, u32[]{:S(2)}) collective-permute-start(bf16[512,1536]{1,0:T(8,128)(2,1)} %multiply_convert_fusion.refs_0_), channel_id=1, source_target_pairs={{0,1},{1,0},{2,3},{3,2},{4,5},{5,4},{6,7},{7,6},{8,9},{9,8},{10,11... | collective-permute-start | bytes 4718600 | tf_op jit(solution)/shard_map/ppermute | solution.py:980
  285.6 60.8 %collective-permute-start.21 = (bf16[512,1536]{1,0:T(8,128)(2,1)}, bf16[512,1536]{1,0:T(8,128)(2,1)}, u32[]{:S(2)}, u32[]{:S(2)}) collective-permute-start(bf16[512,1536]{1,0:T(8,128)(2,1)} %multiply_convert_fusion.refs_0_), channel_id=1, source_target_pairs={{0,2},{2,0},{4,6},{6,4},{1,3},{3,1},{5,7},{7,5},{8,10},{10,8},{12,... | collective-permute-start | bytes 4718600 | tf_op jit(solution)/shard_map/ppermute | solution.py:997
  286.2 60.2 %collective-permute-start.25 = (bf16[512,1536]{1,0:T(8,128)(2,1)}, bf16[512,1536]{1,0:T(8,128)(2,1)S(1)}, u32[]{:S(2)}, u32[]{:S(2)}) collective-permute-start(bf16[512,1536]{1,0:T(8,128)(2,1)} %bitcast.23.refs_2_), channel_id=1, source_target_pairs={{0,4},{2,6},{4,0},{6,2},{1,5},{3,7},{5,1},{7,3},{8,12},{10,14},{12... | collective-permute-start | bytes 4718600 | tf_op jit(solution)/shard_map/ppermute | solution.py:997
  313.6 50.7 %collective-permute-start.29 = (bf16[512,1536]{1,0:T(8,128)(2,1)}, bf16[512,1536]{1,0:T(8,128)(2,1)}, u32[]{:S(2)}, u32[]{:S(2)}) collective-permute-start(bf16[512,1536]{1,0:T(8,128)(2,1)} %collective-permute-done.28.refs_2_), channel_id=1, source_target_pairs={{0,1},{1,0},{2,3},{3,2},{4,5},{5,4},{6,7},{7,6},{8,9},{9,8},{10,11... | collective-permute-start | bytes 4718600 | tf_op jit(solution)/shard_map/ppermute | solution.py:980
  313.6 43.0 %collective-permute-start.23 = (bf16[512,1536]{1,0:T(8,128)(2,1)}, bf16[512,1536]{1,0:T(8,128)(2,1)}, u32[]{:S(2)}, u32[]{:S(2)}) collective-permute-start(bf16[512,1536]{1,0:T(8,128)(2,1)} %multiply_convert_fusion.refs_0_), channel_id=1, source_target_pairs={{0,4},{2,6},{4,0},{6,2},{1,5},{3,7},{5,1},{7,3},{8,12},{10,14},{12... | collective-permute-start | bytes 4718600 | tf_op jit(solution)/shard_map/ppermute | solution.py:997
  346.4 18.2 %collective-permute-start.27 = (bf16[512,1536]{1,0:T(8,128)(2,1)}, bf16[512,1536]{1,0:T(8,128)(2,1)S(1)}, u32[]{:S(2)}, u32[]{:S(2)}) collective-permute-start(bf16[512,1536]{1,0:T(8,128)(2,1)} %collective-permute-done.21.refs_0_), channel_id=1, source_target_pairs={{0,1},{1,0},{2,3},{3,2},{4,5},{5,4},{6,7},{7,6},{8,9},{9,8},{10,11... | collective-permute-start | bytes 4718600 | tf_op jit(solution)/shard_map/ppermute | solution.py:980
  346.4 38.3 %collective-permute-start.26 = (bf16[512,1536]{1,0:T(8,128)(2,1)S(1)}, bf16[512,1536]{1,0:T(8,128)(2,1)S(1)}, u32[]{:S(2)}, u32[]{:S(2)}) collective-permute-start(bf16[512,1536]{1,0:T(8,128)(2,1)S(1)} %collective-permute-done.25.refs_2_), channel_id=1, source_target_pairs={{0,1},{1,0},{2,3},{3,2},{4,5},{5,4},{6,7},{7,6},{8,9},{9,8},{10,11... | collective-permute-start | bytes 4718600 | tf_op jit(solution)/shard_map/ppermute | solution.py:980
  356.6 29.3 %collective-permute-start.24 = (bf16[512,1536]{1,0:T(8,128)(2,1)}, bf16[512,1536]{1,0:T(8,128)(2,1)S(1)}, u32[]{:S(2)}, u32[]{:S(2)}) collective-permute-start(bf16[512,1536]{1,0:T(8,128)(2,1)} %collective-permute-done.23.refs_0_), channel_id=1, source_target_pairs={{0,1},{1,0},{2,3},{3,2},{4,5},{5,4},{6,7},{7,6},{8,9},{9,8},{10,11... | collective-permute-start | bytes 4718600 | tf_op jit(solution)/shard_map/ppermute | solution.py:980
  359.6 45.7 %collective-permute-start.33 = (bf16[256,1536]{1,0:T(8,128)(2,1)}, bf16[256,1536]{1,0:T(8,128)(2,1)}, u32[]{:S(2)}, u32[]{:S(2)}) collective-permute-start(bf16[256,1536]{1,0:T(8,128)(2,1)} %slice.327), channel_id=1, source_target_pairs={{0,2},{2,0},{4,6},{6,4},{1,3},{3,1},{5,7},{7,5},{8,10},{10,8},{12,... | collective-permute-start | bytes 2359304 | tf_op jit(solution)/shard_map/ppermute | solution.py:997
  364.3 41.1 %collective-permute-start.32 = (bf16[256,1536]{1,0:T(8,128)(2,1)}, bf16[256,1536]{1,0:T(8,128)(2,1)}, u32[]{:S(2)}, u32[]{:S(2)}) collective-permute-start(bf16[256,1536]{1,0:T(8,128)(2,1)} %slice.326), channel_id=1, source_target_pairs={{0,4},{2,6},{4,0},{6,2},{1,5},{3,7},{5,1},{7,3},{8,12},{10,14},{12... | collective-permute-start | bytes 2359304 | tf_op jit(solution)/shard_map/ppermute | solution.py:997
  364.7 43.3 %collective-permute-start.30 = (bf16[256,1536]{1,0:T(8,128)(2,1)}, bf16[256,1536]{1,0:T(8,128)(2,1)}, u32[]{:S(2)}, u32[]{:S(2)}) collective-permute-start(bf16[256,1536]{1,0:T(8,128)(2,1)} %slice.325), channel_id=1, source_target_pairs={{0,2},{2,0},{4,6},{6,4},{1,3},{3,1},{5,7},{7,5},{8,10},{10,8},{12,... | collective-permute-start | bytes 2359304 | tf_op jit(solution)/shard_map/ppermute | solution.py:997
  384.7 23.3 %collective-permute-start.22 = (bf16[256,1536]{1,0:T(8,128)(2,1)S(1)}, bf16[256,1536]{1,0:T(8,128)(2,1)}, u32[]{:S(2)}, u32[]{:S(2)}) collective-permute-start(bf16[256,1536]{1,0:T(8,128)(2,1)S(1)} %slice.324), channel_id=1, source_target_pairs={{0,4},{2,6},{4,0},{6,2},{1,5},{3,7},{5,1},{7,3},{8,12},{10,14},{12... | collective-permute-start | bytes 2359304 | tf_op jit(solution)/shard_map/ppermute | solution.py:997
  412.4 24.3 %collective-permute-start.38 = (bf16[512,1536]{1,0:T(8,128)(2,1)}, bf16[512,1536]{1,0:T(8,128)(2,1)}, u32[]{:S(2)}, u32[]{:S(2)}) collective-permute-start(bf16[512,1536]{1,0:T(8,128)(2,1)} %slice_bitcast_fusion.9), channel_id=1, source_target_pairs={{0,1},{1,0},{2,3},{3,2},{4,5},{5,4},{6,7},{7,6},{8,9},{9,8},{10,11... | collective-permute-start | bytes 4718600 | tf_op jit(solution)/shard_map/ppermute | solution.py:980
  440.6 20.2 %collective-permute-start.39 = (bf16[256,1536]{1,0:T(8,128)(2,1)}, bf16[256,1536]{1,0:T(8,128)(2,1)}, u32[]{:S(2)}, u32[]{:S(2)}) collective-permute-start(bf16[256,1536]{1,0:T(8,128)(2,1)} %get-tuple-element.290), channel_id=1, source_target_pairs={{0,2},{2,0},{4,6},{6,4},{1,3},{3,1},{5,7},{7,5},{8,10},{10,8},{12,... | collective-permute-start | bytes 2359304 | tf_op jit(solution)/shard_map/ppermute | solution.py:997
  443.7 19.8 %collective-permute-start.37 = (bf16[256,1536]{1,0:T(8,128)(2,1)S(1)}, bf16[256,1536]{1,0:T(8,128)(2,1)}, u32[]{:S(2)}, u32[]{:S(2)}) collective-permute-start(bf16[256,1536]{1,0:T(8,128)(2,1)S(1)} %get-tuple-element.291), channel_id=1, source_target_pairs={{0,4},{2,6},{4,0},{6,2},{1,5},{3,7},{5,1},{7,3},{8,12},{10,14},{12... | collective-permute-start | bytes 2359304 | tf_op jit(solution)/shard_map/ppermute | solution.py:997
  466.1 36.0 %collective-permute-start.44 = (bf16[512,1536]{1,0:T(8,128)(2,1)}, bf16[512,1536]{1,0:T(8,128)(2,1)}, u32[]{:S(2)}, u32[]{:S(2)}) collective-permute-start(bf16[512,1536]{1,0:T(8,128)(2,1)} %pad_maximum_fusion.6), channel_id=1, source_target_pairs={{0,2},{2,0},{4,6},{6,4},{1,3},{3,1},{5,7},{7,5},{8,10},{10,8},{12,... | collective-permute-start | bytes 4718600 | tf_op jit(solution)/shard_map/ppermute | solution.py:997
  468.5 35.6 %collective-permute-start.45 = (bf16[512,1536]{1,0:T(8,128)(2,1)}, bf16[512,1536]{1,0:T(8,128)(2,1)S(1)}, u32[]{:S(2)}, u32[]{:S(2)}) collective-permute-start(bf16[512,1536]{1,0:T(8,128)(2,1)} %pad_maximum_fusion.7), channel_id=1, source_target_pairs={{0,4},{2,6},{4,0},{6,2},{1,5},{3,7},{5,1},{7,3},{8,12},{10,14},{12... | collective-permute-start | bytes 4718600 | tf_op jit(solution)/shard_map/ppermute | solution.py:997
  470.7 33.3 %collective-permute-start.43 = (bf16[512,1536]{1,0:T(8,128)(2,1)}, bf16[512,1536]{1,0:T(8,128)(2,1)}, u32[]{:S(2)}, u32[]{:S(2)}) collective-permute-start(bf16[512,1536]{1,0:T(8,128)(2,1)} %slice_bitcast_fusion.8), channel_id=1, source_target_pairs={{0,1},{1,0},{2,3},{3,2},{4,5},{5,4},{6,7},{7,6},{8,9},{9,8},{10,11... | collective-permute-start | bytes 4718600 | tf_op jit(solution)/shard_map/ppermute | solution.py:980
  513.4 269.8 %reduce-scatter.11.cloned.1.call-start = ((), (), s32[]{:S(2)}) async-start(), calls=%async_computation.16 | async-start | bytes 737280 | tf_op jit(solution)/shard_map/reduce_scatter | solution.py:1491
  532.2 14.9 %collective-permute-start.67 = (bf16[4,48,1536]{2,1,0:T(8,128)(2,1)}, bf16[4,48,1536]{2,1,0:T(8,128)(2,1)S(1)}, u32[]{:S(2)}, u32[]{:S(2)}) collective-permute-start(bf16[4,48,1536]{2,1,0:T(8,128)(2,1)} %pad_maximum_fusion.14), channel_id=1, source_target_pairs={{0,2},{2,0},{4,6},{6,4},{1,3},{3,1},{5,7},{7,5},{8,10},{10,8},{12,... | collective-permute-start | bytes 1769480 | tf_op jit(solution)/shard_map/ppermute | solution.py:997
  533.8 14.7 %collective-permute-start.69 = (bf16[4,48,1536]{2,1,0:T(8,128)(2,1)}, bf16[4,48,1536]{2,1,0:T(8,128)(2,1)}, u32[]{:S(2)}, u32[]{:S(2)}) collective-permute-start(bf16[4,48,1536]{2,1,0:T(8,128)(2,1)} %pad_maximum_fusion.15), channel_id=1, source_target_pairs={{0,4},{2,6},{4,0},{6,2},{1,5},{3,7},{5,1},{7,3},{8,12},{10,14},{12... | collective-permute-start | bytes 1769480 | tf_op jit(solution)/shard_map/ppermute | solution.py:997
  540.4 16.4 %collective-permute-start.42 = (bf16[512,1536]{1,0:T(8,128)(2,1)S(1)}, bf16[512,1536]{1,0:T(8,128)(2,1)}, u32[]{:S(2)}, u32[]{:S(2)}) collective-permute-start(bf16[512,1536]{1,0:T(8,128)(2,1)S(1)} %slice_bitcast_fusion.13), channel_id=1, source_target_pairs={{0,1},{1,0},{2,3},{3,2},{4,5},{5,4},{6,7},{7,6},{8,9},{9,8},{10,11... | collective-permute-start | bytes 4718600 | tf_op jit(solution)/shard_map/ppermute | solution.py:980
  550.8 297.1 %reduce-scatter.9.cloned.1.call-start = ((), (), s32[]{:S(2)}) async-start(), calls=%async_computation.15 | async-start | bytes 3932160 | tf_op jit(solution)/shard_map/reduce_scatter | solution.py:1335
  556.8 87.1 %collective-permute-start.40 = (bf16[512,1536]{1,0:T(8,128)(2,1)}, bf16[512,1536]{1,0:T(8,128)(2,1)}, u32[]{:S(2)}, u32[]{:S(2)}) collective-permute-start(bf16[512,1536]{1,0:T(8,128)(2,1)} %slice_bitcast_fusion.15), channel_id=1, source_target_pairs={{0,1},{1,0},{2,3},{3,2},{4,5},{5,4},{6,7},{7,6},{8,9},{9,8},{10,11... | collective-permute-start | bytes 4718600 | tf_op jit(solution)/shard_map/ppermute | solution.py:980
  560.2 20.3 %collective-permute-start.46 = (bf16[256,1536]{1,0:T(8,128)(2,1)}, bf16[256,1536]{1,0:T(8,128)(2,1)}, u32[]{:S(2)}, u32[]{:S(2)}) collective-permute-start(bf16[256,1536]{1,0:T(8,128)(2,1)} %get-tuple-element.288), channel_id=1, source_target_pairs={{0,4},{2,6},{4,0},{6,2},{1,5},{3,7},{5,1},{7,3},{8,12},{10,14},{12... | collective-permute-start | bytes 2359304 | tf_op jit(solution)/shard_map/ppermute | solution.py:997
  563.5 19.8 %collective-permute-start.50 = (bf16[256,1536]{1,0:T(8,128)(2,1)S(1)}, bf16[256,1536]{1,0:T(8,128)(2,1)}, u32[]{:S(2)}, u32[]{:S(2)}) collective-permute-start(bf16[256,1536]{1,0:T(8,128)(2,1)S(1)} %get-tuple-element.289), channel_id=1, source_target_pairs={{0,2},{2,0},{4,6},{6,4},{1,3},{3,1},{5,7},{7,5},{8,10},{10,8},{12,... | collective-permute-start | bytes 2359304 | tf_op jit(solution)/shard_map/ppermute | solution.py:997
  584.9 58.9 %collective-permute-start.48 = (bf16[512,1536]{1,0:T(8,128)(2,1)S(1)}, bf16[512,1536]{1,0:T(8,128)(2,1)}, u32[]{:S(2)}, u32[]{:S(2)}) collective-permute-start(bf16[512,1536]{1,0:T(8,128)(2,1)S(1)} %pad_maximum_fusion.8), channel_id=1, source_target_pairs={{0,2},{2,0},{4,6},{6,4},{1,3},{3,1},{5,7},{7,5},{8,10},{10,8},{12,... | collective-permute-start | bytes 4718600 | tf_op jit(solution)/shard_map/ppermute | solution.py:997
  587.4 56.4 %collective-permute-start.51 = (bf16[512,1536]{1,0:T(8,128)(2,1)}, bf16[512,1536]{1,0:T(8,128)(2,1)}, u32[]{:S(2)}, u32[]{:S(2)}) collective-permute-start(bf16[512,1536]{1,0:T(8,128)(2,1)} %pad_maximum_fusion.9), channel_id=1, source_target_pairs={{0,4},{2,6},{4,0},{6,2},{1,5},{3,7},{5,1},{7,3},{8,12},{10,14},{12... | collective-permute-start | bytes 4718600 | tf_op jit(solution)/shard_map/ppermute | solution.py:997
  628.5 11.3 %collective-permute-start.52 = (bf16[768,1024]{1,0:T(8,128)(2,1)}, bf16[768,1024]{1,0:T(8,128)(2,1)S(1)}, u32[]{:S(2)}, u32[]{:S(2)}) collective-permute-start(bf16[768,1024]{1,0:T(8,128)(2,1)} %fusion.28), channel_id=1, source_target_pairs={{0,1},{1,0},{2,3},{3,2},{4,5},{5,4},{6,7},{7,6},{8,9},{9,8},{10,11... | collective-permute-start | bytes 4718600 | tf_op jit(solution)/shard_map/ppermute | solution.py:980
  649.7 23.9 %all-to-all-start.2 = ((bf16[4,192,1024]{2,1,0:T(8,128)(2,1)}), bf16[4,192,1024]{2,1,0:T(8,128)(2,1)S(1)}, u32[]{:S(2)}, u32[]{:S(2)}) async-start(bf16[4,192,1024]{2,1,0:T(8,128)(2,1)} %bitcast.44), calls=%async_computation.2 | async-start | bytes 3145728 | tf_op jit(solution)/shard_map/all_to_all | solution.py:1371
  654.0 201.2 %reduce-scatter.13.cloned.1.call-start = ((), (), s32[]{:S(2)}) async-start(), calls=%async_computation.17 | async-start | bytes 6389760 | tf_op jit(solution)/shard_map/reduce_scatter | solution.py:1383
  674.7 58.7 %all-to-all-start.3 = ((bf16[4,576,1024]{2,1,0:T(8,128)(2,1)}), bf16[4,576,1024]{2,1,0:T(8,128)(2,1)}, u32[]{:S(2)}, u32[]{:S(2)}) async-start(bf16[4,576,1024]{2,1,0:T(8,128)(2,1)} %bitcast.235), calls=%async_computation.4 | async-start | bytes 9437184 | tf_op jit(solution)/shard_map/all_to_all | solution.py:1372
  769.3 74.5 %all-to-all-start.4 = ((bf16[4,784,384]{2,1,0:T(8,128)(2,1)}), bf16[4,784,384]{2,1,0:T(8,128)(2,1)}, u32[]{:S(2)}, u32[]{:S(2)}) async-start(bf16[4,784,384]{2,1,0:T(8,128)(2,1)} %pad_maximum_fusion.1), calls=%async_computation.5 | async-start | bytes 4816896 | tf_op jit(solution)/shard_map/all_to_all | solution.py:1421
  781.5 20.1 %collective-permute-start.56 = (bf16[256,1536]{1,0:T(8,128)(2,1)S(1)}, bf16[256,1536]{1,0:T(8,128)(2,1)}, u32[]{:S(2)}, u32[]{:S(2)}) collective-permute-start(bf16[256,1536]{1,0:T(8,128)(2,1)S(1)} %get-tuple-element.286), channel_id=1, source_target_pairs={{0,4},{2,6},{4,0},{6,2},{1,5},{3,7},{5,1},{7,3},{8,12},{10,14},{12... | collective-permute-start | bytes 2359304 | tf_op jit(solution)/shard_map/ppermute | solution.py:997
  783.2 31.7 %collective-permute-start.70 = (bf16[48,1536]{1,0:T(8,128)(2,1)}, bf16[48,1536]{1,0:T(8,128)(2,1)S(1)}, u32[]{:S(2)}, u32[]{:S(2)}) collective-permute-start(bf16[48,1536]{1,0:T(8,128)(2,1)} %reduce-scatter.11.cloned.1.call-done), channel_id=1, source_target_pairs={{0,0},{2,1},{4,8},{6,9},{8,2},{10,3},{12,10},{14,11},{16,4},{18,5}... | collective-permute-start | bytes 442376 | tf_op jit(solution)/shard_map/ppermute | solution.py:1525
  787.5 20.9 %collective-permute-start.59 = (bf16[256,1536]{1,0:T(8,128)(2,1)S(1)}, bf16[256,1536]{1,0:T(8,128)(2,1)S(1)}, u32[]{:S(2)}, u32[]{:S(2)}) collective-permute-start(bf16[256,1536]{1,0:T(8,128)(2,1)S(1)} %get-tuple-element.287), channel_id=1, source_target_pairs={{0,2},{2,0},{4,6},{6,4},{1,3},{3,1},{5,7},{7,5},{8,10},{10,8},{12,... | collective-permute-start | bytes 2359304 | tf_op jit(solution)/shard_map/ppermute | solution.py:997
  804.2 54.9 %collective-permute-start.57 = (bf16[512,1536]{1,0:T(8,128)(2,1)}, bf16[512,1536]{1,0:T(8,128)(2,1)}, u32[]{:S(2)}, u32[]{:S(2)}) collective-permute-start(bf16[512,1536]{1,0:T(8,128)(2,1)} %pad_maximum_fusion.10), channel_id=1, source_target_pairs={{0,2},{2,0},{4,6},{6,4},{1,3},{3,1},{5,7},{7,5},{8,10},{10,8},{12,... | collective-permute-start | bytes 4718600 | tf_op jit(solution)/shard_map/ppermute | solution.py:997
  809.8 52.9 %collective-permute-start.60 = (bf16[512,1536]{1,0:T(8,128)(2,1)}, bf16[512,1536]{1,0:T(8,128)(2,1)}, u32[]{:S(2)}, u32[]{:S(2)}) collective-permute-start(bf16[512,1536]{1,0:T(8,128)(2,1)} %pad_maximum_fusion.11), channel_id=1, source_target_pairs={{0,4},{2,6},{4,0},{6,2},{1,5},{3,7},{5,1},{7,3},{8,12},{10,14},{12... | collective-permute-start | bytes 4718600 | tf_op jit(solution)/shard_map/ppermute | solution.py:997
  815.7 28.1 %collective-permute-start.73 = (f32[16,2]{0,1:T(2,128)S(1)}, f32[16,2]{0,1:T(2,128)S(1)}, u32[]{:S(2)}, u32[]{:S(2)}) collective-permute-start(f32[16,2]{0,1:T(2,128)S(1)} %add.324), channel_id=1, source_target_pairs={{0,2},{2,0},{4,6},{6,4},{1,3},{3,1},{5,7},{7,5},{8,10},{10,8},{12,... | collective-permute-start | bytes 392 | tf_op jit(solution)/shard_map/ppermute | solution.py:1068
  816.6 61.7 %collective-permute-start.53 = (bf16[512,1536]{1,0:T(8,128)(2,1)}, bf16[512,1536]{1,0:T(8,128)(2,1)}, u32[]{:S(2)}, u32[]{:S(2)}) collective-permute-start(bf16[512,1536]{1,0:T(8,128)(2,1)} %get-tuple-element.275), channel_id=1, source_target_pairs={{0,1},{1,0},{2,3},{3,2},{4,5},{5,4},{6,7},{7,6},{8,9},{9,8},{10,11... | collective-permute-start | bytes 4718600 | tf_op jit(solution)/shard_map/ppermute | solution.py:980
  850.5 41.9 %all-to-all-start.5 = ((bf16[8,48,1616]{2,1,0:T(8,128)(2,1)}), bf16[8,48,1616]{2,1,0:T(8,128)(2,1)S(1)}, u32[]{:S(2)}, u32[]{:S(2)}) async-start(bf16[8,48,1616]{2,1,0:T(8,128)(2,1)} %pad_maximum_fusion.12), calls=%async_computation.7 | async-start | bytes 2555904 | tf_op jit(solution)/shard_map/all_to_all | solution.py:1430
  856.4 18.5 %collective-permute-start.61 = (bf16[48,1664]{1,0:T(8,128)(2,1)S(1)}, bf16[48,1664]{1,0:T(8,128)(2,1)S(1)}, u32[]{:S(2)}, u32[]{:S(2)}) collective-permute-start(bf16[48,1664]{1,0:T(8,128)(2,1)S(1)} %get-tuple-element.293), channel_id=1, source_target_pairs={{0,4},{2,6},{4,0},{6,2},{1,5},{3,7},{5,1},{7,3},{8,12},{10,14},{12... | collective-permute-start | bytes 479240 | tf_op jit(solution)/shard_map/ppermute | solution.py:997
  857.9 17.0 %collective-permute-start.63 = (bf16[48,1664]{1,0:T(8,128)(2,1)S(1)}, bf16[48,1664]{1,0:T(8,128)(2,1)S(1)}, u32[]{:S(2)}, u32[]{:S(2)}) collective-permute-start(bf16[48,1664]{1,0:T(8,128)(2,1)S(1)} %get-tuple-element.295), channel_id=1, source_target_pairs={{0,2},{2,0},{4,6},{6,4},{1,3},{3,1},{5,7},{7,5},{8,10},{10,8},{12,... | collective-permute-start | bytes 479240 | tf_op jit(solution)/shard_map/ppermute | solution.py:997
  859.1 23.5 %collective-permute-start.75 = (f32[16,2]{0,1:T(2,128)S(1)}, f32[16,2]{0,1:T(2,128)S(1)}, u32[]{:S(2)}, u32[]{:S(2)}) collective-permute-start(f32[16,2]{0,1:T(2,128)S(1)} %add.326), channel_id=1, source_target_pairs={{0,8},{8,0},{16,24},{24,16},{1,9},{9,1},{17,25},{25,17},{2,10},{10... | collective-permute-start | bytes 392 | tf_op jit(solution)/shard_map/ppermute | solution.py:1068
  (106 other events, 1890.5 us)
Sparse Core Ops, SparseCore 0:
  16.0 135.2 all-gather.4
  154.7 60.4 all-gather.6
  216.8 36.2 all-gather.10
  254.5 62.3 all-gather.8
  513.5 33.2 reduce-scatter.6
  551.0 19.9 reduce-scatter.10
  573.2 58.6 reduce-scatter.8
  672.4 89.9 reduce-scatter.12

commit v3 on v2

--- a/solution.py
+++ b/solution.py
@@ -754,6 +754,52 @@
     )(parts, context, key, value, query, rate, gain)
 
 
+def take_heads(chip, chips, heads, w_pair):
+    rows = heads * HD
+    size = 128
+    span = 2 * rows
+    tail_at = 3 * D // 2 // 128
+
+    def kernel(chip_ref, low_ref, query_ref, tail_ref, out_ref, gains_ref):
+        def turned(value):
+            return value.astype(f32).T
+
+        out_ref[:span] = turned(low_ref[...]).astype(bf16)
+        query = turned(query_ref[...])
+        odd = chip_ref[0] % 2 == 1
+        out_ref[span : span + rows] = jnp.where(odd, query[rows:], query[:rows]).astype(bf16)
+        tail = turned(tail_ref[...])
+        gains_ref[...] = tail[NP : NP + 8]
+        rates = jnp.zeros((heads, size), f32)
+        for at in range(chips):
+            low = NP + 2 + at * heads
+            rates = jnp.where(chip_ref[0] == at, tail[low : low + heads], rates)
+        out_ref[span + rows :] = jnp.concatenate(
+            [rates, jnp.zeros((RATE_ROWS - heads, size), f32)], axis=0
+        ).astype(bf16)
+
+    return pl.pallas_call(
+        kernel,
+        grid_spec=pltpu.PrefetchScalarGridSpec(
+            num_scalar_prefetch=1,
+            grid=(D // size,),
+            in_specs=[
+                pl.BlockSpec((size, span), lambda at, chip_ref: (at, chip_ref[0])),
+                pl.BlockSpec((size, span), lambda at, chip_ref: (at, chips + chip_ref[0] // 2)),
+                pl.BlockSpec((size, 128), lambda at, chip_ref: (at, tail_at)),
+            ],
+            out_specs=[
+                pl.BlockSpec((span + rows + RATE_ROWS, size), lambda at, chip_ref: (0, at)),
+                pl.BlockSpec((8, size), lambda at, chip_ref: (0, at)),
+            ],
+        ),
+        out_shape=[
+            jax.ShapeDtypeStruct((span + rows + RATE_ROWS, D), bf16),
+            jax.ShapeDtypeStruct((8, D), f32),
+        ],
+    )(chip, w_pair, w_pair, w_pair)
+
+
 def project_blocks(first, blocks, tokens, gain, weight, old=()):
     columns = weight.shape[0]
     count = len(tokens)
@@ -798,32 +844,32 @@
     )(*tokens, gain, weight, *old)
 
 
-def merge_blocks(chip, groups, grads, grad_part, normed, weight):
+def merge_part(heads, grads_ref, part_ref, held):
+    for head in range(heads):
+        for which in range(3):
+            low = (3 * head + which) * HD
+            there = spot(heads, head, which)
+            held[there, :] = (
+                grads_ref[there, :].astype(f32) + part_ref[0, low : low + HD, :].astype(f32)
+            ).astype(bf16)
+    end = 3 * heads * HD
+    held[end:, :] = grads_ref[end:, :]
+
+
+def merge_blocks(chip, groups, grads, grad_part, normed):
     columns, tokens = grads.shape
     chips, part_rows, width = grad_part.shape
     heads = part_rows // (3 * HD)
-    blocks = tokens // GROUP
-    per = width // GROUP
+    blocks = tokens // width
     cut = D // groups
 
-    def kernel(
-        chip_ref, grads_ref, part_ref, normed_ref, weight_ref, out_ref, weight_out, total, held
-    ):
+    def kernel(chip_ref, grads_ref, part_ref, normed_ref, weight_out, total, held):
         at = pl.program_id(0)
-        for head in range(heads):
-            for which in range(3):
-                low = (3 * head + which) * HD
-                there = spot(heads, head, which)
-                held[there, :] = (
-                    grads_ref[there, :].astype(f32) + part_ref[0, low : low + HD, :].astype(f32)
-                ).astype(bf16)
-        held[part_rows:, :] = grads_ref[part_rows:, :]
-        merged = held[...]
-        out_ref[...] = dot_tn(merged, weight_ref[...]).astype(bf16)
-        part = dot_nn(merged, normed_ref[...])
+        merge_part(heads, grads_ref, part_ref, held)
+        part = dot_nn(held[...], normed_ref[...])
 
         @pl.when(at == 0)
-        def first():
+        def begin():
             total[...] = part
 
         @pl.when(at > 0)
@@ -831,12 +877,9 @@
             total[...] += part
 
         @pl.when(at == blocks - 1)
-        def last():
+        def end():
             for group in range(groups):
                 weight_out[group] = total[:, group * cut : (group + 1) * cut].astype(bf16)
-
-    def spread(at, chip_ref):
-        return ((at // per) ^ chip_ref[0], 0, at % per)
 
     return pl.pallas_call(
         kernel,
@@ -844,42 +887,88 @@
             num_scalar_prefetch=1,
             grid=(blocks,),
             in_specs=[
-                pl.BlockSpec((columns, GROUP), lambda at, chip_ref: (0, at)),
-                pl.BlockSpec((1, part_rows, GROUP), spread),
-                pl.BlockSpec((GROUP, D), lambda at, chip_ref: (at, 0)),
-                pl.BlockSpec((columns, D), lambda at, chip_ref: (0, 0)),
+                pl.BlockSpec((columns, width), lambda at, chip_ref: (0, at)),
+                pl.BlockSpec((1, part_rows, width), lambda at, chip_ref: (at ^ chip_ref[0], 0, 0)),
+                pl.BlockSpec((width, D), lambda at, chip_ref: (at, 0)),
             ],
-            out_specs=[
-                pl.BlockSpec((GROUP, D), lambda at, chip_ref: (at, 0)),
-                pl.BlockSpec((groups, columns, cut), lambda at, chip_ref: (0, 0, 0)),
-            ],
-            scratch_shapes=[pltpu.VMEM((columns, D), f32), pltpu.VMEM((columns, GROUP), bf16)],
+            out_specs=pl.BlockSpec((groups, columns, cut), lambda at, chip_ref: (0, 0, 0)),
+            scratch_shapes=[pltpu.VMEM((columns, D), f32), pltpu.VMEM((columns, width), bf16)],
         ),
-        out_shape=[
-            jax.ShapeDtypeStruct((tokens, D), bf16),
-            jax.ShapeDtypeStruct((groups, columns, cut), bf16),
-        ],
-        compiler_params=pltpu.CompilerParams(vmem_limit_bytes=50 * 2**20),
+        out_shape=jax.ShapeDtypeStruct((groups, columns, cut), bf16),
+        compiler_params=pltpu.CompilerParams(vmem_limit_bytes=44 * 2**20),
         cost_estimate=pl.CostEstimate(
-            flops=blocks * 4 * GROUP * D * columns * 2,
-            bytes_accessed=blocks * GROUP * (D * 4 + columns * 4),
+            flops=2 * tokens * D * columns * 2,
+            bytes_accessed=tokens * (D * 2 + columns * 4),
             transcendentals=0,
         ),
-    )(chip, grads, grad_part, normed, weight)
+    )(chip, grads, grad_part, normed)
+
+
+def back_blocks(chip, first, count, grads, grad_part, weight):
+    columns = grads.shape[0]
+    part_rows = grad_part.shape[1]
+    heads = part_rows // (3 * HD)
+
+    def kernel(chip_ref, grads_ref, part_ref, weight_ref, own_ref, other_ref, held):
+        merge_part(heads, grads_ref, part_ref, held)
+        out = dot_tn(held[...], weight_ref[...]).astype(bf16)
+
+        @pl.when(pl.program_id(0) % 2 == 0)
+        def own():
+            own_ref[0] = out
+
+        @pl.when(pl.program_id(0) % 2 == 1)
+        def other():
+            other_ref[0] = out
+
+    block = pl.BlockSpec((1, GROUP, D), lambda at, chip_ref: (at // 2, 0, 0))
+    blocks = jax.ShapeDtypeStruct((count, GROUP, D), bf16)
+    return pl.pallas_call(
+        kernel,
+        grid_spec=pltpu.PrefetchScalarGridSpec(
+            num_scalar_prefetch=1,
+            grid=(2 * count,),
+            in_specs=[
+                pl.BlockSpec((columns, GROUP), lambda at, chip_ref: (0, 2 * first + at)),
+                pl.BlockSpec(
+                    (1, part_rows, GROUP),
+                    lambda at, chip_ref: ((first + at // 2) ^ chip_ref[0], 0, at % 2),
+                ),
+                pl.BlockSpec(
+                    (columns, D), lambda at, chip_ref: (0, 0), pipeline_mode=pl.Buffered(1)
+                ),
+            ],
+            out_specs=[block, block],
+            scratch_shapes=[pltpu.VMEM((columns, GROUP), bf16)],
+        ),
+        out_shape=[blocks, blocks],
+        compiler_params=pltpu.CompilerParams(vmem_limit_bytes=32 * 2**20),
+        cost_estimate=pl.CostEstimate(
+            flops=count * 4 * GROUP * D * columns * 2,
+            bytes_accessed=count * 2 * GROUP * (D * 2 + columns * 4),
+            transcendentals=0,
+        ),
+    )(chip, grads, grad_part, weight)
 
 
 def ffn_chunk(place, chunks, normed, grad, w_gate_up, w_down, old=()):
     own = w_down.shape[0]
+    given = [piece for block in (*normed, *grad) for piece in block]
+    spans, at = [], 0
+    for block in (*normed, *grad):
+        spans.append(slice(at, at + len(block)))
+        at += len(block)
+    count = len(given)
 
     def kernel(*refs):
-        w_gate_up_ref, w_down_ref = refs[4:6]
+        w_gate_up_ref, w_down_ref = refs[count : count + 2]
         all_normed, all_grad, all_hidden, all_grads, out_ref, back_ref = refs[-6:]
         for at in range(2):
 
             @pl.when(pl.program_id(0) == at)
-            def one(normed_ref=refs[at], grad_ref=refs[2 + at]):
-                low = normed_ref[...]
-                grad_low = grad_ref[...]
+            def one(normed_refs=refs[spans[at]], grad_refs=refs[spans[2 + at]]):
+                low = jnp.concatenate([ref[...] for ref in normed_refs], axis=0)
+                grad_low = jnp.concatenate([ref[...] for ref in grad_refs], axis=0)
                 all_normed[...] = low
                 all_grad[...] = grad_low
                 gate = dot_nn(low, w_gate_up_ref[:, :own])
@@ -896,14 +985,16 @@
                 back_ref[0] = dot_nt(all_grads[...], w_gate_up_ref[...]).astype(bf16)
 
     tokens = chunks * 2 * GROUP
-    whole = pl.BlockSpec((GROUP, D), lambda i: (0, 0))
+    once = pl.Buffered(1)
     return pl.pallas_call(
         kernel,
         grid=(2,),
-        in_specs=[whole] * 4
+        in_specs=[
+            pl.BlockSpec(piece.shape, lambda i: (0, 0), pipeline_mode=once) for piece in given
+        ]
         + [
-            pl.BlockSpec((D, 2 * own), lambda i: (0, 0)),
-            pl.BlockSpec((own, D), lambda i: (0, 0)),
+            pl.BlockSpec((D, 2 * own), lambda i: (0, 0), pipeline_mode=once),
+            pl.BlockSpec((own, D), lambda i: (0, 0), pipeline_mode=once),
         ]
         + [pl.BlockSpec(memory_space=pl.ANY)] * len(old),
         out_specs=[
@@ -922,18 +1013,52 @@
             jax.ShapeDtypeStruct((2, GROUP, D), bf16),
             jax.ShapeDtypeStruct((2, GROUP, D), bf16),
         ],
-        input_output_aliases={6 + at: at for at in range(len(old))},
-        compiler_params=pltpu.CompilerParams(vmem_limit_bytes=56 * 2**20),
+        input_output_aliases={count + 2 + at: at for at in range(len(old))},
+        compiler_params=pltpu.CompilerParams(vmem_limit_bytes=40 * 2**20),
         cost_estimate=pl.CostEstimate(
             flops=2 * GROUP * D * own * 12, bytes_accessed=20 * GROUP * D, transcendentals=2 * GROUP * own
         ),
-    )(*normed, *grad, w_gate_up, w_down, *old)
+    )(*given, w_gate_up, w_down, *old)
+
+
+def context_product(context, grad_far, persist, grad_side, w_pair):
+    size = 256
+    columns = grad_far.shape[0]
+
+    def kernel(context_ref, far_ref, persist_ref, side_ref, weight_ref, out_ref):
+        out_ref[:, :columns] = (
+            dot_nt(context_ref[...], far_ref[...]) + dot_nt(persist_ref[...], side_ref[...])
+        ).astype(bf16)
+        own = dot_nn(weight_ref[...], side_ref[...]).astype(bf16)
+        out_ref[:, columns:] = jnp.concatenate([own, jnp.zeros((size, 128 - NP), bf16)], axis=1)
+
+    once = pl.Buffered(1)
+    return pl.pallas_call(
+        kernel,
+        grid=(D // size,),
+        in_specs=[
+            pl.BlockSpec((size, context.shape[1]), lambda at: (at, 0)),
+            pl.BlockSpec(grad_far.shape, lambda at: (0, 0), pipeline_mode=once),
+            pl.BlockSpec((size, NP), lambda at: (at, 0)),
+            pl.BlockSpec(grad_side.shape, lambda at: (0, 0), pipeline_mode=once),
+            pl.BlockSpec((size, columns), lambda at: (at, 0)),
+        ],
+        out_specs=pl.BlockSpec((size, columns + 128), lambda at: (at, 0)),
+        out_shape=jax.ShapeDtypeStruct((D, columns + 128), bf16),
+        compiler_params=pltpu.CompilerParams(vmem_limit_bytes=32 * 2**20),
+        cost_estimate=pl.CostEstimate(
+            flops=2 * D * columns * context.shape[1],
+            bytes_accessed=4 * D * columns * 2,
+            transcendentals=0,
+        ),
+    )(context, grad_far, persist, grad_side, w_pair)
 
 
 def tokens_product(left, right):
     tokens, rows = left.shape
     columns = right.shape[1]
-    steps = tokens // GROUP
+    size = 2 * GROUP
+    steps = tokens // size
 
     def kernel(left_ref, right_ref, out_ref, total):
         at = pl.program_id(0)
@@ -955,8 +1080,8 @@
         kernel,
         grid=(steps,),
         in_specs=[
-            pl.BlockSpec((GROUP, rows), lambda at: (at, 0)),
-            pl.BlockSpec((GROUP, columns), lambda at: (at, 0)),
+            pl.BlockSpec((size, rows), lambda at: (at, 0)),
+            pl.BlockSpec((size, columns), lambda at: (at, 0)),
         ],
         out_specs=pl.BlockSpec((rows, columns), lambda at: (0, 0)),
         out_shape=jax.ShapeDtypeStruct((rows, columns), bf16),
@@ -990,6 +1115,10 @@
 
 def after(value, *events):
     return lax.optimization_barrier((value, *events))[0]
+
+
+def together(*values):
+    return lax.optimization_barrier(values)
 
 
 def chip_swap(value, step):
@@ -1148,7 +1277,20 @@
     w_context = w_pair[:, : 2 * half]
     w_tail = w_pair[:, 3 * half :]
     persist = w_tail[:, :NP]
+    if chips == 4:
+        cut = GROUP // 2
+        corner = jnp.concatenate(
+            [chip_swap(along[:cut], 2), chip_swap(across[cut:], 1)], axis=0
+        )
+        token_halves = [tokens, along, across, corner]
+    else:
+        token_halves = chip_parts(tokens)
     mem_shard = jnp.concatenate([memory_first, memory_second], axis=1)
+    if chips == 4:
+        mem_shard = after(mem_shard, corner)
+        gate_weight_, up_weight_ = after(gate_weight, corner), up_weight
+    else:
+        gate_weight_, up_weight_ = gate_weight, up_weight
     if near:
         mem_pair = by_core(core, mem_shard, core_swap(mem_shard))
         mem_line = line_gather(mem_pair).reshape(groups * 2 * shard, 2 * MH)
@@ -1160,29 +1302,46 @@
         mem_mine = lax.dynamic_index_in_dim(mem_all, chip, 1, keepdims=False).reshape(rows, 2 * MH)
     mem_mine = mem_mine.astype(f32)
     first_init, second_init = mem_mine[:, :MH], mem_mine[:, MH:]
+    w_gate_up = lax.all_to_all(
+        pack_columns(chain, gate_weight_, up_weight_), ("chip", "core"), 0, 0, tiled=True
+    ).reshape(chain * shard, 2 * ff_own)
+    chip_index = chip.astype(jnp.int32)[None]
+    if chips == 4 and 2 * rows % 128 == 0:
+        w_flat, gains = take_heads(chip_index, chips, heads, w_pair)
+    else:
+        w_main = jnp.concatenate(
+            [
+                lax.dynamic_slice_in_dim(w_pair, chip * 2 * rows, 2 * rows, 1),
+                lax.dynamic_slice_in_dim(w_pair, 2 * half + chip * rows, rows, 1),
+                lax.dynamic_slice_in_dim(w_tail, NP + 2 + chip * heads, heads, 1),
+                jnp.zeros((D, RATE_ROWS - heads), bf16),
+            ],
+            axis=1,
+        )
+        w_flat = w_main.T
+        gains = w_tail[:, NP : NP + 2].astype(f32).T
+    w_flat = after(w_flat, w_gate_up)
+    gain_one, gain_two = gains[:1], gains[1:2]
+
+    out_order = []
+    for side in range(2):
+        for piece in range(pieces):
+            spot_, part = divmod(piece, per_head)
+            at_chip, turn = divmod(spot_, heads)
+            source = side * pieces + (turn * chips + at_chip) * per_head + part
+            out_order.append((source, 2 * piece + side))
+    out_moved = lax.ppermute(output_weight, ("dp", "chip", "core"), out_order)
     if chips == 4:
-        cut = GROUP // 2
-        corner = jnp.concatenate(
-            [chip_swap(along[:cut], 2), chip_swap(across[cut:], 1)], axis=0
-        )
-        token_halves = [tokens, along, across, corner]
+        w_lines = lax.all_gather(
+            jnp.concatenate([after(out_moved, w_pair), down_weight], axis=0), "dp", axis=0
+        )
+        out_lines = w_lines[:, :shard]
+        w_down = w_lines[:, shard:].reshape(-1, D)
+        w_gate_up = lax.all_gather(after(w_gate_up, w_pair), "dp", axis=0, tiled=True)
     else:
-        token_halves = chip_parts(tokens)
-    w_gate_up = lax.all_to_all(
-        pack_columns(chain, gate_weight, up_weight), ("chip", "core"), 0, 0, tiled=True
-    ).reshape(chain * shard, 2 * ff_own)
-    w_main = jnp.concatenate(
-        [
-            lax.dynamic_slice_in_dim(w_pair, chip * 2 * rows, 2 * rows, 1),
-            lax.dynamic_slice_in_dim(w_pair, 2 * half + chip * rows, rows, 1),
-            lax.dynamic_slice_in_dim(w_tail, NP + 2 + chip * heads, heads, 1),
-            jnp.zeros((D, RATE_ROWS - heads), bf16),
-        ],
-        axis=1,
-    )
-    w_flat = after(w_main, w_gate_up).T
-    gains = w_tail[:, NP : NP + 2].astype(f32).T
-    gain_one, gain_two = gains[:1], gains[1:]
+        w_gate_up = lax.all_gather(w_gate_up, "dp", axis=0, tiled=True)
+        w_down = lax.all_gather(down_weight, "dp", axis=0, tiled=True)
+        w_output = gather_chips(out_moved)
 
     ids = segments[0].reshape(chain, GROUP)
     first_id, last_id = ids[:, 0], ids[:, GROUP - 1]
@@ -1219,6 +1378,9 @@
 
     scalars = jnp.stack([own_heads(1.0 - decay), own_heads(momentum)])
 
+    if chips == 4:
+        grad_low = after(grad_out, w_flat)
+        along_low, across_high = chip_swap(grad_low[:cut], 1), chip_swap(grad_low[cut:], 2)
     token_blocks = []
     for part in token_halves:
         token_blocks += [part, core_swap(part)]
@@ -1228,43 +1390,52 @@
             start, chain, token_blocks[start : start + 8], gain_one, w_flat, placed
         )
     normed_all, main = placed
-
-    out_order = []
-    for side in range(2):
-        for piece in range(pieces):
-            spot_, part = divmod(piece, per_head)
-            at_chip, turn = divmod(spot_, heads)
-            source = side * pieces + (turn * chips + at_chip) * per_head + part
-            out_order.append((source, 2 * piece + side))
-    out_moved = lax.ppermute(output_weight, ("dp", "chip", "core"), out_order)
-    w_output = gather_chips(after(out_moved, token_halves[3]))
-
-    w_gate_up = lax.all_gather(w_gate_up, "dp", axis=0, tiled=True)
-    w_down = lax.all_gather(down_weight, "dp", axis=0, tiled=True)
+    if chips == 4:
+        main, along_low, across_high = together(main, along_low, across_high)
+
 
     def pair_rows(own):
         return jnp.concatenate([own, core_swap(own)], axis=0)
 
     if chips == 4:
-        grad_along, grad_across = [chip_swap(after(grad_out, main), step) for step in (1, 2)]
+        corner_along, corner_across = chip_swap(along_low, 2), chip_swap(across_high, 1)
     recalled, saved = memory_forward(
         flags, main, retain, update, first_init, second_init, scalars, chips
     )
     normed = normed_all[:width]
     low = matmul(w_pair[:, : 3 * half], normed, 0, 1, bf16)
     side = matmul(w_context, persist, 0, 0, bf16)
+    if chips == 4:
+        recalled, corner_along, corner_across, out_lines = together(
+            recalled, corner_along, corner_across, out_lines
+        )
+        out_along, out_across = chip_swap(out_lines, 1), chip_swap(out_lines, 2)
     recalled = after(lax.all_to_all(recalled, "chip", 0, 0, tiled=True), low, side)
+    if chips == 4:
+        recalled, out_along, out_across = together(recalled, out_along, out_across)
     recalled = recalled.reshape(chips, heads, HD, width).swapaxes(0, 1).reshape(half, width)
     context = by_core(core, recalled, core_swap(recalled))
     if chips == 4:
-        grad_along, grad_across = after(grad_along, context), after(grad_across, context)
-        grad_corner = (chip_swap(grad_along[:cut], 2), chip_swap(grad_across[cut:], 1))
-        grad_halves = [grad_out, grad_along, grad_across, grad_corner]
-    else:
-        grad_halves = chip_parts(after(grad_out, context))
+        upper = groups // 2
+        out_corner = (chip_swap(out_along[:upper], 2), chip_swap(out_across[upper:], 1))
+        grad_low = after(grad_out, context)
+        along_high, across_low = chip_swap(grad_low[cut:], 1), chip_swap(grad_low[:cut], 2)
 
     far = matmul(w_context, context, 0, 0, bf16)
     mixed, total = attention_forward(scale, core_index, low, far, side, id_row, id_col)
+
+    if chips == 4:
+        mixed, along_high, across_low, *out_corner = together(
+            mixed, along_high, across_low, *out_corner
+        )
+        stacked = jnp.stack([out_lines, out_along, out_across, jnp.concatenate(out_corner, axis=0)])
+        w_output = jnp.stack(
+            [
+                lax.dynamic_index_in_dim(stacked, chip ^ at, 0, keepdims=False)
+                for at in range(chips)
+            ],
+            axis=1,
+        ).reshape(half, D)
 
     def pair_sum(left, right, left_dim, right_dim):
         def block(which):
@@ -1278,71 +1449,89 @@
     middle = tokens.astype(f32) + pair_sum(mixed, w_output, 0, 0)
     inverse_two = inverse_rms(middle)
     normed_own = (middle * inverse_two * gain_two).astype(bf16)
+    def chunk(step, normed, grad, arrays):
+        def both(pieces):
+            return (tuple(pieces), tuple(core_swap(piece) for piece in pieces))
+
+        *arrays, out, back = ffn_chunk(
+            step, chips, both(normed), both(grad), w_gate_up, w_down, arrays
+        )
+        return tuple(arrays), out, back
+
+    def over_cores(part):
+        return part[0].astype(f32) + core_swap(part[1]).astype(f32)
+
+    def halves(value, first, second):
+        return chip_swap(value[:cut], first), chip_swap(value[cut:], second)
+
     if chips == 4:
-        normed_halves = [normed_own, chip_swap(normed_own, 1), chip_swap(normed_own, 2), None]
+        first = halves(normed_own, 1, 2)
+        arrays, out_own, back_own = chunk(0, (normed_own,), (grad_out,), ())
+        arrays, first = together(arrays, first)
+        later = after(normed_own, arrays[0])
+        second = (chip_swap(later[cut:], 1), chip_swap(later[:cut], 2))
+        arrays, out_first, back_first = chunk(1, first, (along_low, across_high), arrays)
+        arrays, second = together(arrays, second)
+        corner = (
+            chip_swap(after(first[0], arrays[0]), 2),
+            chip_swap(after(first[1], arrays[0]), 1),
+        )
+        arrays, out_second, back_second = chunk(2, second, (along_high, across_low), arrays)
+        arrays, corner = together(arrays, corner)
+        sent = halves(after(over_cores(back_first), arrays[0]).astype(bf16), 1, 2)
+        arrays, out_corner, back_corner = chunk(3, corner, (corner_along, corner_across), arrays)
+        back_corner, sent = together(back_corner, sent)
+        all_normed, all_grad, all_hidden, all_grad_gate_up = arrays
+        corner_low = over_cores(back_corner).astype(bf16)
+        from_corner = halves(corner_low, 1, 2)
+        grad_down_w = tokens_product(after(all_hidden, corner_low), all_grad)
+        grad_down_w, from_corner = together(grad_down_w, from_corner)
+
+        def add_corner(part, from_corner):
+            from_along, from_across = from_corner
+            return (
+                jnp.concatenate([part[:cut] + from_across, part[cut:] + from_along], axis=0)
+            ).astype(bf16)
+
+        last = add_corner(over_cores(back_second), from_corner)
+        grad_gate_up_w = tokens_product(after(all_normed, last), all_grad_gate_up)
+        grad_gate_up_w, last = together(grad_gate_up_w, halves(last, 1, 2))
+
+        def all_parts(own, sent, last):
+            low = own[:cut] + sent[0].astype(f32) + last[1].astype(f32)
+            high = own[cut:] + sent[1].astype(f32) + last[0].astype(f32)
+            return jnp.concatenate([low, high], axis=0)
+
+        grad_normed_two = all_parts(over_cores(back_own), sent, last)
+        out_corner = over_cores(after(out_corner, grad_gate_up_w)).astype(bf16)
+        out_first = over_cores(after(out_first, grad_gate_up_w)).astype(bf16)
+        out_second = over_cores(after(out_second, grad_gate_up_w))
+        out_own = over_cores(after(out_own, grad_gate_up_w))
     else:
-        normed_halves = chip_parts(normed_own)
-
-    outs, grad_normeds, arrays = [], [], ()
-    for step in range(chips):
-        normed_half, grad_half = normed_halves[step], grad_halves[step]
-        if chips == 4 and 0 < step < 3:
-            normed_half = after(normed_half, outs[0])
-            normed_halves[step] = normed_half
-        elif chips == 4 and step == 3:
-            normed_half = jnp.concatenate([after(part, outs[2]) for part in normed_corner], axis=0)
-            grad_half = jnp.concatenate([after(part, outs[2]) for part in grad_half], axis=0)
-        if chips == 4 and step == 2:
-            normed_corner = (
-                chip_swap(normed_halves[1][:cut], 2),
-                chip_swap(normed_halves[2][cut:], 1),
-            )
-        *arrays, out, grad_normed = ffn_chunk(
-            step,
-            chips,
-            (normed_half, core_swap(normed_half)),
-            (grad_half, core_swap(grad_half)),
-            w_gate_up,
-            w_down,
-            arrays,
-        )
-        outs.append(out)
-        grad_normeds.append(grad_normed)
-    all_normed, all_grad, all_hidden, all_grad_gate_up = arrays
-
-    def pair_sums(parts, *events):
-        return [
-            part[0].astype(f32) + core_swap(after(part, *events)[1]).astype(f32) for part in parts
-        ]
-
-    grad_normeds = pair_sums(grad_normeds)
-    if chips == 4:
-        corner_low = grad_normeds[3].astype(bf16)
-        grad_down_w = tokens_product(after(all_hidden, corner_low), all_grad)
-        first_sum, second_sum = corner_sums(corner_low, grad_normeds, grad_down_w)
-        grad_gate_up_w = tokens_product(
-            after(all_normed, first_sum, second_sum), all_grad_gate_up
-        )
-        grad_normed_two = side_sums(grad_normeds[0], first_sum, second_sum, grad_gate_up_w)
-        outs = pair_sums(outs, grad_gate_up_w)
-    else:
-        grad_normed_two = chip_sums(grad_normeds)
+        grads_by_step, normeds_by_step = chip_parts(grad_out), chip_parts(normed_own)
+        outs, backs, arrays = [], [], ()
+        for step in range(chips):
+            arrays, out, back = chunk(step, (normeds_by_step[step],), (grads_by_step[step],), arrays)
+            outs.append(over_cores(out))
+            backs.append(over_cores(back))
+        all_normed, all_grad, all_hidden, all_grad_gate_up = arrays
+        grad_normed_two = chip_sums(backs)
         grad_down_w = tokens_product(all_hidden, all_grad)
         grad_gate_up_w = tokens_product(all_normed, all_grad_gate_up)
-        outs = pair_sums(outs)
     grad_middle = grad_out.astype(f32) + norm_back(grad_normed_two, middle, inverse_two, gain_two)
     down_part = lax.psum_scatter(grad_down_w, "dp", scatter_dimension=0, tiled=True).astype(f32)
     gate_up_scattered = lax.psum_scatter(grad_gate_up_w, "dp", scatter_dimension=0, tiled=True)
 
     grad_attended = pair_rows(grad_middle.astype(bf16))
     grad_output_w = matmul(mixed, grad_attended, 1, 0, bf16)
+    output_part = lax.psum_scatter(grad_output_w, "dp", scatter_dimension=0, tiled=True)
     grad_mixed = matmul(w_output, grad_attended, 1, 1, bf16)
+    events = ()
     if chips == 4:
-        out_corner = after(outs[3].astype(bf16), grad_normed_two)
-        out_first, out_second = corner_sums(out_corner, outs, grad_mixed, grad_output_w)
-        events = (out_first, out_second)
-    else:
-        events = ()
+        from_corner = halves(after(out_corner, grad_normed_two), 1, 2)
+        out_last = add_corner(out_second, after(from_corner, grad_mixed))
+        out_sent = halves(after(out_first, grad_normed_two), 1, 2)
+        events = (out_last,)
     grad_part, grad_far, grad_side = attention_backward(
         scale,
         core_index,
@@ -1353,35 +1542,33 @@
         id_col,
         mixed,
         total,
-        after(grad_mixed, grad_output_w, *events),
+        after(grad_mixed, *events),
     )
     grad_side = grad_side.astype(bf16)
     if chips == 4:
-        out_sum = side_sums(outs[0], out_first, out_second, grad_far)
+        grad_far, out_sent, out_last = together(grad_far, out_sent, halves(out_last, 1, 2))
+        out_sum = all_parts(out_own, out_sent, out_last)
     else:
         out_sum = chip_sums(outs)
     result = (middle + out_sum).astype(bf16)
 
     def half_rows(which):
-        return lax.dynamic_slice_in_dim(w_context, which * half, half, 0)
+        return lax.dynamic_slice(w_pair, (which * half, 0), (half, 2 * half))
 
     pull_other = core_swap(matmul(half_rows(1 - core), grad_far, 1, 0, bf16))
     pull = (matmul(half_rows(core), grad_far, 1, 0) + pull_other.astype(f32)).astype(bf16)
     pull = pull.reshape(heads, chips, HD, width).swapaxes(0, 1).reshape(chips, rows, width)
-    pull = lax.all_to_all(after(pull, out_sum), "chip", 0, 0, tiled=True)
+    pull = after(lax.all_to_all(pull, "chip", 0, 0, tiled=True), result)
     grad_part = lax.all_to_all(
         after(grad_part.reshape(chips, 3 * rows, width), pull), "chip", 0, 0, tiled=True
     )
-    grad_context_w = jnp.concatenate(
-        [
-            (matmul(context, grad_far, 1, 1) + matmul(persist, grad_side, 1, 1)).astype(bf16),
-            matmul(w_context, grad_side, 1, 0, bf16),
-            jnp.zeros((D, 128 - NP), bf16),
-        ],
-        axis=1,
-    )
+    grad_context_w = context_product(context, grad_far, persist, grad_side, w_pair)
     context_part = lax.psum_scatter(grad_context_w, "dp", scatter_dimension=0, tiled=True)
     context_part = context_part.reshape(chips, 2 * shard, 2 * half + 128)
+    output_part = output_part.reshape(chips, shard, 2, half).swapaxes(1, 2)
+    context_part = jnp.concatenate(
+        [context_part, output_part.reshape(chips, 2 * shard, half)], axis=2
+    )
     grads, grad_first, grad_second, grad_scalars = memory_backward(
         flags,
         main,
@@ -1391,78 +1578,90 @@
         second_init,
         scalars,
         saved,
-        after(pull, down_part, grad_context_w),
-    )
-    grad_tokens, grad_heads_w = merge_blocks(
-        chip.astype(jnp.int32)[None],
-        groups,
-        grads,
-        after(grad_part, grads),
-        normed_all,
-        w_flat,
-    )
-    grad_blocks = grad_tokens.reshape(chips, 2, GROUP, D)
-    grad_normeds = [
-        grad_blocks[step, 0].astype(f32) + core_swap(grad_blocks[step, 1]).astype(f32)
-        for step in range(chips)
-    ]
-    grad_mem = jnp.concatenate([grad_first, grad_second], axis=1).astype(bf16)
-    if near and MH == D // groups:
-        spread = jnp.zeros((groups, 4 * shard, MH), bf16)
-        spread = lax.dynamic_update_slice_in_dim(
-            spread,
-            jnp.concatenate(
-                [grad_first.reshape(heads, HD, MH), grad_second.reshape(heads, HD, MH)], axis=1
-            ).astype(bf16),
-            core * heads,
-            0,
-        )
-        grad_heads_w = jnp.concatenate([grad_heads_w, spread], axis=1)
-    heads_part = lax.all_to_all(grad_heads_w, "dp", 0, 0, tiled=True)
-    tokens_wide = tokens.astype(f32)
-    if chips == 4:
-        first_sum, second_sum = corner_sums(grad_normeds[3].astype(bf16), grad_normeds)
-        marks = (grad_tokens, first_sum)
-        heads_part = after(heads_part, first_sum, second_sum)
-    else:
-        marks = (grad_tokens, grad_tokens)
-    heads_sum = jnp.sum(heads_part.astype(f32), axis=0).astype(bf16)
-    heads_part = lax.all_to_all(
-        jnp.concatenate(
-            [
-                heads_sum[:all_rows].T.reshape(chain, shard, all_rows),
-                gate_up_scattered.reshape(chain, shard, 2 * ff_own),
-            ],
-            axis=2,
-        ),
+        after(pull, down_part, gate_up_scattered, grad_context_w),
+    )
+    grads, grad_part = together(grads, grad_part)
+    gate_up_part = lax.all_to_all(
+        after(gate_up_scattered, grad_part).reshape(chain, shard, 2 * ff_own),
         ("chip", "core"),
         0,
         0,
         tiled=True,
     )
-    gate_up_part = heads_part[:, :, all_rows:]
-    heads_part = heads_part[:, :, :all_rows]
-    context_part = after(context_part, *marks)
-    context_part = chip_sums(
-        [
-            lax.dynamic_index_in_dim(context_part, chip ^ step, 0, keepdims=False)
-            for step in range(chips)
-        ]
-    ).astype(bf16)
+    grad_mem = jnp.concatenate([grad_first, grad_second], axis=1).astype(bf16)
+    corner_own, corner_other = back_blocks(chip_index, chips - 1, 1, grads, grad_part, w_flat)
+    side_own, side_other = back_blocks(
+        chip_index, 0, chips - 1, grads, after(grad_part, corner_own), w_flat
+    )
+    side_own, corner_other, gate_up_part = together(
+        side_own, core_swap(corner_other), gate_up_part
+    )
+    corner_low = (corner_own[0].astype(f32) + corner_other[0].astype(f32)).astype(bf16)
+    side_other = core_swap(side_other)
+    grad_heads_w = merge_blocks(
+        chip_index, groups, grads, after(grad_part, corner_low, side_own), normed_all
+    )
+    if near:
+        spread = jnp.zeros((groups, 2 * shard, 2 * MH), bf16)
+        spread = lax.dynamic_update_slice_in_dim(
+            spread, grad_mem.reshape(heads, 2 * shard, 2 * MH), core * heads, 0
+        )
+        mem_line = lax.all_to_all(after(spread, gate_up_part), "dp", 0, 0, tiled=True)
+        grad_heads_w, mem_line = together(grad_heads_w, mem_line)
     if chips == 4:
-        grad_normed = side_sums(grad_normeds[0], first_sum, second_sum, heads_sum)
+        grad_heads_w, side_other, from_corner = together(
+            grad_heads_w, side_other, halves(corner_low, 1, 2)
+        )
+    heads_sum = lax.psum_scatter(grad_heads_w, "dp", scatter_dimension=0)
+    grad_normeds = [
+        side_own[step].astype(f32) + side_other[step].astype(f32) for step in range(chips - 1)
+    ]
+    grad_normeds.append(corner_low)
+    tokens_wide = tokens.astype(f32)
+    if chips == 4:
+        from_along, from_across = (part.astype(f32) for part in from_corner)
+        first_sum = jnp.concatenate(
+            [grad_normeds[1][:cut], grad_normeds[1][cut:] + from_across], axis=0
+        ).astype(bf16)
+        second_sum = jnp.concatenate(
+            [grad_normeds[2][:cut] + from_along, grad_normeds[2][cut:]], axis=0
+        ).astype(bf16)
+        heads_sum = after(heads_sum, first_sum, second_sum)
+        marks = (corner_low, first_sum)
+    else:
+        marks = (corner_low, side_own)
+    heads_part = lax.all_to_all(
+        heads_sum.T.reshape(chain, shard, all_rows), ("chip", "core"), 0, 0, tiled=True
+    )
+    context_parts = [
+        lax.dynamic_index_in_dim(after(context_part, *marks), chip ^ step, 0, keepdims=False)
+        for step in range(chips)
+    ]
+    if chips == 4:
+        context_first, context_second = corner_sums(
+            context_parts[3].astype(bf16), context_parts, heads_sum
+        )
+        grad_normed = side_sums(grad_normeds[0], first_sum, second_sum, context_first)
+        context_part = side_sums(
+            context_parts[0], context_first, context_second, grad_normed
+        ).astype(bf16)
     else:
         grad_normed = chip_sums(grad_normeds)
+        context_part = chip_sums(context_parts).astype(bf16)
     grad_tokens_one = norm_back(grad_normed, tokens_wide, inverse_rms(tokens_wide), gain_one)
     grad_inputs = (grad_middle + grad_tokens_one).astype(bf16)
     marks = (*marks, heads_sum, grad_normed, heads_part)
+    heads_part = after(heads_part, grad_inputs)
 
     def own_rows(part):
         mine = lax.dynamic_slice_in_dim(part, core * shard, shard, 0)
         other = core_swap(lax.dynamic_slice_in_dim(part, (1 - core) * shard, shard, 0))
         return mine, other
 
-    mine, other = own_rows(context_part)
+    output_part = jnp.concatenate(
+        [context_part[:shard, 2 * half + 128 :], context_part[shard:, 2 * half + 128 :]], axis=1
+    )
+    mine, other = own_rows(context_part[:, : 2 * half + 128])
     persist_part = (mine.astype(f32) + other.astype(f32))[:, 2 * half : 2 * half + NP]
     by_side = by_core(core, mine[None], other[None])
     grad_keys_own, grad_values_own, grad_queries_own, grad_rates_own, gain_one_part = (
@@ -1481,28 +1680,10 @@
     gate_part, up_part, gain_two_part = unpack_columns(
         gate_up_part, gate_weight, up_weight, ffn_gain[:, None]
     )
-    parts = grad_output_w.reshape(groups, chips, shard, D)
-    output_part = chip_sums(
-        [
-            lax.dynamic_index_in_dim(parts, chip ^ step, 1, keepdims=False)
-            for step in range(chips)
-        ]
-    ).astype(bf16)
-    output_part = lax.psum_scatter(
-        output_part.reshape(groups * shard, D), "dp", scatter_dimension=0, tiled=True
-    )
-    if near and MH == D // groups:
-        mem_sum = heads_sum[all_rows:]
-        mem_sum = jnp.concatenate([mem_sum[: 2 * shard], mem_sum[2 * shard :]], axis=1)
-        mine, other = own_rows(mem_sum)
-        mem_part = mine.astype(f32) + other.astype(f32)
-    elif near:
-        spread = jnp.zeros((groups, 2 * shard, 2 * MH), bf16)
-        spread = lax.dynamic_update_slice_in_dim(
-            spread, grad_mem.reshape(heads, 2 * shard, 2 * MH), core * heads, 0
-        )
-        mem_line = lax.all_to_all(spread, "dp", 0, 0, tiled=True)
-        mine, other = own_rows(jnp.sum(mem_line.astype(f32), axis=0).astype(bf16))
+    if near:
+        mine, other = own_rows(
+            jnp.sum(after(mem_line, *marks).astype(f32), axis=0).astype(bf16)
+        )
         mem_part = mine.astype(f32) + other.astype(f32)
     else:
         spread = jnp.zeros((heads, chips, HD, 2 * MH), bf16)

time: 928 us -> 847 us (0.913)
  waiting for transfers between devices: 254 us -> 182 us
  matrix products: 67.5 us -> 45.5 us
  starting transfers between devices: 99.3 us -> 117 us
  other arithmetic: 96 us -> 85.6 us
    ppermute x32 -> x40, waiting for transfers between devices: 172 us -> 84.5 us  [chip_swap(): lax.ppermute(value, 'chip', [(index, index ^ step) for index in range(cou...]
    dot_general x12 -> x9, matrix products: 67.5 us -> 45.5 us  [matmul(): lax.dot_general(left, right, (((left_dim,), (right_dim,)), ((), ())), pre...]
    pallas_call x6 -> x10, Pallas kernels: 111 us -> 130 us  [the longest x4 63.8 us: ffn_chunk(): pl.pallas_call(kernel, grid=(2,), in_specs=[pl.BlockSpec(piece.shape, lam...]
    all_to_all x4 -> x5, waiting for transfers between devices: 1.27 us -> 19.7 us  [the longest x1 15.1 us: on_device(): pull = after(lax.all_to_all(pull, 'chip', 0, 0, tiled=True), result)]
    add x5 -> x8, other arithmetic: 13.5 us -> 25.2 us  [the longest x5 15 us: over_cores(): return part[0].astype(f32) + core_swap(part[1]).astype(f32)]
    pallas_call x1, Pallas kernels: 25.1 us -> 13.8 us  [merge_blocks(): pl.pallas_call(kernel, grid_spec=pltpu.PrefetchScalarGridSpec(num_scalar_...]
    unnamed x168 -> x200, local copies, waits for them, and re-layouts: 32.4 us -> 41.8 us
    ppermute x32 -> x40, starting transfers between devices: 31.2 us -> 39.6 us  [chip_swap(): lax.ppermute(value, 'chip', [(index, index ^ step) for index in range(cou...]
  transfers between devices with their start and end apart: 91 -> 104, of which waited for: 36 -> 31; matrix products, arithmetic and copies ran while one was open for 24% -> 21% of each run, Pallas kernels for 31% -> 35%
where the time goes in v3:
time: 847 us; the launch traced here: 841 us
  Pallas kernels  301 us (36%)
  waiting for transfers between devices  182 us (21%)
  starting transfers between devices  117 us (14%)
  local copies, waits for them, and re-layouts  93.7 us (11%)
  other arithmetic  85.6 us (10%)
  matrix products  45.5 us (5%)
  between operations  15.9 us (2%)
    ppermute x40, waiting for transfers between devices, chip_swap(): lax.ppermute(value, 'chip', [(index, index ^ step) for index in range(cou...  84.5 us
    pallas_call x4, Pallas kernels, ffn_chunk(): pl.pallas_call(kernel, grid=(2,), in_specs=[pl.BlockSpec(piece.shape, lam...  63.8 us
    dot_general x9, matrix products, matmul(): lax.dot_general(left, right, (((left_dim,), (right_dim,)), ((), ())), pre...  45.5 us
    pallas_call x1, Pallas kernels, memory_backward(): pl.pallas_call(lambda *refs: memory_backward_kernel(heads, blocks, *refs)...  44.9 us
    unnamed x200, local copies, waits for them, and re-layouts  41.8 us
    ppermute x40, starting transfers between devices, chip_swap(): lax.ppermute(value, 'chip', [(index, index ^ step) for index in range(cou...  39.6 us
    pallas_call x1, Pallas kernels, attention_backward(): pl.pallas_call(lambda *refs: attention_backward_kernel(scale, *refs), gri...  33.1 us
    pallas_call x2, Pallas kernels, tokens_product(): pl.pallas_call(kernel, grid=(steps,), in_specs=[pl.BlockSpec((size, rows)...  31.1 us
  transfers between devices with their start and end apart: 104, of which 31 were waited for; matrix products, arithmetic and copies ran while one was open for 21% of the time, Pallas kernels for 35%

profile of v3, /device:TPU:2, one launch (start us, length us, event | category | flops | bytes accessed | tf_op | source)
XLA Modules:
  0.0 840.8 jit_solution(13245196893430171790)
XLA Ops:
  18.0 4.4 collective-permute-start.20
  23.7 46.1 %collective-permute-done.2.refs_2_ = bf16[512,1536]{1,0:T(8,128)(2,1)} collective-permute-done((bf16[512,1536]{1,0:T(8,128)(2,1)S(1)}, bf16[512,1536]{1,0:T(8,128)(2,1)}, u32[]{:S(2)}, u32[]{:S(2)}) %collective-permute-start.2) | collective-permute-done | bytes 1572896 | tf_op jit(solution)/shard_map/ppermute | solution.py:1126
  74.4 13.0 %collective-permute-done.6 = bf16[256,1536]{1,0:T(8,128)(2,1)S(1)} collective-permute-done((bf16[256,1536]{1,0:T(8,128)(2,1)S(1)}, bf16[256,1536]{1,0:T(8,128)(2,1)S(1)}, u32[]{:S(2)}, u32[]{:S(2)}) %collective-permute-start.6) | collective-permute-done | bytes 786464 | tf_op jit(solution)/shard_map/ppermute | solution.py:1126
  87.5 4.8 collective-permute-done.7
  97.3 5.1 collective-permute-done.12
  102.3 6.9 collective-permute-start.13
  112.8 3.3 collective-permute-done.13
  116.1 9.2 %collective-permute-start.14 = (bf16[96,768]{1,0:T(8,128)(2,1)S(1)}, bf16[96,768]{1,0:T(8,128)(2,1)S(1)}, u32[]{:S(2)}, u32[]{:S(2)}) collective-permute-start(bf16[96,768]{1,0:T(8,128)(2,1)S(1)} %collective-permute-done.13), channel_id=1, source_target_pairs={{0,8},{8,16},{16,24},{1,9},{9,17},{17,25},{2,10},{10,18},{18,26},{... | collective-permute-start | bytes 442376 | tf_op jit(solution)/shard_map/ppermute | solution.py:1179
  130.4 7.1 all-to-all-start
  137.9 2.9 collective-permute-done.17
  141.9 3.5 all-gather.5.cloned.1.call-done.low_ref.query_ref.tail_ref.weight_ref
  145.4 8.5 %shard_map.306 = (bf16[592,1536]{1,0:T(8,128)(2,1)}, f32[8,1536]{1,0:T(8,128)}) custom-call(s32[1]{0:T(128)} %bitcast.6.chip_ref, bf16[1536,2432]{1,0:T(8,128)(2,1)} %all-gather.5.cloned.1.call-done.low_ref.query_ref.tail_ref.weight_ref, bf16[1536,2432]{1,0:T(8,128)(2,1)} %all-gather.5.cloned.1.call-done.low_ref.query_ref.tail_ref.weight_ref, ...), custom_call_target="tpu_custom_call" | custom-call | tf_op jit(solution)/shard_map/pallas_call | solution.py:781
  159.5 19.4 %shard_map.308 = (bf16[4096,1536]{1,0:T(8,128)(2,1)}, bf16[592,4096]{1,0:T(8,128)(2,1)}) custom-call(bf16[512,1536]{1,0:T(8,128)(2,1)S(1)} %bitcast.202, bf16[512,1536]{1,0:T(8,128)(2,1)} %collective-permute-done.1.refs_1_, bf16[512,1536]{1,0:T(8,128)(2,1)} %collective-permute-done.2.refs_2_, bf16[512,1536]{1,0:T(8,128)(2,1)} %collective-permute-done.3.refs_3_, ...), custom_call_target="tpu_custom_call" | custom-call | flops 14898167808 | bytes 31834112 | tf_op jit(solution)/shard_map/pallas_call | solution.py:820
  181.0 23.3 %shard_map.309 = (bf16[4,192,1024]{2,1,0:T(8,128)(2,1)S(1)}, f32[8,4,192,384]{3,2,1,0:T(8,128)}) custom-call(s32[5,8]{1,0:T(8,128)S(1)} %stack.77.refs_0_, bf16[592,4096]{1,0:T(8,128)(2,1)} %get-tuple-element.176.refs_1_, f32[8,1,512]{2,1,0:T(1,128)S(1)} %get-tuple-element.457.refs_2_, f32[8,1,512]{2,1,0:T(1,128)S(1)} %get-tuple-element.456.refs_3_, ...), custom_call_target="tpu_custom_call" | custom-call | flops 16911433728 | bytes 14155776 | tf_op jit(solution)/shard_map/pallas_call | solution.py:148
  210.1 5.5 all-to-all-start.1
  215.7 13.0 %fusion.2.refs_1_.refs_2_ = bf16[2304,1024]{1,0:T(8,128)(2,1)} fusion(bf16[1536,2432]{1,0:T(8,128)(2,1)} %all-gather.5.cloned.1.call-done.low_ref.query_ref.tail_ref.weight_ref, bf16[4096,1536]{1,0:T(8,128)(2,1)} %get-tuple-element.173.normed_ref), kind=kOutput, calls=%fused_computation.2 | convolution fusion | flops 7250116608 | bytes 14942208 | tf_op jit(solution)/shard_map/dot_general | solution.py:1099
  230.8 8.6 %all-to-all-done.1 = bf16[4,192,1024]{2,1,0:T(8,128)(2,1)} async-done(((bf16[4,192,1024]{2,1,0:T(8,128)(2,1)}), bf16[4,192,1024]{2,1,0:T(8,128)(2,1)}, u32[]{:S(2)}, u32[]{:S(2)}) %all-to-all-start.1) | async-done | bytes 1572896 | tf_op jit(solution)/shard_map/all_to_all | solution.py:1413
  239.5 2.8 copy.103
  249.0 4.6 maximum_select_fusion.context_ref
  256.6 6.5 fusion.9.refs_3_
  264.1 21.7 %shard_map.310 = (bf16[768,1024]{1,0:T(8,128)(2,1)S(1)}, f32[8,1,1024]{2,1,0:T(1,128)S(1)}) custom-call(s32[1]{0:T(128)} %bitcast.1.refs_0_, bf16[2304,1024]{1,0:T(8,128)(2,1)} %fusion.2.refs_1_.refs_2_, bf16[2304,1024]{1,0:T(8,128)(2,1)} %fusion.2.refs_1_.refs_2_, bf16[1536,1024]{1,0:T(8,128)(2,1)} %fusion.9.refs_3_, bf16[1536,64]{1,0:T(8,128)(2,1)S(1)} %copy-done.62, ...), custom_call_target="tpu_custom_call" | custom-call | flops 13690208256 | bytes 9437184 | tf_op jit(solution)/shard_map/pallas_call | solution.py:500
  291.8 2.9 collective-permute-done.28
  299.9 2.6 fusion.82
  308.2 16.0 %shard_map.311 = (bf16[4096,1536]{1,0:T(8,128)(2,1)}, bf16[4096,1536]{1,0:T(8,128)(2,1)}, bf16[4096,512]{1,0:T(8,128)(2,1)}, bf16[4096,1024]{1,0:T(8,128)(2,1)},...) custom-call(bf16[512,1536]{1,0:T(8,128)(2,1)} %multiply_convert_fusion.refs_0_, ...), custom_call_target="tpu_custom_call" | custom-call | flops 9663676416 | bytes 15728640 | tf_op jit(solution)/shard_map/pallas_call | solution.py:989
  326.5 3.1 fusion.81
  331.7 16.6 %shard_map.312 = (bf16[4096,1536]{1,0:T(8,128)(2,1)}, bf16[4096,1536]{1,0:T(8,128)(2,1)}, bf16[4096,512]{1,0:T(8,128)(2,1)}, bf16[4096,1024]{1,0:T(8,128)(2,1)},...) custom-call(bf16[256,1536]{1,0:T(8,128)(2,1)} %collective-permute-do, ...), custom_call_target="tpu_custom_call", output_to_operand_aliasing={{0}: (10, {}), {1}: (11, {}), {2}: (12, {}), {3}: (13, {})} | custom-call | flops 9663676416 | bytes 15728640 | tf_op jit(solution)/shard_map/pallas_call | solution.py:989
  364.4 15.4 %shard_map.313 = (bf16[4096,1536]{1,0:T(8,128)(2,1)}, bf16[4096,1536]{1,0:T(8,128)(2,1)}, bf16[4096,512]{1,0:T(8,128)(2,1)}, bf16[4096,1024]{1,0:T(8,128)(2,1)},...) custom-call(bf16[256,1536]{1,0:T(8,128)(2,1)S(1)} %copy-done.42, ...), custom_call_target="tpu_custom_call", output_to_operand_aliasing={{0}: (10, {}), {1}: (11, {}), {2}: (12, {}), {3}: (13, {})} | custom-call | flops 9663676416 | bytes 15728640 | tf_op jit(solution)/shard_map/pallas_call | solution.py:989
  380.4 3.0 convert_add_fusion.7
  385.8 15.8 %shard_map.314 = (bf16[4096,1536]{1,0:T(8,128)(2,1)}, bf16[4096,1536]{1,0:T(8,128)(2,1)}, bf16[4096,512]{1,0:T(8,128)(2,1)}, bf16[4096,1024]{1,0:T(8,128)(2,1)},...) custom-call(bf16[256,1536]{1,0:T(8,128)(2,1)} %collective-permute-do, ...), custom_call_target="tpu_custom_call", output_to_operand_aliasing={{0}: (10, {}), {1}: (11, {}), {2}: (12, {}), {3}: (13, {})} | custom-call | flops 9663676416 | bytes 15728640 | tf_op jit(solution)/shard_map/pallas_call | solution.py:989
  411.7 12.0 %shard_map.316 = bf16[512,1536]{1,0:T(8,128)(2,1)} custom-call(bf16[4096,512]{1,0:T(8,128)(2,1)} %get-tuple-element.240.left_ref, bf16[4096,1536]{1,0:T(8,128)(2,1)} %get-tuple-element.241.right_ref), custom_call_target="tpu_custom_call" | custom-call | flops 6442450944 | bytes 16777216 | tf_op jit(solution)/shard_map/pallas_call | solution.py:1079
  423.7 5.5 collective-permute-done.54
  430.7 4.1 convert_add_fusion.4
  439.9 19.1 %shard_map.315 = bf16[1536,1024]{1,0:T(8,128)(2,1)S(1)} custom-call(bf16[4096,1536]{1,0:T(8,128)(2,1)} %get-tuple-element.232.left_ref, bf16[4096,1024]{1,0:T(8,128)(2,1)} %get-tuple-element.233.right_ref), custom_call_target="tpu_custom_call" | custom-call | flops 12884901888 | bytes 20971520 | tf_op jit(solution)/shard_map/pallas_call | solution.py:1079
  460.6 3.2 slice_bitcast_fusion.2
  464.0 3.6 fusion.46
  483.8 4.7 fusion.37.refs_9_
  488.5 4.0 convolution_convert_fusion
  495.9 3.9 collective-permute-done.66
  504.9 33.1 %shard_map.317 = (bf16[2304,1024]{1,0:T(8,128)(2,1)}, bf16[1536,1024]{1,0:T(8,128)(2,1)}, f32[1536,64]{1,0:T(8,128)S(1)}) custom-call(s32[1]{0:T(128)} %bitcast.1.refs_0_, bf16[2304,1024]{1,0:T(8,128)(2,1)} %fusion.2.refs_1_.refs_2_, bf16[2304,1024]{1,0:T(8,128)(2,1)} %fusion.2.refs_1_.refs_2_, bf16[1536,1024]{1,0:T(8,128)(2,1)} %fusion.9.refs_3_, ...), custom_call_target="tpu_custom_call" | custom-call | flops 34225520640 | bytes 22020096 | tf_op jit(solution)/shard_map/pallas_call | solution.py:599
  538.0 7.2 fusion.34
  547.2 4.2 convert_add_fusion.5
  553.4 3.1 copy-done
  559.4 8.7 %shard_map.318 = bf16[1536,1664]{1,0:T(8,128)(2,1)S(1)} custom-call(bf16[1536,1024]{1,0:T(8,128)(2,1)S(1)} %copy-done.9, bf16[1536,1024]{1,0:T(8,128)(2,1)S(1)} %copy-done.11, bf16[1536,64]{1,0:T(8,128)(2,1)S(1)} %slice.428.persist_ref, bf16[1536,64]{1,0:T(8,128)(2,1)S(1)} %copy-done.27, bf16[1536,2432]{1,0:T(8,128)(2,1)S(1)} %copy-done), custom_call_target="tpu_custom_call" | custom-call | flops 4831838208 | bytes 18874368 | tf_op jit(solution)/shard_map/pallas_call | solution.py:1036
  572.3 4.7 add_convert_fusion.1
  578.4 5.8 all-to-all-start.2
  584.2 2.8 fusion.47
  588.8 15.1 %all-to-all-done.2.refs_8_ = bf16[4,192,1024]{2,1,0:T(8,128)(2,1)} async-done(((bf16[4,192,1024]{2,1,0:T(8,128)(2,1)}), bf16[4,192,1024]{2,1,0:T(8,128)(2,1)}, u32[]{:S(2)}, u32[]{:S(2)}) %all-to-all-start.2) | async-done | bytes 1572896 | tf_op jit(solution)/shard_map/all_to_all | solution.py:1561
  603.9 5.7 all-to-all-start.3
  609.6 44.9 %shard_map.319 = (bf16[592,4096]{1,0:T(8,128)(2,1)}, f32[192,384]{1,0:T(8,128)}, f32[192,384]{1,0:T(8,128)}, f32[8,384]{1,0:T(8,128)}) custom-call(s32[5,8]{1,0:T(8,128)} %copy-done.56, bf16[592,4096]{1,0:T(8,128)(2,1)} %get-tuple-element.176.refs_1_, f32[8,1,512]{2,1,0:T(1,128)} %copy-done.55, f32[8,1,512]{2,1,0:T(1,128)} %copy-done.54, ...), custom_call_target="tpu_custom_call" | custom-call | flops 45902462976 | bytes 18874368 | tf_op jit(solution)/shard_map/pallas_call | solution.py:389
  654.5 7.7 all-to-all-done.3.part_ref
  664.6 5.4 shard_map.320
  670.0 12.2 %shard_map.321 = (bf16[3,512,1536]{2,1,0:T(8,128)(2,1)S(1)}, bf16[3,512,1536]{2,1,0:T(8,128)(2,1)}) custom-call(s32[1]{0:T(128)} %bitcast.6.chip_ref, bf16[592,4096]{1,0:T(8,128)(2,1)S(1)} %copy-done.61, bf16[4,576,1024]{2,1,0:T(8,128)(2,1)} %all-to-all-done.3.part_ref, bf16[592,1536]{1,0:T(8,128)(2,1)S(1)} %copy-done.58), custom_call_target="tpu_custom_call" | custom-call | flops 11173625856 | bytes 16711680 | tf_op jit(solution)/shard_map/pallas_call | solution.py:926
  684.8 4.3 all-to-all-start.4
  695.6 4.6 all-to-all-done.4.parts_ref
  700.2 3.5 all-to-all-start.5
  708.8 13.8 %shard_map.322 = bf16[4,592,384]{2,1,0:T(8,128)(2,1)} custom-call(s32[1]{0:T(128)} %bitcast.6.chip_ref, bf16[592,4096]{1,0:T(8,128)(2,1)} %get-tuple-element.276.grads_ref, bf16[4,576,1024]{2,1,0:T(8,128)(2,1)} %all-to-all-done.3.part_ref, bf16[4096,1536]{1,0:T(8,128)(2,1)} %get-tuple-element.173.normed_ref), custom_call_target="tpu_custom_call" | custom-call | flops 14898167808 | bytes 22282240 | tf_op jit(solution)/shard_map/pallas_call | solution.py:884
  726.7 3.8 convert_add_fusion.10
  748.8 25.2 %collective-permute-done.85 = f32[16,2]{0,1:T(2,128)S(1)} collective-permute-done((f32[16,2]{0,1:T(2,128)S(1)}, f32[16,2]{0,1:T(2,128)S(1)}, u32[]{:S(2)}, u32[]{:S(2)}) %collective-permute-start.85) | collective-permute-done | bytes 160 | tf_op jit(solution)/shard_map/ppermute | solution.py:1197
  774.0 3.5 collective-permute-done.86
  785.9 4.6 all-to-all-start.6
  793.9 4.3 fusion.14
  804.6 4.0 collective-permute-done.80
  813.4 7.6 collective-permute-done.82
  822.5 7.8 shard_map.323
  (524 shorter events, 221.7 us)
Async XLA Ops:
  7.2 138.1 %all-gather.5.cloned.1.call-start = ((), (), s32[]{:S(2)}) async-start(), calls=%async_computation.12 | async-start | bytes 7938048 | tf_op jit(solution)/shard_map/all_gather | solution.py:1109
  15.9 53.9 %collective-permute-start.2 = (bf16[512,1536]{1,0:T(8,128)(2,1)S(1)}, bf16[512,1536]{1,0:T(8,128)(2,1)}, u32[]{:S(2)}, u32[]{:S(2)}) collective-permute-start(bf16[512,1536]{1,0:T(8,128)(2,1)S(1)} %bitcast.199), channel_id=1, source_target_pairs={{0,2},{2,0},{4,6},{6,4},{1,3},{3,1},{5,7},{7,5},{8,10},{10,8},{12,... | collective-permute-start | bytes 4718600 | tf_op jit(solution)/shard_map/ppermute | solution.py:1126
  16.0 56.6 %collective-permute-start.4 = (bf16[512,1536]{1,0:T(8,128)(2,1)S(1)}, bf16[512,1536]{1,0:T(8,128)(2,1)}, u32[]{:S(2)}, u32[]{:S(2)}) collective-permute-start(bf16[512,1536]{1,0:T(8,128)(2,1)S(1)} %bitcast.200), channel_id=1, source_target_pairs={{0,4},{2,6},{4,0},{6,2},{1,5},{3,7},{5,1},{7,3},{8,12},{10,14},{12... | collective-permute-start | bytes 4718600 | tf_op jit(solution)/shard_map/ppermute | solution.py:1126
  18.0 140.9 %collective-permute-start.1 = (bf16[512,1536]{1,0:T(8,128)(2,1)S(1)}, bf16[512,1536]{1,0:T(8,128)(2,1)}, u32[]{:S(2)}, u32[]{:S(2)}) collective-permute-start(bf16[512,1536]{1,0:T(8,128)(2,1)S(1)} %bitcast.201), channel_id=1, source_target_pairs={{0,1},{1,0},{2,3},{3,2},{4,5},{5,4},{6,7},{7,6},{8,9},{9,8},{10,11... | collective-permute-start | bytes 4718600 | tf_op jit(solution)/shard_map/ppermute | solution.py:1105
  18.0 135.8 %collective-permute-start.20 = (bf16[48,1536]{1,0:T(8,128)(2,1)}, bf16[48,1536]{1,0:T(8,128)(2,1)}, u32[]{:S(2)}, u32[]{:S(2)}) collective-permute-start(bf16[48,1536]{1,0:T(8,128)(2,1)} %param.24), channel_id=1, source_target_pairs={{0,0},{1,2},{8,4},{9,6},{2,8},{3,10},{10,12},{11,14},{4,16},{5,18}... | collective-permute-start | bytes 442376 | tf_op jit(solution)/shard_map/ppermute | solution.py:1333
  116.1 21.6 %collective-permute-start.14 = (bf16[96,768]{1,0:T(8,128)(2,1)S(1)}, bf16[96,768]{1,0:T(8,128)(2,1)S(1)}, u32[]{:S(2)}, u32[]{:S(2)}) collective-permute-start(bf16[96,768]{1,0:T(8,128)(2,1)S(1)} %collective-permute-done.13), channel_id=1, source_target_pairs={{0,8},{8,16},{16,24},{1,9},{9,17},{17,25},{2,10},{10,18},{18,26},{... | collective-permute-start | bytes 442376 | tf_op jit(solution)/shard_map/ppermute | solution.py:1179
  128.2 31.3 %collective-permute-start.3 = (bf16[512,1536]{1,0:T(8,128)(2,1)}, bf16[512,1536]{1,0:T(8,128)(2,1)}, u32[]{:S(2)}, u32[]{:S(2)}) collective-permute-start(bf16[512,1536]{1,0:T(8,128)(2,1)} %collective-permute-done.2.refs_2_), channel_id=1, source_target_pairs={{0,1},{1,0},{2,3},{3,2},{4,5},{5,4},{6,7},{7,6},{8,9},{9,8},{10,11... | collective-permute-start | bytes 4718600 | tf_op jit(solution)/shard_map/ppermute | solution.py:1105
  130.4 23.4 %all-to-all-start = ((bf16[8,48,1024]{2,1,0:T(8,128)(2,1)}), bf16[8,48,1024]{2,1,0:T(8,128)(2,1)}, u32[]{:S(2)}, u32[]{:S(2)}) async-start(bf16[8,48,1024]{2,1,0:T(8,128)(2,1)} %shard_map.307), calls=%async_computation | async-start | bytes 1572864 | tf_op jit(solution)/shard_map/all_to_all | solution.py:1305
  137.5 67.9 %all-gather.9.cloned.1.call-start = ((), (), s32[]{:S(2)}) async-start(), calls=%async_computation.19 | async-start | bytes 2703360 | tf_op jit(solution)/shard_map/all_gather | solution.py:1335
  137.7 21.8 %collective-permute-start.5 = (bf16[512,1536]{1,0:T(8,128)(2,1)}, bf16[512,1536]{1,0:T(8,128)(2,1)}, u32[]{:S(2)}, u32[]{:S(2)}) collective-permute-start(bf16[512,1536]{1,0:T(8,128)(2,1)} %collective-permute-done.4.refs_4_), channel_id=1, source_target_pairs={{0,1},{1,0},{2,3},{3,2},{4,5},{5,4},{6,7},{7,6},{8,9},{9,8},{10,11... | collective-permute-start | bytes 4718600 | tf_op jit(solution)/shard_map/ppermute | solution.py:1105
  155.8 23.1 %collective-permute-start.10 = (bf16[256,1536]{1,0:T(8,128)(2,1)S(1)}, bf16[256,1536]{1,0:T(8,128)(2,1)}, u32[]{:S(2)}, u32[]{:S(2)}) collective-permute-start(bf16[256,1536]{1,0:T(8,128)(2,1)S(1)} %get-tuple-element.437), channel_id=1, source_target_pairs={{0,4},{2,6},{4,0},{6,2},{1,5},{3,7},{5,1},{7,3},{8,12},{10,14},{12... | collective-permute-start | bytes 2359304 | tf_op jit(solution)/shard_map/ppermute | solution.py:1126
  158.9 20.0 %collective-permute-start.9 = (bf16[256,1536]{1,0:T(8,128)(2,1)S(1)}, bf16[256,1536]{1,0:T(8,128)(2,1)}, u32[]{:S(2)}, u32[]{:S(2)}) collective-permute-start(bf16[256,1536]{1,0:T(8,128)(2,1)S(1)} %get-tuple-element.438), channel_id=1, source_target_pairs={{0,2},{2,0},{4,6},{6,4},{1,3},{3,1},{5,7},{7,5},{8,10},{10,8},{12,... | collective-permute-start | bytes 2359304 | tf_op jit(solution)/shard_map/ppermute | solution.py:1126
  178.9 28.5 %collective-permute-start.18 = (bf16[256,1536]{1,0:T(8,128)(2,1)}, bf16[256,1536]{1,0:T(8,128)(2,1)S(1)}, u32[]{:S(2)}, u32[]{:S(2)}) collective-permute-start(bf16[256,1536]{1,0:T(8,128)(2,1)} %collective-permute-done.9.refs_4_), channel_id=1, source_target_pairs={{0,4},{2,6},{4,0},{6,2},{1,5},{3,7},{5,1},{7,3},{8,12},{10,14},{12... | collective-permute-start | bytes 2359304 | tf_op jit(solution)/shard_map/ppermute | solution.py:1126
  179.3 28.1 %collective-permute-start.19 = (bf16[256,1536]{1,0:T(8,128)(2,1)}, bf16[256,1536]{1,0:T(8,128)(2,1)S(1)}, u32[]{:S(2)}, u32[]{:S(2)}) collective-permute-start(bf16[256,1536]{1,0:T(8,128)(2,1)} %collective-permute-done.10.refs_5_), channel_id=1, source_target_pairs={{0,2},{2,0},{4,6},{6,4},{1,3},{3,1},{5,7},{7,5},{8,10},{10,8},{12,... | collective-permute-start | bytes 2359304 | tf_op jit(solution)/shard_map/ppermute | solution.py:1126
  207.4 32.1 %collective-permute-start.21 = (bf16[4,48,1536]{2,1,0:T(8,128)(2,1)}, bf16[4,48,1536]{2,1,0:T(8,128)(2,1)}, u32[]{:S(2)}, u32[]{:S(2)}) collective-permute-start(bf16[4,48,1536]{2,1,0:T(8,128)(2,1)} %slice.427), channel_id=1, source_target_pairs={{0,2},{2,0},{4,6},{6,4},{1,3},{3,1},{5,7},{7,5},{8,10},{10,8},{12,... | collective-permute-start | bytes 1769480 | tf_op jit(solution)/shard_map/ppermute | solution.py:1126
  208.5 31.0 %collective-permute-start.22 = (bf16[4,48,1536]{2,1,0:T(8,128)(2,1)}, bf16[4,48,1536]{2,1,0:T(8,128)(2,1)}, u32[]{:S(2)}, u32[]{:S(2)}) collective-permute-start(bf16[4,48,1536]{2,1,0:T(8,128)(2,1)} %slice.427), channel_id=1, source_target_pairs={{0,4},{2,6},{4,0},{6,2},{1,5},{3,7},{5,1},{7,3},{8,12},{10,14},{12... | collective-permute-start | bytes 1769480 | tf_op jit(solution)/shard_map/ppermute | solution.py:1126
  210.1 29.3 %all-to-all-start.1 = ((bf16[4,192,1024]{2,1,0:T(8,128)(2,1)}), bf16[4,192,1024]{2,1,0:T(8,128)(2,1)}, u32[]{:S(2)}, u32[]{:S(2)}) async-start(bf16[4,192,1024]{2,1,0:T(8,128)(2,1)} %copy-done.26), calls=%async_computation.1 | async-start | bytes 3145728 | tf_op jit(solution)/shard_map/all_to_all | solution.py:1413
  215.7 91.1 %all-gather.7.cloned.1.call-start = ((), (), s32[]{:S(2)}) async-start(), calls=%async_computation.13 | async-start | bytes 3932160 | tf_op jit(solution)/shard_map/all_gather | solution.py:1340
  243.5 307.9 %reduce-scatter.6.cloned.1.call-start = ((), (), s32[]{:S(2)}) async-start(), calls=%async_computation.14 | async-start | bytes 1966080 | tf_op jit(solution)/shard_map/reduce_scatter | solution.py:1522
  245.2 40.7 %collective-permute-start.26 = (bf16[2,48,1536]{2,1,0:T(8,128)(2,1)}, bf16[2,48,1536]{2,1,0:T(8,128)(2,1)}, u32[]{:S(2)}, u32[]{:S(2)}) collective-permute-start(bf16[2,48,1536]{2,1,0:T(8,128)(2,1)} %slice.336), channel_id=1, source_target_pairs={{0,4},{2,6},{4,0},{6,2},{1,5},{3,7},{5,1},{7,3},{8,12},{10,14},{12... | collective-permute-start | bytes 884744 | tf_op jit(solution)/shard_map/ppermute | solution.py:1126
  248.3 37.5 %collective-permute-start.27 = (bf16[2,48,1536]{2,1,0:T(8,128)(2,1)}, bf16[2,48,1536]{2,1,0:T(8,128)(2,1)}, u32[]{:S(2)}, u32[]{:S(2)}) collective-permute-start(bf16[2,48,1536]{2,1,0:T(8,128)(2,1)} %slice.337), channel_id=1, source_target_pairs={{0,2},{2,0},{4,6},{6,4},{1,3},{3,1},{5,7},{7,5},{8,10},{10,8},{12,... | collective-permute-start | bytes 884744 | tf_op jit(solution)/shard_map/ppermute | solution.py:1126
  255.0 30.8 %collective-permute-start.24 = (bf16[256,1536]{1,0:T(8,128)(2,1)}, bf16[256,1536]{1,0:T(8,128)(2,1)S(1)}, u32[]{:S(2)}, u32[]{:S(2)}) collective-permute-start(bf16[256,1536]{1,0:T(8,128)(2,1)} %get-tuple-element.436), channel_id=1, source_target_pairs={{0,2},{2,0},{4,6},{6,4},{1,3},{3,1},{5,7},{7,5},{8,10},{10,8},{12,... | collective-permute-start | bytes 2359304 | tf_op jit(solution)/shard_map/ppermute | solution.py:1126
  256.2 29.7 %collective-permute-start.25 = (bf16[256,1536]{1,0:T(8,128)(2,1)}, bf16[256,1536]{1,0:T(8,128)(2,1)S(1)}, u32[]{:S(2)}, u32[]{:S(2)}) collective-permute-start(bf16[256,1536]{1,0:T(8,128)(2,1)} %get-tuple-element.435), channel_id=1, source_target_pairs={{0,4},{2,6},{4,0},{6,2},{1,5},{3,7},{5,1},{7,3},{8,12},{10,14},{12... | collective-permute-start | bytes 2359304 | tf_op jit(solution)/shard_map/ppermute | solution.py:1126
  298.2 31.4 %collective-permute-start.35 = (bf16[256,1536]{1,0:T(8,128)(2,1)}, bf16[256,1536]{1,0:T(8,128)(2,1)}, u32[]{:S(2)}, u32[]{:S(2)}) collective-permute-start(bf16[256,1536]{1,0:T(8,128)(2,1)} %collective-permute-done.9.refs_4_), channel_id=1, source_target_pairs={{0,1},{1,0},{2,3},{3,2},{4,5},{5,4},{6,7},{7,6},{8,9},{9,8},{10,11... | collective-permute-start | bytes 2359304 | tf_op jit(solution)/shard_map/ppermute | solution.py:1105
  298.5 31.0 %collective-permute-start.36 = (bf16[256,1536]{1,0:T(8,128)(2,1)}, bf16[256,1536]{1,0:T(8,128)(2,1)}, u32[]{:S(2)}, u32[]{:S(2)}) collective-permute-start(bf16[256,1536]{1,0:T(8,128)(2,1)} %collective-permute-done.10.refs_5_), channel_id=1, source_target_pairs={{0,1},{1,0},{2,3},{3,2},{4,5},{5,4},{6,7},{7,6},{8,9},{9,8},{10,11... | collective-permute-start | bytes 2359304 | tf_op jit(solution)/shard_map/ppermute | solution.py:1105
  302.5 23.4 %collective-permute-start.31 = (bf16[256,1536]{1,0:T(8,128)(2,1)}, bf16[256,1536]{1,0:T(8,128)(2,1)}, u32[]{:S(2)}, u32[]{:S(2)}) collective-permute-start(bf16[256,1536]{1,0:T(8,128)(2,1)} %get-tuple-element.434), channel_id=1, source_target_pairs={{0,2},{2,0},{4,6},{6,4},{1,3},{3,1},{5,7},{7,5},{8,10},{10,8},{12,... | collective-permute-start | bytes 2359304 | tf_op jit(solution)/shard_map/ppermute | solution.py:1126
  304.6 21.3 %collective-permute-start.32 = (bf16[256,1536]{1,0:T(8,128)(2,1)}, bf16[256,1536]{1,0:T(8,128)(2,1)}, u32[]{:S(2)}, u32[]{:S(2)}) collective-permute-start(bf16[256,1536]{1,0:T(8,128)(2,1)} %get-tuple-element.433), channel_id=1, source_target_pairs={{0,4},{2,6},{4,0},{6,2},{1,5},{3,7},{5,1},{7,3},{8,12},{10,14},{12... | collective-permute-start | bytes 2359304 | tf_op jit(solution)/shard_map/ppermute | solution.py:1126
  326.4 25.6 %collective-permute-start.41 = (bf16[256,1536]{1,0:T(8,128)(2,1)S(1)}, bf16[256,1536]{1,0:T(8,128)(2,1)S(1)}, u32[]{:S(2)}, u32[]{:S(2)}) collective-permute-start(bf16[256,1536]{1,0:T(8,128)(2,1)S(1)} %copy-done.33), channel_id=1, source_target_pairs={{0,1},{1,0},{2,3},{3,2},{4,5},{5,4},{6,7},{7,6},{8,9},{9,8},{10,11... | collective-permute-start | bytes 2359304 | tf_op jit(solution)/shard_map/ppermute | solution.py:1105
  329.6 23.7 %collective-permute-start.42 = (bf16[256,1536]{1,0:T(8,128)(2,1)S(1)}, bf16[256,1536]{1,0:T(8,128)(2,1)S(1)}, u32[]{:S(2)}, u32[]{:S(2)}) collective-permute-start(bf16[256,1536]{1,0:T(8,128)(2,1)S(1)} %copy-done.35), channel_id=1, source_target_pairs={{0,1},{1,0},{2,3},{3,2},{4,5},{5,4},{6,7},{7,6},{8,9},{9,8},{10,11... | collective-permute-start | bytes 2359304 | tf_op jit(solution)/shard_map/ppermute | solution.py:1105
  329.6 20.5 %collective-permute-start.37 = (bf16[256,1536]{1,0:T(8,128)(2,1)}, bf16[256,1536]{1,0:T(8,128)(2,1)S(1)}, u32[]{:S(2)}, u32[]{:S(2)}) collective-permute-start(bf16[256,1536]{1,0:T(8,128)(2,1)} %get-tuple-element.432), channel_id=1, source_target_pairs={{0,2},{2,0},{4,6},{6,4},{1,3},{3,1},{5,7},{7,5},{8,10},{10,8},{12,... | collective-permute-start | bytes 2359304 | tf_op jit(solution)/shard_map/ppermute | solution.py:1126
  330.2 19.8 %collective-permute-start.38 = (bf16[256,1536]{1,0:T(8,128)(2,1)S(1)}, bf16[256,1536]{1,0:T(8,128)(2,1)}, u32[]{:S(2)}, u32[]{:S(2)}) collective-permute-start(bf16[256,1536]{1,0:T(8,128)(2,1)S(1)} %get-tuple-element.431), channel_id=1, source_target_pairs={{0,4},{2,6},{4,0},{6,2},{1,5},{3,7},{5,1},{7,3},{8,12},{10,14},{12... | collective-permute-start | bytes 2359304 | tf_op jit(solution)/shard_map/ppermute | solution.py:1126
  351.9 28.5 %collective-permute-start.50 = (bf16[512,1536]{1,0:T(8,128)(2,1)}, bf16[512,1536]{1,0:T(8,128)(2,1)}, u32[]{:S(2)}, u32[]{:S(2)}) collective-permute-start(bf16[512,1536]{1,0:T(8,128)(2,1)} %slice_bitcast_fusion.8), channel_id=1, source_target_pairs={{0,1},{1,0},{2,3},{3,2},{4,5},{5,4},{6,7},{7,6},{8,9},{9,8},{10,11... | collective-permute-start | bytes 4718600 | tf_op jit(solution)/shard_map/ppermute | solution.py:1105
  352.9 32.1 %collective-permute-start.47 = (bf16[256,1536]{1,0:T(8,128)(2,1)S(1)}, bf16[256,1536]{1,0:T(8,128)(2,1)S(1)}, u32[]{:S(2)}, u32[]{:S(2)}) collective-permute-start(bf16[256,1536]{1,0:T(8,128)(2,1)S(1)} %copy-done.29), channel_id=1, source_target_pairs={{0,1},{1,0},{2,3},{3,2},{4,5},{5,4},{6,7},{7,6},{8,9},{9,8},{10,11... | collective-permute-start | bytes 2359304 | tf_op jit(solution)/shard_map/ppermute | solution.py:1105
  354.2 31.6 %collective-permute-start.48 = (bf16[256,1536]{1,0:T(8,128)(2,1)S(1)}, bf16[256,1536]{1,0:T(8,128)(2,1)}, u32[]{:S(2)}, u32[]{:S(2)}) collective-permute-start(bf16[256,1536]{1,0:T(8,128)(2,1)S(1)} %copy-done.31), channel_id=1, source_target_pairs={{0,1},{1,0},{2,3},{3,2},{4,5},{5,4},{6,7},{7,6},{8,9},{9,8},{10,11... | collective-permute-start | bytes 2359304 | tf_op jit(solution)/shard_map/ppermute | solution.py:1105
  355.1 24.7 %collective-permute-start.43 = (bf16[256,1536]{1,0:T(8,128)(2,1)}, bf16[256,1536]{1,0:T(8,128)(2,1)}, u32[]{:S(2)}, u32[]{:S(2)}) collective-permute-start(bf16[256,1536]{1,0:T(8,128)(2,1)} %collective-permute-done.31.refs_0_), channel_id=1, source_target_pairs={{0,4},{2,6},{4,0},{6,2},{1,5},{3,7},{5,1},{7,3},{8,12},{10,14},{12... | collective-permute-start | bytes 2359304 | tf_op jit(solution)/shard_map/ppermute | solution.py:1126
  357.2 22.6 %collective-permute-start.44 = (bf16[256,1536]{1,0:T(8,128)(2,1)}, bf16[256,1536]{1,0:T(8,128)(2,1)}, u32[]{:S(2)}, u32[]{:S(2)}) collective-permute-start(bf16[256,1536]{1,0:T(8,128)(2,1)} %collective-permute-done.32.refs_1_), channel_id=1, source_target_pairs={{0,2},{2,0},{4,6},{6,4},{1,3},{3,1},{5,7},{7,5},{8,10},{10,8},{12,... | collective-permute-start | bytes 2359304 | tf_op jit(solution)/shard_map/ppermute | solution.py:1126
  405.8 24.9 %collective-permute-start.59 = (bf16[512,1536]{1,0:T(8,128)(2,1)}, bf16[512,1536]{1,0:T(8,128)(2,1)}, u32[]{:S(2)}, u32[]{:S(2)}) collective-permute-start(bf16[512,1536]{1,0:T(8,128)(2,1)} %slice_bitcast_fusion.5), channel_id=1, source_target_pairs={{0,1},{1,0},{2,3},{3,2},{4,5},{5,4},{6,7},{7,6},{8,9},{9,8},{10,11... | collective-permute-start | bytes 4718600 | tf_op jit(solution)/shard_map/ppermute | solution.py:1105
  407.4 27.4 %collective-permute-start.49 = (bf16[512,1536]{1,0:T(8,128)(2,1)}, bf16[512,1536]{1,0:T(8,128)(2,1)}, u32[]{:S(2)}, u32[]{:S(2)}) collective-permute-start(bf16[512,1536]{1,0:T(8,128)(2,1)} %slice_bitcast_fusion.9), channel_id=1, source_target_pairs={{0,1},{1,0},{2,3},{3,2},{4,5},{5,4},{6,7},{7,6},{8,9},{9,8},{10,11... | collective-permute-start | bytes 4718600 | tf_op jit(solution)/shard_map/ppermute | solution.py:1105
  430.4 179.1 %reduce-scatter.8.cloned.1.call-start = ((), (), s32[]{:S(2)}) async-start(), calls=%async_computation.15 | async-start | bytes 3932160 | tf_op jit(solution)/shard_map/reduce_scatter | solution.py:1523
  438.3 22.3 %collective-permute-start.56 = (bf16[256,1536]{1,0:T(8,128)(2,1)}, bf16[256,1536]{1,0:T(8,128)(2,1)S(1)}, u32[]{:S(2)}, u32[]{:S(2)}) collective-permute-start(bf16[256,1536]{1,0:T(8,128)(2,1)} %get-tuple-element.410), channel_id=1, source_target_pairs={{0,2},{2,0},{4,6},{6,4},{1,3},{3,1},{5,7},{7,5},{8,10},{10,8},{12,... | collective-permute-start | bytes 2359304 | tf_op jit(solution)/shard_map/ppermute | solution.py:1126
  438.9 21.7 %collective-permute-start.57 = (bf16[256,1536]{1,0:T(8,128)(2,1)}, bf16[256,1536]{1,0:T(8,128)(2,1)S(1)}, u32[]{:S(2)}, u32[]{:S(2)}) collective-permute-start(bf16[256,1536]{1,0:T(8,128)(2,1)} %get-tuple-element.409), channel_id=1, source_target_pairs={{0,4},{2,6},{4,0},{6,2},{1,5},{3,7},{5,1},{7,3},{8,12},{10,14},{12... | collective-permute-start | bytes 2359304 | tf_op jit(solution)/shard_map/ppermute | solution.py:1126
  463.9 227.2 %reduce-scatter.12.cloned.1.call-start = ((), (), s32[]{:S(2)}) async-start(), calls=%async_computation.17 | async-start | bytes 2949120 | tf_op jit(solution)/shard_map/reduce_scatter | solution.py:1527
  472.6 20.4 %collective-permute-start.64 = (bf16[512,1536]{1,0:T(8,128)(2,1)}, bf16[512,1536]{1,0:T(8,128)(2,1)}, u32[]{:S(2)}, u32[]{:S(2)}) collective-permute-start(bf16[512,1536]{1,0:T(8,128)(2,1)} %slice_bitcast_fusion.3), channel_id=1, source_target_pairs={{0,1},{1,0},{2,3},{3,2},{4,5},{5,4},{6,7},{7,6},{8,9},{9,8},{10,11... | collective-permute-start | bytes 4718600 | tf_op jit(solution)/shard_map/ppermute | solution.py:1105
  475.8 71.4 %collective-permute-start.58 = (bf16[512,1536]{1,0:T(8,128)(2,1)}, bf16[512,1536]{1,0:T(8,128)(2,1)}, u32[]{:S(2)}, u32[]{:S(2)}) collective-permute-start(bf16[512,1536]{1,0:T(8,128)(2,1)} %slice_bitcast_fusion.6), channel_id=1, source_target_pairs={{0,1},{1,0},{2,3},{3,2},{4,5},{5,4},{6,7},{7,6},{8,9},{9,8},{10,11... | collective-permute-start | bytes 4718600 | tf_op jit(solution)/shard_map/ppermute | solution.py:1105
  479.1 20.7 %collective-permute-start.66 = (bf16[256,1536]{1,0:T(8,128)(2,1)}, bf16[256,1536]{1,0:T(8,128)(2,1)}, u32[]{:S(2)}, u32[]{:S(2)}) collective-permute-start(bf16[256,1536]{1,0:T(8,128)(2,1)} %get-tuple-element.424), channel_id=1, source_target_pairs={{0,2},{2,0},{4,6},{6,4},{1,3},{3,1},{5,7},{7,5},{8,10},{10,8},{12,... | collective-permute-start | bytes 2359304 | tf_op jit(solution)/shard_map/ppermute | solution.py:1126
  480.4 20.7 %collective-permute-start.67 = (bf16[256,1536]{1,0:T(8,128)(2,1)}, bf16[256,1536]{1,0:T(8,128)(2,1)}, u32[]{:S(2)}, u32[]{:S(2)}) collective-permute-start(bf16[256,1536]{1,0:T(8,128)(2,1)} %get-tuple-element.423), channel_id=1, source_target_pairs={{0,4},{2,6},{4,0},{6,2},{1,5},{3,7},{5,1},{7,3},{8,12},{10,14},{12... | collective-permute-start | bytes 2359304 | tf_op jit(solution)/shard_map/ppermute | solution.py:1126
  483.1 54.8 %collective-permute-start.62 = (bf16[256,1536]{1,0:T(8,128)(2,1)}, bf16[256,1536]{1,0:T(8,128)(2,1)}, u32[]{:S(2)}, u32[]{:S(2)}) collective-permute-start(bf16[256,1536]{1,0:T(8,128)(2,1)} %get-tuple-element.426), channel_id=1, source_target_pairs={{0,2},{2,0},{4,6},{6,4},{1,3},{3,1},{5,7},{7,5},{8,10},{10,8},{12,... | collective-permute-start | bytes 2359304 | tf_op jit(solution)/shard_map/ppermute | solution.py:1126
  492.5 230.1 %reduce-scatter.10.cloned.1.call-start = ((), (), s32[]{:S(2)}) async-start(), calls=%async_computation.16 | async-start | bytes 6389760 | tf_op jit(solution)/shard_map/reduce_scatter | solution.py:1566
  493.0 45.0 %collective-permute-start.63 = (bf16[256,1536]{1,0:T(8,128)(2,1)}, bf16[256,1536]{1,0:T(8,128)(2,1)S(1)}, u32[]{:S(2)}, u32[]{:S(2)}) collective-permute-start(bf16[256,1536]{1,0:T(8,128)(2,1)} %get-tuple-element.425), channel_id=1, source_target_pairs={{0,4},{2,6},{4,0},{6,2},{1,5},{3,7},{5,1},{7,3},{8,12},{10,14},{12... | collective-permute-start | bytes 2359304 | tf_op jit(solution)/shard_map/ppermute | solution.py:1126
  503.1 34.9 %collective-permute-start.68 = (bf16[256,1536]{1,0:T(8,128)(2,1)S(1)}, bf16[256,1536]{1,0:T(8,128)(2,1)S(1)}, u32[]{:S(2)}, u32[]{:S(2)}) collective-permute-start(bf16[256,1536]{1,0:T(8,128)(2,1)S(1)} %get-tuple-element.406), channel_id=1, source_target_pairs={{0,2},{2,0},{4,6},{6,4},{1,3},{3,1},{5,7},{7,5},{8,10},{10,8},{12,... | collective-permute-start | bytes 2359304 | tf_op jit(solution)/shard_map/ppermute | solution.py:1126
  503.8 34.3 %collective-permute-start.69 = (bf16[256,1536]{1,0:T(8,128)(2,1)S(1)}, bf16[256,1536]{1,0:T(8,128)(2,1)S(1)}, u32[]{:S(2)}, u32[]{:S(2)}) collective-permute-start(bf16[256,1536]{1,0:T(8,128)(2,1)S(1)} %get-tuple-element.405), channel_id=1, source_target_pairs={{0,4},{2,6},{4,0},{6,2},{1,5},{3,7},{5,1},{7,3},{8,12},{10,14},{12... | collective-permute-start | bytes 2359304 | tf_op jit(solution)/shard_map/ppermute | solution.py:1126
  545.3 25.2 %collective-permute-start.70 = (bf16[768,1024]{1,0:T(8,128)(2,1)}, bf16[768,1024]{1,0:T(8,128)(2,1)}, u32[]{:S(2)}, u32[]{:S(2)}) collective-permute-start(bf16[768,1024]{1,0:T(8,128)(2,1)} %fusion.34), channel_id=1, source_target_pairs={{0,1},{1,0},{2,3},{3,2},{4,5},{5,4},{6,7},{7,6},{8,9},{9,8},{10,11... | collective-permute-start | bytes 4718600 | tf_op jit(solution)/shard_map/ppermute | solution.py:1105
  578.4 25.5 %all-to-all-start.2 = ((bf16[4,192,1024]{2,1,0:T(8,128)(2,1)}), bf16[4,192,1024]{2,1,0:T(8,128)(2,1)}, u32[]{:S(2)}, u32[]{:S(2)}) async-start(bf16[4,192,1024]{2,1,0:T(8,128)(2,1)} %bitcast.206), calls=%async_computation.2 | async-start | bytes 3145728 | tf_op jit(solution)/shard_map/all_to_all | solution.py:1561
  603.9 58.3 %all-to-all-start.3 = ((bf16[4,576,1024]{2,1,0:T(8,128)(2,1)}), bf16[4,576,1024]{2,1,0:T(8,128)(2,1)}, u32[]{:S(2)}, u32[]{:S(2)}) async-start(bf16[4,576,1024]{2,1,0:T(8,128)(2,1)} %bitcast.207), calls=%async_computation.5 | async-start | bytes 9437184 | tf_op jit(solution)/shard_map/all_to_all | solution.py:1562
  684.3 42.3 %collective-permute-start.72 = (bf16[3,512,1536]{2,1,0:T(8,128)(2,1)}, bf16[3,512,1536]{2,1,0:T(8,128)(2,1)}, u32[]{:S(2)}, u32[]{:S(2)}) collective-permute-start(bf16[3,512,1536]{2,1,0:T(8,128)(2,1)} %get-tuple-element.291), channel_id=1, source_target_pairs={{0,1},{1,0},{2,3},{3,2},{4,5},{5,4},{6,7},{7,6},{8,9},{9,8},{10,11... | collective-permute-start | bytes 14155784 | tf_op jit(solution)/shard_map/ppermute | solution.py:1105
  700.2 22.4 %all-to-all-start.5 = ((bf16[4,96,768]{2,1,0:T(8,128)(2,1)}), bf16[4,96,768]{2,1,0:T(8,128)(2,1)S(1)}, u32[]{:S(2)}, u32[]{:S(2)}) async-start(bf16[4,96,768]{2,1,0:T(8,128)(2,1)} %maximum_dynamic-update-slice_fusion), calls=%async_computation.7 | async-start | bytes 1179648 | tf_op jit(solution)/shard_map/all_to_all | solution.py:1609
  703.6 70.3 %reduce-scatter.14.cloned.1.call-start = ((), (), s32[]{:S(2)}) async-start(), calls=%async_computation.18 | async-start | bytes 2273280 | tf_op jit(solution)/shard_map/reduce_scatter | solution.py:1615
  733.2 50.8 %collective-permute-start.75 = (bf16[512,1536]{1,0:T(8,128)(2,1)}, bf16[512,1536]{1,0:T(8,128)(2,1)}, u32[]{:S(2)}, u32[]{:S(2)}) collective-permute-start(bf16[512,1536]{1,0:T(8,128)(2,1)} %pad_maximum_fusion.9), channel_id=1, source_target_pairs={{0,2},{2,0},{4,6},{6,4},{1,3},{3,1},{5,7},{7,5},{8,10},{10,8},{12,... | collective-permute-start | bytes 4718600 | tf_op jit(solution)/shard_map/ppermute | solution.py:1126
  736.4 47.5 %collective-permute-start.77 = (bf16[512,1536]{1,0:T(8,128)(2,1)}, bf16[512,1536]{1,0:T(8,128)(2,1)}, u32[]{:S(2)}, u32[]{:S(2)}) collective-permute-start(bf16[512,1536]{1,0:T(8,128)(2,1)} %pad_maximum_fusion.10), channel_id=1, source_target_pairs={{0,4},{2,6},{4,0},{6,2},{1,5},{3,7},{5,1},{7,3},{8,12},{10,14},{12... | collective-permute-start | bytes 4718600 | tf_op jit(solution)/shard_map/ppermute | solution.py:1126
  737.7 41.1 %collective-permute-start.76 = (bf16[48,2432]{1,0:T(8,128)(2,1)}, bf16[48,2432]{1,0:T(8,128)(2,1)}, u32[]{:S(2)}, u32[]{:S(2)}) collective-permute-start(bf16[48,2432]{1,0:T(8,128)(2,1)} %get-tuple-element.418), channel_id=1, source_target_pairs={{0,4},{2,6},{4,0},{6,2},{1,5},{3,7},{5,1},{7,3},{8,12},{10,14},{12... | collective-permute-start | bytes 700424 | tf_op jit(solution)/shard_map/ppermute | solution.py:1126
  739.4 39.5 %collective-permute-start.79 = (bf16[48,2432]{1,0:T(8,128)(2,1)}, bf16[48,2432]{1,0:T(8,128)(2,1)}, u32[]{:S(2)}, u32[]{:S(2)}) collective-permute-start(bf16[48,2432]{1,0:T(8,128)(2,1)} %get-tuple-element.417), channel_id=1, source_target_pairs={{0,2},{2,0},{4,6},{6,4},{1,3},{3,1},{5,7},{7,5},{8,10},{10,8},{12,... | collective-permute-start | bytes 700424 | tf_op jit(solution)/shard_map/ppermute | solution.py:1126
  743.3 30.7 %collective-permute-start.85 = (f32[16,2]{0,1:T(2,128)S(1)}, f32[16,2]{0,1:T(2,128)S(1)}, u32[]{:S(2)}, u32[]{:S(2)}) collective-permute-start(f32[16,2]{0,1:T(2,128)S(1)} %add.309), channel_id=1, source_target_pairs={{0,2},{2,0},{4,6},{6,4},{1,3},{3,1},{5,7},{7,5},{8,10},{10,8},{12,... | collective-permute-start | bytes 392 | tf_op jit(solution)/shard_map/ppermute | solution.py:1197
  777.5 20.7 %collective-permute-start.87 = (f32[16,2]{0,1:T(2,128)S(1)}, f32[16,2]{0,1:T(2,128)S(1)}, u32[]{:S(2)}, u32[]{:S(2)}) collective-permute-start(f32[16,2]{0,1:T(2,128)S(1)} %add.311), channel_id=1, source_target_pairs={{0,8},{8,0},{16,24},{24,16},{1,9},{9,1},{17,25},{25,17},{2,10},{10... | collective-permute-start | bytes 392 | tf_op jit(solution)/shard_map/ppermute | solution.py:1197
  782.5 22.1 %collective-permute-start.78 = (bf16[96,2432]{1,0:T(8,128)(2,1)}, bf16[96,2432]{1,0:T(8,128)(2,1)}, u32[]{:S(2)}, u32[]{:S(2)}) collective-permute-start(bf16[96,2432]{1,0:T(8,128)(2,1)} %pad_maximum_fusion.13), channel_id=1, source_target_pairs={{0,2},{2,0},{4,6},{6,4},{1,3},{3,1},{5,7},{7,5},{8,10},{10,8},{12,... | collective-permute-start | bytes 1400840 | tf_op jit(solution)/shard_map/ppermute | solution.py:1126
  (138 other events, 1796.6 us)
Sparse Core Ops, SparseCore 0:
  16.0 129.2 all-gather.4
  155.8 46.5 all-gather.8
  243.6 63.1 all-gather.6
  430.5 33.2 reduce-scatter.5
  466.0 59.2 reduce-scatter.7
  527.4 48.0 reduce-scatter.11
  577.8 91.1 reduce-scatter.9
  726.8 39.6 reduce-scatter.13

commit v4 on v3

--- a/solution.py
+++ b/solution.py
@@ -686,9 +686,9 @@
 
 
 def unpack_columns(parts, gate, up, gain):
-    chain, shard, both = parts.shape
-    own = both // 2
+    chain, shard = parts.shape[:2]
     whole = gate.shape[1]
+    own = whole // chain
     size = whole // (D // shard)
 
     def kernel(parts_ref, gate_ref, up_ref, gain_ref, gate_out, up_out, gain_out):
@@ -712,7 +712,7 @@
     )(parts, gate, up, gain)
 
 
-def unpack_weights(chips, heads, parts, context, key, value, query, rate, gain):
+def unpack_weights(chips, heads, start, parts, context, key, value, query, rate, gain):
     shard = key.shape[0]
 
     def kernel(parts_ref, context_ref, key_ref, value_ref, query_ref, rate_ref, gain_ref, *outs):
@@ -723,14 +723,15 @@
                 place = chip * 2 + core
                 for turn in range(heads):
                     head = head_of(core, chip, turn, chips, heads)
-                    rate_out[:, head : head + 1] = parts_ref[
-                        place, :, 3 * heads * HD + turn : 3 * heads * HD + turn + 1
-                    ].astype(f32)
+                    at = start + 3 * heads * HD + turn
+                    rate_out[:, head : head + 1] = parts_ref[place, :, at : at + 1].astype(f32)
                     columns = slice(head * HD, (head + 1) * HD)
                     for which, (weight, out) in enumerate(
                         ((key_ref, key_out), (value_ref, value_out), (query_ref, query_out))
                     ):
-                        grad = parts_ref[place, :, spot(heads, turn, which)].astype(f32)
+                        there = spot(heads, turn, which)
+                        there = slice(start + there.start, start + there.stop)
+                        grad = parts_ref[place, :, there].astype(f32)
                         total += jnp.sum(
                             grad * weight[:, columns].astype(f32), axis=1, keepdims=True
                         )
@@ -1014,7 +1015,7 @@
             jax.ShapeDtypeStruct((2, GROUP, D), bf16),
         ],
         input_output_aliases={count + 2 + at: at for at in range(len(old))},
-        compiler_params=pltpu.CompilerParams(vmem_limit_bytes=40 * 2**20),
+        compiler_params=pltpu.CompilerParams(vmem_limit_bytes=58 * 2**20),
         cost_estimate=pl.CostEstimate(
             flops=2 * GROUP * D * own * 12, bytes_accessed=20 * GROUP * D, transcendentals=2 * GROUP * own
         ),
@@ -1186,8 +1187,8 @@
 
 
 def sum_everywhere(value, marks):
-    steps = [("core", 1)]
-    for axis in ("chip", "dp"):
+    steps = []
+    for axis in ("dp", "core", "chip"):
         step = 1
         while step < lax.axis_size(axis):
             steps.append((axis, step))
@@ -1523,9 +1524,9 @@
     gate_up_scattered = lax.psum_scatter(grad_gate_up_w, "dp", scatter_dimension=0, tiled=True)
 
     grad_attended = pair_rows(grad_middle.astype(bf16))
+    grad_mixed = matmul(w_output, grad_attended, 1, 1, bf16)
     grad_output_w = matmul(mixed, grad_attended, 1, 0, bf16)
     output_part = lax.psum_scatter(grad_output_w, "dp", scatter_dimension=0, tiled=True)
-    grad_mixed = matmul(w_output, grad_attended, 1, 1, bf16)
     events = ()
     if chips == 4:
         from_corner = halves(after(out_corner, grad_normed_two), 1, 2)
@@ -1542,15 +1543,11 @@
         id_col,
         mixed,
         total,
-        after(grad_mixed, *events),
+        after(grad_mixed, grad_output_w, *events),
     )
     grad_side = grad_side.astype(bf16)
     if chips == 4:
         grad_far, out_sent, out_last = together(grad_far, out_sent, halves(out_last, 1, 2))
-        out_sum = all_parts(out_own, out_sent, out_last)
-    else:
-        out_sum = chip_sums(outs)
-    result = (middle + out_sum).astype(bf16)
 
     def half_rows(which):
         return lax.dynamic_slice(w_pair, (which * half, 0), (half, 2 * half))
@@ -1558,17 +1555,17 @@
     pull_other = core_swap(matmul(half_rows(1 - core), grad_far, 1, 0, bf16))
     pull = (matmul(half_rows(core), grad_far, 1, 0) + pull_other.astype(f32)).astype(bf16)
     pull = pull.reshape(heads, chips, HD, width).swapaxes(0, 1).reshape(chips, rows, width)
-    pull = after(lax.all_to_all(pull, "chip", 0, 0, tiled=True), result)
+    ready = pull
+    pull = lax.all_to_all(pull, "chip", 0, 0, tiled=True)
     grad_part = lax.all_to_all(
         after(grad_part.reshape(chips, 3 * rows, width), pull), "chip", 0, 0, tiled=True
     )
-    grad_context_w = context_product(context, grad_far, persist, grad_side, w_pair)
+    grad_context_w = context_product(
+        context, after(grad_far, ready), persist, grad_side, w_pair
+    )
+    grad_context_w, pull = together(grad_context_w, pull)
     context_part = lax.psum_scatter(grad_context_w, "dp", scatter_dimension=0, tiled=True)
     context_part = context_part.reshape(chips, 2 * shard, 2 * half + 128)
-    output_part = output_part.reshape(chips, shard, 2, half).swapaxes(1, 2)
-    context_part = jnp.concatenate(
-        [context_part, output_part.reshape(chips, 2 * shard, half)], axis=2
-    )
     grads, grad_first, grad_second, grad_scalars = memory_backward(
         flags,
         main,
@@ -1580,39 +1577,38 @@
         saved,
         after(pull, down_part, gate_up_scattered, grad_context_w),
     )
-    grads, grad_part = together(grads, grad_part)
-    gate_up_part = lax.all_to_all(
-        after(gate_up_scattered, grad_part).reshape(chain, shard, 2 * ff_own),
-        ("chip", "core"),
-        0,
-        0,
-        tiled=True,
-    )
+    if chips == 4:
+        out_sum = all_parts(after(out_own, grads), out_sent, out_last)
+    else:
+        out_sum = chip_sums(outs)
+    result = (middle + out_sum).astype(bf16)
+    grads, grad_part, result = together(grads, grad_part, result)
     grad_mem = jnp.concatenate([grad_first, grad_second], axis=1).astype(bf16)
     corner_own, corner_other = back_blocks(chip_index, chips - 1, 1, grads, grad_part, w_flat)
+    corner_other = core_swap(corner_other)
     side_own, side_other = back_blocks(
-        chip_index, 0, chips - 1, grads, after(grad_part, corner_own), w_flat
-    )
-    side_own, corner_other, gate_up_part = together(
-        side_own, core_swap(corner_other), gate_up_part
+        chip_index, 0, chips - 1, grads, after(grad_part, corner_other), w_flat
     )
     corner_low = (corner_own[0].astype(f32) + corner_other[0].astype(f32)).astype(bf16)
     side_other = core_swap(side_other)
     grad_heads_w = merge_blocks(
         chip_index, groups, grads, after(grad_part, corner_low, side_own), normed_all
     )
+    if chips == 4:
+        grad_heads_w, side_other, from_corner = together(
+            grad_heads_w, side_other, halves(corner_low, 1, 2)
+        )
+    heads_sum = lax.psum_scatter(grad_heads_w, "dp", scatter_dimension=0)
     if near:
         spread = jnp.zeros((groups, 2 * shard, 2 * MH), bf16)
         spread = lax.dynamic_update_slice_in_dim(
-            spread, grad_mem.reshape(heads, 2 * shard, 2 * MH), core * heads, 0
-        )
-        mem_line = lax.all_to_all(after(spread, gate_up_part), "dp", 0, 0, tiled=True)
-        grad_heads_w, mem_line = together(grad_heads_w, mem_line)
-    if chips == 4:
-        grad_heads_w, side_other, from_corner = together(
-            grad_heads_w, side_other, halves(corner_low, 1, 2)
-        )
-    heads_sum = lax.psum_scatter(grad_heads_w, "dp", scatter_dimension=0)
+            spread, after(grad_mem, grad_heads_w).reshape(heads, 2 * shard, 2 * MH), core * heads, 0
+        )
+        mem_line = lax.psum_scatter(
+            spread.reshape(groups * 2 * shard, 2 * MH), "dp", scatter_dimension=0, tiled=True
+        )
+    else:
+        mem_line = grad_mem
     grad_normeds = [
         side_own[step].astype(f32) + side_other[step].astype(f32) for step in range(chips - 1)
     ]
@@ -1630,28 +1626,41 @@
         marks = (corner_low, first_sum)
     else:
         marks = (corner_low, side_own)
+    heads_sum = heads_sum.T
     heads_part = lax.all_to_all(
-        heads_sum.T.reshape(chain, shard, all_rows), ("chip", "core"), 0, 0, tiled=True
+        jnp.concatenate(
+            [
+                gate_up_scattered.reshape(chain, shard, 2 * ff_own),
+                heads_sum.reshape(chain, shard, all_rows),
+            ],
+            axis=2,
+        ),
+        ("chip", "core"),
+        0,
+        0,
+        tiled=True,
+    )
+    output_part = output_part.reshape(chips, shard, 2, half).swapaxes(1, 2)
+    context_part = jnp.concatenate(
+        [context_part, output_part.reshape(chips, 2 * shard, half)], axis=2
     )
     context_parts = [
-        lax.dynamic_index_in_dim(after(context_part, *marks), chip ^ step, 0, keepdims=False)
+        lax.dynamic_index_in_dim(after(context_part, grad_heads_w), chip ^ step, 0, keepdims=False)
         for step in range(chips)
     ]
     if chips == 4:
         context_first, context_second = corner_sums(
             context_parts[3].astype(bf16), context_parts, heads_sum
         )
-        grad_normed = side_sums(grad_normeds[0], first_sum, second_sum, context_first)
-        context_part = side_sums(
-            context_parts[0], context_first, context_second, grad_normed
-        ).astype(bf16)
+        grad_normed = side_sums(grad_normeds[0], first_sum, second_sum, heads_sum)
+        context_part = side_sums(context_parts[0], context_first, context_second).astype(bf16)
     else:
         grad_normed = chip_sums(grad_normeds)
         context_part = chip_sums(context_parts).astype(bf16)
     grad_tokens_one = norm_back(grad_normed, tokens_wide, inverse_rms(tokens_wide), gain_one)
     grad_inputs = (grad_middle + grad_tokens_one).astype(bf16)
-    marks = (*marks, heads_sum, grad_normed, heads_part)
-    heads_part = after(heads_part, grad_inputs)
+    marks = (corner_own, side_own, grad_heads_w, grad_inputs, grad_inputs)
+    grad_inputs, heads_part = together(grad_inputs, heads_part)
 
     def own_rows(part):
         mine = lax.dynamic_slice_in_dim(part, core * shard, shard, 0)
@@ -1668,6 +1677,7 @@
         unpack_weights(
             chips,
             heads,
+            2 * ff_own,
             heads_part,
             by_side,
             key_weight,
@@ -1678,12 +1688,10 @@
         )
     )
     gate_part, up_part, gain_two_part = unpack_columns(
-        gate_up_part, gate_weight, up_weight, ffn_gain[:, None]
+        heads_part, gate_weight, up_weight, ffn_gain[:, None]
     )
     if near:
-        mine, other = own_rows(
-            jnp.sum(after(mem_line, *marks).astype(f32), axis=0).astype(bf16)
-        )
+        mine, other = own_rows(after(mem_line, heads_sum))
         mem_part = mine.astype(f32) + other.astype(f32)
     else:
         spread = jnp.zeros((heads, chips, HD, 2 * MH), bf16)

time: 847 us -> 809 us (0.955)
  waiting for transfers between devices: 182 us -> 161 us
  local copies, waits for them, and re-layouts: 93.7 us -> 80.8 us
  Pallas kernels: 301 us -> 312 us
  starting transfers between devices: 117 us -> 107 us
    all_to_all x4 -> x2, waiting for transfers between devices: 19.7 us -> 0.01 us  [the longest x1 0.01 us: on_device(): pull = lax.all_to_all(pull, 'chip', 0, 0, tiled=True)]
    ppermute x5, waiting for transfers between devices: 29.9 us -> 14.7 us  [sum_everywhere(): other = lax.ppermute(value, axis, pairs)]
    unnamed x200 -> x190, local copies, waits for them, and re-layouts: 41.8 us -> 30.6 us
    pallas_call x4, Pallas kernels: 63.8 us -> 73.4 us  [ffn_chunk(): pl.pallas_call(kernel, grid=(2,), in_specs=[pl.BlockSpec(piece.shape, lam...]
    all_to_all x4 -> x2, starting transfers between devices: 18.2 us -> 10.3 us  [the longest x1 5.88 us: on_device(): pull = lax.all_to_all(pull, 'chip', 0, 0, tiled=True)]
  transfers between devices with their start and end apart: 104 -> 103, of which waited for: 31 -> 33; matrix products, arithmetic and copies ran while one was open for 21% -> 21% of each run, Pallas kernels for 35% -> 37%
where the time goes in v4:
time: 809 us; the launch traced here: 804 us
  Pallas kernels  312 us (39%)
  waiting for transfers between devices  161 us (20%)
  starting transfers between devices  107 us (13%)
  local copies, waits for them, and re-layouts  80.8 us (10%)
  other arithmetic  79.6 us (10%)
  matrix products  47.1 us (6%)
  between operations  15.8 us (2%)
    ppermute x40, waiting for transfers between devices, chip_swap(): lax.ppermute(value, 'chip', [(index, index ^ step) for index in range(cou...  84.9 us
    pallas_call x4, Pallas kernels, ffn_chunk(): pl.pallas_call(kernel, grid=(2,), in_specs=[pl.BlockSpec(piece.shape, lam...  73.4 us
    dot_general x9, matrix products, matmul(): lax.dot_general(left, right, (((left_dim,), (right_dim,)), ((), ())), pre...  47.1 us
    pallas_call x1, Pallas kernels, memory_backward(): pl.pallas_call(lambda *refs: memory_backward_kernel(heads, blocks, *refs)...  45.6 us
    ppermute x40, starting transfers between devices, chip_swap(): lax.ppermute(value, 'chip', [(index, index ^ step) for index in range(cou...  37.9 us
    pallas_call x1, Pallas kernels, attention_backward(): pl.pallas_call(lambda *refs: attention_backward_kernel(scale, *refs), gri...  33.1 us
    pallas_call x2, Pallas kernels, tokens_product(): pl.pallas_call(kernel, grid=(steps,), in_specs=[pl.BlockSpec((size, rows)...  32.7 us
    unnamed x190, local copies, waits for them, and re-layouts  30.6 us
  transfers between devices with their start and end apart: 103, of which 33 were waited for; matrix products, arithmetic and copies ran while one was open for 21% of the time, Pallas kernels for 37%

profile of v4, /device:TPU:2, one launch (start us, length us, event | category | flops | bytes accessed | tf_op | source)
XLA Modules:
  0.0 803.8 jit_solution(3880015284333678927)
XLA Ops:
  18.0 4.4 collective-permute-start.20
  23.7 46.0 %collective-permute-done.1.refs_2_ = bf16[512,1536]{1,0:T(8,128)(2,1)S(1)} collective-permute-done((bf16[512,1536]{1,0:T(8,128)(2,1)S(1)}, bf16[512,1536]{1,0:T(8,128)(2,1)S(1)}, u32[]{:S(2)}, u32[]{:S(2)}) %collective-permute-start.1) | collective-permute-done | bytes 1572896 | tf_op jit(solution)/shard_map/ppermute | solution.py:1127
  73.4 12.9 %collective-permute-done.5 = bf16[256,1536]{1,0:T(8,128)(2,1)S(1)} collective-permute-done((bf16[256,1536]{1,0:T(8,128)(2,1)S(1)}, bf16[256,1536]{1,0:T(8,128)(2,1)S(1)}, u32[]{:S(2)}, u32[]{:S(2)}) %collective-permute-start.5) | collective-permute-done | bytes 786464 | tf_op jit(solution)/shard_map/ppermute | solution.py:1127
  86.3 5.9 collective-permute-done.6
  97.3 5.1 collective-permute-done.12
  102.3 6.4 collective-permute-start.13
  111.9 3.0 collective-permute-done.13
  114.9 10.0 %collective-permute-start.14 = (bf16[96,768]{1,0:T(8,128)(2,1)S(1)}, bf16[96,768]{1,0:T(8,128)(2,1)S(1)}, u32[]{:S(2)}, u32[]{:S(2)}) collective-permute-start(bf16[96,768]{1,0:T(8,128)(2,1)S(1)} %collective-permute-done.13), channel_id=1, source_target_pairs={{0,8},{8,16},{16,24},{1,9},{9,17},{17,25},{2,10},{10,18},{18,26},{... | collective-permute-start | bytes 442376 | tf_op jit(solution)/shard_map/ppermute | solution.py:1180
  129.2 8.5 %all-to-all-start = ((bf16[8,48,1024]{2,1,0:T(8,128)(2,1)}), bf16[8,48,1024]{2,1,0:T(8,128)(2,1)S(1)}, u32[]{:S(2)}, u32[]{:S(2)}) async-start(bf16[8,48,1024]{2,1,0:T(8,128)(2,1)} %shard_map.307), calls=%async_computation | async-start | bytes 1572864 | tf_op jit(solution)/shard_map/all_to_all | solution.py:1306
  138.1 2.5 collective-permute-done.17
  141.0 5.1 all-gather.5.cloned.1.call-done.low_ref.query_ref.tail_ref.weight_ref
  146.2 8.4 %shard_map.306 = (bf16[592,1536]{1,0:T(8,128)(2,1)}, f32[8,1536]{1,0:T(8,128)}) custom-call(s32[1]{0:T(128)} %bitcast.3.chip_ref, bf16[1536,2432]{1,0:T(8,128)(2,1)} %all-gather.5.cloned.1.call-done.low_ref.query_ref.tail_ref.weight_ref, bf16[1536,2432]{1,0:T(8,128)(2,1)} %all-gather.5.cloned.1.call-done.low_ref.query_ref.tail_ref.weight_ref, ...), custom_call_target="tpu_custom_call" | custom-call | tf_op jit(solution)/shard_map/pallas_call | solution.py:782
  161.6 19.4 %shard_map.308 = (bf16[4096,1536]{1,0:T(8,128)(2,1)}, bf16[592,4096]{1,0:T(8,128)(2,1)}) custom-call(bf16[512,1536]{1,0:T(8,128)(2,1)S(1)} %bitcast.198, bf16[512,1536]{1,0:T(8,128)(2,1)} %collective-permute-done.refs_1_, bf16[512,1536]{1,0:T(8,128)(2,1)} %copy-done.72, bf16[512,1536]{1,0:T(8,128)(2,1)} %collective-permute-done.2.refs_3_, ...), custom_call_target="tpu_custom_call" | custom-call | flops 14898167808 | bytes 31834112 | tf_op jit(solution)/shard_map/pallas_call | solution.py:821
  183.1 23.3 %shard_map.309 = (bf16[4,192,1024]{2,1,0:T(8,128)(2,1)S(1)}, f32[8,4,192,384]{3,2,1,0:T(8,128)}) custom-call(s32[5,8]{1,0:T(8,128)S(1)} %stack.74.refs_0_, bf16[592,4096]{1,0:T(8,128)(2,1)} %get-tuple-element.173.refs_1_, f32[8,1,512]{2,1,0:T(1,128)S(1)} %get-tuple-element.451.refs_2_, f32[8,1,512]{2,1,0:T(1,128)S(1)} %get-tuple-element.450.refs_3_, ...), custom_call_target="tpu_custom_call" | custom-call | flops 16911433728 | bytes 14155776 | tf_op jit(solution)/shard_map/pallas_call | solution.py:148
  211.7 5.7 all-to-all-start.1
  217.4 13.0 %fusion.2.refs_1_.refs_2_ = bf16[2304,1024]{1,0:T(8,128)(2,1)} fusion(bf16[1536,2432]{1,0:T(8,128)(2,1)} %all-gather.5.cloned.1.call-done.low_ref.query_ref.tail_ref.weight_ref, bf16[4096,1536]{1,0:T(8,128)(2,1)} %get-tuple-element.181.normed_ref), kind=kOutput, calls=%fused_computation.2 | convolution fusion | flops 7250116608 | bytes 14942208 | tf_op jit(solution)/shard_map/dot_general | solution.py:1100
  232.6 9.0 %all-to-all-done.1 = bf16[4,192,1024]{2,1,0:T(8,128)(2,1)} async-done(((bf16[4,192,1024]{2,1,0:T(8,128)(2,1)}), bf16[4,192,1024]{2,1,0:T(8,128)(2,1)}, u32[]{:S(2)}, u32[]{:S(2)}) %all-to-all-start.1) | async-done | bytes 1572896 | tf_op jit(solution)/shard_map/all_to_all | solution.py:1414
  241.6 2.8 copy.103
  249.7 4.4 maximum_select_fusion.context_ref
  256.1 6.6 fusion.9.refs_3_
  262.7 21.7 %shard_map.310 = (bf16[768,1024]{1,0:T(8,128)(2,1)S(1)}, f32[8,1,1024]{2,1,0:T(1,128)S(1)}) custom-call(s32[1]{0:T(128)} %bitcast.21.refs_0_, bf16[2304,1024]{1,0:T(8,128)(2,1)} %fusion.2.refs_1_.refs_2_, bf16[2304,1024]{1,0:T(8,128)(2,1)} %fusion.2.refs_1_.refs_2_, bf16[1536,1024]{1,0:T(8,128)(2,1)} %fusion.9.refs_3_, bf16[1536,64]{1,0:T(8,128)(2,1)S(1)} %copy-done.25, ...), custom_call_target="tpu_custom_call" | custom-call | flops 13690208256 | bytes 9437184 | tf_op jit(solution)/shard_map/pallas_call | solution.py:500
  288.8 2.9 collective-permute-done.28
  302.8 5.8 all-gather.7.cloned.1.call-done.refs_4_.refs_8_
  308.6 18.3 %shard_map.311 = (bf16[4096,1536]{1,0:T(8,128)(2,1)}, bf16[4096,1536]{1,0:T(8,128)(2,1)}, bf16[4096,512]{1,0:T(8,128)(2,1)}, bf16[4096,1024]{1,0:T(8,128)(2,1)},...) custom-call(bf16[512,1536]{1,0:T(8,128)(2,1)} %copy-done.32, ...), custom_call_target="tpu_custom_call" | custom-call | flops 9663676416 | bytes 15728640 | tf_op jit(solution)/shard_map/pallas_call | solution.py:990
  331.3 18.3 %shard_map.312 = (bf16[4096,1536]{1,0:T(8,128)(2,1)}, bf16[4096,1536]{1,0:T(8,128)(2,1)}, bf16[4096,512]{1,0:T(8,128)(2,1)}, bf16[4096,1024]{1,0:T(8,128)(2,1)},...) custom-call(bf16[256,1536]{1,0:T(8,128)(2,1)} %collective-permute-do, ...), custom_call_target="tpu_custom_call", output_to_operand_aliasing={{0}: (10, {}), {1}: (11, {}), {2}: (12, {}), {3}: (13, {})} | custom-call | flops 9663676416 | bytes 15728640 | tf_op jit(solution)/shard_map/pallas_call | solution.py:990
  354.3 18.5 %shard_map.313 = (bf16[4096,1536]{1,0:T(8,128)(2,1)}, bf16[4096,1536]{1,0:T(8,128)(2,1)}, bf16[4096,512]{1,0:T(8,128)(2,1)}, bf16[4096,1024]{1,0:T(8,128)(2,1)},...) custom-call(bf16[256,1536]{1,0:T(8,128)(2,1)} %collective-permute-do, ...), custom_call_target="tpu_custom_call", output_to_operand_aliasing={{0}: (10, {}), {1}: (11, {}), {2}: (12, {}), {3}: (13, {})} | custom-call | flops 9663676416 | bytes 15728640 | tf_op jit(solution)/shard_map/pallas_call | solution.py:990
  377.8 18.3 %shard_map.314 = (bf16[4096,1536]{1,0:T(8,128)(2,1)}, bf16[4096,1536]{1,0:T(8,128)(2,1)}, bf16[4096,512]{1,0:T(8,128)(2,1)}, bf16[4096,1024]{1,0:T(8,128)(2,1)},...) custom-call(bf16[256,1536]{1,0:T(8,128)(2,1)} %collective-permute-do, ...), custom_call_target="tpu_custom_call", output_to_operand_aliasing={{0}: (10, {}), {1}: (11, {}), {2}: (12, {}), {3}: (13, {})} | custom-call | flops 9663676416 | bytes 15728640 | tf_op jit(solution)/shard_map/pallas_call | solution.py:990
  407.1 12.0 %shard_map.316 = bf16[512,1536]{1,0:T(8,128)(2,1)} custom-call(bf16[4096,512]{1,0:T(8,128)(2,1)} %get-tuple-element.241.left_ref, bf16[4096,1536]{1,0:T(8,128)(2,1)} %get-tuple-element.242.right_ref), custom_call_target="tpu_custom_call" | custom-call | flops 6442450944 | bytes 16777216 | tf_op jit(solution)/shard_map/pallas_call | solution.py:1080
  419.1 5.4 collective-permute-done.55
  425.9 4.1 convert_add_fusion.8
  435.4 20.7 %shard_map.315 = bf16[1536,1024]{1,0:T(8,128)(2,1)} custom-call(bf16[4096,1536]{1,0:T(8,128)(2,1)} %get-tuple-element.236.left_ref, bf16[4096,1024]{1,0:T(8,128)(2,1)} %get-tuple-element.237.right_ref), custom_call_target="tpu_custom_call" | custom-call | flops 12884901888 | bytes 20971520 | tf_op jit(solution)/shard_map/pallas_call | solution.py:1080
  456.1 3.2 slice_bitcast_fusion.5
  465.6 2.5 fusion.74
  478.3 4.3 convolution_convert_fusion
  482.6 6.4 fusion.38.refs_9_
  500.2 33.1 %shard_map.317 = (bf16[2304,1024]{1,0:T(8,128)(2,1)}, bf16[1536,1024]{1,0:T(8,128)(2,1)}, f32[1536,64]{1,0:T(8,128)S(1)}) custom-call(s32[1]{0:T(128)} %bitcast.21.refs_0_, bf16[2304,1024]{1,0:T(8,128)(2,1)} %fusion.2.refs_1_.refs_2_, bf16[2304,1024]{1,0:T(8,128)(2,1)} %fusion.2.refs_1_.refs_2_, bf16[1536,1024]{1,0:T(8,128)(2,1)} %fusion.9.refs_3_, ...), custom_call_target="tpu_custom_call" | custom-call | flops 34225520640 | bytes 22020096 | tf_op jit(solution)/shard_map/pallas_call | solution.py:599
  534.5 6.5 fusion.35
  544.9 4.8 add_convert_fusion.1
  551.0 5.9 all-to-all-start.2
  558.7 4.2 convert_add_fusion.1
  564.9 3.1 copy-done
  570.9 8.7 %shard_map.318 = bf16[1536,1664]{1,0:T(8,128)(2,1)S(1)} custom-call(bf16[1536,1024]{1,0:T(8,128)(2,1)S(1)} %copy-done.6, bf16[1536,1024]{1,0:T(8,128)(2,1)S(1)} %copy-done.9, bf16[1536,64]{1,0:T(8,128)(2,1)S(1)} %slice.428.persist_ref, bf16[1536,64]{1,0:T(8,128)(2,1)S(1)} %copy-done.11, bf16[1536,2432]{1,0:T(8,128)(2,1)S(1)} %copy-done), custom_call_target="tpu_custom_call" | custom-call | flops 4831838208 | bytes 18874368 | tf_op jit(solution)/shard_map/pallas_call | solution.py:1037
  581.8 5.0 all-to-all-start.3
  587.7 45.6 %shard_map.319 = (bf16[592,4096]{1,0:T(8,128)(2,1)}, f32[192,384]{1,0:T(8,128)}, f32[192,384]{1,0:T(8,128)}, f32[8,384]{1,0:T(8,128)}) custom-call(s32[5,8]{1,0:T(8,128)} %copy-done.20, bf16[592,4096]{1,0:T(8,128)(2,1)} %get-tuple-element.173.refs_1_, f32[8,1,512]{2,1,0:T(1,128)} %copy-done.19, f32[8,1,512]{2,1,0:T(1,128)} %copy-done.18, ...), custom_call_target="tpu_custom_call" | custom-call | flops 45902462976 | bytes 18874368 | tf_op jit(solution)/shard_map/pallas_call | solution.py:389
  636.8 3.1 all-to-all-done.3.part_ref
  642.2 4.5 shard_map.320
  646.8 3.4 collective-permute-done.71
  650.2 12.3 %shard_map.321 = (bf16[3,512,1536]{2,1,0:T(8,128)(2,1)S(1)}, bf16[3,512,1536]{2,1,0:T(8,128)(2,1)}) custom-call(s32[1]{0:T(128)} %bitcast.3.chip_ref, bf16[592,4096]{1,0:T(8,128)(2,1)S(1)} %copy-done.24, bf16[4,576,1024]{2,1,0:T(8,128)(2,1)} %all-to-all-done.3.part_ref, bf16[592,1536]{1,0:T(8,128)(2,1)S(1)} %copy-done.22), custom_call_target="tpu_custom_call" | custom-call | flops 11173625856 | bytes 16711680 | tf_op jit(solution)/shard_map/pallas_call | solution.py:927
  666.8 13.9 %shard_map.322 = bf16[4,592,384]{2,1,0:T(8,128)(2,1)} custom-call(s32[1]{0:T(128)} %bitcast.3.chip_ref, bf16[592,4096]{1,0:T(8,128)(2,1)} %get-tuple-element.279.grads_ref, bf16[4,576,1024]{2,1,0:T(8,128)(2,1)} %all-to-all-done.3.part_ref, bf16[4096,1536]{1,0:T(8,128)(2,1)} %get-tuple-element.181.normed_ref), custom_call_target="tpu_custom_call" | custom-call | flops 14898167808 | bytes 22282240 | tf_op jit(solution)/shard_map/pallas_call | solution.py:885
  680.6 3.6 collective-permute-done.73
  684.7 4.0 convert_add_fusion.10
  699.6 2.7 collective-permute-done.84
  703.1 2.7 reshape.421
  717.8 4.9 reduce-scatter.11.cloned.1.call-done
  724.7 3.1 collective-permute-done.76
  727.8 3.2 collective-permute-done.75
  733.5 4.4 all-to-all-start.4
  744.1 3.9 fusion.14
  748.0 4.5 fusion.18
  753.6 10.8 %collective-permute-done.88 = f32[16,2]{0,1:T(2,128)S(1)} collective-permute-done((f32[16,2]{0,1:T(2,128)S(1)}, f32[16,2]{0,1:T(2,128)S(1)}, u32[]{:S(2)}, u32[]{:S(2)}) %collective-permute-start.88) | collective-permute-done | bytes 160 | tf_op jit(solution)/shard_map/ppermute | solution.py:1198
  767.5 2.5 collective-permute-start.82
  770.6 8.3 %collective-permute-done.82 = bf16[48,1536]{1,0:T(8,128)(2,1)S(1)} collective-permute-done((bf16[48,1536]{1,0:T(8,128)(2,1)S(1)}, bf16[48,1536]{1,0:T(8,128)(2,1)S(1)}, u32[]{:S(2)}, u32[]{:S(2)}) %collective-permute-start.82) | collective-permute-done | bytes 147488 | tf_op jit(solution)/shard_map/ppermute | solution.py:1714
  782.1 8.0 %shard_map.323 = (f32[48,1536]{1,0:T(8,128)}, f32[48,1536]{1,0:T(8,128)}, f32[48,1536]{1,0:T(8,128)}, f32[48,16]{1,0:T(8,128)}, f32[48,1]{1,0:T(8,128)}) custom-call(bf16[8,48,1616]{2,1,0:T(8,128)(2,1)} %copy-done.37, bf16[2,48,1664]{2,1,0:T(8,128)(2,1)} %maximum_select_fusion.2.context_ref, bf16[48,1536]{1,0:T(8,128)(2,1)} %key_ref.3, ...), custom_call_target="tpu_custom_call" | custom-call | tf_op jit(solution)/shard_map/pallas_call | solution.py:746
  791.5 2.7 shard_map.324
  (514 shorter events, 199.4 us)
Async XLA Ops:
  7.2 139.0 %all-gather.5.cloned.1.call-start = ((), (), s32[]{:S(2)}) async-start(), calls=%async_computation.11 | async-start | bytes 7938048 | tf_op jit(solution)/shard_map/all_gather | solution.py:1110
  15.9 53.8 %collective-permute-start.1 = (bf16[512,1536]{1,0:T(8,128)(2,1)S(1)}, bf16[512,1536]{1,0:T(8,128)(2,1)S(1)}, u32[]{:S(2)}, u32[]{:S(2)}) collective-permute-start(bf16[512,1536]{1,0:T(8,128)(2,1)S(1)} %bitcast.195), channel_id=1, source_target_pairs={{0,2},{2,0},{4,6},{6,4},{1,3},{3,1},{5,7},{7,5},{8,10},{10,8},{12,... | collective-permute-start | bytes 4718600 | tf_op jit(solution)/shard_map/ppermute | solution.py:1127
  16.0 55.5 %collective-permute-start.3 = (bf16[512,1536]{1,0:T(8,128)(2,1)S(1)}, bf16[512,1536]{1,0:T(8,128)(2,1)}, u32[]{:S(2)}, u32[]{:S(2)}) collective-permute-start(bf16[512,1536]{1,0:T(8,128)(2,1)S(1)} %bitcast.196), channel_id=1, source_target_pairs={{0,4},{2,6},{4,0},{6,2},{1,5},{3,7},{5,1},{7,3},{8,12},{10,14},{12... | collective-permute-start | bytes 4718600 | tf_op jit(solution)/shard_map/ppermute | solution.py:1127
  18.0 142.2 %collective-permute-start = (bf16[512,1536]{1,0:T(8,128)(2,1)S(1)}, bf16[512,1536]{1,0:T(8,128)(2,1)}, u32[]{:S(2)}, u32[]{:S(2)}) collective-permute-start(bf16[512,1536]{1,0:T(8,128)(2,1)S(1)} %bitcast.197), channel_id=1, source_target_pairs={{0,1},{1,0},{2,3},{3,2},{4,5},{5,4},{6,7},{7,6},{8,9},{9,8},{10,11... | collective-permute-start | bytes 4718600 | tf_op jit(solution)/shard_map/ppermute | solution.py:1106
  18.0 136.5 %collective-permute-start.20 = (bf16[48,1536]{1,0:T(8,128)(2,1)}, bf16[48,1536]{1,0:T(8,128)(2,1)}, u32[]{:S(2)}, u32[]{:S(2)}) collective-permute-start(bf16[48,1536]{1,0:T(8,128)(2,1)} %param.24), channel_id=1, source_target_pairs={{0,0},{1,2},{8,4},{9,6},{2,8},{3,10},{10,12},{11,14},{4,16},{5,18}... | collective-permute-start | bytes 442376 | tf_op jit(solution)/shard_map/ppermute | solution.py:1334
  114.9 22.9 %collective-permute-start.14 = (bf16[96,768]{1,0:T(8,128)(2,1)S(1)}, bf16[96,768]{1,0:T(8,128)(2,1)S(1)}, u32[]{:S(2)}, u32[]{:S(2)}) collective-permute-start(bf16[96,768]{1,0:T(8,128)(2,1)S(1)} %collective-permute-done.13), channel_id=1, source_target_pairs={{0,8},{8,16},{16,24},{1,9},{9,17},{17,25},{2,10},{10,18},{18,26},{... | collective-permute-start | bytes 442376 | tf_op jit(solution)/shard_map/ppermute | solution.py:1180
  126.9 34.7 %collective-permute-start.2 = (bf16[512,1536]{1,0:T(8,128)(2,1)}, bf16[512,1536]{1,0:T(8,128)(2,1)}, u32[]{:S(2)}, u32[]{:S(2)}) collective-permute-start(bf16[512,1536]{1,0:T(8,128)(2,1)} %copy-done.72), channel_id=1, source_target_pairs={{0,1},{1,0},{2,3},{3,2},{4,5},{5,4},{6,7},{7,6},{8,9},{9,8},{10,11... | collective-permute-start | bytes 4718600 | tf_op jit(solution)/shard_map/ppermute | solution.py:1106
  129.2 25.4 %all-to-all-start = ((bf16[8,48,1024]{2,1,0:T(8,128)(2,1)}), bf16[8,48,1024]{2,1,0:T(8,128)(2,1)S(1)}, u32[]{:S(2)}, u32[]{:S(2)}) async-start(bf16[8,48,1024]{2,1,0:T(8,128)(2,1)} %shard_map.307), calls=%async_computation | async-start | bytes 1572864 | tf_op jit(solution)/shard_map/all_to_all | solution.py:1306
  137.7 69.9 %all-gather.9.cloned.1.call-start = ((), (), s32[]{:S(2)}) async-start(), calls=%async_computation.19 | async-start | bytes 2703360 | tf_op jit(solution)/shard_map/all_gather | solution.py:1336
  137.9 23.7 %collective-permute-start.4 = (bf16[512,1536]{1,0:T(8,128)(2,1)}, bf16[512,1536]{1,0:T(8,128)(2,1)}, u32[]{:S(2)}, u32[]{:S(2)}) collective-permute-start(bf16[512,1536]{1,0:T(8,128)(2,1)} %collective-permute-done.3.refs_4_), channel_id=1, source_target_pairs={{0,1},{1,0},{2,3},{3,2},{4,5},{5,4},{6,7},{7,6},{8,9},{9,8},{10,11... | collective-permute-start | bytes 4718600 | tf_op jit(solution)/shard_map/ppermute | solution.py:1106
  140.6 21.0 %collective-permute-start.7 = (bf16[512,1536]{1,0:T(8,128)(2,1)}, bf16[512,1536]{1,0:T(8,128)(2,1)}, u32[]{:S(2)}, u32[]{:S(2)}) collective-permute-start(bf16[512,1536]{1,0:T(8,128)(2,1)} %copy-done.73), channel_id=1, source_target_pairs={{0,1},{1,0},{2,3},{3,2},{4,5},{5,4},{6,7},{7,6},{8,9},{9,8},{10,11... | collective-permute-start | bytes 4718600 | tf_op jit(solution)/shard_map/ppermute | solution.py:1106
  158.0 23.0 %collective-permute-start.9 = (bf16[256,1536]{1,0:T(8,128)(2,1)S(1)}, bf16[256,1536]{1,0:T(8,128)(2,1)}, u32[]{:S(2)}, u32[]{:S(2)}) collective-permute-start(bf16[256,1536]{1,0:T(8,128)(2,1)S(1)} %get-tuple-element.432), channel_id=1, source_target_pairs={{0,2},{2,0},{4,6},{6,4},{1,3},{3,1},{5,7},{7,5},{8,10},{10,8},{12,... | collective-permute-start | bytes 2359304 | tf_op jit(solution)/shard_map/ppermute | solution.py:1127
  160.2 20.8 %collective-permute-start.10 = (bf16[256,1536]{1,0:T(8,128)(2,1)S(1)}, bf16[256,1536]{1,0:T(8,128)(2,1)}, u32[]{:S(2)}, u32[]{:S(2)}) collective-permute-start(bf16[256,1536]{1,0:T(8,128)(2,1)S(1)} %get-tuple-element.431), channel_id=1, source_target_pairs={{0,4},{2,6},{4,0},{6,2},{1,5},{3,7},{5,1},{7,3},{8,12},{10,14},{12... | collective-permute-start | bytes 2359304 | tf_op jit(solution)/shard_map/ppermute | solution.py:1127
  181.0 28.5 %collective-permute-start.18 = (bf16[256,1536]{1,0:T(8,128)(2,1)}, bf16[256,1536]{1,0:T(8,128)(2,1)S(1)}, u32[]{:S(2)}, u32[]{:S(2)}) collective-permute-start(bf16[256,1536]{1,0:T(8,128)(2,1)} %collective-permute-done.9.refs_4_), channel_id=1, source_target_pairs={{0,4},{2,6},{4,0},{6,2},{1,5},{3,7},{5,1},{7,3},{8,12},{10,14},{12... | collective-permute-start | bytes 2359304 | tf_op jit(solution)/shard_map/ppermute | solution.py:1127
  181.7 27.9 %collective-permute-start.19 = (bf16[256,1536]{1,0:T(8,128)(2,1)}, bf16[256,1536]{1,0:T(8,128)(2,1)}, u32[]{:S(2)}, u32[]{:S(2)}) collective-permute-start(bf16[256,1536]{1,0:T(8,128)(2,1)} %collective-permute-done.10.refs_5_), channel_id=1, source_target_pairs={{0,2},{2,0},{4,6},{6,4},{1,3},{3,1},{5,7},{7,5},{8,10},{10,8},{12,... | collective-permute-start | bytes 2359304 | tf_op jit(solution)/shard_map/ppermute | solution.py:1127
  209.5 32.0 %collective-permute-start.21 = (bf16[4,48,1536]{2,1,0:T(8,128)(2,1)}, bf16[4,48,1536]{2,1,0:T(8,128)(2,1)}, u32[]{:S(2)}, u32[]{:S(2)}) collective-permute-start(bf16[4,48,1536]{2,1,0:T(8,128)(2,1)} %slice.425), channel_id=1, source_target_pairs={{0,2},{2,0},{4,6},{6,4},{1,3},{3,1},{5,7},{7,5},{8,10},{10,8},{12,... | collective-permute-start | bytes 1769480 | tf_op jit(solution)/shard_map/ppermute | solution.py:1127
  210.5 31.1 %collective-permute-start.22 = (bf16[4,48,1536]{2,1,0:T(8,128)(2,1)}, bf16[4,48,1536]{2,1,0:T(8,128)(2,1)}, u32[]{:S(2)}, u32[]{:S(2)}) collective-permute-start(bf16[4,48,1536]{2,1,0:T(8,128)(2,1)} %slice.425), channel_id=1, source_target_pairs={{0,4},{2,6},{4,0},{6,2},{1,5},{3,7},{5,1},{7,3},{8,12},{10,14},{12... | collective-permute-start | bytes 1769480 | tf_op jit(solution)/shard_map/ppermute | solution.py:1127
  211.7 29.9 %all-to-all-start.1 = ((bf16[4,192,1024]{2,1,0:T(8,128)(2,1)}), bf16[4,192,1024]{2,1,0:T(8,128)(2,1)}, u32[]{:S(2)}, u32[]{:S(2)}) async-start(bf16[4,192,1024]{2,1,0:T(8,128)(2,1)} %copy-done.10), calls=%async_computation.1 | async-start | bytes 3145728 | tf_op jit(solution)/shard_map/all_to_all | solution.py:1414
  217.4 91.2 %all-gather.7.cloned.1.call-start = ((), (), s32[]{:S(2)}) async-start(), calls=%async_computation.12 | async-start | bytes 3932160 | tf_op jit(solution)/shard_map/all_gather | solution.py:1341
  245.5 317.4 %reduce-scatter.7.cloned.1.call-start = ((), (), s32[]{:S(2)}) async-start(), calls=%async_computation.13 | async-start | bytes 1966080 | tf_op jit(solution)/shard_map/reduce_scatter | solution.py:1523
  246.6 37.9 %collective-permute-start.26 = (bf16[2,48,1536]{2,1,0:T(8,128)(2,1)S(1)}, bf16[2,48,1536]{2,1,0:T(8,128)(2,1)S(1)}, u32[]{:S(2)}, u32[]{:S(2)}) collective-permute-start(bf16[2,48,1536]{2,1,0:T(8,128)(2,1)S(1)} %slice.336), channel_id=1, source_target_pairs={{0,4},{2,6},{4,0},{6,2},{1,5},{3,7},{5,1},{7,3},{8,12},{10,14},{12... | collective-permute-start | bytes 884744 | tf_op jit(solution)/shard_map/ppermute | solution.py:1127
  248.7 35.7 %collective-permute-start.27 = (bf16[2,48,1536]{2,1,0:T(8,128)(2,1)S(1)}, bf16[2,48,1536]{2,1,0:T(8,128)(2,1)S(1)}, u32[]{:S(2)}, u32[]{:S(2)}) collective-permute-start(bf16[2,48,1536]{2,1,0:T(8,128)(2,1)S(1)} %slice.337), channel_id=1, source_target_pairs={{0,2},{2,0},{4,6},{6,4},{1,3},{3,1},{5,7},{7,5},{8,10},{10,8},{12,... | collective-permute-start | bytes 884744 | tf_op jit(solution)/shard_map/ppermute | solution.py:1127
  254.2 30.2 %collective-permute-start.24 = (bf16[256,1536]{1,0:T(8,128)(2,1)S(1)}, bf16[256,1536]{1,0:T(8,128)(2,1)}, u32[]{:S(2)}, u32[]{:S(2)}) collective-permute-start(bf16[256,1536]{1,0:T(8,128)(2,1)S(1)} %get-tuple-element.430), channel_id=1, source_target_pairs={{0,2},{2,0},{4,6},{6,4},{1,3},{3,1},{5,7},{7,5},{8,10},{10,8},{12,... | collective-permute-start | bytes 2359304 | tf_op jit(solution)/shard_map/ppermute | solution.py:1127
  255.4 29.0 %collective-permute-start.25 = (bf16[256,1536]{1,0:T(8,128)(2,1)S(1)}, bf16[256,1536]{1,0:T(8,128)(2,1)}, u32[]{:S(2)}, u32[]{:S(2)}) collective-permute-start(bf16[256,1536]{1,0:T(8,128)(2,1)S(1)} %get-tuple-element.429), channel_id=1, source_target_pairs={{0,4},{2,6},{4,0},{6,2},{1,5},{3,7},{5,1},{7,3},{8,12},{10,14},{12... | collective-permute-start | bytes 2359304 | tf_op jit(solution)/shard_map/ppermute | solution.py:1127
  294.2 33.5 %collective-permute-start.36 = (bf16[256,1536]{1,0:T(8,128)(2,1)}, bf16[256,1536]{1,0:T(8,128)(2,1)}, u32[]{:S(2)}, u32[]{:S(2)}) collective-permute-start(bf16[256,1536]{1,0:T(8,128)(2,1)} %collective-permute-done.9.refs_4_), channel_id=1, source_target_pairs={{0,1},{1,0},{2,3},{3,2},{4,5},{5,4},{6,7},{7,6},{8,9},{9,8},{10,11... | collective-permute-start | bytes 2359304 | tf_op jit(solution)/shard_map/ppermute | solution.py:1106
  294.5 33.7 %collective-permute-start.37 = (bf16[256,1536]{1,0:T(8,128)(2,1)}, bf16[256,1536]{1,0:T(8,128)(2,1)}, u32[]{:S(2)}, u32[]{:S(2)}) collective-permute-start(bf16[256,1536]{1,0:T(8,128)(2,1)} %collective-permute-done.10.refs_5_), channel_id=1, source_target_pairs={{0,1},{1,0},{2,3},{3,2},{4,5},{5,4},{6,7},{7,6},{8,9},{9,8},{10,11... | collective-permute-start | bytes 2359304 | tf_op jit(solution)/shard_map/ppermute | solution.py:1106
  299.3 27.6 %collective-permute-start.32 = (bf16[256,1536]{1,0:T(8,128)(2,1)}, bf16[256,1536]{1,0:T(8,128)(2,1)}, u32[]{:S(2)}, u32[]{:S(2)}) collective-permute-start(bf16[256,1536]{1,0:T(8,128)(2,1)} %get-tuple-element.428), channel_id=1, source_target_pairs={{0,2},{2,0},{4,6},{6,4},{1,3},{3,1},{5,7},{7,5},{8,10},{10,8},{12,... | collective-permute-start | bytes 2359304 | tf_op jit(solution)/shard_map/ppermute | solution.py:1127
  301.6 25.4 %collective-permute-start.33 = (bf16[256,1536]{1,0:T(8,128)(2,1)}, bf16[256,1536]{1,0:T(8,128)(2,1)}, u32[]{:S(2)}, u32[]{:S(2)}) collective-permute-start(bf16[256,1536]{1,0:T(8,128)(2,1)} %get-tuple-element.427), channel_id=1, source_target_pairs={{0,4},{2,6},{4,0},{6,2},{1,5},{3,7},{5,1},{7,3},{8,12},{10,14},{12... | collective-permute-start | bytes 2359304 | tf_op jit(solution)/shard_map/ppermute | solution.py:1127
  327.5 24.4 %collective-permute-start.42 = (bf16[256,1536]{1,0:T(8,128)(2,1)}, bf16[256,1536]{1,0:T(8,128)(2,1)}, u32[]{:S(2)}, u32[]{:S(2)}) collective-permute-start(bf16[256,1536]{1,0:T(8,128)(2,1)} %collective-permute-done.24.refs_4_), channel_id=1, source_target_pairs={{0,1},{1,0},{2,3},{3,2},{4,5},{5,4},{6,7},{7,6},{8,9},{9,8},{10,11... | collective-permute-start | bytes 2359304 | tf_op jit(solution)/shard_map/ppermute | solution.py:1106
  327.7 24.7 %collective-permute-start.43 = (bf16[256,1536]{1,0:T(8,128)(2,1)}, bf16[256,1536]{1,0:T(8,128)(2,1)}, u32[]{:S(2)}, u32[]{:S(2)}) collective-permute-start(bf16[256,1536]{1,0:T(8,128)(2,1)} %collective-permute-done.25.refs_5_), channel_id=1, source_target_pairs={{0,1},{1,0},{2,3},{3,2},{4,5},{5,4},{6,7},{7,6},{8,9},{9,8},{10,11... | collective-permute-start | bytes 2359304 | tf_op jit(solution)/shard_map/ppermute | solution.py:1106
  328.2 21.5 %collective-permute-start.38 = (bf16[256,1536]{1,0:T(8,128)(2,1)S(1)}, bf16[256,1536]{1,0:T(8,128)(2,1)}, u32[]{:S(2)}, u32[]{:S(2)}) collective-permute-start(bf16[256,1536]{1,0:T(8,128)(2,1)S(1)} %get-tuple-element.426), channel_id=1, source_target_pairs={{0,2},{2,0},{4,6},{6,4},{1,3},{3,1},{5,7},{7,5},{8,10},{10,8},{12,... | collective-permute-start | bytes 2359304 | tf_op jit(solution)/shard_map/ppermute | solution.py:1127
  351.8 22.4 %collective-permute-start.50 = (bf16[512,1536]{1,0:T(8,128)(2,1)S(1)}, bf16[512,1536]{1,0:T(8,128)(2,1)S(1)}, u32[]{:S(2)}, u32[]{:S(2)}) collective-permute-start(bf16[512,1536]{1,0:T(8,128)(2,1)S(1)} %slice_bitcast_fusion.8), channel_id=1, source_target_pairs={{0,1},{1,0},{2,3},{3,2},{4,5},{5,4},{6,7},{7,6},{8,9},{9,8},{10,11... | collective-permute-start | bytes 4718600 | tf_op jit(solution)/shard_map/ppermute | solution.py:1106
  351.9 24.8 %collective-permute-start.48 = (bf16[256,1536]{1,0:T(8,128)(2,1)S(1)}, bf16[256,1536]{1,0:T(8,128)(2,1)}, u32[]{:S(2)}, u32[]{:S(2)}) collective-permute-start(bf16[256,1536]{1,0:T(8,128)(2,1)S(1)} %copy-done.70), channel_id=1, source_target_pairs={{0,1},{1,0},{2,3},{3,2},{4,5},{5,4},{6,7},{7,6},{8,9},{9,8},{10,11... | collective-permute-start | bytes 2359304 | tf_op jit(solution)/shard_map/ppermute | solution.py:1106
  352.4 25.4 %collective-permute-start.49 = (bf16[256,1536]{1,0:T(8,128)(2,1)}, bf16[256,1536]{1,0:T(8,128)(2,1)}, u32[]{:S(2)}, u32[]{:S(2)}) collective-permute-start(bf16[256,1536]{1,0:T(8,128)(2,1)} %collective-permute-done.19.refs_5_), channel_id=1, source_target_pairs={{0,1},{1,0},{2,3},{3,2},{4,5},{5,4},{6,7},{7,6},{8,9},{9,8},{10,11... | collective-permute-start | bytes 2359304 | tf_op jit(solution)/shard_map/ppermute | solution.py:1106
  352.5 20.3 %collective-permute-start.44 = (bf16[256,1536]{1,0:T(8,128)(2,1)}, bf16[256,1536]{1,0:T(8,128)(2,1)}, u32[]{:S(2)}, u32[]{:S(2)}) collective-permute-start(bf16[256,1536]{1,0:T(8,128)(2,1)} %collective-permute-done.32.refs_0_), channel_id=1, source_target_pairs={{0,4},{2,6},{4,0},{6,2},{1,5},{3,7},{5,1},{7,3},{8,12},{10,14},{12... | collective-permute-start | bytes 2359304 | tf_op jit(solution)/shard_map/ppermute | solution.py:1127
  353.7 19.9 %collective-permute-start.45 = (bf16[256,1536]{1,0:T(8,128)(2,1)}, bf16[256,1536]{1,0:T(8,128)(2,1)}, u32[]{:S(2)}, u32[]{:S(2)}) collective-permute-start(bf16[256,1536]{1,0:T(8,128)(2,1)} %collective-permute-done.33.refs_1_), channel_id=1, source_target_pairs={{0,2},{2,0},{4,6},{6,4},{1,3},{3,1},{5,7},{7,5},{8,10},{10,8},{12,... | collective-permute-start | bytes 2359304 | tf_op jit(solution)/shard_map/ppermute | solution.py:1127
  376.0 20.1 %collective-permute-start.51 = (bf16[256,1536]{1,0:T(8,128)(2,1)S(1)}, bf16[256,1536]{1,0:T(8,128)(2,1)S(1)}, u32[]{:S(2)}, u32[]{:S(2)}) collective-permute-start(bf16[256,1536]{1,0:T(8,128)(2,1)S(1)} %get-tuple-element.424), channel_id=1, source_target_pairs={{0,2},{2,0},{4,6},{6,4},{1,3},{3,1},{5,7},{7,5},{8,10},{10,8},{12,... | collective-permute-start | bytes 2359304 | tf_op jit(solution)/shard_map/ppermute | solution.py:1127
  400.9 25.0 %collective-permute-start.31 = (bf16[512,1536]{1,0:T(8,128)(2,1)}, bf16[512,1536]{1,0:T(8,128)(2,1)}, u32[]{:S(2)}, u32[]{:S(2)}) collective-permute-start(bf16[512,1536]{1,0:T(8,128)(2,1)} %slice_bitcast_fusion.9), channel_id=1, source_target_pairs={{0,1},{1,0},{2,3},{3,2},{4,5},{5,4},{6,7},{7,6},{8,9},{9,8},{10,11... | collective-permute-start | bytes 4718600 | tf_op jit(solution)/shard_map/ppermute | solution.py:1106
  402.7 27.4 %collective-permute-start.53 = (bf16[512,1536]{1,0:T(8,128)(2,1)}, bf16[512,1536]{1,0:T(8,128)(2,1)}, u32[]{:S(2)}, u32[]{:S(2)}) collective-permute-start(bf16[512,1536]{1,0:T(8,128)(2,1)} %slice_bitcast_fusion.7), channel_id=1, source_target_pairs={{0,1},{1,0},{2,3},{3,2},{4,5},{5,4},{6,7},{7,6},{8,9},{9,8},{10,11... | collective-permute-start | bytes 4718600 | tf_op jit(solution)/shard_map/ppermute | solution.py:1106
  425.6 162.0 %reduce-scatter.9.cloned.1.call-start = ((), (), s32[]{:S(2)}) async-start(), calls=%async_computation.14 | async-start | bytes 3932160 | tf_op jit(solution)/shard_map/reduce_scatter | solution.py:1524
  433.6 22.5 %collective-permute-start.57 = (bf16[256,1536]{1,0:T(8,128)(2,1)}, bf16[256,1536]{1,0:T(8,128)(2,1)S(1)}, u32[]{:S(2)}, u32[]{:S(2)}) collective-permute-start(bf16[256,1536]{1,0:T(8,128)(2,1)} %get-tuple-element.404), channel_id=1, source_target_pairs={{0,2},{2,0},{4,6},{6,4},{1,3},{3,1},{5,7},{7,5},{8,10},{10,8},{12,... | collective-permute-start | bytes 2359304 | tf_op jit(solution)/shard_map/ppermute | solution.py:1127
  434.3 21.8 %collective-permute-start.58 = (bf16[256,1536]{1,0:T(8,128)(2,1)}, bf16[256,1536]{1,0:T(8,128)(2,1)S(1)}, u32[]{:S(2)}, u32[]{:S(2)}) collective-permute-start(bf16[256,1536]{1,0:T(8,128)(2,1)} %get-tuple-element.403), channel_id=1, source_target_pairs={{0,4},{2,6},{4,0},{6,2},{1,5},{3,7},{5,1},{7,3},{8,12},{10,14},{12... | collective-permute-start | bytes 2359304 | tf_op jit(solution)/shard_map/ppermute | solution.py:1127
  459.4 243.7 %reduce-scatter.15.cloned.1.call-start = ((), (), s32[]{:S(2)}) async-start(), calls=%async_computation.17 | async-start | bytes 2949120 | tf_op jit(solution)/shard_map/reduce_scatter | solution.py:1529
  470.2 21.8 %collective-permute-start.63 = (bf16[512,1536]{1,0:T(8,128)(2,1)}, bf16[512,1536]{1,0:T(8,128)(2,1)}, u32[]{:S(2)}, u32[]{:S(2)}) collective-permute-start(bf16[512,1536]{1,0:T(8,128)(2,1)} %slice_bitcast_fusion.4), channel_id=1, source_target_pairs={{0,1},{1,0},{2,3},{3,2},{4,5},{5,4},{6,7},{7,6},{8,9},{9,8},{10,11... | collective-permute-start | bytes 4718600 | tf_op jit(solution)/shard_map/ppermute | solution.py:1106
  474.8 20.6 %collective-permute-start.65 = (bf16[256,1536]{1,0:T(8,128)(2,1)}, bf16[256,1536]{1,0:T(8,128)(2,1)}, u32[]{:S(2)}, u32[]{:S(2)}) collective-permute-start(bf16[256,1536]{1,0:T(8,128)(2,1)} %get-tuple-element.418), channel_id=1, source_target_pairs={{0,2},{2,0},{4,6},{6,4},{1,3},{3,1},{5,7},{7,5},{8,10},{10,8},{12,... | collective-permute-start | bytes 2359304 | tf_op jit(solution)/shard_map/ppermute | solution.py:1127
  476.1 20.7 %collective-permute-start.66 = (bf16[256,1536]{1,0:T(8,128)(2,1)}, bf16[256,1536]{1,0:T(8,128)(2,1)}, u32[]{:S(2)}, u32[]{:S(2)}) collective-permute-start(bf16[256,1536]{1,0:T(8,128)(2,1)} %get-tuple-element.417), channel_id=1, source_target_pairs={{0,4},{2,6},{4,0},{6,2},{1,5},{3,7},{5,1},{7,3},{8,12},{10,14},{12... | collective-permute-start | bytes 2359304 | tf_op jit(solution)/shard_map/ppermute | solution.py:1127
  490.2 43.1 %collective-permute-start.61 = (bf16[256,1536]{1,0:T(8,128)(2,1)}, bf16[256,1536]{1,0:T(8,128)(2,1)S(1)}, u32[]{:S(2)}, u32[]{:S(2)}) collective-permute-start(bf16[256,1536]{1,0:T(8,128)(2,1)} %get-tuple-element.420), channel_id=1, source_target_pairs={{0,2},{2,0},{4,6},{6,4},{1,3},{3,1},{5,7},{7,5},{8,10},{10,8},{12,... | collective-permute-start | bytes 2359304 | tf_op jit(solution)/shard_map/ppermute | solution.py:1127
  490.6 42.7 %collective-permute-start.62 = (bf16[256,1536]{1,0:T(8,128)(2,1)}, bf16[256,1536]{1,0:T(8,128)(2,1)S(1)}, u32[]{:S(2)}, u32[]{:S(2)}) collective-permute-start(bf16[256,1536]{1,0:T(8,128)(2,1)} %get-tuple-element.419), channel_id=1, source_target_pairs={{0,4},{2,6},{4,0},{6,2},{1,5},{3,7},{5,1},{7,3},{8,12},{10,14},{12... | collective-permute-start | bytes 2359304 | tf_op jit(solution)/shard_map/ppermute | solution.py:1127
  498.6 34.7 %collective-permute-start.67 = (bf16[256,1536]{1,0:T(8,128)(2,1)S(1)}, bf16[256,1536]{1,0:T(8,128)(2,1)S(1)}, u32[]{:S(2)}, u32[]{:S(2)}) collective-permute-start(bf16[256,1536]{1,0:T(8,128)(2,1)S(1)} %get-tuple-element.400), channel_id=1, source_target_pairs={{0,2},{2,0},{4,6},{6,4},{1,3},{3,1},{5,7},{7,5},{8,10},{10,8},{12,... | collective-permute-start | bytes 2359304 | tf_op jit(solution)/shard_map/ppermute | solution.py:1127
  499.4 33.9 %collective-permute-start.68 = (bf16[256,1536]{1,0:T(8,128)(2,1)S(1)}, bf16[256,1536]{1,0:T(8,128)(2,1)S(1)}, u32[]{:S(2)}, u32[]{:S(2)}) collective-permute-start(bf16[256,1536]{1,0:T(8,128)(2,1)S(1)} %get-tuple-element.399), channel_id=1, source_target_pairs={{0,4},{2,6},{4,0},{6,2},{1,5},{3,7},{5,1},{7,3},{8,12},{10,14},{12... | collective-permute-start | bytes 2359304 | tf_op jit(solution)/shard_map/ppermute | solution.py:1127
  551.0 30.8 %all-to-all-start.2 = ((bf16[4,192,1024]{2,1,0:T(8,128)(2,1)}), bf16[4,192,1024]{2,1,0:T(8,128)(2,1)}, u32[]{:S(2)}, u32[]{:S(2)}) async-start(bf16[4,192,1024]{2,1,0:T(8,128)(2,1)} %bitcast.50), calls=%async_computation.2 | async-start | bytes 3145728 | tf_op jit(solution)/shard_map/all_to_all | solution.py:1559
  581.8 58.0 %all-to-all-start.3 = ((bf16[4,576,1024]{2,1,0:T(8,128)(2,1)}), bf16[4,576,1024]{2,1,0:T(8,128)(2,1)}, u32[]{:S(2)}, u32[]{:S(2)}) async-start(bf16[4,576,1024]{2,1,0:T(8,128)(2,1)} %bitcast.210), calls=%async_computation.5 | async-start | bytes 9437184 | tf_op jit(solution)/shard_map/all_to_all | solution.py:1560
  586.8 125.3 %reduce-scatter.13.cloned.1.call-start = ((), (), s32[]{:S(2)}) async-start(), calls=%async_computation.16 | async-start | bytes 6389760 | tf_op jit(solution)/shard_map/reduce_scatter | solution.py:1567
  587.5 135.2 %reduce-scatter.11.cloned.1.call-start = ((), (), s32[]{:S(2)}) async-start(), calls=%async_computation.15 | async-start | bytes 2273280 | tf_op jit(solution)/shard_map/reduce_scatter | solution.py:1601
  662.5 22.1 %collective-permute-start.72 = (bf16[3,512,1536]{2,1,0:T(8,128)(2,1)}, bf16[3,512,1536]{2,1,0:T(8,128)(2,1)}, u32[]{:S(2)}, u32[]{:S(2)}) collective-permute-start(bf16[3,512,1536]{2,1,0:T(8,128)(2,1)} %get-tuple-element.285), channel_id=1, source_target_pairs={{0,1},{1,0},{2,3},{3,2},{4,5},{5,4},{6,7},{7,6},{8,9},{9,8},{10,11... | collective-permute-start | bytes 14155784 | tf_op jit(solution)/shard_map/ppermute | solution.py:1106
  684.6 67.9 %reduce-scatter.17.cloned.1.call-start = ((), (), s32[]{:S(2)}) async-start(), calls=%async_computation.18 | async-start | bytes 737280 | tf_op jit(solution)/shard_map/reduce_scatter | solution.py:1607
  690.3 37.5 %collective-permute-start.76 = (bf16[512,1536]{1,0:T(8,128)(2,1)}, bf16[512,1536]{1,0:T(8,128)(2,1)S(1)}, u32[]{:S(2)}, u32[]{:S(2)}) collective-permute-start(bf16[512,1536]{1,0:T(8,128)(2,1)} %pad_maximum_fusion.10), channel_id=1, source_target_pairs={{0,4},{2,6},{4,0},{6,2},{1,5},{3,7},{5,1},{7,3},{8,12},{10,14},{12... | collective-permute-start | bytes 4718600 | tf_op jit(solution)/shard_map/ppermute | solution.py:1127
  693.4 37.6 %collective-permute-start.75 = (bf16[512,1536]{1,0:T(8,128)(2,1)}, bf16[512,1536]{1,0:T(8,128)(2,1)}, u32[]{:S(2)}, u32[]{:S(2)}) collective-permute-start(bf16[512,1536]{1,0:T(8,128)(2,1)} %pad_maximum_fusion.9), channel_id=1, source_target_pairs={{0,2},{2,0},{4,6},{6,4},{1,3},{3,1},{5,7},{7,5},{8,10},{10,8},{12,... | collective-permute-start | bytes 4718600 | tf_op jit(solution)/shard_map/ppermute | solution.py:1127
  708.9 43.7 %collective-permute-start.87 = (f32[16,2]{0,1:T(2,128)S(1)}, f32[16,2]{0,1:T(2,128)S(1)}, u32[]{:S(2)}, u32[]{:S(2)}) collective-permute-start(f32[16,2]{0,1:T(2,128)S(1)} %add.313), channel_id=1, source_target_pairs={{0,2},{2,0},{4,6},{6,4},{1,3},{3,1},{5,7},{7,5},{8,10},{10,8},{12,... | collective-permute-start | bytes 392 | tf_op jit(solution)/shard_map/ppermute | solution.py:1198
  715.9 22.1 %collective-permute-start.77 = (bf16[48,2432]{1,0:T(8,128)(2,1)}, bf16[48,2432]{1,0:T(8,128)(2,1)}, u32[]{:S(2)}, u32[]{:S(2)}) collective-permute-start(bf16[48,2432]{1,0:T(8,128)(2,1)} %get-tuple-element.410), channel_id=1, source_target_pairs={{0,4},{2,6},{4,0},{6,2},{1,5},{3,7},{5,1},{7,3},{8,12},{10,14},{12... | collective-permute-start | bytes 700424 | tf_op jit(solution)/shard_map/ppermute | solution.py:1127
  716.4 21.6 %collective-permute-start.79 = (bf16[48,2432]{1,0:T(8,128)(2,1)}, bf16[48,2432]{1,0:T(8,128)(2,1)}, u32[]{:S(2)}, u32[]{:S(2)}) collective-permute-start(bf16[48,2432]{1,0:T(8,128)(2,1)} %get-tuple-element.412), channel_id=1, source_target_pairs={{0,2},{2,0},{4,6},{6,4},{1,3},{3,1},{5,7},{7,5},{8,10},{10,8},{12,... | collective-permute-start | bytes 700424 | tf_op jit(solution)/shard_map/ppermute | solution.py:1127
  733.5 47.5 %all-to-all-start.4 = ((bf16[8,48,1616]{2,1,0:T(8,128)(2,1)}), bf16[8,48,1616]{2,1,0:T(8,128)(2,1)S(1)}, u32[]{:S(2)}, u32[]{:S(2)}) async-start(bf16[8,48,1616]{2,1,0:T(8,128)(2,1)} %pad_maximum_fusion.11), calls=%async_computation.7 | async-start | bytes 2555904 | tf_op jit(solution)/shard_map/all_to_all | solution.py:1630
  741.2 24.6 %collective-permute-start.80 = (bf16[96,2432]{1,0:T(8,128)(2,1)}, bf16[96,2432]{1,0:T(8,128)(2,1)}, u32[]{:S(2)}, u32[]{:S(2)}) collective-permute-start(bf16[96,2432]{1,0:T(8,128)(2,1)} %pad_maximum_fusion.15), channel_id=1, source_target_pairs={{0,4},{2,6},{4,0},{6,2},{1,5},{3,7},{5,1},{7,3},{8,12},{10,14},{12... | collective-permute-start | bytes 1400840 | tf_op jit(solution)/shard_map/ppermute | solution.py:1127
  743.5 22.3 %collective-permute-start.78 = (bf16[96,2432]{1,0:T(8,128)(2,1)}, bf16[96,2432]{1,0:T(8,128)(2,1)S(1)}, u32[]{:S(2)}, u32[]{:S(2)}) collective-permute-start(bf16[96,2432]{1,0:T(8,128)(2,1)} %pad_maximum_fusion.14), channel_id=1, source_target_pairs={{0,2},{2,0},{4,6},{6,4},{1,3},{3,1},{5,7},{7,5},{8,10},{10,8},{12,... | collective-permute-start | bytes 1400840 | tf_op jit(solution)/shard_map/ppermute | solution.py:1127
  (132 other events, 1819.5 us)
Sparse Core Ops, SparseCore 0:
  16.0 130.0 all-gather.4
  156.7 46.5 all-gather.8
  245.6 62.9 all-gather.6
  425.7 33.4 reduce-scatter.6
  461.4 59.2 reduce-scatter.8
  522.8 48.0 reduce-scatter.14
  589.9 90.1 reduce-scatter.12
  684.7 37.9 reduce-scatter.10
  725.6 21.1 reduce-scatter.16
